TPU v7x, 32 devices: a whole 2x2x4 slice. The times are simulated.
32 devices in a mesh: seq: 16 (over z, y, x), batch: 2 (over core).
Axes of the slice: x: 2, y: 2, z: 4, core: 2. Of those that a mesh axis runs over, the one named last changes fastest.
Arguments:
- tokens: bfloat16 [4, 1024, 2304], P('batch', 'seq'), may hold values from -6 to 6
- segments: int32 [4, 1024], P('batch', 'seq'), may hold values from 0 to 8, as said below
- positions: int32 [4, 1024], P('batch', 'seq'), may hold values from 0 to 1023, as said below
- cotangent: bfloat16 [4, 1024, 2304], P('batch', 'seq'), may hold values from -6 to 6
- query_codes: int32 [2304, 2048], P('seq'), may hold values from -128 to 127
- key_codes: int32 [2304, 1024], P('seq'), may hold values from -128 to 127
- value_codes: int32 [2304, 1024], P('seq'), may hold values from -128 to 127
- output_codes: int32 [2048, 2304], P('seq'), may hold values from -128 to 127
- gate_codes: int32 [2304, 9216], P('seq'), may hold values from -128 to 127
- up_codes: int32 [2304, 9216], P('seq'), may hold values from -128 to 127
- down_codes: int32 [9216, 2304], P('seq'), may hold values from -128 to 127
- query_scale: float32 [2048], replicated, may hold values from 0.00014 to 0.0014
- key_scale: float32 [1024], replicated, may hold values from 0.00014 to 0.0014
- value_scale: float32 [1024], replicated, may hold values from 0.00014 to 0.00056
- output_scale: float32 [2304], replicated, may hold values from 0.00015 to 0.0006
- gate_scale: float32 [9216], replicated, may hold values from 0.00014 to 0.00056
- up_scale: float32 [9216], replicated, may hold values from 0.00014 to 0.00056
- down_scale: float32 [2304], replicated, may hold values from 7e-05 to 0.00028
- attention_gain: float32 [2304], replicated, may hold values from 0.1 to 1.9
- attention_post_gain: float32 [2304], replicated, may hold values from 0.1 to 1.9
- feed_gain: float32 [2304], replicated, may hold values from 0.1 to 1.9
- feed_post_gain: float32 [2304], replicated, may hold values from 0.1 to 1.9
Outputs:
- out_tokens: bfloat16 [4, 1024, 2304], P('batch', 'seq')
- grad_tokens: bfloat16 [4, 1024, 2304], P('batch', 'seq')
- grad_query: float32 [2304, 2048], P('seq')
- grad_key: float32 [2304, 1024], P('seq')
- grad_value: float32 [2304, 1024], P('seq')
- grad_output: float32 [2048, 2304], P('seq')
- grad_gate: float32 [2304, 9216], P('seq')
- grad_up: float32 [2304, 9216], P('seq')
- grad_down: float32 [9216, 2304], P('seq')
- grad_attention_gain: float32 [2304], replicated
- grad_attention_post: float32 [2304], replicated
- grad_feed_gain: float32 [2304], replicated
- grad_feed_post: float32 [2304], replicated
Inputs may be any that keep to these rules, and one draw needn't show every extreme that they name: `segments`: along each sequence the numbers start at 0, never fall and rise by one where a document begins; in each group of 2 sequences on one index of batch, one sequence is a single document, and the other sequence holds exactly 9 documents. `positions`: A token's index in its sequence minus the index of the first token of its document (the first token with the same segment number).
All inputs are finite; a program needn't handle non-finite values.
Results may differ from a plain program's by a relative error of at most 0.024.
Values may be sent and summed in bfloat16 or wider, within the bound.
A program may use at most 1.1875 GiB of HBM per device.

v0:
```python
import jax
import jax.numpy as jnp
from jax import lax
from jax.sharding import PartitionSpec as P

D = 2304
HEADS = 8
KV_HEADS = 4
HEAD = 256
FF = 9216


cap_limit = 50.0


def normed(value, gain):
    return value * lax.rsqrt(jnp.mean(value * value, axis=-1, keepdims=True) + 1e-06) * gain


def angles(places, head):
    freqs = 10000.0 ** (-(jnp.arange(head // 2, dtype=jnp.float32) * 2.0 / head))
    return places.astype(jnp.float32)[..., None] * freqs


def rotate(values, turn, sign):
    cosine = jnp.cos(turn)[..., None, :]
    sine = sign * jnp.sin(turn)[..., None, :]
    half = values.shape[-1] // 2
    first = values[..., :half]
    second = values[..., half:]
    return jnp.concatenate(
        [first * cosine - second * sine, second * cosine + first * sine], axis=-1
    )


def levels(codes, step):
    offset = jnp.where(step > 1.0, 0.5 * step, 0.0)
    return jnp.floor(codes / step) * step + offset


def width_step(number):
    remainder = number % 3
    return jnp.where(remainder == 0, 1.0, jnp.where(remainder == 1, 16.0, 64.0)).astype(jnp.float32)


def dequantized(piece, column_scale, step):
    return (levels(piece.astype(jnp.float32), step) * column_scale[None, :]).astype(jnp.bfloat16)


def forward_product(rows, codes, column_scale, steps):
    piece = lax.all_gather(codes, "seq", axis=0, tiled=True)
    outs = [
        jnp.dot(
            rows[member],
            dequantized(piece, column_scale, steps[member]),
            preferred_element_type=jnp.float32,
        )
        for member in range(len(steps))
    ]
    return (jnp.stack(outs), codes)


def backward_product(grads, codes, column_scale, steps):
    piece = lax.all_gather(codes, "seq", axis=0, tiled=True)
    outs = [
        lax.dot_general(
            grads[member],
            dequantized(piece, column_scale, steps[member]),
            (((1,), (1,)), ((), ())),
            preferred_element_type=jnp.float32,
        )
        for member in range(len(steps))
    ]
    return jnp.stack(outs)


def weight_terms(left, right):
    return lax.psum_scatter(
        lax.dot_general(left, right, (((0,), (0,)), ((), ())), preferred_element_type=jnp.float32),
        "seq",
        scatter_dimension=0,
        tiled=True,
    )


def on_device(
    tokens,
    segments,
    positions,
    cotangent,
    query_codes,
    key_codes,
    value_codes,
    output_codes,
    gate_codes,
    up_codes,
    down_codes,
    query_scale,
    key_scale,
    value_scale,
    output_scale,
    gate_scale,
    up_scale,
    down_scale,
    attention_gain,
    attention_post_gain,
    feed_gain,
    feed_post_gain,
):
    group, block, width = tokens.shape
    q_width = HEADS * HEAD
    kv_width = KV_HEADS * HEAD
    pairs = HEADS // KV_HEADS
    scale = HEAD ** (-0.5)
    steps = [width_step(lax.axis_index("batch") * group + member) for member in range(group)]
    first_index = lax.axis_index("seq") * block
    token_index = first_index + jnp.arange(block, dtype=jnp.int32)
    turn = angles(positions, HEAD)
    source = tokens.astype(jnp.float32)
    first_normed = normed(source, attention_gain).astype(jnp.bfloat16)
    qkv_codes = jnp.concatenate([query_codes, key_codes, value_codes], axis=1).astype(jnp.bfloat16)
    qkv_scale = jnp.concatenate([query_scale, key_scale, value_scale])
    projected, qkv_kept = forward_product(first_normed, qkv_codes, qkv_scale, steps)
    queries = (
        rotate(projected[..., :q_width].reshape(group, block, HEADS, HEAD), turn, 1.0)
        .astype(jnp.bfloat16)
        .reshape(group, block, KV_HEADS, pairs, HEAD)
    )
    keys = rotate(
        projected[..., q_width : q_width + kv_width].reshape(group, block, KV_HEADS, HEAD),
        turn,
        1.0,
    ).astype(jnp.bfloat16)
    values = (
        projected[..., q_width + kv_width :]
        .reshape(group, block, KV_HEADS, HEAD)
        .astype(jnp.bfloat16)
    )
    key_rows = jnp.transpose(keys, (1, 0, 2, 3))
    value_rows = jnp.transpose(values, (1, 0, 2, 3))
    segment_rows = segments.T
    piece_keys = lax.all_gather(key_rows, "seq", axis=0, tiled=True)
    piece_values = lax.all_gather(value_rows, "seq", axis=0, tiled=True)
    piece_segments = lax.all_gather(segment_rows, "seq", axis=0, tiled=True)
    count = piece_keys.shape[0]
    key_index = jnp.arange(count, dtype=jnp.int32)
    raw = (
        jnp.einsum("sqgjd,ksgd->sqgjk", queries, piece_keys, preferred_element_type=jnp.float32)
        * scale
    )
    allowed = (segments[:, :, None] == piece_segments.T[:, None, :]) & (
        key_index[None, None, :] <= token_index[None, :, None]
    )
    kernel = jnp.where(
        allowed[:, :, None, None, :], jnp.exp(cap_limit * jnp.tanh(raw / cap_limit)), 0.0
    )
    summed = jnp.einsum(
        "sqgjk,ksgd->sqgjd",
        kernel.astype(jnp.bfloat16),
        piece_values,
        preferred_element_type=jnp.float32,
    )
    totals = jnp.sum(kernel, axis=-1)
    attended = summed / totals[..., None]
    attended_low = attended.reshape(group, block, q_width).astype(jnp.bfloat16)
    attention_raw, output_kept = forward_product(
        attended_low, output_codes.astype(jnp.bfloat16), output_scale, steps
    )
    mixed = source + normed(attention_raw, attention_post_gain)
    second_normed = normed(mixed, feed_gain).astype(jnp.bfloat16)
    pair_codes = jnp.concatenate([gate_codes, up_codes], axis=1).astype(jnp.bfloat16)
    pair_scale = jnp.concatenate([gate_scale, up_scale])
    gate_up, pair_kept = forward_product(second_normed, pair_codes, pair_scale, steps)
    gate = gate_up[..., :FF]
    upward = gate_up[..., FF:]
    hidden = (jax.nn.gelu(gate, approximate=True) * upward).astype(jnp.bfloat16)
    down_raw, down_kept = forward_product(
        hidden, down_codes.astype(jnp.bfloat16), down_scale, steps
    )
    branch, pull_out = jax.vjp(normed, down_raw, feed_post_gain)
    output = (mixed + branch).astype(jnp.bfloat16)
    upstream = cotangent.astype(jnp.float32)
    grad_down_raw, grad_post_feed = pull_out(upstream)
    down_low = grad_down_raw.astype(jnp.bfloat16)
    grad_hidden = backward_product(down_low, down_kept, down_scale, steps)
    _, pull_glu = jax.vjp(
        lambda left, right: jax.nn.gelu(left, approximate=True) * right, gate, upward
    )
    grad_gate, grad_upward = pull_glu(grad_hidden)
    pair_low = jnp.concatenate([grad_gate, grad_upward], axis=-1).astype(jnp.bfloat16)
    grad_second = backward_product(pair_low, pair_kept, pair_scale, steps)
    _, pull_feed = jax.vjp(normed, mixed, feed_gain)
    grad_mixed_part, grad_pre_feed = pull_feed(grad_second)
    grad_mixed = upstream + grad_mixed_part
    _, pull_post = jax.vjp(normed, attention_raw, attention_post_gain)
    grad_attention, grad_post_attention = pull_post(grad_mixed)
    attention_low = grad_attention.astype(jnp.bfloat16)
    grad_attended = backward_product(attention_low, output_kept, output_scale, steps).reshape(
        group, block, KV_HEADS, pairs, HEAD
    )
    grad_sums = (grad_attended / totals[..., None]).astype(jnp.bfloat16)
    offsets = jnp.sum(grad_attended * attended, axis=-1) / totals
    all_keys, all_values, all_segments = (
        lax.all_gather(key_rows, "seq", axis=0, tiled=True),
        lax.all_gather(value_rows, "seq", axis=0, tiled=True),
        lax.all_gather(segment_rows, "seq", axis=0, tiled=True),
    )
    length = all_keys.shape[0]
    step_keys = min(512, length)
    rounds = length // step_keys

    def back_block(grad_queries, items):
        piece_keys, piece_values, piece_segments, begin = items
        key_index = begin + jnp.arange(step_keys, dtype=jnp.int32)
        raw = (
            jnp.einsum("sqgjd,ksgd->sqgjk", queries, piece_keys, preferred_element_type=jnp.float32)
            * scale
        )
        bent = jnp.tanh(raw / cap_limit)
        allowed = (segments[:, :, None] == piece_segments.T[:, None, :]) & (
            key_index[None, None, :] <= token_index[None, :, None]
        )
        kernel = jnp.where(allowed[:, :, None, None, :], jnp.exp(cap_limit * bent), 0.0)
        grad_kernel = (
            jnp.einsum(
                "sqgjd,ksgd->sqgjk", grad_sums, piece_values, preferred_element_type=jnp.float32
            )
            - offsets[..., None]
        )
        grad_raw = (kernel * grad_kernel * (1.0 - bent * bent)).astype(jnp.bfloat16)
        grad_queries = (
            grad_queries
            + jnp.einsum(
                "sqgjk,ksgd->sqgjd", grad_raw, piece_keys, preferred_element_type=jnp.float32
            )
            * scale
        )
        grad_keys = (
            jnp.einsum("sqgjk,sqgjd->ksgd", grad_raw, queries, preferred_element_type=jnp.float32)
            * scale
        )
        grad_values = jnp.einsum(
            "sqgjk,sqgjd->ksgd",
            kernel.astype(jnp.bfloat16),
            grad_sums,
            preferred_element_type=jnp.float32,
        )
        return (grad_queries, (grad_keys, grad_values))

    scan_items = (
        all_keys.reshape(rounds, step_keys, group, KV_HEADS, HEAD),
        all_values.reshape(rounds, step_keys, group, KV_HEADS, HEAD),
        all_segments.reshape(rounds, step_keys, group),
        jnp.arange(rounds, dtype=jnp.int32) * step_keys,
    )
    grad_queries, (key_terms, value_terms) = lax.scan(
        back_block, jnp.zeros((group, block, KV_HEADS, pairs, HEAD), jnp.float32), scan_items
    )
    own_keys, own_values = (
        lax.psum_scatter(
            key_terms.reshape(length, group, KV_HEADS, HEAD), "seq", scatter_dimension=0, tiled=True
        ),
        lax.psum_scatter(
            value_terms.reshape(length, group, KV_HEADS, HEAD),
            "seq",
            scatter_dimension=0,
            tiled=True,
        ),
    )
    grad_query_lin = rotate(grad_queries.reshape(group, block, HEADS, HEAD), turn, -1.0).reshape(
        group, block, q_width
    )
    grad_key_lin = rotate(jnp.transpose(own_keys, (1, 0, 2, 3)), turn, -1.0).reshape(
        group, block, kv_width
    )
    grad_value_lin = jnp.transpose(own_values, (1, 0, 2, 3)).reshape(group, block, kv_width)
    qkv_low = jnp.concatenate([grad_query_lin, grad_key_lin, grad_value_lin], axis=-1).astype(
        jnp.bfloat16
    )
    grad_first = backward_product(qkv_low, qkv_kept, qkv_scale, steps)
    _, pull_in = jax.vjp(normed, source, attention_gain)
    grad_source_part, grad_pre_attention = pull_in(grad_first)
    grad_in = (grad_mixed + grad_source_part).astype(jnp.bfloat16)
    rows_total = group * block
    qkv_grad = weight_terms(
        first_normed.reshape(rows_total, D), qkv_low.reshape(rows_total, q_width + 2 * kv_width)
    )
    out_grad = weight_terms(
        attended_low.reshape(rows_total, q_width), attention_low.reshape(rows_total, D)
    )
    pair_grad = weight_terms(
        second_normed.reshape(rows_total, D), pair_low.reshape(rows_total, 2 * FF)
    )
    down_grad = weight_terms(hidden.reshape(rows_total, FF), down_low.reshape(rows_total, D))
    qkv_grad, out_grad, pair_grad, down_grad = (
        lax.psum(qkv_grad.astype(jnp.bfloat16), "batch").astype(jnp.float32),
        lax.psum(out_grad.astype(jnp.bfloat16), "batch").astype(jnp.float32),
        lax.psum(pair_grad.astype(jnp.bfloat16), "batch").astype(jnp.float32),
        lax.psum(down_grad.astype(jnp.bfloat16), "batch").astype(jnp.float32),
    )
    gain_first, gain_second, gain_third, gain_fourth = lax.psum(
        (grad_pre_attention, grad_post_attention, grad_pre_feed, grad_post_feed), ("seq", "batch")
    )
    return (
        output,
        grad_in,
        qkv_grad[:, :q_width],
        qkv_grad[:, q_width : q_width + kv_width],
        qkv_grad[:, q_width + kv_width :],
        out_grad,
        pair_grad[:, :FF],
        pair_grad[:, FF:],
        down_grad,
        gain_first,
        gain_second,
        gain_third,
        gain_fourth,
    )


def solution(mesh):
    return jax.shard_map(
        on_device,
        mesh=mesh,
        in_specs=(
            P("batch", "seq", None),
            P("batch", "seq"),
            P("batch", "seq"),
            P("batch", "seq", None),
            P("seq", None),
            P("seq", None),
            P("seq", None),
            P("seq", None),
            P("seq", None),
            P("seq", None),
            P("seq", None),
            P(),
            P(),
            P(),
            P(),
            P(),
            P(),
            P(),
            P(),
            P(),
            P(),
            P(),
        ),
        out_specs=(
            P("batch", "seq", None),
            P("batch", "seq", None),
            P("seq", None),
            P("seq", None),
            P("seq", None),
            P("seq", None),
            P("seq", None),
            P("seq", None),
            P("seq", None),
            P(),
            P(),
            P(),
            P(),
        ),
        check_vma=False,
    )
```

profile of v0, /device:TPU:0, one launch (start us, length us, event | category | flops | bytes accessed | tf_op | source)
XLA Modules:
  0.0 6918.9 jit_solution(11062124047490283180)
XLA Ops:
  14.7 211.8 %all-gather.8.cloned.1.call-done = bf16[2304,4096]{1,0:T(8,128)(2,1)} async-done(((bf16[144,4096]{1,0:T(8,128)(2,1)}), bf16[2304,4096]{1,0:T(8,128)(2,1)}) %all-gather.8.cloned.1.call-update) | async-done | bytes 18874384 | tf_op jit(solution)/shard_map/all_gather | solution.py:51
  226.4 20.8 fusion.65
  247.3 15.5 convolution_bitcast_fusion.8
  262.8 3.5 convolution_bitcast_fusion.9
  270.1 4.4 convert_element_type.169
  283.9 38.1 all-gather
  324.3 26.4 all-gather.14.cloned.1.call-done
  350.7 14.0 fusion.70
  366.2 62.5 all-gather.12.cloned.1.call-done
  428.7 5.9 fusion.88
  434.6 72.3 %all-gather.10.cloned.1.call-done = bf16[1024,2,4,256]{3,0,2,1:T(8,128)(2,1)} async-done(((bf16[64,2,4,256]{3,0,2,1:T(8,128)(2,1)}), bf16[1024,2,4,256]{3,0,2,1:T(8,128)(2,1)}) %all-gather.10.cloned.1.call-update) | async-done | bytes 4194320 | tf_op jit(solution)/shard_map/all_gather | solution.py:143
  506.9 5.7 fusion.143
  514.4 7.0 convolution_bitcast_fusion.10
  527.5 416.2 %all-gather.18.cloned.1.call-done = bf16[9216,2304]{1,0:T(8,128)(2,1)} async-done(((bf16[576,2304]{1,0:T(8,128)(2,1)}), bf16[9216,2304]{1,0:T(8,128)(2,1)}) %all-gather.18.cloned.1.call-update) | async-done | bytes 42467344 | tf_op jit(solution)/shard_map/all_gather | solution.py:51
  943.7 41.5 fusion.50
  985.3 796.8 %all-gather.16.cloned.1.call-done = bf16[2304,18432]{1,0:T(8,128)(2,1)} async-done(((bf16[144,18432]{1,0:T(8,128)(2,1)}), bf16[2304,18432]{1,0:T(8,128)(2,1)}) %all-gather.16.cloned.1.call-update) | async-done | bytes 84934672 | tf_op jit(solution)/shard_map/all_gather | solution.py:51
  1782.0 81.3 %fusion.40 = (bf16[2304,18432]{1,0:T(8,128)(2,1)}, bf16[2304,18432]{1,0:T(8,128)(2,1)}) fusion(bf16[2304,18432]{1,0:T(8,128)(2,1)} %all-gather.16.cloned.1.call-done, f32[18432]{0:T(1024)S(1)} %pad_maximum_fusion.14, f32[]{:T(128)S(6)} %select_n.60, f32[]{:T(128)S(6)} %select_n.59, f32[]{:T(128)S(6)} %select_n.64, f32[]{:T(128)S(6)} %select_n.63), kind=kLoop, calls=%fused_computation.45 | loop fusion | flops 552075264 | bytes 254877712 | tf_op jit(solution)/shard_map/convert_element_type | solution.py:47
  1863.4 29.6 convolution_bitcast_fusion.3
  1893.0 33.3 convolution_bitcast_fusion.4
  1926.3 4.3 multiply_convert_fusion.1
  1930.6 16.4 convolution_bitcast_fusion.16
  1947.0 17.2 convolution_bitcast_fusion.17
  1966.8 20.7 convolution_bitcast_fusion.6
  1987.5 20.6 convolution_bitcast_fusion.7
  2008.1 10.4 multiply_convert_fusion
  2018.4 34.9 convolution_bitcast_fusion.14
  2053.3 34.3 convolution_bitcast_fusion.15
  2094.7 6.8 convolution_bitcast_fusion.18
  2101.6 6.7 convolution_bitcast_fusion.19
  2109.4 30.6 while.17
  2118.0 3.8 bitcast_dynamic-update-slice_fusion.4
  2133.3 3.8 bitcast_dynamic-update-slice_fusion.4
  2142.1 7.9 convolution_bitcast_fusion.5
  2152.5 163.8 %reduce-scatter.9.cloned.1.call-done = f32[64,2,4,256]{3,0,2,1:T(8,128)} async-done(((f32[1024,2,4,256]{3,0,2,1:T(8,128)}), f32[64,2,4,256]{3,0,2,1:T(8,128)}) %reduce-scatter.9.cloned.1.call-update) | async-done | bytes 524304 | tf_op jit(solution)/shard_map/reduce_scatter | solution.py:260
  2317.5 181.4 %reduce-scatter.11.cloned.1.call-done = f32[64,2,4,256]{3,0,2,1:T(8,128)} async-done(((f32[1024,2,4,256]{3,0,2,1:T(8,128)}), f32[64,2,4,256]{3,0,2,1:T(8,128)}) %reduce-scatter.11.cloned.1.call-update) | async-done | bytes 524304 | tf_op jit(solution)/shard_map/reduce_scatter | solution.py:263
  2500.0 15.3 convolution_bitcast_fusion.2
  2517.2 32.1 convolution_bitcast_fusion.1
  2551.1 59.3 convolution_bitcast_fusion
  2610.7 181.1 %reduce-scatter.15.cloned.1.call-done = f32[128,2304]{1,0:T(8,128)} async-done(((f32[2048,2304]{1,0:T(8,128)}), f32[128,2304]{1,0:T(8,128)}) %reduce-scatter.15.cloned.1.call-update) | async-done | bytes 1179664 | tf_op jit(solution)/shard_map/reduce_scatter | solution.py:78
  2793.9 546.5 %reduce-scatter.13.cloned.1.call-done = f32[144,4096]{1,0:T(8,128)} async-done(((f32[2304,4096]{1,0:T(8,128)}), f32[144,4096]{1,0:T(8,128)}) %reduce-scatter.13.cloned.1.call-update) | async-done | bytes 2359312 | tf_op jit(solution)/shard_map/reduce_scatter | solution.py:78
  3343.2 1162.7 %reduce-scatter.17.cloned.1.call-done = f32[576,2304]{1,0:T(8,128)} async-done(((f32[9216,2304]{1,0:T(8,128)}), f32[576,2304]{1,0:T(8,128)}) %reduce-scatter.17.cloned.1.call-update) | async-done | bytes 5308432 | tf_op jit(solution)/shard_map/reduce_scatter | solution.py:78
  4505.9 4.3 convert_element_type.186
  4510.2 2305.6 %reduce-scatter.19.cloned.1.call-done = f32[144,18432]{1,0:T(8,128)} async-done(((f32[2304,18432]{1,0:T(8,128)}), f32[144,18432]{1,0:T(8,128)}) %reduce-scatter.19.cloned.1.call-update) | async-done | bytes 10616848
  6815.8 7.0 convert_element_type.184
  6824.1 13.3 convolution_bitcast_fusion.12
  6837.5 13.6 convolution_bitcast_fusion.13
  6852.8 41.9 all-reduce.1
  6903.7 5.4 fusion.138
  (303 shorter events, 95.2 us)
Async XLA Ops:
  7.2 219.2 %all-gather.8.cloned.1.call-start = ((), (), s32[]{:S(2)}) async-start(), calls=%async_computation.6 | async-start | bytes 20054016 | tf_op jit(solution)/shard_map/all_gather | solution.py:51
  12.1 338.6 %all-gather.14.cloned.1.call-start = ((), (), s32[]{:S(2)}) async-start(), calls=%async_computation.9 | async-start | bytes 10027008 | tf_op jit(solution)/shard_map/all_gather | solution.py:51
  13.1 415.7 %all-gather.12.cloned.1.call-start = ((), (), s32[]{:S(2)}) async-start(), calls=%async_computation.8 | async-start | bytes 4456448 | tf_op jit(solution)/shard_map/all_gather | solution.py:142
  13.5 233.8 %copy-start.67 = (f32[2,64]{1,0:T(2,128)}, f32[2,64]{1,0:T(2,128)S(1)}, u32[]{:S(2)}) copy-start(f32[2,64]{1,0:T(2,128)S(1)} %fusion.118) | copy-start | bytes 1540
  13.5 233.8 %copy-start.62 = (f32[2,64]{1,0:T(2,128)}, f32[2,64]{1,0:T(2,128)S(1)}, u32[]{:S(2)}) copy-start(f32[2,64]{1,0:T(2,128)S(1)} %fusion.128) | copy-start | bytes 1540
  14.4 350.6 %copy-start.36 = (f32[2,64,128]{2,1,0:T(8,128)}, f32[2,64,128]{2,1,0:T(8,128)S(1)}, u32[]{:S(2)}) copy-start(f32[2,64,128]{2,1,0:T(8,128)S(1)} %get-tuple-element.342) | copy-start | bytes 196612
  14.7 248.1 %copy-start.22 = (bf16[2,64,2304]{2,1,0:T(8,128)(2,1)}, bf16[2,64,2304]{2,1,0:T(8,128)(2,1)S(1)}, u32[]{:S(2)}) copy-start(bf16[2,64,2304]{2,1,0:T(8,128)(2,1)S(1)} %fusion.110) | copy-start | bytes 1769476
  247.3 15.5 copy-start
  269.3 237.6 %all-gather.10.cloned.1.call-start = ((), (), s32[]{:S(2)}) async-start(), calls=%async_computation.7 | async-start | bytes 4456448 | tf_op jit(solution)/shard_map/all_gather | solution.py:143
  270.1 673.6 %all-gather.18.cloned.1.call-start = ((), (), s32[]{:S(2)}) async-start(), calls=%async_computation.11 | async-start | bytes 45121536 | tf_op jit(solution)/shard_map/all_gather | solution.py:51
  274.5 1507.5 %all-gather.16.cloned.1.call-start = ((), (), s32[]{:S(2)}) async-start(), calls=%async_computation.10 | async-start | bytes 90243072 | tf_op jit(solution)/shard_map/all_gather | solution.py:51
  283.2 41.1 copy-start.55
  283.2 41.1 copy-start.56
  283.2 67.5 copy-start.64
  283.2 2033.1 %reduce-scatter.9.cloned.1.call-start = ((), (), s32[]{:S(2)}) async-start(), calls=%async_computation.12 | async-start | bytes 8912896 | tf_op jit(solution)/shard_map/reduce_scatter | solution.py:260
  364.7 64.0 copy-start.41
  434.6 78.0 %copy-start.57 = (f32[2,64,4,2]{1,3,2,0:T(2,128)}, f32[2,64,4,2]{1,3,2,0:T(2,128)S(1)}, u32[]{:S(2)}) copy-start(f32[2,64,4,2]{1,3,2,0:T(2,128)S(1)} %get-tuple-element.343) | copy-start | bytes 12292
  514.4 8.9 slice-start.2
  525.1 418.6 %copy-start.65 = (f32[2304]{0:T(1024)S(1)}, f32[2304]{0:T(1024)}, u32[]{:S(2)}) copy-start(f32[2304]{0:T(1024)} %param.41) | copy-start | bytes 27652
  525.9 459.3 %copy-start.59 = (f32[2,64]{1,0:T(2,128)}, f32[2,64]{1,0:T(2,128)S(1)}, u32[]{:S(2)}) copy-start(f32[2,64]{1,0:T(2,128)S(1)} %fusion.129) | copy-start | bytes 1540
  526.3 458.9 %copy-start.66 = (f32[2,64]{1,0:T(2,128)}, f32[2,64]{1,0:T(2,128)S(1)}, u32[]{:S(2)}) copy-start(f32[2,64]{1,0:T(2,128)S(1)} %get-tuple-element.306) | copy-start | bytes 1540
  526.3 458.9 %copy-start.61 = (f32[2,64]{1,0:T(2,128)}, f32[2,64]{1,0:T(2,128)S(1)}, u32[]{:S(2)}) copy-start(f32[2,64]{1,0:T(2,128)S(1)} %fusion.130) | copy-start | bytes 1540
  527.5 1365.5 %copy-start.26 = (bf16[2,64,2304]{2,1,0:T(8,128)(2,1)}, bf16[2,64,2304]{2,1,0:T(8,128)(2,1)S(1)}, u32[]{:S(2)}) copy-start(bf16[2,64,2304]{2,1,0:T(8,128)(2,1)S(1)} %multiply_convert_fusion.2) | copy-start | bytes 1769476
  1893.0 33.3 copy-start.3
  1930.6 16.4 copy-start.9
  1947.0 17.4 copy-start.32
  1947.0 17.4 copy-start.53
  1947.0 18.5 copy-start.8
  1966.8 20.7 copy-start.28
  2018.4 34.9 copy-start.4
  2053.3 34.3 copy-start.43
  2053.3 37.2 copy-start.60
  2140.1 358.7 %reduce-scatter.11.cloned.1.call-start = ((), (), s32[]{:S(2)}) async-start(), calls=%async_computation.13 | async-start | bytes 8912896 | tf_op jit(solution)/shard_map/reduce_scatter | solution.py:263
  2140.9 650.9 %reduce-scatter.15.cloned.1.call-start = ((), (), s32[]{:S(2)}) async-start(), calls=%async_computation.15 | async-start | bytes 20054016 | tf_op jit(solution)/shard_map/reduce_scatter | solution.py:78
  2150.1 1190.3 %reduce-scatter.13.cloned.1.call-start = ((), (), s32[]{:S(2)}) async-start(), calls=%async_computation.14 | async-start | bytes 40108032 | tf_op jit(solution)/shard_map/reduce_scatter | solution.py:78
  2151.4 348.6 %copy-start.23 = (bf16[2,64,2304]{2,1,0:T(8,128)(2,1)S(1)}, bf16[2,64,2304]{2,1,0:T(8,128)(2,1)}, u32[]{:S(2)}) copy-start(bf16[2,64,2304]{2,1,0:T(8,128)(2,1)} %copy-done.22) | copy-start | bytes 1769476
  2500.0 15.3 copy-start.24
  2515.3 1990.6 %reduce-scatter.17.cloned.1.call-start = ((), (), s32[]{:S(2)}) async-start(), calls=%async_computation.16 | async-start | bytes 90243072 | tf_op jit(solution)/shard_map/reduce_scatter | solution.py:78
  2549.3 4266.5 %reduce-scatter.19.cloned.1.call-start = ((), (), s32[]{:S(2)}) async-start(), calls=%async_computation.17 | async-start | bytes 180486144
  2610.4 4286.6 %all-reduce.5.cloned.1.call-start = ((), (), s32[]{:S(2)}) async-start(), calls=%async_computation.18 | async-start | bytes 19464192 | tf_op jit(solution)/shard_map/psum | solution.py:296
  6837.4 13.7 copy-start.19
  6837.4 13.7 copy-start.47
  6837.4 13.7 copy-start.63
  6837.5 15.3 copy-start.51
  6837.5 15.3 copy-start.52
  6837.5 15.3 copy-start.54
  6837.5 57.2 copy-start.68
  6837.5 57.2 copy-start.21
  (49 other events, 211.4 us)
Sparse Core Ops, SparseCore 0:
  12.2 214.1 all-gather.7
  229.8 120.8 all-gather.13
  354.0 74.6 all-gather.11
  431.9 74.9 all-gather.9
  510.1 433.5 all-gather.17
  947.0 834.9 all-gather.15
  2140.2 176.0 reduce-scatter.8
  2318.6 180.2 reduce-scatter.10
  2504.6 287.0 reduce-scatter.14
  2797.6 542.7 reduce-scatter.12
  3346.6 1159.2 reduce-scatter.16
  4513.1 2302.6 reduce-scatter.18
  6823.0 41.2 all-reduce.4
where the time goes:
time: 6930 us; the launch traced here: 6920 us
  waiting for transfers between devices  6130 us (88%)
  matrix products  429 us (6%)
  other arithmetic  236 us (3%)
  blocking collectives  80 us (1%)
    unnamed x14, waiting for transfers between devices  2310 us
    reduce_scatter x3, waiting for transfers between devices, weight_terms(): lax.psum_scatter(lax.dot_general(left, right, (((0,), (0,)), ((), ())), p...  1890 us
    all_gather x4, waiting for transfers between devices, forward_product(): piece = lax.all_gather(codes, 'seq', axis=0, tiled=True)  1450 us
    reduce_scatter x1, waiting for transfers between devices, on_device(): lax.psum_scatter(value_terms.reshape(length, group, KV_HEADS, HEAD), 'seq...  181 us
    reduce_scatter x1, waiting for transfers between devices, on_device(): lax.psum_scatter(key_terms.reshape(length, group, KV_HEADS, HEAD), 'seq',...  164 us
    convert_element_type x4, other arithmetic, dequantized(): (levels(piece.astype(jnp.float32), step) * column_scale[None, :]).astype(...  158 us
    dot_general x8, matrix products, backward_product(): lax.dot_general(grads[member], dequantized(piece, column_scale, steps[mem...  151 us
  transfers between devices with their start and end apart: 13, of which 12 were waited for; matrix products, arithmetic and copies ran while one was open for 4% of the time, Pallas kernels for 0%

commit v1 on v0

v1 whole, which is shorter than its diff:
```python
import functools

import jax
import jax.numpy as jnp
from jax import lax
from jax.experimental import pallas as pl
from jax.experimental.pallas import tpu as pltpu
from jax.sharding import PartitionSpec as P

D = 2304
HEADS = 8
KV_HEADS = 4
HEAD = 256
FF = 9216
MESH = pl.DeviceIdType.MESH
F32 = jnp.float32
BF16 = jnp.bfloat16


cap_limit = 50.0


class Grid:
    def __init__(self, n):
        self.n = n
        self.planes = 4 if n % 8 == 0 else 2
        self.plane = n // self.planes
        wide = 1
        while wide * wide < self.plane:
            wide *= 2
        self.wide = wide

    def snake(self, p):
        y, x = p // self.wide, p % self.wide
        return y * self.wide + x + (y % 2) * (self.wide - 1 - 2 * x)


def remote(src, dst, send, recv, chip, core):
    return pltpu.make_async_remote_copy(
        src_ref=src, dst_ref=dst, send_sem=send, recv_sem=recv, device_id=(chip, core), device_id_type=MESH
    )


def greet(barrier, chip, core):
    pl.semaphore_signal(barrier, inc=1, device_id=(chip, core), device_id_type=MESH)


def places(grid, levels):
    c, b = lax.axis_index("seq"), lax.axis_index("batch")
    pn = grid.plane
    z, p = c // pn, c % pn
    q = grid.snake(p)
    zi = z % levels
    right = z * pn + grid.snake((q + 1) % pn)
    left = z * pn + grid.snake((q + pn - 1) % pn)
    return c, b, z, q, zi, right, left


def enter(grid, levels, halves):
    c, b, z, q, zi, right, left = places(grid, levels)
    barrier = pltpu.get_barrier_semaphore()
    greet(barrier, right, b)
    greet(barrier, left, b)
    pl.when(zi > 0)(lambda: greet(barrier, c - grid.plane, b))
    pl.when(zi < levels - 1)(lambda: greet(barrier, c + grid.plane, b))
    if halves:
        greet(barrier, (c + grid.n // 2) % grid.n, b)
    count = 2 + jnp.where(zi > 0, 1, 0) + jnp.where(zi < levels - 1, 1, 0) + (1 if halves else 0)
    pl.semaphore_wait(barrier, count)


def line_order(levels):
    return [(0, 0)] + [(sign, d) for d in range(1, levels) for sign in (-1, 1)]


def present(zi, sign, d, levels):
    if d == 0:
        return None
    return (zi - d >= 0) if sign < 0 else (zi + d < levels)


def guarded(condition, action):
    if condition is None:
        action()
    else:
        pl.when(condition)(action)


def gather_kernel(grid, levels, halves, x_ref, pos_ref, out_ref, posout_ref, zs, zr, rs, rr, ls, xs, xr, ps, pr):
    n, pn = grid.n, grid.plane
    steps = pn // 2
    c, b, z, q, zi, right, left = places(grid, levels)
    rows = x_ref.shape[1]
    half = rows // 2
    enter(grid, levels, halves)

    def slot(zj, qj):
        return zj * pn + grid.snake((qj + pn) % pn)

    def block(us, zj, qj, part=None):
        u0, nu = us
        at = out_ref.at[pl.ds(u0, nu), slot(zj, qj)]
        if part is None:
            return at
        return out_ref.at[pl.ds(u0, nu), slot(zj, qj), pl.ds(part * half, half)]

    own = slot(zi, q)
    member = c // (n // 2)
    partner = (c + n // 2) % n
    if halves:
        local = pltpu.make_async_copy(x_ref.at[member], out_ref.at[member, own], ls.at[0])
        swap = remote(x_ref.at[1 - member], out_ref.at[member, own], xs.at[0], xr.at[0], partner, b)
        swap.start()
        passes = [(member, 1), (1 - member, 1)]
    else:
        local = pltpu.make_async_copy(x_ref, out_ref.at[:, own], ls.at[0])
        passes = [(0, 2)]
    local.start()

    def z_copy(k, us, zj, sign):
        way = 0 if sign > 0 else 1
        return remote(
            block(us, zj, q), block(us, zj, q), zs.at[k, way, zj], zr.at[k, way, zj], c + sign * pn, b
        )

    def r_copy(k, us, zj, way, step):
        part = way if step == steps else None
        place = q - (step - 1) if way == 0 else q + (step - 1)
        ref = block(us, zj, place, part)
        return remote(ref, ref, rs.at[k, way, step - 1, zj], rr.at[k, way, step - 1, zj], right if way == 0 else left, b)

    def r_landing(k, us, zj, way, step):
        part = way if step == steps else None
        place = q - step if way == 0 else q + step
        ref = block(us, zj, place, part)
        return remote(ref, ref, rs.at[k, way, step - 1, zj], rr.at[k, way, step - 1, zj], right, b)

    def arrive(k, us, sign, d):
        zj = zi + sign * d

        def go():
            if d > 0:
                z_copy(k, us, zj, -sign).wait_recv()
            if sign <= 0:
                pl.when(zi < levels - 1)(lambda: z_copy(k, us, zj, 1).start())
            if sign >= 0:
                pl.when(zi > 0)(lambda: z_copy(k, us, zj, -1).start())
            for way in (0, 1):
                r_copy(k, us, zj, way, 1).start()

        guarded(present(zi, sign, d, levels), go)

    def onward(k, us, sign, d):
        zj = zi + sign * d

        def go():
            for step in range(1, steps + 1):
                for way in (0, 1):
                    r_landing(k, us, zj, way, step).wait_recv()
                    if step < steps:
                        r_copy(k, us, zj, way, step + 1).start()

        guarded(present(zi, sign, d, levels), go)

    def finish(k, us, sign, d):
        zj = zi + sign * d

        def go():
            if sign <= 0:
                pl.when(zi < levels - 1)(lambda: z_copy(k, us, zj, 1).wait_send())
            if sign >= 0:
                pl.when(zi > 0)(lambda: z_copy(k, us, zj, -1).wait_send())
            for way in (0, 1):
                for step in range(1, steps + 1):
                    r_copy(k, us, zj, way, step).wait_send()

        guarded(present(zi, sign, d, levels), go)

    if pos_ref is not None:
        size = levels * pn
        base = c - c % size
        for off in range(1, size):
            to = base + (c % size + off) % size
            remote(pos_ref, posout_ref.at[c % size], ps.at[off], pr.at[c % size], to, b).start()
    local.wait()
    groups = [(k, us, sign, d) for k, us in enumerate(passes) for sign, d in line_order(levels)]
    if halves:
        swap_in = remote(x_ref.at[1 - member], out_ref.at[1 - member, own], xs.at[0], xr.at[0], partner, b)
    for i, group in enumerate(groups):
        if halves and group[0] == 1 and group[3] == 0:
            swap_in.wait_recv()
        arrive(*group)
        if i > 0:
            onward(*groups[i - 1])
    onward(*groups[-1])
    for group in groups:
        finish(*group)
    if halves:
        swap.wait_send()


def gather(grid, x, levels, halves, cid):
    n, pn = grid.n, grid.plane
    count = levels * pn
    steps = pn // 2
    passes = 2 if halves else 1

    def kernel(x_ref, out_ref, *sems):
        gather_kernel(grid, levels, halves, x_ref, None, out_ref, None, *sems, None, None)

    return pl.pallas_call(
        kernel,
        out_shape=jax.ShapeDtypeStruct((2, count) + x.shape[1:], x.dtype),
        in_specs=[pl.BlockSpec(memory_space=pl.ANY)],
        out_specs=pl.BlockSpec(memory_space=pl.ANY),
        scratch_shapes=[
            pltpu.SemaphoreType.DMA((passes, 2, levels)),
            pltpu.SemaphoreType.DMA((passes, 2, levels)),
            pltpu.SemaphoreType.DMA((passes, 2, steps, levels)),
            pltpu.SemaphoreType.DMA((passes, 2, steps, levels)),
            pltpu.SemaphoreType.DMA((1,)),
            pltpu.SemaphoreType.DMA((1,)),
            pltpu.SemaphoreType.DMA((1,)),
        ],
        compiler_params=pltpu.CompilerParams(collective_id=cid, has_side_effects=True),
        name="gather_%d" % count,
    )(x)


def scatter_kernel(
    grid, levels, halves, p_ref, out_ref, acc, ring_half, ring_full, line, swapped, ls, zs, zr, rs, rr, xs, xr
):
    n, pn = grid.n, grid.plane
    steps = pn // 2
    c, b, z, q, zi, right, left = places(grid, levels)
    rows = p_ref.shape[2]
    half = rows // 2
    member = c // (n // 2)
    partner = (c + n // 2) % n

    def slot(zj, qj):
        return zj * pn + grid.snake((qj + 2 * pn) % pn)

    load = pltpu.make_async_copy(p_ref, acc, ls.at[0])
    load.start()
    enter(grid, levels, halves)
    load.wait()
    passes = [(1 - member, 1), (member, 1)] if halves else [(0, 2)]
    far_first = [(sign, d) for d in range(levels - 1, 0, -1) for sign in (-1, 1)] + [(0, 0)]

    def block(us, zj, qj, part=None):
        u0, nu = us
        if part is None:
            return acc.at[pl.ds(u0, nu), slot(zj, qj)]
        return acc.at[pl.ds(u0, nu), slot(zj, qj), pl.ds(part * half, half)]

    def add(us, into, others, lo, count):
        u0, nu = us

        def one(i, carry):
            u, r = u0 + i // (count // 16), lo + (i % (count // 16)) * 16
            total = into(u, r)[...].astype(F32)
            for other in others:
                total = total + other(u, r)[...].astype(F32)
            into(u, r)[...] = total.astype(BF16)
            return carry

        lax.fori_loop(0, nu * (count // 16), one, 0)

    def acc_at(s):
        return lambda u, r: acc.at[u, s, pl.ds(r, 16)]

    def full_at(way, step, zj):
        return lambda u, r: ring_full.at[way, step - 2, zj, u, pl.ds(r, 16)]

    def half_at(way, zj):
        return lambda u, r: ring_half.at[way, zj, u, pl.ds(r - way * half, 16)]

    def line_at(way, zj):
        return lambda u, r: line.at[way, zj, u, pl.ds(r, 16)]

    def r_copy(k, us, zj, way, step):
        u0, nu = us
        sign = 1 if way == 0 else -1
        target = q + sign * (steps + 1 - step)
        if step == 1:
            src, dst = block(us, zj, target, way), ring_half.at[way, zj, pl.ds(u0, nu)]
        else:
            src, dst = block(us, zj, target), ring_full.at[way, step - 2, zj, pl.ds(u0, nu)]
        return remote(src, dst, rs.at[k, way, step - 1, zj], rr.at[k, way, step - 1, zj], right if way == 0 else left, b)

    def z_copy(k, us, zj, way):
        u0, nu = us
        return remote(
            block(us, zj, q),
            line.at[way, zj, pl.ds(u0, nu)],
            zs.at[k, way, zj],
            zr.at[k, way, zj],
            c + (pn if way == 0 else -pn),
            b,
        )

    def begin(k, us, sign, d):
        def go():
            for way in (0, 1):
                r_copy(k, us, zi + sign * d, way, 1).start()

        guarded(present(zi, sign, d, levels), go)

    def onward(k, us, sign, d):
        zj = zi + sign * d

        def go():
            for step in range(1, steps + 1):
                for way in (0, 1):
                    r_copy(k, us, zj, way, step).wait_recv()
                    if step < steps:
                        s = slot(zj, q + (1 if way == 0 else -1) * (steps - step))
                        if step == 1:
                            add(us, acc_at(s), [half_at(way, zj)], way * half, half)
                        else:
                            add(us, acc_at(s), [full_at(way, step, zj)], 0, rows)
                        r_copy(k, us, zj, way, step + 1).start()
            s = slot(zj, q)
            if steps > 1:
                add(us, acc_at(s), [full_at(0, steps, zj), full_at(1, steps, zj)], 0, rows)
            else:
                add(us, acc_at(s), [half_at(0, zj)], 0, half)
                add(us, acc_at(s), [half_at(1, zj)], half, half)
            if sign > 0:

                def below():
                    z_copy(k, us, zj, 0).wait_recv()
                    add(us, acc_at(s), [line_at(0, zj)], 0, rows)

                pl.when(zi > 0)(below)
                z_copy(k, us, zj, 0).start()
            elif sign < 0:

                def above():
                    z_copy(k, us, zj, 1).wait_recv()
                    add(us, acc_at(s), [line_at(1, zj)], 0, rows)

                pl.when(zi < levels - 1)(above)
                z_copy(k, us, zj, 1).start()
            else:

                def below():
                    z_copy(k, us, zj, 0).wait_recv()
                    add(us, acc_at(s), [line_at(0, zj)], 0, rows)

                def above():
                    z_copy(k, us, zj, 1).wait_recv()
                    add(us, acc_at(s), [line_at(1, zj)], 0, rows)

                pl.when(zi > 0)(below)
                pl.when(zi < levels - 1)(above)

        guarded(present(zi, sign, d, levels), go)

    def finish(k, us, sign, d):
        zj = zi + sign * d

        def go():
            for way in (0, 1):
                for step in range(1, steps + 1):
                    r_copy(k, us, zj, way, step).wait_send()
            if sign != 0:
                z_copy(k, us, zj, 0 if sign > 0 else 1).wait_send()

        guarded(present(zi, sign, d, levels), go)

    groups = [(k, us, sign, d) for k, us in enumerate(passes) for sign, d in far_first]
    own = slot(zi, q)
    if halves:
        swap = remote(acc.at[1 - member, own], swapped, xs.at[0], xr.at[0], partner, b)
    begin(*groups[0])
    for i, group in enumerate(groups):
        if i + 1 < len(groups):
            begin(*groups[i + 1])
        onward(*group)
        if halves and group[0] == 0 and group[3] == 0:
            swap.start()

    def give(src, u):
        def one(i, carry):
            out_ref[u, pl.ds(i * 16, 16)] = src.at[pl.ds(i * 16, 16)][...]
            return carry

        lax.fori_loop(0, rows // 16, one, 0)

    if halves:
        give(acc.at[member, own], member)
        swap.wait_recv()
        give(swapped, 1 - member)
    else:
        give(acc.at[0, own], 0)
        give(acc.at[1, own], 1)
    for group in groups:
        finish(*group)
    if halves:
        swap.wait_send()


def scatter_part(grid, p, levels, halves, cid):
    pn = grid.plane
    steps = pn // 2
    passes = 2 if halves else 1
    _, count, rows, width = p.shape
    return pl.pallas_call(
        functools.partial(scatter_kernel, grid, levels, halves),
        out_shape=jax.ShapeDtypeStruct((2, rows, width), BF16),
        in_specs=[pl.BlockSpec(memory_space=pl.ANY)],
        out_specs=pl.BlockSpec(memory_space=pltpu.VMEM),
        scratch_shapes=[
            pltpu.VMEM((2, count, rows, width), BF16),
            pltpu.VMEM((2, levels, 2, rows // 2, width), BF16),
            pltpu.VMEM((2, max(steps - 1, 1), levels, 2, rows, width), BF16),
            pltpu.VMEM((2, levels, 2, rows, width), BF16),
            pltpu.VMEM((rows, width), BF16),
            pltpu.SemaphoreType.DMA((1,)),
            pltpu.SemaphoreType.DMA((passes, 2, levels)),
            pltpu.SemaphoreType.DMA((passes, 2, levels)),
            pltpu.SemaphoreType.DMA((passes, 2, steps, levels)),
            pltpu.SemaphoreType.DMA((passes, 2, steps, levels)),
            pltpu.SemaphoreType.DMA((1,)),
            pltpu.SemaphoreType.DMA((1,)),
        ],
        compiler_params=pltpu.CompilerParams(
            collective_id=cid, has_side_effects=True, vmem_limit_bytes=60 * 2**20
        ),
        name="scatter_%d" % count,
    )(p)


def scatter(grid, p, levels, halves, cid):
    _, count, rows, width = p.shape
    blocks = 2 * (2 * levels * (grid.plane // 2 + 2) + count)
    parts = 1
    while blocks * rows * (width // parts) * 2 > 48 * 2**20:
        parts += 1
        while width % (128 * parts):
            parts += 1
    piece = width // parts
    outs = [scatter_part(grid, p[..., i * piece : (i + 1) * piece], levels, halves, cid) for i in range(parts)]
    return outs[0] if parts == 1 else jnp.concatenate(outs, axis=-1)


def exchange_kernel(grid, pick, x_ref, small_ref, out_ref, all_ref, ls, ss, sr, fs, fr, ts, tr):
    n = grid.n
    c, b = lax.axis_index("seq"), lax.axis_index("batch")
    barrier = pltpu.get_barrier_semaphore()
    greet(barrier, c, 1 - b)
    for off in range(1, n):
        greet(barrier, (c + off) % n, b)
    pl.semaphore_wait(barrier, n)

    def out_copy(i):
        to = (c + 2 * i + b) % n
        return remote(x_ref.at[pick(to)], out_ref.at[c], ss.at[i], sr.at[i], to, b)

    def landed(i):
        frm = (c + n - 2 * i - b) % n
        return remote(x_ref.at[0], out_ref.at[frm], ss.at[i], sr.at[i], c, 1 - b)

    def pass_on(i):
        frm = (c + n - 2 * i - b) % n
        return remote(out_ref.at[frm], out_ref.at[frm], fs.at[i], fr.at[i], c, 1 - b)

    def passed(i):
        frm = (c + n - 2 * i - (1 - b)) % n
        return remote(out_ref.at[frm], out_ref.at[frm], fs.at[i], fr.at[i], c, 1 - b)

    def tell(off):
        return remote(small_ref, all_ref.at[c], ts.at[off], tr.at[off], (c + off) % n, b)

    def told(off):
        return remote(small_ref, all_ref.at[(c + n - off) % n], ts.at[off], tr.at[off], (c + off) % n, b)

    for off in range(1, n):
        tell(off).start()
    keep = pltpu.make_async_copy(small_ref, all_ref.at[c], ts.at[0])
    keep.start()
    local = pltpu.make_async_copy(x_ref.at[pick(c)], out_ref.at[c], ls.at[0])
    for i in range(1, n // 2):
        out_copy(i).start()
    pl.when(b == 1)(lambda: out_copy(0).start())

    def own():
        local.start()
        local.wait()

    pl.when(b == 0)(own)
    pl.when(b == 1)(lambda: landed(0).wait_recv())
    pass_on(0).start()
    for i in range(1, n // 2):
        landed(i).wait_recv()
        pass_on(i).start()
    keep.wait()
    for off in range(1, n):
        told(off).wait_recv()
    for i in range(n // 2):
        passed(i).wait_recv()
    for i in range(n // 2):
        pass_on(i).wait_send()
    for i in range(1, n // 2):
        out_copy(i).wait_send()
    pl.when(b == 1)(lambda: out_copy(0).wait_send())
    for off in range(1, n):
        tell(off).wait_send()


def exchange(grid, x, small, pick, cid):
    n = grid.n
    sems = [pltpu.SemaphoreType.DMA((n // 2,)) for _ in range(4)]
    return pl.pallas_call(
        functools.partial(exchange_kernel, grid, pick),
        out_shape=(
            jax.ShapeDtypeStruct((n,) + x.shape[1:], x.dtype),
            jax.ShapeDtypeStruct((n,) + small.shape, small.dtype),
        ),
        in_specs=[pl.BlockSpec(memory_space=pl.ANY)] * 2,
        out_specs=(pl.BlockSpec(memory_space=pl.ANY),) * 2,
        scratch_shapes=[pltpu.SemaphoreType.DMA((1,))]
        + sems
        + [pltpu.SemaphoreType.DMA((n,)), pltpu.SemaphoreType.DMA((n,))],
        compiler_params=pltpu.CompilerParams(collective_id=cid, has_side_effects=True),
        name="exchange",
    )(x, small)


def return_kernel(grid, x_ref, out_ref, mine, theirs, ls, ps, pr, ss, sr, fs, fr):
    n = grid.n
    c, b = lax.axis_index("seq"), lax.axis_index("batch")
    half = n // 2
    barrier = pltpu.get_barrier_semaphore()
    greet(barrier, c, 1 - b)
    for off in range(1, n):
        greet(barrier, (c + off) % n, b)

    def target(i, core):
        return (c + 2 * i + core) % n

    def load(i):
        return pltpu.make_async_copy(x_ref.at[target(i, b)], mine.at[i], ls.at[i])

    def give(i):
        return remote(x_ref.at[target(i, 1 - b)], theirs.at[i], ps.at[i], pr.at[i], c, 1 - b)

    def out_copy(i):
        return remote(mine.at[i], out_ref.at[c], ss.at[i], sr.at[i], target(i, b), b)

    def frm(i, core):
        return (c + n - 2 * i - core) % n

    def landed(i):
        return remote(mine.at[i], out_ref.at[frm(i, b)], ss.at[i], sr.at[i], c, 1 - b)

    def pass_on(i):
        at = out_ref.at[frm(i, b)]
        return remote(at, at, fs.at[i], fr.at[i], c, 1 - b)

    def passed(i):
        at = out_ref.at[frm(i, 1 - b)]
        return remote(at, at, fs.at[i], fr.at[i], c, 1 - b)

    local = pltpu.make_async_copy(mine.at[0], out_ref.at[c], ss.at[0])
    for i in range(half):
        load(i).start()
    pl.semaphore_wait(barrier, n)
    order = list(range(1, half)) + [0]
    for i in order:
        give(i).start()
    rows = x_ref.shape[1]
    step = 16 if rows % 16 == 0 else rows
    for i in order:
        load(i).wait()
        give(i).wait_recv()

        def one(r, carry):
            at = pl.ds(pl.multiple_of(r * step, step), step)
            mine[i, at] = (mine[i, at].astype(F32) + theirs[i, at].astype(F32)).astype(BF16)
            return carry

        lax.fori_loop(0, rows // step, one, 0)
        if i > 0:
            out_copy(i).start()
        else:
            pl.when(b == 1)(lambda: out_copy(0).start())
            pl.when(b == 0)(lambda: local.start())
    for i in order:
        if i > 0:
            landed(i).wait_recv()
        else:
            pl.when(b == 1)(lambda: landed(0).wait_recv())
            pl.when(b == 0)(lambda: local.wait())
        pass_on(i).start()
    for i in range(half):
        passed(i).wait_recv()
    for i in range(half):
        give(i).wait_send()
        pass_on(i).wait_send()
    for i in range(1, half):
        out_copy(i).wait_send()
    pl.when(b == 1)(lambda: out_copy(0).wait_send())


def give_back(grid, x, cid):
    n = grid.n
    shape = (n // 2,) + x.shape[1:]
    return pl.pallas_call(
        functools.partial(return_kernel, grid),
        out_shape=jax.ShapeDtypeStruct(x.shape, x.dtype),
        in_specs=[pl.BlockSpec(memory_space=pl.ANY)],
        out_specs=pl.BlockSpec(memory_space=pl.ANY),
        scratch_shapes=[pltpu.VMEM(shape, BF16), pltpu.VMEM(shape, BF16)]
        + [pltpu.SemaphoreType.DMA((n // 2,)) for _ in range(7)],
        compiler_params=pltpu.CompilerParams(collective_id=cid, has_side_effects=True, vmem_limit_bytes=40 * 2**20),
        name="give_back",
    )(x)


def pair_kernel(x_ref, out_ref, other, ss, sr):
    c, b = lax.axis_index("seq"), lax.axis_index("batch")
    barrier = pltpu.get_barrier_semaphore()
    greet(barrier, c, 1 - b)
    pl.semaphore_wait(barrier, 1)
    copy = remote(x_ref, other, ss.at[0], sr.at[0], c, 1 - b)
    copy.start()
    copy.wait()

    def one(r, carry):
        at = pl.ds(pl.multiple_of(r * 16, 16), 16)
        out_ref[at] = x_ref[at].astype(F32) + other[at].astype(F32)
        return carry

    lax.fori_loop(0, x_ref.shape[0] // 16, one, 0)


def pair_sum(x, cid):
    return pl.pallas_call(
        pair_kernel,
        out_shape=jax.ShapeDtypeStruct(x.shape, F32),
        in_specs=[pl.BlockSpec(memory_space=pltpu.VMEM)],
        out_specs=pl.BlockSpec(memory_space=pltpu.VMEM),
        scratch_shapes=[pltpu.VMEM(x.shape, BF16), pltpu.SemaphoreType.DMA((1,)), pltpu.SemaphoreType.DMA((1,))],
        compiler_params=pltpu.CompilerParams(collective_id=cid, has_side_effects=True, vmem_limit_bytes=40 * 2**20),
        name="pair_sum",
    )(x)


def normed(value, gain):
    return value * lax.rsqrt(jnp.mean(value * value, axis=-1, keepdims=True) + 1e-06) * gain


def angles(places, head):
    freqs = 10000.0 ** (-(jnp.arange(head // 2, dtype=F32) * 2.0 / head))
    return places.astype(F32)[..., None] * freqs


def rotate(values, cosine, sine):
    half = values.shape[-1] // 2
    first = values[..., :half]
    second = values[..., half:]
    return jnp.concatenate([first * cosine - second * sine, second * cosine + first * sine], axis=-1)


def width_step(number):
    remainder = number % 3
    return jnp.where(remainder == 0, 1.0, jnp.where(remainder == 1, 16.0, 64.0)).astype(F32)


def dequantized(codes, column_scale, step):
    offset = jnp.where(step > 1.0, 0.5 * step, 0.0)
    level = jnp.floor(codes.astype(F32) / step) * step + offset
    return (level * column_scale[None, :]).astype(BF16)


def dot(left, right):
    return jnp.dot(left, right, preferred_element_type=F32)


def dot_t(left, right):
    return lax.dot_general(left, right, (((1,), (1,)), ((), ())), preferred_element_type=F32)


def t_dot(left, right):
    return lax.dot_general(left, right, (((0,), (0,)), ((), ())), preferred_element_type=F32)


def on_device(
    grid,
    tokens,
    segments,
    positions,
    cotangent,
    query_codes,
    key_codes,
    value_codes,
    output_codes,
    gate_codes,
    up_codes,
    down_codes,
    query_scale,
    key_scale,
    value_scale,
    output_scale,
    gate_scale,
    up_scale,
    down_scale,
    attention_gain,
    attention_post_gain,
    feed_gain,
    feed_post_gain,
):
    n = grid.n
    group, block, _ = tokens.shape
    length = n * block
    pairs = HEADS // KV_HEADS
    scale = HEAD ** (-0.5)
    chip, core = lax.axis_index("seq"), lax.axis_index("batch")
    half = n // 2
    member = chip // half
    head = chip % HEADS
    kv_head = head // pairs
    parts = half // HEADS
    copies = n // HEADS
    asked = length // parts
    first_asked = ((chip % half) // HEADS) * asked
    steps = [width_step(core * group + m) for m in range(group)]
    step = width_step(core * group + member)
    rows_d = D // n
    units = FF // n

    q_parts = jnp.transpose(query_codes.reshape(rows_d, HEADS, HEAD), (1, 0, 2))
    k_parts = jnp.repeat(jnp.transpose(key_codes.reshape(rows_d, KV_HEADS, HEAD), (1, 0, 2)), pairs, axis=0)
    v_parts = jnp.repeat(jnp.transpose(value_codes.reshape(rows_d, KV_HEADS, HEAD), (1, 0, 2)), pairs, axis=0)
    qkv_parts = jnp.concatenate([q_parts, k_parts, v_parts], axis=-1).astype(BF16)
    small = jnp.zeros((8, 128), jnp.int32).at[:group, :block].set(positions)
    qkv_codes, all_places = exchange(grid, qkv_parts, small, lambda to: to % HEADS, 1)
    pair_parts = jnp.concatenate(
        [gate_codes.reshape(rows_d, n, units), up_codes.reshape(rows_d, n, units)], axis=-1
    )
    pair_parts = jnp.transpose(pair_parts, (1, 0, 2)).astype(BF16)
    pair_codes, _ = exchange(grid, pair_parts, small, lambda to: to, 2)
    pair_codes = pair_codes.reshape(D, 2 * units)
    out_low = output_codes.astype(BF16)
    got = [
        lax.ppermute(
            out_low, "seq", [(h * copies + j, h + HEADS * ((j + copies - t) % copies)) for h in range(HEADS) for j in range(copies)]
        )
        for t in range(copies)
    ]
    out_codes = jnp.roll(jnp.stack(got), chip // HEADS, axis=0).reshape(HEAD, D)

    qkv_scale = jnp.concatenate(
        [
            lax.dynamic_slice_in_dim(query_scale, head * HEAD, HEAD),
            lax.dynamic_slice_in_dim(key_scale, kv_head * HEAD, HEAD),
            lax.dynamic_slice_in_dim(value_scale, kv_head * HEAD, HEAD),
        ]
    )
    qkv_matrix = dequantized(qkv_codes.reshape(D, 3 * HEAD), qkv_scale, step)
    out_matrix = dequantized(out_codes, output_scale, step)
    pair_scale = jnp.concatenate(
        [
            lax.dynamic_slice_in_dim(gate_scale, chip * units, units),
            lax.dynamic_slice_in_dim(up_scale, chip * units, units),
        ]
    )
    pair_matrices = [dequantized(pair_codes, pair_scale, s) for s in steps]
    down_matrices = [dequantized(down_codes, down_scale, s) for s in steps]

    source = tokens.astype(F32)
    first_normed = normed(source, attention_gain).astype(BF16)
    seen = gather(grid, first_normed, grid.planes // 2, True, 3).reshape(length, D)
    places_all = lax.dynamic_index_in_dim(all_places[:, :group, :block], member, 1, False).reshape(length)
    turn = angles(places_all, HEAD)
    cosine, sine = jnp.cos(turn), jnp.sin(turn)
    if parts == 1:
        seen_asked, places_asked, cosine_q, sine_q = seen, places_all, cosine, sine
        projected = dot(seen, qkv_matrix)
        q_lin, kv_lin = projected[:, :HEAD], projected[:, HEAD:]
    else:
        seen_asked, places_asked, cosine_q, sine_q = [
            lax.dynamic_slice_in_dim(a, first_asked, asked) for a in (seen, places_all, cosine, sine)
        ]
        q_lin, kv_lin = dot(seen_asked, qkv_matrix[:, :HEAD]), dot(seen, qkv_matrix[:, HEAD:])
    queries = rotate(q_lin, cosine_q, sine_q).astype(BF16)
    keys = rotate(kv_lin[:, :HEAD], cosine, sine).astype(BF16)
    values = kv_lin[:, HEAD:].astype(BF16)
    q_index = first_asked + jnp.arange(asked, dtype=jnp.int32)
    key_index = jnp.arange(length, dtype=jnp.int32)
    allowed = (key_index[None, :] <= q_index[:, None]) & (key_index[None, :] >= (q_index - places_asked)[:, None])
    bent = jnp.tanh(dot_t(queries, keys) * scale / cap_limit)
    kernel = jnp.where(allowed, jnp.exp(cap_limit * bent), 0.0)
    totals = jnp.sum(kernel, axis=-1, keepdims=True)
    kernel_low = kernel.astype(BF16)
    attended = dot(kernel_low, values) / totals
    attended_low = attended.astype(BF16)

    def spread(part):
        if parts > 1:
            part = lax.dynamic_update_slice_in_dim(jnp.zeros((length, D), BF16), part, first_asked, 0)
        return part.reshape(2, half, block, D)

    attention_raw = scatter(
        grid, spread(dot(attended_low, out_matrix).astype(BF16)), grid.planes // 2, True, 4
    ).astype(F32)

    mixed = source + normed(attention_raw, attention_post_gain)
    second_normed = normed(mixed, feed_gain).astype(BF16)
    fed = gather(grid, second_normed, grid.planes, False, 5).reshape(group, length, D)
    gate_up = [dot(fed[m], pair_matrices[m]) for m in range(group)]
    hidden = [(jax.nn.gelu(g[:, :units], approximate=True) * g[:, units:]).astype(BF16) for g in gate_up]
    down_part = jnp.stack([dot(hidden[m], down_matrices[m]).astype(BF16) for m in range(group)])
    down_raw = scatter(grid, down_part.reshape(group, n, block, D), grid.planes, False, 6).astype(F32)
    branch, pull_out = jax.vjp(normed, down_raw, feed_post_gain)
    output = (mixed + branch).astype(BF16)
    upstream = cotangent.astype(F32)
    grad_down_raw, grad_post_feed = pull_out(upstream)
    down_low = gather(grid, grad_down_raw.astype(BF16), grid.planes, False, 5).reshape(group, length, D)
    pair_low, second_part = [], []
    for m in range(group):
        grad_hidden = dot_t(down_low[m], down_matrices[m])
        _, pull_glu = jax.vjp(
            lambda left, right: jax.nn.gelu(left, approximate=True) * right,
            gate_up[m][:, :units],
            gate_up[m][:, units:],
        )
        pair_low.append(jnp.concatenate(pull_glu(grad_hidden), axis=-1).astype(BF16))
        second_part.append(dot_t(pair_low[m], pair_matrices[m]).astype(BF16))
    grad_second = scatter(
        grid, jnp.stack(second_part).reshape(group, n, block, D), grid.planes, False, 6
    ).astype(F32)
    pair_grad = sum(t_dot(fed[m], pair_low[m]) for m in range(group)).astype(BF16)
    down_grad = sum(t_dot(hidden[m], down_low[m]) for m in range(group)).astype(BF16)
    pair_got = give_back(grid, pair_grad.reshape(n, rows_d, 2 * units), 7)
    gate_grad = jnp.transpose(pair_got[..., :units], (1, 0, 2)).reshape(rows_d, FF).astype(F32)
    up_grad = jnp.transpose(pair_got[..., units:], (1, 0, 2)).reshape(rows_d, FF).astype(F32)
    down_grad = pair_sum(down_grad, 8)

    _, pull_feed = jax.vjp(normed, mixed, feed_gain)
    grad_mixed_part, grad_pre_feed = pull_feed(grad_second)
    grad_mixed = upstream + grad_mixed_part
    _, pull_post = jax.vjp(normed, attention_raw, attention_post_gain)
    grad_attention, grad_post_attention = pull_post(grad_mixed)
    attention_low = gather(grid, grad_attention.astype(BF16), grid.planes // 2, True, 3).reshape(length, D)
    if parts > 1:
        attention_low = lax.dynamic_slice_in_dim(attention_low, first_asked, asked)
    grad_attended = dot_t(attention_low, out_matrix)
    grad_sums = (grad_attended / totals).astype(BF16)
    offsets = jnp.sum(grad_attended * attended, axis=-1, keepdims=True) / totals
    grad_kernel = dot_t(grad_sums, values) - offsets
    grad_raw = (kernel * grad_kernel * (1.0 - bent * bent)).astype(BF16)
    grad_q = dot(grad_raw, keys) * scale
    grad_k = t_dot(grad_raw, queries) * scale
    grad_v = t_dot(kernel_low, grad_sums)
    q_low = rotate(grad_q, cosine_q, -sine_q).astype(BF16)
    kv_low = jnp.concatenate([rotate(grad_k, cosine, -sine), grad_v], axis=-1).astype(BF16)
    if parts == 1:
        qkv_low = jnp.concatenate([q_low, kv_low], axis=-1)
        first_part = dot_t(qkv_low, qkv_matrix)
        qkv_grad = t_dot(seen, qkv_low)
    else:
        first_part = dot_t(kv_low, qkv_matrix[:, HEAD:])
        q_back = dot_t(q_low, qkv_matrix[:, :HEAD])
        first_part = lax.dynamic_update_slice_in_dim(
            first_part, lax.dynamic_slice_in_dim(first_part, first_asked, asked) + q_back, first_asked, 0
        )
        qkv_grad = jnp.concatenate([t_dot(seen_asked, q_low), t_dot(seen, kv_low)], axis=-1)
    grad_first = scatter(
        grid, first_part.astype(BF16).reshape(2, half, block, D), grid.planes // 2, True, 4
    ).astype(F32)
    _, pull_in = jax.vjp(normed, source, attention_gain)
    grad_source_part, grad_pre_attention = pull_in(grad_first)
    grad_in = (grad_mixed + grad_source_part).astype(BF16)
    qkv_got = give_back(grid, qkv_grad.astype(BF16).reshape(n, rows_d, 3 * HEAD), 9).astype(F32)
    qkv_got = jnp.sum(qkv_got.reshape(copies, HEADS, rows_d, 3 * HEAD), axis=0)
    query_grad = jnp.transpose(qkv_got[..., :HEAD], (1, 0, 2)).reshape(rows_d, HEADS * HEAD)
    kv_grad = jnp.sum(qkv_got[..., HEAD:].reshape(KV_HEADS, pairs, rows_d, 2 * HEAD), axis=1)
    key_grad = jnp.transpose(kv_grad[..., :HEAD], (1, 0, 2)).reshape(rows_d, KV_HEADS * HEAD)
    value_grad = jnp.transpose(kv_grad[..., HEAD:], (1, 0, 2)).reshape(rows_d, KV_HEADS * HEAD)
    out_part = pair_sum(t_dot(attended_low, attention_low).astype(BF16), 10).astype(BF16)
    out_part = jnp.roll(out_part.reshape(copies, HEAD // copies, D), -(chip // HEADS), axis=0)
    out_grad = sum(
        lax.ppermute(
            out_part[t],
            "seq",
            [(h + HEADS * i, h * copies + (i + t) % copies) for h in range(HEADS) for i in range(copies)],
        ).astype(F32)
        for t in range(copies)
    )
    gains = lax.psum(
        (grad_pre_attention, grad_post_attention, grad_pre_feed, grad_post_feed), ("seq", "batch")
    )
    return (
        output,
        grad_in,
        query_grad,
        key_grad,
        value_grad,
        out_grad,
        gate_grad,
        up_grad,
        down_grad,
    ) + tuple(gains)


def solution(mesh):
    rows = P("seq", None)
    return jax.shard_map(
        functools.partial(on_device, Grid(mesh.shape["seq"])),
        mesh=mesh,
        in_specs=(P("batch", "seq", None), P("batch", "seq"), P("batch", "seq"), P("batch", "seq", None))
        + (rows,) * 7
        + (P(),) * 11,
        out_specs=(P("batch", "seq", None),) * 2 + (rows,) * 7 + (P(),) * 4,
        check_vma=False,
    )
```

time: 6930 us -> 1250 us (0.18)
  waiting for transfers between devices: 6130 us -> 0.01 us
  Pallas kernels: 0 us -> 837 us
  matrix products: 429 us -> 138 us
  other arithmetic: 236 us -> 107 us
    unnamed x14 -> x0, waiting for transfers between devices: 2310 us -> none
    reduce_scatter x5 -> x0, waiting for transfers between devices: 2240 us -> none  [the longest x3 1890 us: weight_terms(): lax.psum_scatter(lax.dot_general(left, right, (((0,), (0,)), ((), ())), p...]
    all_gather x6 -> x0, waiting for transfers between devices: 1590 us -> none  [the longest x4 1450 us: forward_product(): piece = lax.all_gather(codes, 'seq', axis=0, tiled=True)]
    pallas_call x0 -> x14, Pallas kernels: none -> 837 us  [the longest x4 347 us: gather(): pl.pallas_call(kernel, out_shape=jax.ShapeDtypeStruct((2, count) + x.shap...]
    dot_general x32 -> x24, matrix products: 429 us -> 138 us  [the longest x8 54.6 us: dot_t(): lax.dot_general(left, right, (((1,), (1,)), ((), ())), preferred_element_...]
    convert_element_type x19 -> x16, other arithmetic: 193 us -> 44.7 us  [the longest x5 21.8 us: dequantized(): return (level * column_scale[None, :]).astype(BF16)]
  transfers between devices with their start and end apart: 13 -> 4, of which waited for: 12 -> 0; matrix products, arithmetic and copies ran while one was open for 4% -> 10% of each run, Pallas kernels for 0% -> 20%
where the time goes in v1:
time: 1250 us; the launch traced here: 1240 us
  Pallas kernels  837 us (67%)
  matrix products  138 us (11%)
  other arithmetic  107 us (9%)
  local copies, waits for them, and re-layouts  81.4 us (7%)
  blocking collectives  58.5 us (5%)
  starting transfers between devices  16.6 us (1%)
    pallas_call x4, Pallas kernels, gather(): pl.pallas_call(kernel, out_shape=jax.ShapeDtypeStruct((2, count) + x.shap...  347 us
    pallas_call x4, Pallas kernels, scatter_part(): pl.pallas_call(functools.partial(scatter_kernel, grid, levels, halves), o...  273 us
    pallas_call x2, Pallas kernels, exchange(): pl.pallas_call(functools.partial(exchange_kernel, grid, pick), out_shape=...  112 us
    pallas_call x2, Pallas kernels, give_back(): pl.pallas_call(functools.partial(return_kernel, grid), out_shape=jax.Shap...  97 us
    psum x1, blocking collectives, on_device(): lax.psum((grad_pre_attention, grad_post_attention, grad_pre_feed, grad_po...  58.5 us
    dot_general x8, matrix products, dot_t(): lax.dot_general(left, right, (((1,), (1,)), ((), ())), preferred_element_...  54.6 us
    dot_general x8, matrix products, dot(): return jnp.dot(left, right, preferred_element_type=F32)  43.4 us
    dot_general x8, matrix products, t_dot(): lax.dot_general(left, right, (((0,), (0,)), ((), ())), preferred_element_...  39.8 us
  transfers between devices with their start and end apart: 4, of which 0 were waited for; matrix products, arithmetic and copies ran while one was open for 10% of the time, Pallas kernels for 20%

profile of v1, /device:TPU:0, one launch (start us, length us, event | category | flops | bytes accessed | tf_op | source)
XLA Modules:
  0.0 1240.9 jit_solution(17918918939965215449)
XLA Ops:
  2.9 4.0 collective-permute-start.1
  7.0 6.0 collective-permute-start
  17.2 57.5 %exchange.2 = (bf16[16,144,768]{2,1,0:T(8,128)(2,1)}, s32[16,8,128]{2,1,0:T(8,128)}) custom-call(bf16[8,144,768]{2,1,0:T(8,128)(2,1)} %pad_maximum_fusion.4.x_ref, s32[8,128]{1,0:T(8,128)} %scatter.4.small_ref), custom_call_target="tpu_custom_call" | custom-call | tf_op jit(solution)/shard_map/exchange/pallas_call | solution.py:516
  76.9 70.8 %gather_8.2 = bf16[2,8,64,2304]{3,2,1,0:T(8,128)(2,1)} custom-call(bf16[2,64,2304]{2,1,0:T(8,128)(2,1)} %fusion.38.x_ref), custom_call_target="tpu_custom_call" | custom-call | tf_op jit(solution)/shard_map/gather_8/pallas_call | solution.py:211
  160.7 4.4 convert.78
  165.1 5.8 reshape.321
  173.3 4.2 maximum_bitcast_fusion.x_ref
  177.5 54.6 %exchange.3 = (bf16[16,144,1152]{2,1,0:T(8,128)(2,1)}, s32[16,8,128]{2,1,0:T(8,128)}) custom-call(bf16[16,144,1152]{2,1,0:T(8,128)(2,1)} %maximum_bitcast_fusion.x_ref, s32[8,128]{1,0:T(8,128)} %scatter.4.small_ref), custom_call_target="tpu_custom_call" | custom-call | tf_op jit(solution)/shard_map/exchange/pallas_call | solution.py:516
  232.8 4.4 multiply_add_fusion
  239.8 8.9 fusion.118
  248.8 9.5 multiply_convert_fusion.1
  258.3 5.8 fusion.8
  264.1 4.0 fusion.86
  281.5 56.9 %scatter_8.2 = bf16[2,64,2304]{2,1,0:T(8,128)(2,1)} custom-call(bf16[2,8,64,2304]{3,2,1,0:T(8,128)(2,1)} %bitcast.105), custom_call_target="tpu_custom_call" | custom-call | tf_op jit(solution)/shard_map/scatter_8/pallas_call | solution.py:410
  343.5 109.9 %gather_16.2 = bf16[2,16,64,2304]{3,2,1,0:T(8,128)(2,1)} custom-call(bf16[2,64,2304]{2,1,0:T(8,128)(2,1)} %multiply_convert_fusion.11.x_ref), custom_call_target="tpu_custom_call" | custom-call | tf_op jit(solution)/shard_map/gather_16/pallas_call | solution.py:211
  453.4 8.5 fusion.117
  461.9 8.3 fusion.120
  474.7 6.3 fusion.119
  484.2 5.8 convolution_convert_fusion.1
  490.0 6.0 convolution_convert_fusion.2
  496.0 8.3 pad_maximum_fusion.p_ref
  504.3 84.3 %scatter_16.2 = bf16[2,64,2304]{2,1,0:T(8,128)(2,1)} custom-call(bf16[2,16,64,2304]{3,2,1,0:T(8,128)(2,1)} %pad_maximum_fusion.p_ref), custom_call_target="tpu_custom_call" | custom-call | tf_op jit(solution)/shard_map/scatter_16/pallas_call | solution.py:410
  594.4 107.2 %gather_16.3 = bf16[2,16,64,2304]{3,2,1,0:T(8,128)(2,1)} custom-call(bf16[2,64,2304]{2,1,0:T(8,128)(2,1)} %fusion.46.x_ref), custom_call_target="tpu_custom_call" | custom-call | tf_op jit(solution)/shard_map/gather_16/pallas_call | solution.py:211
  701.7 6.9 fusion.116
  708.6 12.4 fusion.24
  721.1 10.0 fusion.17
  731.1 8.5 convolution_convert_fusion.3
  739.7 8.0 convolution_convert_fusion.4
  747.8 8.3 pad_maximum_fusion.1.p_ref
  756.1 76.8 %scatter_16.3 = bf16[2,64,2304]{2,1,0:T(8,128)(2,1)} custom-call(bf16[2,16,64,2304]{3,2,1,0:T(8,128)(2,1)} %pad_maximum_fusion.1.p_ref), custom_call_target="tpu_custom_call" | custom-call | tf_op jit(solution)/shard_map/scatter_16/pallas_call | solution.py:410
  839.2 58.6 %gather_8.3 = bf16[2,8,64,2304]{3,2,1,0:T(8,128)(2,1)} custom-call(bf16[2,64,2304]{2,1,0:T(8,128)(2,1)} %fusion.47.x_ref), custom_call_target="tpu_custom_call" | custom-call | tf_op jit(solution)/shard_map/gather_8/pallas_call | solution.py:211
  897.9 4.3 multiply_reduce_fusion.1
  919.0 4.2 convolution_convert_fusion.6
  923.2 37.4 %give_back.2 = bf16[16,144,768]{2,1,0:T(8,128)(2,1)S(1)} custom-call(bf16[16,144,768]{2,1,0:T(8,128)(2,1)S(1)} %bitcast.104), custom_call_target="tpu_custom_call" | custom-call | tf_op jit(solution)/shard_map/give_back/pallas_call | solution.py:611
  966.3 9.3 fusion.36
  975.6 5.4 fusion.121
  981.0 5.5 convolution_convert_fusion
  986.6 54.7 %scatter_8.3 = bf16[2,64,2304]{2,1,0:T(8,128)(2,1)} custom-call(bf16[2,8,64,2304]{3,2,1,0:T(8,128)(2,1)} %bitcast.127), custom_call_target="tpu_custom_call" | custom-call | tf_op jit(solution)/shard_map/scatter_8/pallas_call | solution.py:410
  1054.0 6.0 collective-permute-start.2
  1060.0 9.8 fusion
  1069.8 59.6 %give_back.3 = bf16[16,144,1152]{2,1,0:T(8,128)(2,1)S(1)} custom-call(bf16[16,144,1152]{2,1,0:T(8,128)(2,1)S(1)} %bitcast.103), custom_call_target="tpu_custom_call" | custom-call | tf_op jit(solution)/shard_map/give_back/pallas_call | solution.py:611
  1133.3 4.3 copy.104
  1137.6 7.3 reshape.344
  1144.8 7.1 copy.105
  1151.9 7.1 reshape.345
  1159.0 7.3 add_convert_fusion.x_ref
  1166.3 5.7 pair_sum.3
  1174.4 58.5 %all-reduce.1 = (f32[2304]{0:T(1024)}, f32[2304]{0:T(1024)}, f32[2304]{0:T(1024)}, f32[2304]{0:T(1024)}) all-reduce(f32[2304]{0:T(1024)} %get-tuple-element.37, f32[2304]{0:T(1024)} %get-tuple-element.32, f32[2304]{0:T(1024)} %get-tuple-element.34, f32[2304]{0:T(1024)} %get-tuple-element.35), channel_id=1, replica_groups=mesh['seq'=16,'batch'=2] {'seq','batch'}, use_global_device_ids=true, to_apply=%region_13.15 | all-reduce | flops 9216 | bytes 73728 | tf_op jit(solution)/shard_map/psum | solution.py:894
  (277 shorter events, 114.3 us)
Async XLA Ops:
  0.6 13.8 %copy-start.22 = (s32[144,1024]{1,0:T(8,128)S(1)}, s32[144,1024]{1,0:T(8,128)}, u32[]{:S(2)}) copy-start(s32[144,1024]{1,0:T(8,128)} %param.30) | copy-start | bytes 1769476
  0.7 14.1 %copy-start.21 = (s32[144,2048]{1,0:T(8,128)S(1)}, s32[144,2048]{1,0:T(8,128)}, u32[]{:S(2)}) copy-start(s32[144,2048]{1,0:T(8,128)} %param.29) | copy-start | bytes 3538948
  2.9 270.9 %collective-permute-start.1 = (bf16[128,2304]{1,0:T(8,128)(2,1)}, bf16[128,2304]{1,0:T(8,128)(2,1)}, u32[]{:S(2)}, u32[]{:S(2)}) collective-permute-start(bf16[128,2304]{1,0:T(8,128)(2,1)} %convert_element_type.200), channel_id=1, source_target_pairs={{0,16},{2,0},{4,18},{6,2},{8,20},{10,4},{12,22},{14,6},{16,24},{18... | collective-permute-start | bytes 1769480 | tf_op jit(solution)/shard_map/ppermute | solution.py:749
  7.0 266.9 %collective-permute-start = (bf16[128,2304]{1,0:T(8,128)(2,1)}, bf16[128,2304]{1,0:T(8,128)(2,1)}, u32[]{:S(2)}, u32[]{:S(2)}) collective-permute-start(bf16[128,2304]{1,0:T(8,128)(2,1)} %convert_element_type.200), channel_id=1, source_target_pairs={{0,0},{2,16},{4,2},{6,18},{8,4},{10,20},{12,6},{14,22},{16,8},{18,... | collective-permute-start | bytes 1769480 | tf_op jit(solution)/shard_map/ppermute | solution.py:749
  13.0 251.1 %copy-start.46 = (f32[128]{0:T(128)}, f32[128]{0:T(128)S(1)}, u32[]{:S(2)}) copy-start(f32[128]{0:T(128)S(1)} %negate_power_fusion) | copy-start | bytes 1540
  15.8 59.8 %copy-start.2 = (bf16[2,64,2304]{2,1,0:T(8,128)(2,1)S(1)}, bf16[2,64,2304]{2,1,0:T(8,128)(2,1)}, u32[]{:S(2)}) copy-start(bf16[2,64,2304]{2,1,0:T(8,128)(2,1)} %param.26) | copy-start | bytes 1769476
  15.8 60.0 %copy-start.35 = (f32[2304]{0:T(1024)S(1)}, f32[2304]{0:T(1024)}, u32[]{:S(2)}) copy-start(f32[2304]{0:T(1024)} %param.43) | copy-start | bytes 27652
  75.8 71.8 %copy-start.48 = (f32[2,64]{1,0:T(2,128)}, f32[2,64]{1,0:T(2,128)S(1)}, u32[]{:S(2)}) copy-start(f32[2,64]{1,0:T(2,128)S(1)} %fusion.54) | copy-start | bytes 1540
  75.8 71.8 %copy-start.44 = (f32[2,64]{1,0:T(2,128)}, f32[2,64]{1,0:T(2,128)S(1)}, u32[]{:S(2)}) copy-start(f32[2,64]{1,0:T(2,128)S(1)} %fusion.101) | copy-start | bytes 1540
  177.5 55.3 %copy-start.52 = (f32[256]{0:T(256)S(1)}, f32[256]{0:T(256)}, u32[]{:S(2)}) copy-start(f32[256]{0:T(256)} %dynamic_slice.25) | copy-start | bytes 3076
  177.5 55.3 %copy-start.53 = (f32[256]{0:T(256)S(1)}, f32[256]{0:T(256)}, u32[]{:S(2)}) copy-start(f32[256]{0:T(256)} %dynamic_slice.24) | copy-start | bytes 3076
  239.8 24.3 %copy-start.33 = (f32[1024]{0:T(1024)}, f32[1024]{0:T(1024)S(1)}, u32[]{:S(2)}) copy-start(f32[1024]{0:T(1024)S(1)} %get-tuple-element.74) | copy-start | bytes 12292
  239.8 30.3 %copy-start.54 = (s32[1024]{0:T(1024)}, s32[1024]{0:T(1024)S(1)}, u32[]{:S(2)}) copy-start(s32[1024]{0:T(1024)S(1)} %get-tuple-element.73) | copy-start | bytes 12292
  239.8 30.3 %copy-start.56 = (s32[1024]{0:T(1024)}, s32[1024]{0:T(1024)S(1)}, u32[]{:S(2)}) copy-start(s32[1024]{0:T(1024)S(1)} %get-tuple-element.79) | copy-start | bytes 12292
  281.5 58.2 %copy-start.23 = (f32[2304]{0:T(1024)S(1)}, f32[2304]{0:T(1024)}, u32[]{:S(2)}) copy-start(f32[2304]{0:T(1024)} %param.44) | copy-start | bytes 27652
  281.5 59.7 %copy-start.24 = (f32[2304]{0:T(1024)S(1)}, f32[2304]{0:T(1024)}, u32[]{:S(2)}) copy-start(f32[2304]{0:T(1024)} %param.45) | copy-start | bytes 27652
  341.2 496.2 %copy-start.41 = (f32[2,64]{1,0:T(2,128)}, f32[2,64]{1,0:T(2,128)S(1)}, u32[]{:S(2)}) copy-start(f32[2,64]{1,0:T(2,128)S(1)} %fusion.103) | copy-start | bytes 1540
  343.5 118.4 %slice-start.6 = ((s8[5308416]{0:T(1024)(128)(4,1)}), s8[1114112]{0:T(1024)(128)(4,1)S(1)}, s32[]{:S(2)}) async-start(s8[5308416]{0:T(1024)(128)(4,1)} %bitcast.115), calls=%async_computation.6 | async-start | bytes 2228224
  453.4 19.2 %slice-start.4 = ((s8[5308416]{0:T(1024)(128)(4,1)}), s8[1114112]{0:T(1024)(128)(4,1)S(1)}, s32[]{:S(2)}) async-start(s8[5308416]{0:T(1024)(128)(4,1)} %bitcast.112), calls=%async_computation.4 | async-start | bytes 2228224
  461.9 10.7 slice-start.5
  470.2 14.0 %slice-start.18 = ((s8[5308416]{0:T(1024)(128)(4,1)}), s8[4194304]{0:T(1024)(128)(4,1)S(1)}, s32[]{:S(2)}) async-start(s8[5308416]{0:T(1024)(128)(4,1)} %bitcast.155), calls=%async_computation.18 | async-start | bytes 8388608
  472.6 11.6 copy-start.11
  474.7 9.5 slice-start.19
  504.3 85.6 %copy-start.7 = (bf16[2,64,2304]{2,1,0:T(8,128)(2,1)S(1)}, bf16[2,64,2304]{2,1,0:T(8,128)(2,1)}, u32[]{:S(2)}) copy-start(bf16[2,64,2304]{2,1,0:T(8,128)(2,1)} %param.28) | copy-start | bytes 1769476
  504.3 85.6 %copy-start.37 = (f32[2304]{0:T(1024)S(1)}, f32[2304]{0:T(1024)}, u32[]{:S(2)}) copy-start(f32[2304]{0:T(1024)} %param.46) | copy-start | bytes 27652
  589.9 111.7 %copy-start.43 = (f32[2,64]{1,0:T(2,128)}, f32[2,64]{1,0:T(2,128)S(1)}, u32[]{:S(2)}) copy-start(f32[2,64]{1,0:T(2,128)S(1)} %fusion.104) | copy-start | bytes 1540
  708.6 12.4 copy-start.4
  708.6 12.4 %copy-start.14 = (bf16[1,16,64,2304]{3,2,1,0:T(8,128)(2,1)S(1)}, bf16[1,16,64,2304]{3,2,1,0:T(8,128)(2,1)}, u32[]{:S(2)}) copy-start(bf16[1,16,64,2304]{3,2,1,0:T(8,128)(2,1)} %get-tuple-element.45) | copy-start | bytes 14155780
  708.6 22.5 %slice-start.2 = ((s8[5308416]{0:T(1024)(128)(4,1)}), s8[4194304]{0:T(1024)(128)(4,1)S(1)}, s32[]{:S(2)}) async-start(s8[5308416]{0:T(1024)(128)(4,1)} %bitcast.110), calls=%async_computation.2 | async-start | bytes 8388608
  708.6 31.1 %slice-start = ((s8[5308416]{0:T(1024)(128)(4,1)}), s8[4194304]{0:T(1024)(128)(4,1)S(1)}, s32[]{:S(2)}) async-start(s8[5308416]{0:T(1024)(128)(4,1)} %bitcast.108), calls=%async_computation | async-start | bytes 8388608
  721.0 10.1 copy-start.66
  721.0 10.1 slice-start.3
  721.0 10.1 copy-start.68
  721.0 18.7 %slice-start.1 = ((s8[5308416]{0:T(1024)(128)(4,1)}), s8[1114112]{0:T(1024)(128)(4,1)S(1)}, s32[]{:S(2)}) async-start(s8[5308416]{0:T(1024)(128)(4,1)} %bitcast.108), calls=%async_computation.1 | async-start | bytes 2228224
  756.1 76.8 %copy-start.3 = (bf16[2,64,2304]{2,1,0:T(8,128)(2,1)S(1)}, bf16[2,64,2304]{2,1,0:T(8,128)(2,1)}, u32[]{:S(2)}) copy-start(bf16[2,64,2304]{2,1,0:T(8,128)(2,1)} %scatter_8.2) | copy-start | bytes 1769476
  839.2 58.7 %copy-start.17 = (f32[1024,256]{0,1:T(8,128)S(1)}, f32[1024,256]{0,1:T(8,128)}, u32[]{:S(2)}) copy-start(f32[1024,256]{0,1:T(8,128)} %copy-done.16) | copy-start | bytes 3145732
  907.3 11.7 slice-start.8
  923.2 40.3 %slice-start.10 = ((s8[4718592]{0:T(1024)(128)(4,1)}), s8[524288]{0:T(1024)(128)(4,1)S(1)}, s32[]{:S(2)}) async-start(s8[4718592]{0:T(1024)(128)(4,1)} %bitcast.124), calls=%async_computation.10 | async-start | bytes 1048576
  964.0 11.6 slice-start.16
  966.3 9.3 copy-start.20
  986.6 54.7 %copy-start.36 = (f32[2304]{0:T(1024)S(1)}, f32[2304]{0:T(1024)}, u32[]{:S(2)}) copy-start(f32[2304]{0:T(1024)} %param.43) | copy-start | bytes 27652
  986.6 54.7 %copy-start.45 = (f32[2,64]{1,0:T(2,128)S(1)}, f32[2,64]{1,0:T(2,128)}, u32[]{:S(2)}) copy-start(f32[2,64]{1,0:T(2,128)} %copy-done.44) | copy-start | bytes 1540
  986.6 57.1 %copy-start.49 = (f32[2,64]{1,0:T(2,128)S(1)}, f32[2,64]{1,0:T(2,128)}, u32[]{:S(2)}) copy-start(f32[2,64]{1,0:T(2,128)} %copy-done.48) | copy-start | bytes 1540
  1046.8 13.2 %slice-start.12 = ((s8[4718592]{0:T(1024)(128)(4,1)}), s8[4194304]{0:T(1024)(128)(4,1)S(1)}, s32[]{:S(2)}) async-start(s8[4718592]{0:T(1024)(128)(4,1)} %bitcast.129), calls=%async_computation.12 | async-start | bytes 8388608
  1053.4 182.5 %collective-permute-start.3 = (bf16[128,2304]{1,0:T(8,128)(2,1)}, bf16[128,2304]{1,0:T(8,128)(2,1)}, u32[]{:S(2)}, u32[]{:S(2)}) collective-permute-start(bf16[128,2304]{1,0:T(8,128)(2,1)} %get-tuple-element.68), channel_id=1, source_target_pairs={{0,2},{16,0},{2,6},{18,4},{4,10},{20,8},{6,14},{22,12},{8,18},{24,... | collective-permute-start | bytes 1769480 | tf_op jit(solution)/shard_map/ppermute | solution.py:887
  1054.0 181.9 %collective-permute-start.2 = (bf16[128,2304]{1,0:T(8,128)(2,1)}, bf16[128,2304]{1,0:T(8,128)(2,1)}, u32[]{:S(2)}, u32[]{:S(2)}) collective-permute-start(bf16[128,2304]{1,0:T(8,128)(2,1)} %get-tuple-element.67), channel_id=1, source_target_pairs={{0,0},{16,2},{2,4},{18,6},{4,8},{20,10},{6,12},{22,14},{8,16},{24,... | collective-permute-start | bytes 1769480 | tf_op jit(solution)/shard_map/ppermute | solution.py:887
  1166.3 66.6 %copy-start.5 = (bf16[2,64,2304]{2,1,0:T(8,128)(2,1)S(1)}, bf16[2,64,2304]{2,1,0:T(8,128)(2,1)}, u32[]{:S(2)}) copy-start(bf16[2,64,2304]{2,1,0:T(8,128)(2,1)} %scatter_16.2) | copy-start | bytes 1769476
  1166.3 66.6 %copy-start.10 = (bf16[2,64,2304]{2,1,0:T(8,128)(2,1)S(1)}, bf16[2,64,2304]{2,1,0:T(8,128)(2,1)}, u32[]{:S(2)}) copy-start(bf16[2,64,2304]{2,1,0:T(8,128)(2,1)} %scatter_8.3) | copy-start | bytes 1769476
  (46 other events, 180.5 us)

commit v2 on v1

v2 whole, which is shorter than its diff:
```python
import functools

import jax
import jax.numpy as jnp
from jax import lax
from jax.experimental import pallas as pl
from jax.experimental.pallas import tpu as pltpu
from jax.sharding import PartitionSpec as P

D = 2304
HEADS = 8
KV_HEADS = 4
HEAD = 256
FF = 9216
MESH = pl.DeviceIdType.MESH
F32 = jnp.float32
BF16 = jnp.bfloat16


cap_limit = 50.0


class Grid:
    def __init__(self, n):
        self.n = n
        self.planes = 4 if n % 8 == 0 else 2
        self.plane = n // self.planes
        wide = 1
        while wide * wide < self.plane:
            wide *= 2
        self.wide = wide

    def snake(self, p):
        y, x = p // self.wide, p % self.wide
        return y * self.wide + x + (y % 2) * (self.wide - 1 - 2 * x)


def remote(src, dst, send, recv, chip, core):
    return pltpu.make_async_remote_copy(
        src_ref=src, dst_ref=dst, send_sem=send, recv_sem=recv, device_id=(chip, core), device_id_type=MESH
    )


def greet(barrier, chip, core):
    pl.semaphore_signal(barrier, inc=1, device_id=(chip, core), device_id_type=MESH)


class Place:
    def __init__(self, grid, levels):
        self.grid, self.levels = grid, levels
        self.n, self.pn = grid.n, grid.plane
        self.steps = self.pn // 2
        self.c, self.b = lax.axis_index("seq"), lax.axis_index("batch")
        self.z, p = self.c // self.pn, self.c % self.pn
        self.q = grid.snake(p)
        self.zi = self.z % levels
        self.right = self.z * self.pn + grid.snake((self.q + 1) % self.pn)
        self.left = self.z * self.pn + grid.snake((self.q + self.pn - 1) % self.pn)
        self.member = self.c // (self.n // 2)
        self.partner = (self.c + self.n // 2) % self.n

    def slot(self, zj, qj):
        return zj * self.pn + self.grid.snake((qj + 2 * self.pn) % self.pn)

    def sibling(self, src, dst, send, recv):
        return remote(src, dst, send, recv, self.c, 1 - self.b)

    def greet_near(self, halves):
        barrier = pltpu.get_barrier_semaphore()
        zi, levels = self.zi, self.levels
        greet(barrier, self.right, self.b)
        greet(barrier, self.left, self.b)
        pl.when(zi > 0)(lambda: greet(barrier, self.c - self.pn, self.b))
        pl.when(zi < levels - 1)(lambda: greet(barrier, self.c + self.pn, self.b))
        if halves:
            greet(barrier, self.partner, self.b)
        count = 2 + jnp.where(zi > 0, 1, 0) + jnp.where(zi < levels - 1, 1, 0) + (1 if halves else 0)
        pl.semaphore_wait(barrier, count)

    def greet_all(self):
        barrier = pltpu.get_barrier_semaphore()
        greet(barrier, self.c, 1 - self.b)

        def one(off, carry):
            greet(barrier, (self.c + off) % self.n, self.b)
            return carry

        lax.fori_loop(1, self.n, one, 0)
        pl.semaphore_wait(barrier, self.n)


def present(zi, sign, d, levels):
    if d == 0:
        return None
    return (zi - d >= 0) if sign < 0 else (zi + d < levels)


def guarded(condition, action):
    if condition is None:
        action()
    else:
        pl.when(condition)(action)


def dma(*shape):
    return pltpu.SemaphoreType.DMA(shape)


ANY = pl.BlockSpec(memory_space=pl.ANY)
INVMEM = pl.BlockSpec(memory_space=pltpu.VMEM)


def params(cid, mib=None):
    if mib is None:
        return pltpu.CompilerParams(collective_id=cid, has_side_effects=True)
    return pltpu.CompilerParams(collective_id=cid, has_side_effects=True, vmem_limit_bytes=mib * 2**20)


def gather_sems(grid, levels, halves):
    passes, steps = (2 if halves else 1), grid.plane // 2
    return [
        dma(passes, 2, levels),
        dma(passes, 2, levels),
        dma(passes, 2, steps, levels),
        dma(passes, 2, steps, levels),
        dma(3),
    ]


def gather_steps(at, halves, x_ref, out_ref, zs, zr, rs, rr, ls):
    levels, steps, zi, q, pn, b = at.levels, at.steps, at.zi, at.q, at.pn, at.b
    half = x_ref.shape[1] // 2
    own = at.slot(zi, q)
    member = at.member

    def block(us, zj, qj, part=None):
        u0, nu = us
        if part is None:
            return out_ref.at[pl.ds(u0, nu), at.slot(zj, qj)]
        return out_ref.at[pl.ds(u0, nu), at.slot(zj, qj), pl.ds(part * half, half)]

    if halves:
        local = pltpu.make_async_copy(x_ref.at[member], out_ref.at[member, own], ls.at[0])
        swap = remote(x_ref.at[1 - member], out_ref.at[member, own], ls.at[1], ls.at[2], at.partner, b)
        swap_in = remote(x_ref.at[1 - member], out_ref.at[1 - member, own], ls.at[1], ls.at[2], at.partner, b)
        swap.start()
        passes = [(member, 1), (1 - member, 1)]
    else:
        local = pltpu.make_async_copy(x_ref, out_ref.at[:, own], ls.at[0])
        passes = [(0, 2)]
    local.start()

    def z_copy(k, us, zj, sign):
        way = 0 if sign > 0 else 1
        ref = block(us, zj, q)
        return remote(ref, ref, zs.at[k, way, zj], zr.at[k, way, zj], at.c + sign * pn, b)

    def r_copy(k, us, zj, way, step, landing=False):
        away = step if landing else step - 1
        ref = block(us, zj, q - away if way == 0 else q + away, way if step == steps else None)
        to = at.right if way == 0 else at.left
        return remote(ref, ref, rs.at[k, way, step - 1, zj], rr.at[k, way, step - 1, zj], to, b)

    def arrive(k, us, sign, d):
        zj = zi + sign * d

        def go():
            if d > 0:
                z_copy(k, us, zj, -sign).wait_recv()
            if sign <= 0:
                pl.when(zi < levels - 1)(lambda: z_copy(k, us, zj, 1).start())
            if sign >= 0:
                pl.when(zi > 0)(lambda: z_copy(k, us, zj, -1).start())
            for way in (0, 1):
                r_copy(k, us, zj, way, 1).start()

        guarded(present(zi, sign, d, levels), go)

    def onward(k, us, sign, d):
        zj = zi + sign * d

        def go():
            for step in range(1, steps + 1):
                for way in (0, 1):
                    r_copy(k, us, zj, way, step, True).wait_recv()
                    if step < steps:
                        r_copy(k, us, zj, way, step + 1).start()

        guarded(present(zi, sign, d, levels), go)

    def finish(k, us, sign, d):
        zj = zi + sign * d

        def go():
            if sign <= 0:
                pl.when(zi < levels - 1)(lambda: z_copy(k, us, zj, 1).wait_send())
            if sign >= 0:
                pl.when(zi > 0)(lambda: z_copy(k, us, zj, -1).wait_send())
            for way in (0, 1):
                for step in range(1, steps + 1):
                    r_copy(k, us, zj, way, step).wait_send()

        guarded(present(zi, sign, d, levels), go)

    local.wait()
    waves = [
        [(k, us, sign, d) for sign in ((0,) if d == 0 else (-1, 1))] for k, us in enumerate(passes) for d in range(levels)
    ]
    for i, wave in enumerate(waves):
        if halves and wave[0][0] == 1 and wave[0][3] == 0:
            swap_in.wait_recv()
        for group in wave:
            arrive(*group)
        if i == 0:
            yield
        else:
            for group in waves[i - 1]:
                onward(*group)
    for group in waves[-1]:
        onward(*group)
    yield
    for wave in waves:
        for group in wave:
            finish(*group)
    if halves:
        swap.wait_send()


def run(steps):
    for _ in steps:
        pass


def gather(grid, x, levels, halves, cid):
    count = levels * grid.plane

    def kernel(x_ref, out_ref, *sems):
        at = Place(grid, levels)
        at.greet_near(halves)
        run(gather_steps(at, halves, x_ref, out_ref, *sems))

    return pl.pallas_call(
        kernel,
        out_shape=jax.ShapeDtypeStruct((2, count) + x.shape[1:], x.dtype),
        in_specs=[INVMEM],
        out_specs=ANY,
        scratch_shapes=gather_sems(grid, levels, halves),
        compiler_params=params(cid, 50),
        name="gather_%d" % count,
    )(x)


def scatter_scratch(grid, levels, halves, rows, width):
    passes, steps = (2 if halves else 1), grid.plane // 2
    return [
        pltpu.VMEM((2, levels * grid.plane, rows, width), BF16),
        pltpu.VMEM((2, levels, 2, rows // 2, width), BF16),
        pltpu.VMEM((2, max(steps - 1, 1), levels, 2, rows, width), BF16),
        pltpu.VMEM((2, levels, 2, rows, width), BF16),
        pltpu.VMEM((rows, width), BF16),
        dma(3),
        dma(passes, 2, levels),
        dma(passes, 2, levels),
        dma(passes, 2, steps, levels),
        dma(passes, 2, steps, levels),
    ]


def scatter_steps(at, halves, out_ref, acc, ring_half, ring_full, line, swapped, ls, zs, zr, rs, rr):
    levels, steps, zi, q, pn, b = at.levels, at.steps, at.zi, at.q, at.pn, at.b
    rows = acc.shape[2]
    half = rows // 2
    member = at.member
    passes = [(1 - member, 1), (member, 1)] if halves else [(0, 2)]

    def block(us, zj, qj, part=None):
        u0, nu = us
        if part is None:
            return acc.at[pl.ds(u0, nu), at.slot(zj, qj)]
        return acc.at[pl.ds(u0, nu), at.slot(zj, qj), pl.ds(part * half, half)]

    def add(us, s, others, lo, count):
        u0, nu = us

        def one(i, carry):
            u, r = u0 + i // (count // 16), lo + (i % (count // 16)) * 16
            total = acc[u, s, pl.ds(r, 16)].astype(F32)
            for other in others:
                total = total + other(u, r)[...].astype(F32)
            acc[u, s, pl.ds(r, 16)] = total.astype(BF16)
            return carry

        lax.fori_loop(0, nu * (count // 16), one, 0)

    def full_at(way, step, zj):
        return lambda u, r: ring_full.at[way, step - 2, zj, u, pl.ds(r, 16)]

    def half_at(way, zj):
        return lambda u, r: ring_half.at[way, zj, u, pl.ds(r - way * half, 16)]

    def line_at(way, zj):
        return lambda u, r: line.at[way, zj, u, pl.ds(r, 16)]

    def r_copy(k, us, zj, way, step):
        u0, nu = us
        sign = 1 if way == 0 else -1
        target = q + sign * (steps + 1 - step)
        if step == 1:
            src, dst = block(us, zj, target, way), ring_half.at[way, zj, pl.ds(u0, nu)]
        else:
            src, dst = block(us, zj, target), ring_full.at[way, step - 2, zj, pl.ds(u0, nu)]
        to = at.right if way == 0 else at.left
        return remote(src, dst, rs.at[k, way, step - 1, zj], rr.at[k, way, step - 1, zj], to, b)

    def z_copy(k, us, zj, way):
        u0, nu = us
        to = at.c + (pn if way == 0 else -pn)
        return remote(block(us, zj, q), line.at[way, zj, pl.ds(u0, nu)], zs.at[k, way, zj], zr.at[k, way, zj], to, b)

    def begin(k, us, sign, d):
        def go():
            for way in (0, 1):
                r_copy(k, us, zi + sign * d, way, 1).start()

        guarded(present(zi, sign, d, levels), go)

    def onward(k, us, sign, d):
        zj = zi + sign * d

        def go():
            for step in range(1, steps + 1):
                for way in (0, 1):
                    r_copy(k, us, zj, way, step).wait_recv()
                    if step < steps:
                        s = at.slot(zj, q + (1 if way == 0 else -1) * (steps - step))
                        if step == 1:
                            add(us, s, [half_at(way, zj)], way * half, half)
                        else:
                            add(us, s, [full_at(way, step, zj)], 0, rows)
                        r_copy(k, us, zj, way, step + 1).start()
            s = at.slot(zj, q)
            if steps > 1:
                add(us, s, [full_at(0, steps, zj), full_at(1, steps, zj)], 0, rows)
            else:
                add(us, s, [half_at(0, zj)], 0, half)
                add(us, s, [half_at(1, zj)], half, half)

            def passed(way):
                z_copy(k, us, zj, way).wait_recv()
                add(us, s, [line_at(way, zj)], 0, rows)

            if sign >= 0:
                pl.when(zi > 0)(lambda: passed(0))
            if sign <= 0:
                pl.when(zi < levels - 1)(lambda: passed(1))
            if sign > 0:
                z_copy(k, us, zj, 0).start()
            if sign < 0:
                z_copy(k, us, zj, 1).start()

        guarded(present(zi, sign, d, levels), go)

    def finish(k, us, sign, d):
        zj = zi + sign * d

        def go():
            for way in (0, 1):
                for step in range(1, steps + 1):
                    r_copy(k, us, zj, way, step).wait_send()
            if sign != 0:
                z_copy(k, us, zj, 0 if sign > 0 else 1).wait_send()

        guarded(present(zi, sign, d, levels), go)

    waves = [
        [(k, us, sign, d) for sign in ((0,) if d == 0 else (-1, 1))]
        for k, us in enumerate(passes)
        for d in range(levels - 1, -1, -1)
    ]
    own = at.slot(zi, q)
    if halves:
        swap = remote(acc.at[1 - member, own], swapped, ls.at[1], ls.at[2], at.partner, b)
    for group in waves[0]:
        begin(*group)
    yield
    for i, wave in enumerate(waves):
        if i + 1 < len(waves):
            for group in waves[i + 1]:
                begin(*group)
        for group in wave:
            onward(*group)
        if halves and wave[0][0] == 0 and wave[0][3] == 0:
            swap.start()
    yield

    def give(src, u):
        def one(i, carry):
            out_ref[u, pl.ds(i * 16, 16)] = src.at[pl.ds(i * 16, 16)][...]
            return carry

        lax.fori_loop(0, rows // 16, one, 0)

    if halves:
        give(acc.at[member, own], member)
        swap.wait_recv()
        give(swapped, 1 - member)
    else:
        give(acc.at[0, own], 0)
        give(acc.at[1, own], 1)
    for wave in waves:
        for group in wave:
            finish(*group)
    if halves:
        swap.wait_send()


def scatter_parts(grid, levels, rows, width):
    blocks = 2 * (2 * levels * (grid.plane // 2 + 2) + levels * grid.plane)
    parts = 1
    while blocks * rows * (width // parts) * 2 > 40 * 2**20:
        parts += 1
        while width % (128 * parts):
            parts += 1
    return parts


def in_parts(grid, levels, call, p, extra):
    parts = scatter_parts(grid, levels, p.shape[2], p.shape[3])
    if parts == 1:
        return call(p, extra)
    piece = p.shape[3] // parts
    sums, others = [], ()
    for i in range(parts):
        got = call(p[..., i * piece : (i + 1) * piece], extra if i == 0 else None)
        sums.append(got[0])
        others = got[1:] if i == 0 else others
    return (jnp.concatenate(sums, axis=-1),) + tuple(others)


def pairwise(n, c, b):
    def to(i):
        return (c + 2 * i + b) % n

    def frm(i, core):
        return (c + n - 2 * i - core) % n

    return to, frm


def share_steps(at, sources, views, ss, sr, fs, fr):
    n, c, b = at.n, at.c, at.b
    half = n // 2
    to, frm = pairwise(n, c, b)
    kinds = len(sources)

    def out_copy(k, i):
        return remote(sources[k](to(i)), views[k](c), ss.at[k, i], sr.at[k, i], to(i), b)

    def landed(k, i):
        return remote(sources[k](c), views[k](frm(i, b)), ss.at[k, i], sr.at[k, i], to(i), b)

    def pass_on(k, i, core):
        ref = views[k](frm(i, core))
        return at.sibling(ref, ref, fs.at[k, i], fr.at[k, i])

    def local(k):
        return pltpu.make_async_copy(sources[k](c), views[k](c), sr.at[k, 0])

    for k in range(kinds):
        for i in range(1, half):
            out_copy(k, i).start()

        @pl.when(b == 1)
        def _():
            out_copy(k, 0).start()

        @pl.when(b == 0)
        def _():
            local(k).start()

    yield
    for i in range(half):
        for k in range(kinds):
            if i > 0:
                landed(k, i).wait_recv()
            else:
                pl.when(b == 1)(lambda: landed(k, 0).wait_recv())
                pl.when(b == 0)(lambda: local(k).wait())
            pass_on(k, i, b).start()
    for k in range(kinds):
        for i in range(half):
            pass_on(k, i, 1 - b).wait_recv()
        for i in range(half):
            pass_on(k, i, b).wait_send()
        for i in range(1, half):
            out_copy(k, i).wait_send()
        pl.when(b == 1)(lambda: out_copy(k, 0).wait_send())


def share_sems(grid, kinds):
    return [dma(kinds, grid.n // 2) for _ in range(4)]


def tell_steps(at, small_ref, all_ref, ts, tr):
    n, c, b = at.n, at.c, at.b

    def tell(off, slot):
        return remote(small_ref, all_ref.at[slot], ts.at[off], tr.at[off], (c + off) % n, b)

    keep = pltpu.make_async_copy(small_ref, all_ref.at[c], ts.at[0])
    keep.start()
    for off in range(1, n):
        tell(off, c).start()
    yield
    keep.wait()
    for off in range(1, n):
        tell(off, (c + n - off) % n).wait_recv()
    for off in range(1, n):
        tell(off, c).wait_send()


def head_rows_steps(at, x_ref, out_ref, hs, hr, fs, fr):
    c, b = at.c, at.b
    copies = at.n // HEADS
    head, rank = c % HEADS, c // HEADS
    mine = rank % 2 == b

    def out_copy(k):
        to = c // copies + HEADS * (2 * k + b)
        return to, remote(x_ref, out_ref.at[c % copies], hs.at[k], hr.at[c % copies], to, b)

    def landed(j):
        return remote(x_ref, out_ref.at[j], hs.at[0], hr.at[j], head * copies + j, b)

    def here(j):
        return pltpu.make_async_copy(x_ref, out_ref.at[j], hr.at[j])

    def pass_on(j):
        return at.sibling(out_ref.at[j], out_ref.at[j], fs.at[j], fr.at[j])

    for k in range(copies // 2):
        to, copy = out_copy(k)
        pl.when(to != c)(lambda: copy.start())
        pl.when(to == c)(lambda: here(c % copies).start())
    yield

    @pl.when(mine)
    def _():
        for j in range(copies):
            pl.when(head * copies + j != c)(lambda: landed(j).wait_recv())
            pl.when(head * copies + j == c)(lambda: here(j).wait())
            pass_on(j).start()
        for j in range(copies):
            pass_on(j).wait_send()

    @pl.when(jnp.logical_not(mine))
    def _():
        for j in range(copies):
            pass_on(j).wait_recv()

    for k in range(copies // 2):
        to, copy = out_copy(k)
        pl.when(to != c)(lambda: copy.wait_send())


def head_rows_sems(grid):
    copies = grid.n // HEADS
    return [dma(copies), dma(copies), dma(copies), dma(copies)]


def add_rows(into, other, rows):
    step = 16 if rows % 16 == 0 else rows

    def one(r, carry):
        at = pl.ds(pl.multiple_of(r * step, step), step)
        into[at] = (into[at].astype(F32) + other[at].astype(F32)).astype(BF16)
        return carry

    lax.fori_loop(0, rows // step, one, 0)


def return_steps(at, x_ref, out_ref, mine, theirs, ls, ps, pr, ss, sr, fs, fr):
    n, c, b = at.n, at.c, at.b
    half = n // 2
    to, frm = pairwise(n, c, b)
    other_to, _ = pairwise(n, c, 1 - b)

    def load(i):
        return pltpu.make_async_copy(x_ref.at[to(i)], mine.at[i], ls.at[i])

    def give(i):
        return at.sibling(x_ref.at[other_to(i)], theirs.at[i], ps.at[i], pr.at[i])

    def out_copy(i):
        return remote(mine.at[i], out_ref.at[c], ss.at[i], sr.at[i], to(i), b)

    def landed(i):
        return remote(mine.at[i], out_ref.at[frm(i, b)], ss.at[i], sr.at[i], to(i), b)

    def pass_on(i, core):
        ref = out_ref.at[frm(i, core)]
        return at.sibling(ref, ref, fs.at[i], fr.at[i])

    local = pltpu.make_async_copy(mine.at[0], out_ref.at[c], ss.at[0])
    order = list(range(1, half)) + [0]
    for i in order:
        load(i).start()
        give(i).start()
    for i in order:
        load(i).wait()
        give(i).wait_recv()
        add_rows(mine.at[i], theirs.at[i], x_ref.shape[1])
        if i > 0:
            out_copy(i).start()
        else:
            pl.when(b == 1)(lambda: out_copy(0).start())
            pl.when(b == 0)(lambda: local.start())
    yield
    for i in order:
        if i > 0:
            landed(i).wait_recv()
        else:
            pl.when(b == 1)(lambda: landed(0).wait_recv())
            pl.when(b == 0)(lambda: local.wait())
        pass_on(i, b).start()
    for i in range(half):
        pass_on(i, 1 - b).wait_recv()
    for i in range(half):
        give(i).wait_send()
        pass_on(i, b).wait_send()
    for i in range(1, half):
        out_copy(i).wait_send()
    pl.when(b == 1)(lambda: out_copy(0).wait_send())


def return_scratch(grid, shape):
    blocks = (grid.n // 2,) + shape
    return [pltpu.VMEM(blocks, BF16), pltpu.VMEM(blocks, BF16)] + [dma(grid.n // 2) for _ in range(7)]


def head_return_steps(at, x_ref, out_ref, mine, theirs, ls, ps, pr, hs, hr, fs, fr):
    c, b = at.c, at.b
    copies = at.n // HEADS
    head, rank = c % HEADS, c // HEADS
    taken = (c % copies) % 2 == b

    def load(k):
        return pltpu.make_async_copy(x_ref.at[2 * k + b], mine.at[k], ls.at[k])

    def give(k):
        return at.sibling(x_ref.at[2 * k + 1 - b], theirs.at[k], ps.at[k], pr.at[k])

    def out_copy(k):
        to = head * copies + 2 * k + b
        return to, remote(mine.at[k], out_ref.at[rank], hs.at[k], hr.at[rank], to, b)

    def landed(i):
        return remote(mine.at[0], out_ref.at[i], hs.at[0], hr.at[i], c // copies + HEADS * i, b)

    def here(k, i):
        return pltpu.make_async_copy(mine.at[k], out_ref.at[i], hr.at[i])

    def pass_on(i):
        return at.sibling(out_ref.at[i], out_ref.at[i], fs.at[i], fr.at[i])

    for k in range(copies // 2):
        load(k).start()
        give(k).start()
    for k in range(copies // 2):
        load(k).wait()
        give(k).wait_recv()
        add_rows(mine.at[k], theirs.at[k], x_ref.shape[1])
        to, copy = out_copy(k)
        pl.when(to != c)(lambda: copy.start())
        pl.when(to == c)(lambda: here(k, rank).start())
    yield

    @pl.when(taken)
    def _():
        for i in range(copies):
            frm = c // copies + HEADS * i
            pl.when(frm != c)(lambda: landed(i).wait_recv())
            pl.when(frm == c)(lambda: here(0, i).wait())
            pass_on(i).start()
        for i in range(copies):
            pass_on(i).wait_send()

    @pl.when(jnp.logical_not(taken))
    def _():
        for i in range(copies):
            pass_on(i).wait_recv()

    for k in range(copies // 2):
        give(k).wait_send()
        to, copy = out_copy(k)
        pl.when(to != c)(lambda: copy.wait_send())


def head_return_scratch(grid, shape):
    copies = grid.n // HEADS
    blocks = (copies // 2,) + shape
    return [pltpu.VMEM(blocks, BF16), pltpu.VMEM(blocks, BF16)] + [dma(copies) for _ in range(7)]


def pair_steps(at, x_ref, out_ref, other, sems):
    copy = at.sibling(x_ref, other, sems.at[0], sems.at[1])
    copy.start()
    yield
    copy.wait_recv()

    def one(r, carry):
        rows = pl.ds(pl.multiple_of(r * 16, 16), 16)
        out_ref[rows] = x_ref[rows].astype(F32) + other[rows].astype(F32)
        return carry

    lax.fori_loop(0, x_ref.shape[0] // 16, one, 0)
    copy.wait_send()


class Split:
    def __init__(self, refs):
        self.refs = list(refs)

    def take(self, count):
        got, self.refs = self.refs[:count], self.refs[count:]
        return got


def together(*tasks):
    for task in tasks:
        next(task, None)
    for task in tasks:
        run(task)


def open_kernel(grid, x, qkv_parts, out_codes, small, cid):
    n, levels = grid.n, grid.planes // 2
    rows_d, width = qkv_parts.shape[1:]
    flat = rows_d % 16 == 0
    copies = n // HEADS
    gs, ss, ts, hs = gather_sems(grid, levels, True), share_sems(grid, 1), [dma(n), dma(n)], head_rows_sems(grid)

    def kernel(x_ref, w_ref, o_ref, small_ref, seen_ref, codes_ref, rows_ref, all_ref, *scratch):
        at = Place(grid, levels)
        refs = Split(scratch)
        at.greet_all()

        def view(j):
            return codes_ref.at[pl.ds(j * rows_d, rows_d)] if flat else codes_ref.at[j]

        together(
            gather_steps(at, True, x_ref, seen_ref, *refs.take(len(gs))),
            share_steps(at, [lambda to: w_ref.at[to % HEADS]], [view], *refs.take(len(ss))),
            tell_steps(at, small_ref, all_ref, *refs.take(2)),
            head_rows_steps(at, o_ref, rows_ref, *refs.take(4)),
        )

    codes_shape = (n * rows_d, width) if flat else (n, rows_d, width)
    return pl.pallas_call(
        kernel,
        out_shape=(
            jax.ShapeDtypeStruct((2, levels * grid.plane) + x.shape[1:], BF16),
            jax.ShapeDtypeStruct(codes_shape, BF16),
            jax.ShapeDtypeStruct((copies,) + out_codes.shape, BF16),
            jax.ShapeDtypeStruct((n,) + small.shape, small.dtype),
        ),
        in_specs=[INVMEM] * 4,
        out_specs=(ANY,) * 4,
        scratch_shapes=gs + ss + ts + hs,
        compiler_params=params(cid, 50),
        name="open",
    )(x, qkv_parts, out_codes, small)


def scatter_kernel(grid, levels, halves, cid, name, tasks=None):
    made, in_specs, out_shapes, out_specs, extra_scratch = tasks if tasks else (None, [], (), (), [])

    def call(p, extra):
        rows, width = p.shape[2:]
        more = () if extra is None else tuple(extra)
        own = scatter_scratch(grid, levels, halves, rows, width)

        def kernel(*refs):
            refs = Split(refs)
            (p_ref,) = refs.take(1)
            more_refs = refs.take(len(more))
            (out_ref,) = refs.take(1)
            out_refs = refs.take(len(out_shapes) if more else 0)
            mine = refs.take(len(own))
            at = Place(grid, levels)
            load = pltpu.make_async_copy(p_ref, mine[0], mine[5].at[0])
            load.start()
            if more:
                at.greet_all()
            else:
                at.greet_near(halves)
            load.wait()
            others = made(at, more_refs, out_refs, refs) if more else []
            together(scatter_steps(at, halves, out_ref, *mine), *others)

        return pl.pallas_call(
            kernel,
            out_shape=(jax.ShapeDtypeStruct((2, rows, width), BF16),) + (out_shapes if more else ()),
            in_specs=[ANY] + (in_specs if more else []),
            out_specs=(INVMEM,) + (out_specs if more else ()),
            scratch_shapes=own + (extra_scratch if more else []),
            compiler_params=params(cid + (0 if more else 20), 60),
            name=name,
        )(p, *more)

    return call


def feed_windows(grid):
    units = FF // grid.n
    window = 128 * max(-(-((c * units) % 128 + units) // 128) for c in range(grid.n))
    return units, window, lambda c: ((c * units) // 128) * 128


def attention_sums(grid, p, gate_codes, up_codes, cid):
    n, levels = grid.n, grid.planes // 2
    rows_d = gate_codes.shape[0]
    flat = rows_d % 16 == 0
    units, window, start = feed_windows(grid)
    ss = share_sems(grid, 2)

    def tasks(at, ins, outs, refs):
        def source(ref):
            return lambda to: ref.at[:, pl.ds(pl.multiple_of(start(to), 128), window)]

        def view(ref):
            return lambda j: ref.at[pl.ds(j * rows_d, rows_d)] if flat else ref.at[j]

        return [share_steps(at, [source(r) for r in ins], [view(r) for r in outs], *refs.take(len(ss)))]

    shape = (n * rows_d, window) if flat else (n, rows_d, window)
    call = scatter_kernel(
        grid,
        levels,
        True,
        cid,
        "attention_sums",
        (tasks, [INVMEM, INVMEM], (jax.ShapeDtypeStruct(shape, BF16),) * 2, (ANY, ANY), ss),
    )
    return in_parts(grid, levels, call, p, (gate_codes, up_codes))


def feed_sums(grid, p, cid):
    return in_parts(grid, grid.planes, scatter_kernel(grid, grid.planes, False, cid, "feed_sums"), p, None)[0]


def feed_back_sums(grid, p, pair_grad, cid):
    rs = return_scratch(grid, pair_grad.shape[1:])

    def tasks(at, ins, outs, refs):
        return [return_steps(at, ins[0], outs[0], *refs.take(len(rs)))]

    call = scatter_kernel(
        grid,
        grid.planes,
        False,
        cid,
        "feed_back_sums",
        (tasks, [ANY], (jax.ShapeDtypeStruct(pair_grad.shape, BF16),), (ANY,), rs),
    )
    return in_parts(grid, grid.planes, call, p, (pair_grad,))


def attention_back_sums(grid, p, qkv_grad, out_grad, down_grad, cid):
    n, levels = grid.n, grid.planes // 2
    rs, hs = return_scratch(grid, qkv_grad.shape[1:]), head_return_scratch(grid, out_grad.shape[1:])
    ps = [pltpu.VMEM(down_grad.shape, BF16), dma(2)]

    def tasks(at, ins, outs, refs):
        return [
            return_steps(at, ins[0], outs[0], *refs.take(len(rs))),
            head_return_steps(at, ins[1], outs[1], *refs.take(len(hs))),
            pair_steps(at, ins[2], outs[2], *refs.take(2)),
        ]

    call = scatter_kernel(
        grid,
        levels,
        True,
        cid,
        "attention_back_sums",
        (
            tasks,
            [ANY, ANY, INVMEM],
            (
                jax.ShapeDtypeStruct(qkv_grad.shape, BF16),
                jax.ShapeDtypeStruct(out_grad.shape, BF16),
                jax.ShapeDtypeStruct(down_grad.shape, F32),
            ),
            (ANY, ANY, INVMEM),
            rs + hs + ps,
        ),
    )
    return in_parts(grid, levels, call, p, (qkv_grad, out_grad, down_grad))


def gains_kernel(grid, gains, cid):
    n = grid.n
    ss = share_sems(grid, 1)

    def kernel(x_ref, out_ref, total, other, sems, *scratch):
        at = Place(grid, grid.planes)
        at.greet_all()
        copy = at.sibling(x_ref, other, sems.at[0], sems.at[1])
        copy.start()
        copy.wait()
        total[...] = x_ref[...] + other[...]
        together(share_steps(at, [lambda to: total], [lambda j: out_ref.at[j]], *scratch))

    return pl.pallas_call(
        kernel,
        out_shape=jax.ShapeDtypeStruct((n,) + gains.shape, F32),
        in_specs=[INVMEM],
        out_specs=INVMEM,
        scratch_shapes=[pltpu.VMEM(gains.shape, F32), pltpu.VMEM(gains.shape, F32), dma(2)] + ss,
        compiler_params=params(cid),
        name="gains",
    )(gains)


def normed(value, gain):
    return value * lax.rsqrt(jnp.mean(value * value, axis=-1, keepdims=True) + 1e-06) * gain


def angles(places, head):
    freqs = 10000.0 ** (-(jnp.arange(head // 2, dtype=F32) * 2.0 / head))
    return places.astype(F32)[..., None] * freqs


def rotate(values, cosine, sine):
    half = values.shape[-1] // 2
    first = values[..., :half]
    second = values[..., half:]
    return jnp.concatenate([first * cosine - second * sine, second * cosine + first * sine], axis=-1)


def width_step(number):
    remainder = number % 3
    return jnp.where(remainder == 0, 1.0, jnp.where(remainder == 1, 16.0, 64.0)).astype(F32)


def dequantized(codes, column_scale, step):
    offset = jnp.where(step > 1.0, 0.5 * step, 0.0)
    level = jnp.floor(codes.astype(F32) / step) * step + offset
    return (level * column_scale[None, :]).astype(BF16)


def dot(left, right):
    return jnp.dot(left, right, preferred_element_type=F32)


def dot_t(left, right):
    return lax.dot_general(left, right, (((1,), (1,)), ((), ())), preferred_element_type=F32)


def t_dot(left, right):
    return lax.dot_general(left, right, (((0,), (0,)), ((), ())), preferred_element_type=F32)


def unwindowed(grid, got):
    n, rows, window = got.shape
    units = FF // n
    inner = n // HEADS
    whole = inner * units
    got = got.astype(F32).reshape(n // inner, inner, rows, window)
    total = 0.0
    for i in range(inner):
        start = i * units // 128 * 128
        total = total + jnp.pad(got[:, i], ((0, 0), (0, 0), (start, whole - start - window)))
    return jnp.transpose(total, (1, 0, 2)).reshape(rows, FF)


def on_device(
    grid,
    tokens,
    segments,
    positions,
    cotangent,
    query_codes,
    key_codes,
    value_codes,
    output_codes,
    gate_codes,
    up_codes,
    down_codes,
    query_scale,
    key_scale,
    value_scale,
    output_scale,
    gate_scale,
    up_scale,
    down_scale,
    attention_gain,
    attention_post_gain,
    feed_gain,
    feed_post_gain,
):
    n = grid.n
    group, block, _ = tokens.shape
    length = n * block
    pairs = HEADS // KV_HEADS
    scale = HEAD ** (-0.5)
    chip, core = lax.axis_index("seq"), lax.axis_index("batch")
    half = n // 2
    member = chip // half
    head = chip % HEADS
    kv_head = head // pairs
    parts = half // HEADS
    copies = n // HEADS
    asked = length // parts
    first_asked = ((chip % half) // HEADS) * asked
    steps = [width_step(core * group + m) for m in range(group)]
    step = width_step(core * group + member)
    rows_d = D // n
    units, window, _ = feed_windows(grid)

    source = tokens.astype(F32)
    first_normed = normed(source, attention_gain).astype(BF16)
    q_parts = jnp.transpose(query_codes.reshape(rows_d, HEADS, HEAD), (1, 0, 2))
    k_parts = jnp.repeat(jnp.transpose(key_codes.reshape(rows_d, KV_HEADS, HEAD), (1, 0, 2)), pairs, axis=0)
    v_parts = jnp.repeat(jnp.transpose(value_codes.reshape(rows_d, KV_HEADS, HEAD), (1, 0, 2)), pairs, axis=0)
    qkv_parts = jnp.concatenate([q_parts, k_parts, v_parts], axis=-1).astype(BF16)
    small = jnp.zeros((8, 128), jnp.int32).at[:group, :block].set(positions)
    seen, qkv_codes, out_codes, all_places = open_kernel(
        grid, first_normed, qkv_parts, output_codes.astype(BF16), small, 1
    )
    seen = seen.reshape(length, D)

    qkv_scale = jnp.concatenate(
        [
            lax.dynamic_slice_in_dim(query_scale, head * HEAD, HEAD),
            lax.dynamic_slice_in_dim(key_scale, kv_head * HEAD, HEAD),
            lax.dynamic_slice_in_dim(value_scale, kv_head * HEAD, HEAD),
        ]
    )
    qkv_matrix = dequantized(qkv_codes.reshape(D, 3 * HEAD), qkv_scale, step)
    out_matrix = dequantized(out_codes.reshape(HEAD, D), output_scale, step)

    places_all = lax.dynamic_index_in_dim(all_places[:, :group, :block], member, 1, False).reshape(length)
    turn = angles(places_all, HEAD)
    cosine, sine = jnp.cos(turn), jnp.sin(turn)
    if parts == 1:
        seen_asked, places_asked, cosine_q, sine_q = seen, places_all, cosine, sine
        projected = dot(seen, qkv_matrix)
        q_lin, kv_lin = projected[:, :HEAD], projected[:, HEAD:]
    else:
        seen_asked, places_asked, cosine_q, sine_q = [
            lax.dynamic_slice_in_dim(a, first_asked, asked) for a in (seen, places_all, cosine, sine)
        ]
        q_lin, kv_lin = dot(seen_asked, qkv_matrix[:, :HEAD]), dot(seen, qkv_matrix[:, HEAD:])
    queries = rotate(q_lin, cosine_q, sine_q).astype(BF16)
    keys = rotate(kv_lin[:, :HEAD], cosine, sine).astype(BF16)
    values = kv_lin[:, HEAD:].astype(BF16)
    q_index = first_asked + jnp.arange(asked, dtype=jnp.int32)
    key_index = jnp.arange(length, dtype=jnp.int32)
    allowed = (key_index[None, :] <= q_index[:, None]) & (key_index[None, :] >= (q_index - places_asked)[:, None])
    bent = jnp.tanh(dot_t(queries, keys) * scale / cap_limit)
    kernel = jnp.where(allowed, jnp.exp(cap_limit * bent), 0.0)
    totals = jnp.sum(kernel, axis=-1, keepdims=True)
    kernel_low = kernel.astype(BF16)
    attended = dot(kernel_low, values) / totals
    attended_low = attended.astype(BF16)

    def spread(part):
        if parts > 1:
            part = lax.dynamic_update_slice_in_dim(jnp.zeros((length, D), BF16), part, first_asked, 0)
        return part.reshape(2, half, block, D)

    attention_raw, gate_got, up_got = attention_sums(
        grid,
        spread(dot(attended_low, out_matrix).astype(BF16)),
        gate_codes.astype(BF16),
        up_codes.astype(BF16),
        2,
    )
    attention_raw = attention_raw.astype(F32)
    first_column = chip * units // 128 * 128
    inset = chip * units - first_column
    pair_codes = jnp.concatenate([gate_got.reshape(D, window), up_got.reshape(D, window)], axis=-1)
    pair_scale = jnp.concatenate(
        [lax.dynamic_slice_in_dim(s, first_column, window) for s in (gate_scale, up_scale)]
    )
    pair_matrices = [dequantized(pair_codes, pair_scale, s) for s in steps]
    down_matrices = [
        lax.dynamic_update_slice(
            jnp.zeros((window, D), BF16), dequantized(down_codes, down_scale, s), (inset, 0)
        )
        for s in steps
    ]

    mixed = source + normed(attention_raw, attention_post_gain)
    second_normed = normed(mixed, feed_gain).astype(BF16)
    fed = gather(grid, second_normed, grid.planes, False, 3).reshape(group, length, D)
    gate_up = [dot(fed[m], pair_matrices[m]) for m in range(group)]
    hidden = [(jax.nn.gelu(g[:, :window], approximate=True) * g[:, window:]).astype(BF16) for g in gate_up]
    down_part = jnp.stack([dot(hidden[m], down_matrices[m]).astype(BF16) for m in range(group)])
    down_raw = feed_sums(grid, down_part.reshape(group, n, block, D), 4).astype(F32)
    branch, pull_out = jax.vjp(normed, down_raw, feed_post_gain)
    output = (mixed + branch).astype(BF16)
    upstream = cotangent.astype(F32)
    grad_down_raw, grad_post_feed = pull_out(upstream)
    down_low = gather(grid, grad_down_raw.astype(BF16), grid.planes, False, 3).reshape(group, length, D)
    pair_low, second_part = [], []
    for m in range(group):
        grad_hidden = dot_t(down_low[m], down_matrices[m])
        _, pull_glu = jax.vjp(
            lambda left, right: jax.nn.gelu(left, approximate=True) * right,
            gate_up[m][:, :window],
            gate_up[m][:, window:],
        )
        pair_low.append(jnp.concatenate(pull_glu(grad_hidden), axis=-1).astype(BF16))
        second_part.append(dot_t(pair_low[m], pair_matrices[m]).astype(BF16))
    pair_grad = sum(t_dot(fed[m], pair_low[m]) for m in range(group)).astype(BF16)
    down_grad = sum(t_dot(hidden[m], down_low[m]) for m in range(group)).astype(BF16)
    down_grad = lax.dynamic_slice(down_grad, (inset, 0), (units, D))
    grad_second, pair_got = feed_back_sums(
        grid, jnp.stack(second_part).reshape(group, n, block, D), pair_grad.reshape(n, rows_d, 2 * window), 5
    )
    grad_second = grad_second.astype(F32)
    gate_grad, up_grad = (unwindowed(grid, pair_got[..., i * window : (i + 1) * window]) for i in range(2))

    _, pull_feed = jax.vjp(normed, mixed, feed_gain)
    grad_mixed_part, grad_pre_feed = pull_feed(grad_second)
    grad_mixed = upstream + grad_mixed_part
    _, pull_post = jax.vjp(normed, attention_raw, attention_post_gain)
    grad_attention, grad_post_attention = pull_post(grad_mixed)
    attention_low = gather(grid, grad_attention.astype(BF16), grid.planes // 2, True, 6).reshape(length, D)
    if parts > 1:
        attention_low = lax.dynamic_slice_in_dim(attention_low, first_asked, asked)
    grad_attended = dot_t(attention_low, out_matrix)
    grad_sums = (grad_attended / totals).astype(BF16)
    offsets = jnp.sum(grad_attended * attended, axis=-1, keepdims=True) / totals
    grad_kernel = dot_t(grad_sums, values) - offsets
    grad_raw = (kernel * grad_kernel * (1.0 - bent * bent)).astype(BF16)
    grad_q = dot(grad_raw, keys) * scale
    grad_k = t_dot(grad_raw, queries) * scale
    grad_v = t_dot(kernel_low, grad_sums)
    q_low = rotate(grad_q, cosine_q, -sine_q).astype(BF16)
    kv_low = jnp.concatenate([rotate(grad_k, cosine, -sine), grad_v], axis=-1).astype(BF16)
    if parts == 1:
        qkv_low = jnp.concatenate([q_low, kv_low], axis=-1)
        first_part = dot_t(qkv_low, qkv_matrix)
        qkv_grad = t_dot(seen, qkv_low)
    else:
        first_part = dot_t(kv_low, qkv_matrix[:, HEAD:])
        q_back = dot_t(q_low, qkv_matrix[:, :HEAD])
        first_part = lax.dynamic_update_slice_in_dim(
            first_part, lax.dynamic_slice_in_dim(first_part, first_asked, asked) + q_back, first_asked, 0
        )
        qkv_grad = jnp.concatenate([t_dot(seen_asked, q_low), t_dot(seen, kv_low)], axis=-1)
    out_part = t_dot(attended_low, attention_low).astype(BF16).reshape(copies, HEAD // copies, D)
    grad_first, qkv_got, out_got, down_grad = attention_back_sums(
        grid,
        first_part.astype(BF16).reshape(2, half, block, D),
        qkv_grad.astype(BF16).reshape(n, rows_d, 3 * HEAD),
        out_part,
        down_grad,
        7,
    )
    grad_first = grad_first.astype(F32)
    _, pull_in = jax.vjp(normed, source, attention_gain)
    grad_source_part, grad_pre_attention = pull_in(grad_first)
    grad_in = (grad_mixed + grad_source_part).astype(BF16)
    qkv_got = jnp.sum(qkv_got.astype(F32).reshape(copies, HEADS, rows_d, 3 * HEAD), axis=0)
    query_grad = jnp.transpose(qkv_got[..., :HEAD], (1, 0, 2)).reshape(rows_d, HEADS * HEAD)
    kv_grad = jnp.sum(qkv_got[..., HEAD:].reshape(KV_HEADS, pairs, rows_d, 2 * HEAD), axis=1)
    key_grad = jnp.transpose(kv_grad[..., :HEAD], (1, 0, 2)).reshape(rows_d, KV_HEADS * HEAD)
    value_grad = jnp.transpose(kv_grad[..., HEAD:], (1, 0, 2)).reshape(rows_d, KV_HEADS * HEAD)
    out_grad = jnp.sum(out_got.astype(F32), axis=0)
    gains = jnp.stack([grad_pre_attention, grad_post_attention, grad_pre_feed, grad_post_feed])
    gains = jnp.sum(gains_kernel(grid, gains.reshape(8, D // 2), 8), axis=0).reshape(4, D)
    return (
        output,
        grad_in,
        query_grad,
        key_grad,
        value_grad,
        out_grad,
        gate_grad,
        up_grad,
        down_grad,
    ) + tuple(gains[i] for i in range(4))


def solution(mesh):
    rows = P("seq", None)
    return jax.shard_map(
        functools.partial(on_device, Grid(mesh.shape["seq"])),
        mesh=mesh,
        in_specs=(P("batch", "seq", None), P("batch", "seq"), P("batch", "seq"), P("batch", "seq", None))
        + (rows,) * 7
        + (P(),) * 11,
        out_specs=(P("batch", "seq", None),) * 2 + (rows,) * 7 + (P(),) * 4,
        check_vma=False,
    )
```

time: 1250 us -> 1020 us (0.82)
  Pallas kernels: 837 us -> 751 us
  blocking collectives: 58.5 us -> 0 us
  local copies, waits for them, and re-layouts: 81.4 us -> 51.9 us
  other arithmetic: 107 us -> 83.4 us
  starting transfers between devices: 16.6 us -> 0 us
    pallas_call x4 -> x3, Pallas kernels: 347 us -> 231 us  [gather(): pl.pallas_call(kernel, out_shape=jax.ShapeDtypeStruct((2, count) + x.shap...]
    psum x1 -> x0, blocking collectives: 58.5 us -> none  [on_device(): lax.psum((grad_pre_attention, grad_post_attention, grad_pre_feed, grad_po...]
    pallas_call x10 -> x6, Pallas kernels: 491 us -> 520 us  [the longest x4 407 us: call(): pl.pallas_call(kernel, out_shape=(jax.ShapeDtypeStruct((2, rows, width),...]
    convert_element_type x4 -> x0, local copies, waits for them, and re-layouts: 25.7 us -> none  [the longest x2 14.2 us: on_device(): jnp.transpose(pair_got[..., units:], (1, 0, 2)).reshape(rows_d, FF)]
    ppermute x4 -> x0, starting transfers between devices: 16.6 us -> none  [the longest x2 10 us: on_device(): lax.ppermute(out_low, 'seq', [(h * copies + j, h + HEADS * ((j + copies -...]
  transfers between devices with their start and end apart: 4 -> 0, of which waited for: 0 -> 0; matrix products, arithmetic and copies ran while one was open for 10% -> 0% of each run, Pallas kernels for 20% -> 0%
where the time goes in v2:
time: 1020 us
  Pallas kernels  751 us (74%)
  matrix products  128 us (13%)
  other arithmetic  83.4 us (8%)
  local copies, waits for them, and re-layouts  51.9 us (5%)
    pallas_call x4, Pallas kernels, call(): pl.pallas_call(kernel, out_shape=(jax.ShapeDtypeStruct((2, rows, width),...  407 us
    pallas_call x3, Pallas kernels, gather(): pl.pallas_call(kernel, out_shape=jax.ShapeDtypeStruct((2, count) + x.shap...  231 us
    pallas_call x1, Pallas kernels, open_kernel(): pl.pallas_call(kernel, out_shape=(jax.ShapeDtypeStruct((2, levels * grid....  97 us
    dot_general x8, matrix products, dot_t(): lax.dot_general(left, right, (((1,), (1,)), ((), ())), preferred_element_...  50 us
    dot_general x8, matrix products, dot(): return jnp.dot(left, right, preferred_element_type=F32)  42.1 us
    dot_general x8, matrix products, t_dot(): lax.dot_general(left, right, (((0,), (0,)), ((), ())), preferred_element_...  36 us

profile of v2, /device:TPU:0, one launch (start us, length us, event | category | flops | bytes accessed | tf_op | source)
XLA Modules:
  0.0 1017.4 jit_solution(8472242757949664547)
XLA Ops:
  11.6 4.5 convert_element_type.170.refs_1_
  19.8 2.6 fusion.14
  23.9 97.0 %open.1 = (bf16[2,8,64,2304]{3,2,1,0:T(8,128)(2,1)}, bf16[2304,768]{1,0:T(8,128)(2,1)}, bf16[2,128,2304]{2,1,0:T(8,128)(2,1)S(1)}, s32[16,8,128]{2,1,0:T(8,128)S(1)}) custom-call(bf16[2,64,2304]{2,1,0:T(8,128)(2,1)S(1)} %fusion.42.x_ref, bf16[8,144,768]{2,1,0:T(8,128)(2,1)} %pad_maximum_fusion.5.w_ref, bf16[128,2304]{1,0:T(8,128)(2,1)S(1)} %convert_element_type.161.o_ref, ...), custom_call_target="tpu_custom_call" | custom-call | tf_op jit(solution)/shard_map/open/pallas_call | solution.py:759
  121.1 7.5 fusion.114
  128.6 2.4 fusion.86
  136.6 3.6 convolution_convert_fusion.5
  140.2 101.0 %attention_sums.1 = (bf16[2,64,2304]{2,1,0:T(8,128)(2,1)}, bf16[2304,640]{1,0:T(8,128)(2,1)}, bf16[2304,640]{1,0:T(8,128)(2,1)}) custom-call(bf16[2,8,64,2304]{3,2,1,0:T(8,128)(2,1)} %bitcast.101, bf16[144,9216]{1,0:T(8,128)(2,1)} %convert_element_type.170.refs_1_, bf16[144,9216]{1,0:T(8,128)(2,1)} %convert_element_type.171.refs_2_), custom_call_target="tpu_custom_call" | custom-call | tf_op jit(solution)/shard_map/attention_sums/pallas_call | solution.py:801
  247.4 7.7 fusion.4
  255.1 90.6 %gather_16.2 = bf16[2,16,64,2304]{3,2,1,0:T(8,128)(2,1)} custom-call(bf16[2,64,2304]{2,1,0:T(8,128)(2,1)S(1)} %multiply_convert_fusion.9.x_ref), custom_call_target="tpu_custom_call" | custom-call | tf_op jit(solution)/shard_map/gather_16/pallas_call | solution.py:242
  345.7 8.5 fusion.116
  354.3 8.5 fusion.120
  362.8 2.3 copy-done.8
  366.1 8.2 convolution_convert_fusion.1
  374.4 6.2 fusion.119
  384.4 5.5 convolution_convert_fusion.2
  390.0 8.3 pad_maximum_fusion.refs_0_
  398.3 80.6 %feed_sums.1 = bf16[2,64,2304]{2,1,0:T(8,128)(2,1)} custom-call(bf16[2,16,64,2304]{3,2,1,0:T(8,128)(2,1)} %pad_maximum_fusion.refs_0_), custom_call_target="tpu_custom_call" | custom-call | tf_op jit(solution)/shard_map/feed_sums/pallas_call | solution.py:801
  483.9 82.0 %gather_16.3 = bf16[2,16,64,2304]{3,2,1,0:T(8,128)(2,1)} custom-call(bf16[2,64,2304]{2,1,0:T(8,128)(2,1)S(1)} %fusion.50.x_ref), custom_call_target="tpu_custom_call" | custom-call | tf_op jit(solution)/shard_map/gather_16/pallas_call | solution.py:242
  565.9 4.8 fusion.115
  570.7 8.2 fusion.21
  578.9 3.3 fusion.121
  582.2 10.9 %convolution_convert_fusion.4 = bf16[1024,2304]{1,0:T(8,128)(2,1)} fusion(bf16[2304,1280]{1,0:T(8,128)(2,1)} %get-tuple-element.66, bf16[1024,640]{1,0:T(8,128)(2,1)S(1)} %get-tuple-element.63, bf16[1024,640]{1,0:T(8,128)(2,1)S(1)} %get-tuple-element.62), kind=kOutput, calls=%fused_computation.23 | convolution fusion | flops 6047399936 | bytes 13238272 | tf_op jit(solution)/shard_map/dot_general | solution.py:958
  593.2 7.2 fusion.28
  600.4 3.3 fusion.122
  606.8 7.9 convolution_convert_fusion.3
  614.7 8.5 pad_maximum_fusion.1.refs_0_
  623.2 9.0 fusion.32
  632.3 10.0 fusion.10
  642.3 128.3 %feed_back_sums.1 = (bf16[2,64,2304]{2,1,0:T(8,128)(2,1)}, bf16[16,144,1280]{2,1,0:T(8,128)(2,1)}) custom-call(bf16[2,16,64,2304]{3,2,1,0:T(8,128)(2,1)} %pad_maximum_fusion.1.refs_0_, bf16[16,144,1280]{2,1,0:T(8,128)(2,1)} %bitcast.114), custom_call_target="tpu_custom_call" | custom-call | tf_op jit(solution)/shard_map/feed_back_sums/pallas_call | solution.py:801
  770.7 3.4 fusion.117
  777.9 2.9 copy.119
  782.0 2.9 copy.120
  785.0 58.7 %gather_8.1 = bf16[2,8,64,2304]{3,2,1,0:T(8,128)(2,1)} custom-call(bf16[2,64,2304]{2,1,0:T(8,128)(2,1)S(1)} %fusion.51.x_ref), custom_call_target="tpu_custom_call" | custom-call | tf_op jit(solution)/shard_map/gather_8/pallas_call | solution.py:242
  843.7 3.9 multiply_reduce_fusion.1
  847.7 2.5 convolution_convert_fusion.7
  850.2 4.0 multiply_convert_fusion.3
  856.0 2.3 fusion.97
  858.3 2.3 fusion.96
  860.5 2.3 fusion.95
  862.8 2.3 fusion.94
  866.9 5.5 convolution_convert_fusion.6
  872.4 6.1 convolution_convert_fusion
  878.5 97.2 %attention_back_sums.1 = (bf16[2,64,2304]{2,1,0:T(8,128)(2,1)}, bf16[16,144,768]{2,1,0:T(8,128)(2,1)}, bf16[2,128,2304]{2,1,0:T(8,128)(2,1)}, f32[576,2304]{1,0:T(8,128)}) custom-call(bf16[2,8,64,2304]{3,2,1,0:T(8,128)(2,1)} %bitcast.134, bf16[16,144,768]{2,1,0:T(8,128)(2,1)} %bitcast.138, bf16[2,128,2304]{2,1,0:T(8,128)(2,1)} %bitcast.144, ...), custom_call_target="tpu_custom_call" | custom-call | tf_op jit(solution)/shard_map/attention_back_sums/pallas_call | solution.py:801
  975.7 4.8 convert_reduce_fusion
  984.5 2.9 fusion.53
  987.3 16.0 %gains.1 = f32[16,8,1152]{2,1,0:T(8,128)} custom-call(f32[8,1152]{1,0:T(8,128)} %reshape.322.x_ref), custom_call_target="tpu_custom_call" | custom-call | tf_op jit(solution)/shard_map/gains/pallas_call | solution.py:915
  1006.9 2.2 bitcast_reduce_fusion
  1014.8 2.4 copy.130
  (288 shorter events, 61.7 us)
Async XLA Ops:
  0.6 7.5 copy-start.26
  0.8 127.8 %copy-start.55 = (f32[128]{0:T(128)}, f32[128]{0:T(128)S(1)}, u32[]{:S(2)}) copy-start(f32[128]{0:T(128)S(1)} %negate_power_fusion) | copy-start | bytes 1540
  2.9 5.6 copy-start.53
  4.4 116.7 %copy-start.64 = (f32[768]{0:T(1024)}, f32[768]{0:T(1024)S(1)}, u32[]{:S(2)}) copy-start(f32[768]{0:T(1024)S(1)} %pad_maximum_fusion.18) | copy-start | bytes 9220
  9.4 6.8 slice-start.6
  11.5 4.6 slice-start.7
  11.6 8.2 slice-start
  23.9 97.1 %copy-start.15 = (bf16[640,2304]{1,0:T(8,128)(2,1)}, bf16[640,2304]{1,0:T(8,128)(2,1)S(1)}, u32[]{:S(2)}) copy-start(bf16[640,2304]{1,0:T(8,128)(2,1)S(1)} %fusion.13) | copy-start | bytes 8847364
  121.1 7.5 copy-start.39
  121.1 13.6 %copy-start.66 = (s32[1024]{0:T(1024)}, s32[1024]{0:T(1024)S(1)}, u32[]{:S(2)}) copy-start(s32[1024]{0:T(1024)S(1)} %get-tuple-element.88) | copy-start | bytes 12292
  121.1 13.6 %copy-start.68 = (s32[1024]{0:T(1024)}, s32[1024]{0:T(1024)S(1)}, u32[]{:S(2)}) copy-start(s32[1024]{0:T(1024)S(1)} %get-tuple-element.94) | copy-start | bytes 12292
  128.6 6.1 copy-start.21
  140.2 103.0 %copy-start.27 = (f32[2304]{0:T(1024)S(1)}, f32[2304]{0:T(1024)}, u32[]{:S(2)}) copy-start(f32[2304]{0:T(1024)} %param.42) | copy-start | bytes 27652
  140.2 105.7 %copy-start.29 = (f32[2304]{0:T(1024)S(1)}, f32[2304]{0:T(1024)}, u32[]{:S(2)}) copy-start(f32[2304]{0:T(1024)} %param.43) | copy-start | bytes 27652
  241.2 6.1 copy-start.17
  255.1 99.2 %copy-start.7 = (bf16[2304,1280]{1,0:T(8,128)(2,1)}, bf16[2304,1280]{1,0:T(8,128)(2,1)S(1)}, u32[]{:S(2)}) copy-start(bf16[2304,1280]{1,0:T(8,128)(2,1)S(1)} %get-tuple-element.67) | copy-start | bytes 17694724
  365.2 9.2 slice-start.4
  365.2 9.2 slice-start.14
  366.1 8.3 copy-start.10
  366.1 8.3 slice-start.5
  366.1 8.3 slice-start.15
  384.4 5.6 copy-start.12
  398.3 81.9 %copy-start.4 = (bf16[2,64,2304]{2,1,0:T(8,128)(2,1)S(1)}, bf16[2,64,2304]{2,1,0:T(8,128)(2,1)}, u32[]{:S(2)}) copy-start(bf16[2,64,2304]{2,1,0:T(8,128)(2,1)} %param.26) | copy-start | bytes 1769476
  398.3 81.9 %copy-start.43 = (f32[2304]{0:T(1024)S(1)}, f32[2304]{0:T(1024)}, u32[]{:S(2)}) copy-start(f32[2304]{0:T(1024)} %param.44) | copy-start | bytes 27652
  570.6 8.2 copy-start.13
  578.9 14.3 %slice-start.10 = ((s8[5242880]{0:T(1024)(128)(4,1)}), s8[4194304]{0:T(1024)(128)(4,1)S(1)}, s32[]{:S(2)}) async-start(s8[5242880]{0:T(1024)(128)(4,1)} %bitcast.121), calls=%async_computation.10 | async-start | bytes 8388608
  582.2 11.0 %slice-start.11 = ((s8[5242880]{0:T(1024)(128)(4,1)}), s8[1048576]{0:T(1024)(128)(4,1)S(1)}, s32[]{:S(2)}) async-start(s8[5242880]{0:T(1024)(128)(4,1)} %bitcast.121), calls=%async_computation.11 | async-start | bytes 2097152
  593.2 7.2 copy-start.11
  600.4 5.3 copy-start.77
  600.4 5.3 copy-start.79
  600.4 5.3 slice-start.2
  614.7 8.5 copy-start.74
  614.7 8.5 copy-start.76
  614.7 17.5 %slice-start.12 = ((s8[4718592]{0:T(1024)(128)(4,1)}), s8[524288]{0:T(1024)(128)(4,1)S(1)}, s32[]{:S(2)}) async-start(s8[4718592]{0:T(1024)(128)(4,1)} %bitcast.126), calls=%async_computation.12 | async-start | bytes 1048576
  623.2 9.1 slice-start.13
  623.2 9.1 copy-start.78
  784.9 58.7 %copy-start.20 = (f32[1024,256]{0,1:T(8,128)S(1)}, f32[1024,256]{0,1:T(8,128)}, u32[]{:S(2)}) copy-start(f32[1024,256]{0,1:T(8,128)} %copy-done.19) | copy-start | bytes 3145732
  785.0 58.7 %copy-start.25 = (bf16[2,128,2304]{2,1,0:T(8,128)(2,1)S(1)}, bf16[2,128,2304]{2,1,0:T(8,128)(2,1)}, u32[]{:S(2)}) copy-start(bf16[2,128,2304]{2,1,0:T(8,128)(2,1)} %get-tuple-element.82) | copy-start | bytes 3538948
  855.2 11.6 %slice-start.16 = ((s8[4718592]{0:T(1024)(128)(4,1)}), s8[4194304]{0:T(1024)(128)(4,1)S(1)}, s32[]{:S(2)}) async-start(s8[4718592]{0:T(1024)(128)(4,1)} %bitcast.152), calls=%async_computation.16 | async-start | bytes 8388608
  866.9 5.5 copy-start.65
  866.9 5.5 copy-start.70
  975.7 4.9 copy-start.18
  975.7 4.9 copy-start.42
  975.7 4.9 copy-start.54
  975.7 6.0 copy-start.48
  975.7 8.8 copy-start.3
  1006.9 7.8 slice-start.8
  1010.5 4.2 slice-start.9
  (50 other events, 120.4 us)

commit v3 on v2

--- a/solution.py
+++ b/solution.py
@@ -211,14 +211,14 @@
             swap_in.wait_recv()
         for group in wave:
             arrive(*group)
-        if i == 0:
             yield
-        else:
+        if i > 0:
             for group in waves[i - 1]:
                 onward(*group)
+                yield
     for group in waves[-1]:
         onward(*group)
-    yield
+        yield
     for wave in waves:
         for group in wave:
             finish(*group)
@@ -248,6 +248,421 @@
         compiler_params=params(cid, 50),
         name="gather_%d" % count,
     )(x)
+
+
+class LevelGather:
+    def __init__(self, at, x_ref, out_ref, zs, zr, rs, rr, ls):
+        self.at, self.x, self.out = at, x_ref, out_ref
+        self.zs, self.zr, self.rs, self.rr, self.ls = zs, zr, rs, rr, ls
+        self.half = x_ref.shape[1] // 2
+
+    def block(self, zj, qj, part=None):
+        if part is None:
+            return self.out.at[:, self.at.slot(zj, qj)]
+        return self.out.at[:, self.at.slot(zj, qj), pl.ds(part * self.half, self.half)]
+
+    def z_copy(self, zj, way):
+        at, ref = self.at, self.block(zj, self.at.q)
+        to = at.c + (at.pn if way == 0 else -at.pn)
+        return remote(ref, ref, self.zs.at[0, way, zj], self.zr.at[0, way, zj], to, at.b)
+
+    def r_copy(self, zj, way, step, landing=False):
+        at = self.at
+        away = step if landing else step - 1
+        ref = self.block(zj, at.q - away if way == 0 else at.q + away, way if step == at.steps else None)
+        to = at.right if way == 0 else at.left
+        return remote(ref, ref, self.rs.at[0, way, step - 1, zj], self.rr.at[0, way, step - 1, zj], to, at.b)
+
+    def begin(self):
+        local = pltpu.make_async_copy(self.x, self.block(self.at.zi, self.at.q), self.ls.at[0])
+        local.start()
+        local.wait()
+        self.send(0)
+
+    def send(self, offset):
+        at = self.at
+        zj = at.zi + offset
+        pl.when((offset <= 0) & (at.zi < at.levels - 1))(lambda: self.z_copy(zj, 0).start())
+        pl.when((offset >= 0) & (at.zi > 0))(lambda: self.z_copy(zj, 1).start())
+        for way in (0, 1):
+            self.r_copy(zj, way, 1).start()
+
+    def arrive(self, sign, d):
+        zj = self.at.zi + sign * d
+        self.z_copy(zj, 0 if sign < 0 else 1).wait_recv()
+        self.send(sign * d)
+
+    def onward(self, sign, d):
+        zj = self.at.zi + sign * d
+        for step in range(1, self.at.steps + 1):
+            for way in (0, 1):
+                self.r_copy(zj, way, step, True).wait_recv()
+                if step < self.at.steps:
+                    self.r_copy(zj, way, step + 1).start()
+
+    def finish(self):
+        at = self.at
+
+        def one(zj, carry):
+            pl.when((zj <= at.zi) & (at.zi < at.levels - 1))(lambda: self.z_copy(zj, 0).wait_send())
+            pl.when((zj >= at.zi) & (at.zi > 0))(lambda: self.z_copy(zj, 1).wait_send())
+            for way in (0, 1):
+                for step in range(1, at.steps + 1):
+                    self.r_copy(zj, way, step).wait_send()
+            return carry
+
+        lax.fori_loop(0, at.levels, one, 0)
+
+    def run(self, compute):
+        at = self.at
+        zi, levels = at.zi, at.levels
+
+        def one(t, carry):
+            pl.when((t < levels) & (zi - t >= 0))(lambda: self.arrive(-1, t))
+            pl.when((t < levels) & (zi + t < levels))(lambda: self.arrive(1, t))
+            e = t - 2
+
+            def side(i, carry):
+                zj = zi + (2 * i - 1) * e
+                here = (e >= 0) & (zj >= 0) & (zj < levels) & ((e > 0) | (i == 0))
+                pl.when(here)(lambda: compute(zj, e == 0))
+                return carry
+
+            lax.fori_loop(0, 2, side, 0)
+            d = t - 1
+            pl.when((d < levels) & (zi - d >= 0))(lambda: self.onward(-1, d))
+            pl.when((d > 0) & (d < levels) & (zi + d < levels))(lambda: self.onward(1, d))
+            return carry
+
+        lax.fori_loop(1, levels + 2, one, 0)
+        self.finish()
+
+
+def member_step(core, group, member):
+    remainder = (core * group + member) % 3
+    return jnp.where(remainder == 0, 1.0, jnp.where(remainder == 1, 16.0, 64.0)).astype(F32)
+
+
+def dequantize(core, group, codes, row_scale, into, rows, first):
+    def one(i, carry):
+        value = codes(pl.multiple_of(i * 16, 16)).astype(F32)
+        for m in range(group):
+            step = member_step(core, group, m)
+            offset = jnp.where(step > 1.0, 0.5 * step, 0.0)
+            level = jnp.floor(value * (1.0 / step)) * step + offset
+            into[m, pl.ds(pl.multiple_of(first + i * 16, 16), 16)] = (level * row_scale[...]).astype(BF16)
+        return carry
+
+    lax.fori_loop(0, rows // 16, one, 0)
+
+
+GELU_A = 0.7978845608028654
+GELU_B = 0.044715
+
+
+class FeedWeights:
+    def __init__(self, at, group, units, gate_ref, up_ref, down_ref, kept, refs):
+        self.at, self.group, self.units = at, group, units
+        self.sources, self.kept = (gate_ref, up_ref, down_ref), kept
+        self.pair, self.down, self.codes, self.down_codes, self.sems = refs
+
+    @staticmethod
+    def scratch(group, units, window):
+        return [
+            pltpu.VMEM((group, D, 2 * window), BF16),
+            pltpu.VMEM((group, window, D), BF16),
+            pltpu.VMEM((D, 2 * window), BF16),
+            pltpu.VMEM((units, D), jnp.int32),
+            dma(5),
+        ]
+
+    def copies(self):
+        window = self.codes.shape[1] // 2
+        gate, up, down = self.sources
+        return [
+            pltpu.make_async_copy(gate, self.codes.at[:, pl.ds(0, window)], self.sems.at[0]),
+            pltpu.make_async_copy(up, self.codes.at[:, pl.ds(window, window)], self.sems.at[1]),
+            pltpu.make_async_copy(down, self.down_codes, self.sems.at[2]),
+        ]
+
+    def keeps(self):
+        return [
+            pltpu.make_async_copy(self.pair, self.kept[0], self.sems.at[3]),
+            pltpu.make_async_copy(self.down, self.kept[1], self.sems.at[4]),
+        ]
+
+    def load(self):
+        for copy in self.copies():
+            copy.start()
+
+    def make(self, pair_scale, down_scale):
+        at, group, units = self.at, self.group, self.units
+        window = self.down.shape[1]
+        inset = (at.c * units) % 128
+        for copy in self.copies():
+            copy.wait()
+        dequantize(at.b, group, lambda r: self.codes[pl.ds(r, 16)], pair_scale, self.pair, D, 0)
+
+        def clear(i, carry):
+            for m in range(group):
+                self.down[m, pl.ds(pl.multiple_of(i * 16, 16), 16)] = jnp.zeros((16, D), BF16)
+            return carry
+
+        if window > units:
+            lax.fori_loop(0, inset // 16, clear, 0)
+            lax.fori_loop((inset + units) // 16, window // 16, clear, 0)
+        dequantize(at.b, group, lambda r: self.down_codes[pl.ds(r, 16)], down_scale, self.down, units, inset)
+        for copy in self.keeps():
+            copy.start()
+
+    def finish(self):
+        for copy in self.keeps():
+            copy.wait()
+
+
+def feed_blocks(grid):
+    return 4 if grid.plane % 4 == 0 else grid.plane
+
+
+def each_chunk(grid, group, zj, fresh, loads, stores, compute, after=None):
+    size = feed_blocks(grid)
+    count = grid.plane // size
+
+    def first(i):
+        return zj * grid.plane + i * size
+
+    for m in range(group):
+        for copy in loads(m, first(0)):
+            copy.start()
+
+    def one(i, carry):
+        for m in range(group):
+            reads, writes = loads(m, first(i)), stores(m, first(i))
+
+            @pl.when(jnp.logical_not(fresh & (i == 0)))
+            def _():
+                for copy in writes:
+                    copy.wait()
+
+            compute(m, reads)
+            for copy in writes:
+                copy.start()
+        if after is not None:
+            after([loads(m, first(i)) for m in range(group)])
+
+        @pl.when(i + 1 < count)
+        def _():
+            for m in range(group):
+                for copy in loads(m, first(i + 1)):
+                    copy.start()
+
+        return carry
+
+    lax.fori_loop(0, count, one, 0)
+
+
+def feed_forward(grid, x, gate_codes, up_codes, down_codes, pair_scale, down_scale, cid):
+    group, rows, _ = x.shape
+    n, levels = grid.n, grid.planes
+    units, window, _ = feed_windows(grid)
+    gs, ws = gather_sems(grid, levels, False), FeedWeights.scratch(group, units, window)
+    size = feed_blocks(grid)
+    count = size * rows
+
+    def kernel(
+        x_ref, gate_ref, up_ref, down_ref, ps_ref, ds_ref, all_ref, pair_ref, part_ref, wp_ref, wd_ref, *scratch
+    ):
+        refs = Split(scratch)
+        at = Place(grid, levels)
+        weights = FeedWeights(at, group, units, gate_ref, up_ref, down_ref, (wp_ref, wd_ref), refs.take(len(ws)))
+        weights.load()
+        moving = LevelGather(at, x_ref, all_ref, *refs.take(len(gs)))
+        xs, gu, part, sems = refs.take(4)
+        at.greet_near(False)
+        moving.begin()
+        weights.make(ps_ref, ds_ref)
+
+        def loads(m, first):
+            return [pltpu.make_async_copy(all_ref.at[m, pl.ds(first, size)], xs.at[m], sems.at[0, m])]
+
+        def stores(m, first):
+            return [
+                pltpu.make_async_copy(gu.at[m], pair_ref.at[m, pl.ds(first, size)], sems.at[1, m]),
+                pltpu.make_async_copy(part.at[m], part_ref.at[m, pl.ds(first, size)], sems.at[2, m]),
+            ]
+
+        def compute(m, reads):
+            reads[0].wait()
+            both = dot(xs[m].reshape(count, D), weights.pair[m])
+            gu[m] = both.astype(BF16).reshape(size, rows, 2 * window)
+            gate, up = both[:, :window], both[:, window:]
+            bend = jnp.tanh(GELU_A * (gate + GELU_B * gate * gate * gate))
+            hidden = (0.5 * gate * (1.0 + bend) * up).astype(BF16)
+            part[m] = dot(hidden, weights.down[m]).astype(BF16).reshape(size, rows, D)
+
+        moving.run(lambda zj, fresh: each_chunk(grid, group, zj, fresh, loads, stores, compute))
+        for m in range(group):
+            for copy in stores(m, 0):
+                copy.wait()
+        weights.finish()
+
+    def blocks(width):
+        return jax.ShapeDtypeStruct((group, n, rows, width), BF16)
+
+    return pl.pallas_call(
+        kernel,
+        out_shape=(
+            blocks(D),
+            blocks(2 * window),
+            blocks(D),
+            jax.ShapeDtypeStruct((group, D, 2 * window), BF16),
+            jax.ShapeDtypeStruct((group, window, D), BF16),
+        ),
+        in_specs=[INVMEM, ANY, ANY, ANY, INVMEM, INVMEM],
+        out_specs=(ANY,) * 5,
+        scratch_shapes=ws
+        + gs
+        + [
+            pltpu.VMEM((group, size, rows, D), BF16),
+            pltpu.VMEM((group, size, rows, 2 * window), BF16),
+            pltpu.VMEM((group, size, rows, D), BF16),
+            dma(3, group),
+        ],
+        compiler_params=params(cid, 60),
+        name="feed_forward",
+    )(x, gate_codes, up_codes, down_codes, pair_scale, down_scale)
+
+
+def feed_backward(grid, x, fed, pair, pair_matrices, down_matrices, cid):
+    group, rows, _ = x.shape
+    n, levels = grid.n, grid.planes
+    units, window, _ = feed_windows(grid)
+    gs = gather_sems(grid, levels, False)
+    size = feed_blocks(grid)
+    count = size * rows
+    tile = 256
+
+    def kernel(x_ref, fed_ref, pair_ref, wp_ref, wd_ref, all_ref, part_ref, pg_ref, dg_ref, *scratch):
+        refs = Split(scratch)
+        at = Place(grid, levels)
+        moving = LevelGather(at, x_ref, all_ref, *refs.take(len(gs)))
+        wp, wd, xs, ys, gu, part, pair_sum, down_sum, dgu, hid, sems = refs.take(11)
+        fetch = [
+            pltpu.make_async_copy(wp_ref, wp, sems.at[4, 0]),
+            pltpu.make_async_copy(wd_ref, wd, sems.at[4, 1]),
+        ]
+        for copy in fetch:
+            copy.start()
+        at.greet_near(False)
+        moving.begin()
+
+        def clear(i, carry):
+            pair_sum[pl.ds(pl.multiple_of(i * 8, 8), 8)] = jnp.zeros((8, 2 * window), F32)
+            return carry
+
+        lax.fori_loop(0, D // 8, clear, 0)
+
+        def clear_down(i, carry):
+            down_sum[pl.ds(pl.multiple_of(i * 8, 8), 8)] = jnp.zeros((8, D), F32)
+            return carry
+
+        lax.fori_loop(0, window // 8, clear_down, 0)
+        for copy in fetch:
+            copy.wait()
+
+        def loads(m, first):
+            blocks = pl.ds(first, size)
+            return [
+                pltpu.make_async_copy(all_ref.at[m, blocks], ys.at[m], sems.at[0, m]),
+                pltpu.make_async_copy(pair_ref.at[m, blocks], gu.at[m], sems.at[1, m]),
+                pltpu.make_async_copy(fed_ref.at[m, blocks], xs.at[m], sems.at[2, m]),
+            ]
+
+        def stores(m, first):
+            return [pltpu.make_async_copy(part.at[m], part_ref.at[m, pl.ds(first, size)], sems.at[3, m])]
+
+        def compute(m, reads):
+            reads[0].wait()
+            grad_hidden = dot_t(ys[m].reshape(count, D), wd[m])
+            reads[1].wait()
+            both = gu[m].reshape(count, 2 * window).astype(F32)
+            gate, up = both[:, :window], both[:, window:]
+            bend = jnp.tanh(GELU_A * (gate + GELU_B * gate * gate * gate))
+            bell = 0.5 * gate * (1.0 + bend)
+            slope = 0.5 * (1.0 + bend) + 0.5 * gate * (1.0 - bend * bend) * GELU_A * (1.0 + 3.0 * GELU_B * gate * gate)
+            mine = pl.ds(m * count, count)
+            dgu[mine, :window] = (grad_hidden * up * slope).astype(BF16)
+            dgu[mine, window:] = (grad_hidden * bell).astype(BF16)
+            hid[mine] = (bell * up).astype(BF16)
+            part[m] = dot_t(dgu[mine], wp[m]).astype(BF16).reshape(size, rows, D)
+
+        def weight_sums(reads):
+            for read in reads:
+                read[2].wait()
+
+            def one(j, carry):
+                cols = pl.ds(pl.multiple_of(j * tile, tile), tile)
+                pair_sum[cols] = pair_sum[cols] + t_dot(xs[:, :, :, cols].reshape(group * count, tile), dgu[...])
+                down_sum[:, cols] = down_sum[:, cols] + t_dot(hid[...], ys[:, :, :, cols].reshape(group * count, tile))
+                return carry
+
+            lax.fori_loop(0, D // tile, one, 0)
+
+        moving.run(lambda zj, fresh: each_chunk(grid, group, zj, fresh, loads, stores, compute, weight_sums))
+
+        def low(i, carry):
+            r = pl.ds(pl.multiple_of(i * 16, 16), 16)
+            wp[0, r] = pair_sum[r].astype(BF16)
+            return carry
+
+        lax.fori_loop(0, D // 16, low, 0)
+        give_pair = pltpu.make_async_copy(wp.at[0], pg_ref, sems.at[4, 0])
+        give_pair.start()
+
+        def low_down(i, carry):
+            r = pl.ds(pl.multiple_of(i * 16, 16), 16)
+            wd[0, r] = down_sum[r].astype(BF16)
+            return carry
+
+        lax.fori_loop(0, window // 16, low_down, 0)
+        give_down = pltpu.make_async_copy(wd.at[0], dg_ref, sems.at[4, 1])
+        give_down.start()
+        for m in range(group):
+            for copy in stores(m, 0):
+                copy.wait()
+        give_pair.wait()
+        give_down.wait()
+
+    def blocks(width):
+        return jax.ShapeDtypeStruct((group, n, rows, width), BF16)
+
+    return pl.pallas_call(
+        kernel,
+        out_shape=(
+            blocks(D),
+            blocks(D),
+            jax.ShapeDtypeStruct((D, 2 * window), BF16),
+            jax.ShapeDtypeStruct((window, D), BF16),
+        ),
+        in_specs=[INVMEM] + [ANY] * 4,
+        out_specs=(ANY,) * 4,
+        scratch_shapes=gs
+        + [
+            pltpu.VMEM((group, D, 2 * window), BF16),
+            pltpu.VMEM((group, window, D), BF16),
+            pltpu.VMEM((group, size, rows, D), BF16),
+            pltpu.VMEM((group, size, rows, D), BF16),
+            pltpu.VMEM((group, size, rows, 2 * window), BF16),
+            pltpu.VMEM((group, size, rows, D), BF16),
+            pltpu.VMEM((D, 2 * window), F32),
+            pltpu.VMEM((window, D), F32),
+            pltpu.VMEM((group * count, 2 * window), BF16),
+            pltpu.VMEM((group * count, window), BF16),
+            dma(5, group),
+        ],
+        compiler_params=params(cid, 62),
+        name="feed_backward",
+    )(x, fed, pair, pair_matrices, down_matrices)
 
 
 def scatter_scratch(grid, levels, halves, rows, width):
@@ -387,11 +802,12 @@
         if i + 1 < len(waves):
             for group in waves[i + 1]:
                 begin(*group)
+            yield
         for group in wave:
             onward(*group)
+            yield
         if halves and wave[0][0] == 0 and wave[0][3] == 0:
             swap.start()
-    yield
 
     def give(src, u):
         def one(i, carry):
@@ -447,7 +863,11 @@
     return to, frm
 
 
-def share_steps(at, sources, views, ss, sr, fs, fr):
+def middle_out(half):
+    return sorted(range(1, half), key=lambda i: abs(2 * i - half))
+
+
+def share_task(at, sources, views, ss, sr, fs, fr):
     n, c, b = at.n, at.c, at.b
     half = n // 2
     to, frm = pairwise(n, c, b)
@@ -466,60 +886,68 @@
     def local(k):
         return pltpu.make_async_copy(sources[k](c), views[k](c), sr.at[k, 0])
 
-    for k in range(kinds):
-        for i in range(1, half):
-            out_copy(k, i).start()
-
-        @pl.when(b == 1)
-        def _():
-            out_copy(k, 0).start()
-
-        @pl.when(b == 0)
-        def _():
-            local(k).start()
-
-    yield
-    for i in range(half):
+    order = middle_out(half) + [0]
+
+    def issue():
+        for i in order:
+            for k in range(kinds):
+                if i > 0:
+                    out_copy(k, i).start()
+                else:
+                    pl.when(b == 1)(lambda: out_copy(k, 0).start())
+                    pl.when(b == 0)(lambda: local(k).start())
+            yield
+
+    def finish():
+        for i in order:
+            for k in range(kinds):
+                if i > 0:
+                    landed(k, i).wait_recv()
+                else:
+                    pl.when(b == 1)(lambda: landed(k, 0).wait_recv())
+                    pl.when(b == 0)(lambda: local(k).wait())
+                pass_on(k, i, b).start()
         for k in range(kinds):
-            if i > 0:
-                landed(k, i).wait_recv()
-            else:
-                pl.when(b == 1)(lambda: landed(k, 0).wait_recv())
-                pl.when(b == 0)(lambda: local(k).wait())
-            pass_on(k, i, b).start()
-    for k in range(kinds):
-        for i in range(half):
-            pass_on(k, i, 1 - b).wait_recv()
-        for i in range(half):
-            pass_on(k, i, b).wait_send()
-        for i in range(1, half):
-            out_copy(k, i).wait_send()
-        pl.when(b == 1)(lambda: out_copy(k, 0).wait_send())
+            for i in range(half):
+                pass_on(k, i, 1 - b).wait_recv()
+            for i in range(half):
+                pass_on(k, i, b).wait_send()
+            for i in range(1, half):
+                out_copy(k, i).wait_send()
+            pl.when(b == 1)(lambda: out_copy(k, 0).wait_send())
+
+    return issue(), finish
 
 
 def share_sems(grid, kinds):
     return [dma(kinds, grid.n // 2) for _ in range(4)]
 
 
-def tell_steps(at, small_ref, all_ref, ts, tr):
+def tell_task(at, small_ref, all_ref, ts, tr):
     n, c, b = at.n, at.c, at.b
 
     def tell(off, slot):
         return remote(small_ref, all_ref.at[slot], ts.at[off], tr.at[off], (c + off) % n, b)
 
     keep = pltpu.make_async_copy(small_ref, all_ref.at[c], ts.at[0])
-    keep.start()
-    for off in range(1, n):
-        tell(off, c).start()
-    yield
-    keep.wait()
-    for off in range(1, n):
-        tell(off, (c + n - off) % n).wait_recv()
-    for off in range(1, n):
-        tell(off, c).wait_send()
-
-
-def head_rows_steps(at, x_ref, out_ref, hs, hr, fs, fr):
+
+    def issue():
+        keep.start()
+        for off in range(1, n):
+            tell(off, c).start()
+        yield
+
+    def finish():
+        keep.wait()
+        for off in range(1, n):
+            tell(off, (c + n - off) % n).wait_recv()
+        for off in range(1, n):
+            tell(off, c).wait_send()
+
+    return issue(), finish
+
+
+def head_rows_task(at, x_ref, out_ref, hs, hr, fs, fr):
     c, b = at.c, at.b
     copies = at.n // HEADS
     head, rank = c % HEADS, c // HEADS
@@ -538,29 +966,33 @@
     def pass_on(j):
         return at.sibling(out_ref.at[j], out_ref.at[j], fs.at[j], fr.at[j])
 
-    for k in range(copies // 2):
-        to, copy = out_copy(k)
-        pl.when(to != c)(lambda: copy.start())
-        pl.when(to == c)(lambda: here(c % copies).start())
-    yield
-
-    @pl.when(mine)
-    def _():
-        for j in range(copies):
-            pl.when(head * copies + j != c)(lambda: landed(j).wait_recv())
-            pl.when(head * copies + j == c)(lambda: here(j).wait())
-            pass_on(j).start()
-        for j in range(copies):
-            pass_on(j).wait_send()
-
-    @pl.when(jnp.logical_not(mine))
-    def _():
-        for j in range(copies):
-            pass_on(j).wait_recv()
-
-    for k in range(copies // 2):
-        to, copy = out_copy(k)
-        pl.when(to != c)(lambda: copy.wait_send())
+    def issue():
+        for k in range(copies // 2):
+            to, copy = out_copy(k)
+            pl.when(to != c)(lambda: copy.start())
+            pl.when(to == c)(lambda: here(c % copies).start())
+            yield
+
+    def finish():
+        @pl.when(mine)
+        def _():
+            for j in range(copies):
+                pl.when(head * copies + j != c)(lambda: landed(j).wait_recv())
+                pl.when(head * copies + j == c)(lambda: here(j).wait())
+                pass_on(j).start()
+            for j in range(copies):
+                pass_on(j).wait_send()
+
+        @pl.when(jnp.logical_not(mine))
+        def _():
+            for j in range(copies):
+                pass_on(j).wait_recv()
+
+        for k in range(copies // 2):
+            to, copy = out_copy(k)
+            pl.when(to != c)(lambda: copy.wait_send())
+
+    return issue(), finish
 
 
 def head_rows_sems(grid):
@@ -579,7 +1011,7 @@
     lax.fori_loop(0, rows // step, one, 0)
 
 
-def return_steps(at, x_ref, out_ref, mine, theirs, ls, ps, pr, ss, sr, fs, fr):
+def return_task(at, x_ref, out_ref, mine, theirs, ls, ps, pr, ss, sr, fs, fr):
     n, c, b = at.n, at.c, at.b
     half = n // 2
     to, frm = pairwise(n, c, b)
@@ -602,35 +1034,41 @@
         return at.sibling(ref, ref, fs.at[i], fr.at[i])
 
     local = pltpu.make_async_copy(mine.at[0], out_ref.at[c], ss.at[0])
-    order = list(range(1, half)) + [0]
-    for i in order:
-        load(i).start()
-        give(i).start()
-    for i in order:
-        load(i).wait()
-        give(i).wait_recv()
-        add_rows(mine.at[i], theirs.at[i], x_ref.shape[1])
-        if i > 0:
-            out_copy(i).start()
-        else:
-            pl.when(b == 1)(lambda: out_copy(0).start())
-            pl.when(b == 0)(lambda: local.start())
-    yield
-    for i in order:
-        if i > 0:
-            landed(i).wait_recv()
-        else:
-            pl.when(b == 1)(lambda: landed(0).wait_recv())
-            pl.when(b == 0)(lambda: local.wait())
-        pass_on(i, b).start()
-    for i in range(half):
-        pass_on(i, 1 - b).wait_recv()
-    for i in range(half):
-        give(i).wait_send()
-        pass_on(i, b).wait_send()
-    for i in range(1, half):
-        out_copy(i).wait_send()
-    pl.when(b == 1)(lambda: out_copy(0).wait_send())
+    order = middle_out(half) + [0]
+
+    def issue():
+        for i in order:
+            load(i).start()
+            give(i).start()
+        for i in order:
+            load(i).wait()
+            give(i).wait_recv()
+            add_rows(mine.at[i], theirs.at[i], x_ref.shape[1])
+            if i > 0:
+                out_copy(i).start()
+            else:
+                pl.when(b == 1)(lambda: out_copy(0).start())
+                pl.when(b == 0)(lambda: local.start())
+            yield
+
+    def finish():
+        for i in order:
+            if i > 0:
+                landed(i).wait_recv()
+            else:
+                pl.when(b == 1)(lambda: landed(0).wait_recv())
+                pl.when(b == 0)(lambda: local.wait())
+            pass_on(i, b).start()
+        for i in range(half):
+            pass_on(i, 1 - b).wait_recv()
+        for i in range(half):
+            give(i).wait_send()
+            pass_on(i, b).wait_send()
+        for i in range(1, half):
+            out_copy(i).wait_send()
+        pl.when(b == 1)(lambda: out_copy(0).wait_send())
+
+    return issue(), finish
 
 
 def return_scratch(grid, shape):
@@ -638,7 +1076,7 @@
     return [pltpu.VMEM(blocks, BF16), pltpu.VMEM(blocks, BF16)] + [dma(grid.n // 2) for _ in range(7)]
 
 
-def head_return_steps(at, x_ref, out_ref, mine, theirs, ls, ps, pr, hs, hr, fs, fr):
+def head_return_task(at, x_ref, out_ref, mine, theirs, ls, ps, pr, hs, hr, fs, fr):
     c, b = at.c, at.b
     copies = at.n // HEADS
     head, rank = c % HEADS, c // HEADS
@@ -663,37 +1101,41 @@
     def pass_on(i):
         return at.sibling(out_ref.at[i], out_ref.at[i], fs.at[i], fr.at[i])
 
-    for k in range(copies // 2):
-        load(k).start()
-        give(k).start()
-    for k in range(copies // 2):
-        load(k).wait()
-        give(k).wait_recv()
-        add_rows(mine.at[k], theirs.at[k], x_ref.shape[1])
-        to, copy = out_copy(k)
-        pl.when(to != c)(lambda: copy.start())
-        pl.when(to == c)(lambda: here(k, rank).start())
-    yield
-
-    @pl.when(taken)
-    def _():
-        for i in range(copies):
-            frm = c // copies + HEADS * i
-            pl.when(frm != c)(lambda: landed(i).wait_recv())
-            pl.when(frm == c)(lambda: here(0, i).wait())
-            pass_on(i).start()
-        for i in range(copies):
-            pass_on(i).wait_send()
-
-    @pl.when(jnp.logical_not(taken))
-    def _():
-        for i in range(copies):
-            pass_on(i).wait_recv()
-
-    for k in range(copies // 2):
-        give(k).wait_send()
-        to, copy = out_copy(k)
-        pl.when(to != c)(lambda: copy.wait_send())
+    def issue():
+        for k in range(copies // 2):
+            load(k).start()
+            give(k).start()
+        for k in range(copies // 2):
+            load(k).wait()
+            give(k).wait_recv()
+            add_rows(mine.at[k], theirs.at[k], x_ref.shape[1])
+            to, copy = out_copy(k)
+            pl.when(to != c)(lambda: copy.start())
+            pl.when(to == c)(lambda: here(k, rank).start())
+            yield
+
+    def finish():
+        @pl.when(taken)
+        def _():
+            for i in range(copies):
+                frm = c // copies + HEADS * i
+                pl.when(frm != c)(lambda: landed(i).wait_recv())
+                pl.when(frm == c)(lambda: here(0, i).wait())
+                pass_on(i).start()
+            for i in range(copies):
+                pass_on(i).wait_send()
+
+        @pl.when(jnp.logical_not(taken))
+        def _():
+            for i in range(copies):
+                pass_on(i).wait_recv()
+
+        for k in range(copies // 2):
+            give(k).wait_send()
+            to, copy = out_copy(k)
+            pl.when(to != c)(lambda: copy.wait_send())
+
+    return issue(), finish
 
 
 def head_return_scratch(grid, shape):
@@ -702,19 +1144,25 @@
     return [pltpu.VMEM(blocks, BF16), pltpu.VMEM(blocks, BF16)] + [dma(copies) for _ in range(7)]
 
 
-def pair_steps(at, x_ref, out_ref, other, sems):
+def pair_task(at, x_ref, out_ref, other, sems):
     copy = at.sibling(x_ref, other, sems.at[0], sems.at[1])
-    copy.start()
-    yield
-    copy.wait_recv()
-
-    def one(r, carry):
-        rows = pl.ds(pl.multiple_of(r * 16, 16), 16)
-        out_ref[rows] = x_ref[rows].astype(F32) + other[rows].astype(F32)
-        return carry
-
-    lax.fori_loop(0, x_ref.shape[0] // 16, one, 0)
-    copy.wait_send()
+
+    def issue():
+        copy.start()
+        yield
+
+    def finish():
+        copy.wait_recv()
+
+        def one(r, carry):
+            rows = pl.ds(pl.multiple_of(r * 16, 16), 16)
+            out_ref[rows] = x_ref[rows].astype(F32) + other[rows].astype(F32)
+            return carry
+
+        lax.fori_loop(0, x_ref.shape[0] // 16, one, 0)
+        copy.wait_send()
+
+    return issue(), finish
 
 
 class Split:
@@ -726,11 +1174,14 @@
         return got
 
 
-def together(*tasks):
-    for task in tasks:
-        next(task, None)
-    for task in tasks:
-        run(task)
+def together(main, *tasks):
+    for _ in main:
+        for issue, _finish in tasks:
+            next(issue, None)
+    for issue, finish in tasks:
+        run(issue)
+    for issue, finish in tasks:
+        finish()
 
 
 def open_kernel(grid, x, qkv_parts, out_codes, small, cid):
@@ -750,9 +1201,9 @@
 
         together(
             gather_steps(at, True, x_ref, seen_ref, *refs.take(len(gs))),
-            share_steps(at, [lambda to: w_ref.at[to % HEADS]], [view], *refs.take(len(ss))),
-            tell_steps(at, small_ref, all_ref, *refs.take(2)),
-            head_rows_steps(at, o_ref, rows_ref, *refs.take(4)),
+            tell_task(at, small_ref, all_ref, *refs.take(2)),
+            share_task(at, [lambda to: w_ref.at[to % HEADS]], [view], *refs.take(len(ss))),
+            head_rows_task(at, o_ref, rows_ref, *refs.take(4)),
         )
 
     codes_shape = (n * rows_d, width) if flat else (n, rows_d, width)
@@ -766,7 +1217,7 @@
         ),
         in_specs=[INVMEM] * 4,
         out_specs=(ANY,) * 4,
-        scratch_shapes=gs + ss + ts + hs,
+        scratch_shapes=gs + ts + ss + hs,
         compiler_params=params(cid, 50),
         name="open",
     )(x, qkv_parts, out_codes, small)
@@ -831,7 +1282,7 @@
         def view(ref):
             return lambda j: ref.at[pl.ds(j * rows_d, rows_d)] if flat else ref.at[j]
 
-        return [share_steps(at, [source(r) for r in ins], [view(r) for r in outs], *refs.take(len(ss)))]
+        return [share_task(at, [source(r) for r in ins], [view(r) for r in outs], *refs.take(len(ss)))]
 
     shape = (n * rows_d, window) if flat else (n, rows_d, window)
     call = scatter_kernel(
@@ -853,7 +1304,7 @@
     rs = return_scratch(grid, pair_grad.shape[1:])
 
     def tasks(at, ins, outs, refs):
-        return [return_steps(at, ins[0], outs[0], *refs.take(len(rs)))]
+        return [return_task(at, ins[0], outs[0], *refs.take(len(rs)))]
 
     call = scatter_kernel(
         grid,
@@ -873,9 +1324,9 @@
 
     def tasks(at, ins, outs, refs):
         return [
-            return_steps(at, ins[0], outs[0], *refs.take(len(rs))),
-            head_return_steps(at, ins[1], outs[1], *refs.take(len(hs))),
-            pair_steps(at, ins[2], outs[2], *refs.take(2)),
+            return_task(at, ins[0], outs[0], *refs.take(len(rs))),
+            head_return_task(at, ins[1], outs[1], *refs.take(len(hs))),
+            pair_task(at, ins[2], outs[2], *refs.take(2)),
         ]
 
     call = scatter_kernel(
@@ -910,7 +1361,7 @@
         copy.start()
         copy.wait()
         total[...] = x_ref[...] + other[...]
-        together(share_steps(at, [lambda to: total], [lambda j: out_ref.at[j]], *scratch))
+        together((), share_task(at, [lambda to: total], [lambda j: out_ref.at[j]], *scratch))
 
     return pl.pallas_call(
         kernel,
@@ -1081,45 +1532,31 @@
     attention_raw = attention_raw.astype(F32)
     first_column = chip * units // 128 * 128
     inset = chip * units - first_column
-    pair_codes = jnp.concatenate([gate_got.reshape(D, window), up_got.reshape(D, window)], axis=-1)
     pair_scale = jnp.concatenate(
         [lax.dynamic_slice_in_dim(s, first_column, window) for s in (gate_scale, up_scale)]
     )
-    pair_matrices = [dequantized(pair_codes, pair_scale, s) for s in steps]
-    down_matrices = [
-        lax.dynamic_update_slice(
-            jnp.zeros((window, D), BF16), dequantized(down_codes, down_scale, s), (inset, 0)
-        )
-        for s in steps
-    ]
+    feed_weights = (
+        gate_got.reshape(D, window),
+        up_got.reshape(D, window),
+        down_codes,
+        pair_scale[None],
+        down_scale[None],
+    )
 
     mixed = source + normed(attention_raw, attention_post_gain)
     second_normed = normed(mixed, feed_gain).astype(BF16)
-    fed = gather(grid, second_normed, grid.planes, False, 3).reshape(group, length, D)
-    gate_up = [dot(fed[m], pair_matrices[m]) for m in range(group)]
-    hidden = [(jax.nn.gelu(g[:, :window], approximate=True) * g[:, window:]).astype(BF16) for g in gate_up]
-    down_part = jnp.stack([dot(hidden[m], down_matrices[m]).astype(BF16) for m in range(group)])
-    down_raw = feed_sums(grid, down_part.reshape(group, n, block, D), 4).astype(F32)
+    fed, gate_up, down_part, pair_matrices, down_matrices = feed_forward(grid, second_normed, *feed_weights, 3)
+    down_raw = feed_sums(grid, down_part, 4).astype(F32)
     branch, pull_out = jax.vjp(normed, down_raw, feed_post_gain)
     output = (mixed + branch).astype(BF16)
     upstream = cotangent.astype(F32)
     grad_down_raw, grad_post_feed = pull_out(upstream)
-    down_low = gather(grid, grad_down_raw.astype(BF16), grid.planes, False, 3).reshape(group, length, D)
-    pair_low, second_part = [], []
-    for m in range(group):
-        grad_hidden = dot_t(down_low[m], down_matrices[m])
-        _, pull_glu = jax.vjp(
-            lambda left, right: jax.nn.gelu(left, approximate=True) * right,
-            gate_up[m][:, :window],
-            gate_up[m][:, window:],
-        )
-        pair_low.append(jnp.concatenate(pull_glu(grad_hidden), axis=-1).astype(BF16))
-        second_part.append(dot_t(pair_low[m], pair_matrices[m]).astype(BF16))
-    pair_grad = sum(t_dot(fed[m], pair_low[m]) for m in range(group)).astype(BF16)
-    down_grad = sum(t_dot(hidden[m], down_low[m]) for m in range(group)).astype(BF16)
+    _, second_part, pair_grad, down_grad = feed_backward(
+        grid, grad_down_raw.astype(BF16), fed, gate_up, pair_matrices, down_matrices, 9
+    )
     down_grad = lax.dynamic_slice(down_grad, (inset, 0), (units, D))
     grad_second, pair_got = feed_back_sums(
-        grid, jnp.stack(second_part).reshape(group, n, block, D), pair_grad.reshape(n, rows_d, 2 * window), 5
+        grid, second_part, pair_grad.reshape(n, rows_d, 2 * window), 5
     )
     grad_second = grad_second.astype(F32)
     gate_grad, up_grad = (unwindowed(grid, pair_got[..., i * window : (i + 1) * window]) for i in range(2))

time: 1020 us -> 969 us (0.950)
  Pallas kernels: 751 us -> 842 us
  matrix products: 128 us -> 39.8 us
  other arithmetic: 83.4 us -> 49.1 us
  local copies, waits for them, and re-layouts: 51.9 us -> 31.9 us
    pallas_call x0 -> x2, Pallas kernels: none -> 233 us  [the longest x1 127 us: feed_backward(): pl.pallas_call(kernel, out_shape=(blocks(D), blocks(D), jax.ShapeDtypeStr...]
    pallas_call x3 -> x1, Pallas kernels: 231 us -> 60.9 us  [gather(): pl.pallas_call(kernel, out_shape=jax.ShapeDtypeStruct((2, count) + x.shap...]
    dot_general x8 -> x4, matrix products: 50 us -> 15.9 us  [dot_t(): lax.dot_general(left, right, (((1,), (1,)), ((), ())), preferred_element_...]
    pallas_call x4, Pallas kernels: 407 us -> 437 us  [call(): pl.pallas_call(kernel, out_shape=(jax.ShapeDtypeStruct((2, rows, width),...]
    dot_general x8 -> x4, matrix products: 42.1 us -> 13.5 us  [dot(): return jnp.dot(left, right, preferred_element_type=F32)]
    dot_general x8 -> x4, matrix products: 36 us -> 10.5 us  [t_dot(): lax.dot_general(left, right, (((0,), (0,)), ((), ())), preferred_element_...]
    another operation x6 -> x4, other arithmetic: 20.4 us -> 3.63 us  [the longest x1 8.46 us: on_device(): jnp.stack(second_part).reshape(group, n, block, D)]
    slice x2 -> x0, local copies, waits for them, and re-layouts: 13.3 us -> none  [the longest x1 8.52 us: on_device(): gate_up = [dot(fed[m], pair_matrices[m]) for m in range(group)]]
where the time goes in v3:
time: 969 us; the launch traced here: 965 us
  Pallas kernels  842 us (87%)
  other arithmetic  49.1 us (5%)
  matrix products  39.8 us (4%)
  local copies, waits for them, and re-layouts  31.9 us (3%)
    pallas_call x4, Pallas kernels, call(): pl.pallas_call(kernel, out_shape=(jax.ShapeDtypeStruct((2, rows, width),...  437 us
    pallas_call x1, Pallas kernels, feed_backward(): pl.pallas_call(kernel, out_shape=(blocks(D), blocks(D), jax.ShapeDtypeStr...  127 us
    pallas_call x1, Pallas kernels, feed_forward(): pl.pallas_call(kernel, out_shape=(blocks(D), blocks(2 * window), blocks(D...  107 us
    pallas_call x1, Pallas kernels, open_kernel(): pl.pallas_call(kernel, out_shape=(jax.ShapeDtypeStruct((2, levels * grid....  95.4 us
    pallas_call x1, Pallas kernels, gather(): pl.pallas_call(kernel, out_shape=jax.ShapeDtypeStruct((2, count) + x.shap...  60.9 us

profile of v3, /device:TPU:0, one launch (start us, length us, event | category | flops | bytes accessed | tf_op | source)
XLA Modules:
  0.0 965.1 jit_solution(12951291359299325243)
XLA Ops:
  1.6 1.3 fusion.29
  7.2 1.3 broadcast_in_dim.24.ds_ref
  11.5 1.3 pad_maximum_fusion.w_ref
  13.2 4.5 convert_element_type.124.refs_1_
  17.7 1.9 convert_element_type.125.refs_2_
  19.6 95.4 %open.1 = (bf16[2,8,64,2304]{3,2,1,0:T(8,128)(2,1)}, bf16[2304,768]{1,0:T(8,128)(2,1)}, bf16[2,128,2304]{2,1,0:T(8,128)(2,1)S(1)}, s32[16,8,128]{2,1,0:T(8,128)S(1)}) custom-call(bf16[2,64,2304]{2,1,0:T(8,128)(2,1)S(1)} %fusion.13.x_ref, bf16[8,144,768]{2,1,0:T(8,128)(2,1)} %pad_maximum_fusion.w_ref, bf16[128,2304]{1,0:T(8,128)(2,1)S(1)} %convert_element_type.115.o_ref, ...), custom_call_target="tpu_custom_call" | custom-call | tf_op jit(solution)/shard_map/open/pallas_call | solution.py:1210
  115.2 7.5 fusion.81
  122.7 2.4 fusion.57
  125.2 1.5 multiply_convert_fusion.2
  126.9 1.8 fusion.2
  128.7 1.7 convolution_divide_fusion
  130.7 3.6 convolution_convert_fusion.1
  134.3 113.7 %attention_sums.1 = (bf16[2,64,2304]{2,1,0:T(8,128)(2,1)}, bf16[2304,640]{1,0:T(8,128)(2,1)}, bf16[2304,640]{1,0:T(8,128)(2,1)}) custom-call(bf16[2,8,64,2304]{3,2,1,0:T(8,128)(2,1)} %bitcast.73, bf16[144,9216]{1,0:T(8,128)(2,1)} %convert_element_type.124.refs_1_, bf16[144,9216]{1,0:T(8,128)(2,1)} %convert_element_type.125.refs_2_), custom_call_target="tpu_custom_call" | custom-call | tf_op jit(solution)/shard_map/attention_sums/pallas_call | solution.py:1252
  248.0 1.3 fusion.25
  249.4 1.5 multiply_reduce_fusion
  250.9 1.2 multiply_convert_fusion.3.x_ref
  252.1 106.6 %feed_forward.1 = (bf16[2,16,64,2304]{3,2,1,0:T(8,128)(2,1)}, bf16[2,16,64,1280]{3,2,1,0:T(8,128)(2,1)}, bf16[2,16,64,2304]{3,2,1,0:T(8,128)(2,1)}, bf16[2,2304,1280]{2,1,0:T(8,128)(2,1)}, bf16[2,640,2304]{2,1,0:T(8,128)(2,1)}) custom-call(bf16[2,64,2304]{2,1,0:T(8,128)(2,1)} %multiply_convert_fusion.3.x_ref, bf16[2304,640]{1,0:T(8,128)(2,1)} %get-tuple-element.51.gate_ref, ...), custom_call_target="tpu_custom_call" | custom-call | tf_op jit(solution)/shard_map/feed_forward/pallas_call | solution.py:512
  358.7 84.3 %feed_sums.1 = bf16[2,64,2304]{2,1,0:T(8,128)(2,1)} custom-call(bf16[2,16,64,2304]{3,2,1,0:T(8,128)(2,1)} %get-tuple-element.53.refs_0_), custom_call_target="tpu_custom_call" | custom-call | tf_op jit(solution)/shard_map/feed_sums/pallas_call | solution.py:1252
  443.1 1.3 fusion.27
  444.4 1.7 fusion.20
  446.1 1.1 fusion.21.x_ref
  447.3 126.6 %feed_backward.1 = (bf16[2,16,64,2304]{3,2,1,0:T(8,128)(2,1)}, bf16[2,16,64,2304]{3,2,1,0:T(8,128)(2,1)}, bf16[2304,1280]{1,0:T(8,128)(2,1)}, bf16[640,2304]{1,0:T(8,128)(2,1)}) custom-call(bf16[2,64,2304]{2,1,0:T(8,128)(2,1)} %fusion.21.x_ref, bf16[2,16,64,2304]{3,2,1,0:T(8,128)(2,1)} %get-tuple-element.54.fed_ref, ...), custom_call_target="tpu_custom_call" | custom-call | tf_op jit(solution)/shard_map/feed_backward/pallas_call | solution.py:639
  573.9 140.7 %feed_back_sums.1 = (bf16[2,64,2304]{2,1,0:T(8,128)(2,1)}, bf16[16,144,1280]{2,1,0:T(8,128)(2,1)}) custom-call(bf16[2,16,64,2304]{3,2,1,0:T(8,128)(2,1)} %get-tuple-element.58.refs_0_, bf16[16,144,1280]{2,1,0:T(8,128)(2,1)} %bitcast.76), custom_call_target="tpu_custom_call" | custom-call | tf_op jit(solution)/shard_map/feed_back_sums/pallas_call | solution.py:1252
  714.6 3.3 fusion.82
  718.9 1.1 fusion.16
  721.9 1.7 constant_dynamic-slice_fusion.refs_3_
  724.7 2.9 copy.93
  728.8 2.9 copy.94
  731.8 60.9 %gather_8.1 = bf16[2,8,64,2304]{3,2,1,0:T(8,128)(2,1)} custom-call(bf16[2,64,2304]{2,1,0:T(8,128)(2,1)S(1)} %fusion.22.x_ref), custom_call_target="tpu_custom_call" | custom-call | tf_op jit(solution)/shard_map/gather_8/pallas_call | solution.py:242
  792.7 3.9 multiply_reduce_fusion.1
  796.7 2.5 convolution_convert_fusion.3
  799.2 4.0 multiply_convert_fusion.1
  805.0 2.3 fusion.68
  807.3 2.3 fusion.67
  809.5 2.3 fusion.66
  811.8 2.3 fusion.65
  814.1 1.8 fusion.12
  815.9 5.5 convolution_convert_fusion.2
  821.4 6.1 convolution_convert_fusion
  827.5 98.7 %attention_back_sums.1 = (bf16[2,64,2304]{2,1,0:T(8,128)(2,1)}, bf16[16,144,768]{2,1,0:T(8,128)(2,1)}, bf16[2,128,2304]{2,1,0:T(8,128)(2,1)}, f32[576,2304]{1,0:T(8,128)}) custom-call(bf16[2,8,64,2304]{3,2,1,0:T(8,128)(2,1)} %bitcast.85, bf16[16,144,768]{2,1,0:T(8,128)(2,1)} %bitcast.86, bf16[2,128,2304]{2,1,0:T(8,128)(2,1)} %bitcast.92, ...), custom_call_target="tpu_custom_call" | custom-call | tf_op jit(solution)/shard_map/attention_back_sums/pallas_call | solution.py:1252
  926.2 4.8 convert_reduce_fusion
  932.4 3.2 fusion.24
  935.6 15.5 %gains.1 = f32[16,8,1152]{2,1,0:T(8,128)} custom-call(f32[8,1152]{1,0:T(8,128)} %reshape.300.x_ref), custom_call_target="tpu_custom_call" | custom-call | tf_op jit(solution)/shard_map/gains/pallas_call | solution.py:1366
  954.6 2.2 bitcast_reduce_fusion
  956.9 1.3 slice_bitcast_fusion.4
  958.2 1.1 copy.90
  961.3 1.2 convert_reduce_fusion.1
  962.5 2.4 copy.102
  (145 shorter events, 22.7 us)
Async XLA Ops:
  0.6 9.3 copy-start.17
  9.9 1.1 copy-start
  9.9 1.1 copy-start.28
  10.0 1.4 copy-start.13
  11.4 1.7 copy-start.14
  13.1 4.6 slice-start
  13.2 4.5 slice-start.1
  122.6 6.0 copy-start.12
  122.7 2.5 copy-start.30
  125.1 1.7 copy-start.20
  125.1 1.7 copy-start.22
  125.1 1.7 copy-start.24
  125.1 1.7 copy-start.26
  128.7 2.0 copy-start.32
  130.7 3.6 copy-start.10
  134.3 115.1 %copy-start.18 = (f32[2304]{0:T(1024)S(1)}, f32[2304]{0:T(1024)}, u32[]{:S(2)}) copy-start(f32[2304]{0:T(1024)} %param.42) | copy-start | bytes 27652
  134.3 116.6 %copy-start.19 = (f32[2304]{0:T(1024)S(1)}, f32[2304]{0:T(1024)}, u32[]{:S(2)}) copy-start(f32[2304]{0:T(1024)} %param.43) | copy-start | bytes 27652
  248.0 2.9 copy-start.1
  358.7 85.7 %copy-start.3 = (bf16[2,64,2304]{2,1,0:T(8,128)(2,1)S(1)}, bf16[2,64,2304]{2,1,0:T(8,128)(2,1)}, u32[]{:S(2)}) copy-start(bf16[2,64,2304]{2,1,0:T(8,128)(2,1)} %param.26) | copy-start | bytes 1769476
  358.7 85.7 %copy-start.29 = (f32[2304]{0:T(1024)S(1)}, f32[2304]{0:T(1024)}, u32[]{:S(2)}) copy-start(f32[2304]{0:T(1024)} %param.44) | copy-start | bytes 27652
  443.0 3.1 copy-start.2
  714.6 3.3 copy-start.5
  717.9 1.1 copy-start.4
  720.0 1.8 copy-start.8
  731.8 61.0 %copy-start.11 = (f32[1024,256]{0,1:T(8,128)S(1)}, f32[1024,256]{0,1:T(8,128)}, u32[]{:S(2)}) copy-start(f32[1024,256]{0,1:T(8,128)} %copy-done.10) | copy-start | bytes 3145732
  731.8 61.0 %copy-start.16 = (bf16[2,128,2304]{2,1,0:T(8,128)(2,1)S(1)}, bf16[2,128,2304]{2,1,0:T(8,128)(2,1)}, u32[]{:S(2)}) copy-start(bf16[2,128,2304]{2,1,0:T(8,128)(2,1)} %get-tuple-element.88) | copy-start | bytes 3538948
  792.7 3.9 copy-start.7
  796.7 2.5 copy-start.33
  799.1 4.0 copy-start.25
  799.2 4.0 copy-start.27
  803.2 1.0 copy-start.21
  803.2 1.0 copy-start.23
  807.2 8.6 slice-start.4
  814.1 1.8 slice-start.5
  815.9 5.5 copy-start.31
  926.2 4.9 copy-start.9
  926.2 6.2 copy-start.6
  954.6 7.8 slice-start.2
  958.2 4.2 slice-start.3
  959.4 1.9 copy-start.15

commit v4 on v3

--- a/solution.py
+++ b/solution.py
@@ -116,8 +116,8 @@
     return pltpu.CompilerParams(collective_id=cid, has_side_effects=True, vmem_limit_bytes=mib * 2**20)
 
 
-def gather_sems(grid, levels, halves):
-    passes, steps = (2 if halves else 1), grid.plane // 2
+def gather_sems(grid, levels, passes=1):
+    steps = grid.plane // 2
     return [
         dma(passes, 2, levels),
         dma(passes, 2, levels),
@@ -127,28 +127,16 @@
     ]
 
 
-def gather_steps(at, halves, x_ref, out_ref, zs, zr, rs, rr, ls):
+def gather_steps(at, x_ref, out_ref, zs, zr, rs, rr, ls, passes=((0, 2),), ready=None):
     levels, steps, zi, q, pn, b = at.levels, at.steps, at.zi, at.q, at.pn, at.b
     half = x_ref.shape[1] // 2
     own = at.slot(zi, q)
-    member = at.member
 
     def block(us, zj, qj, part=None):
         u0, nu = us
         if part is None:
             return out_ref.at[pl.ds(u0, nu), at.slot(zj, qj)]
         return out_ref.at[pl.ds(u0, nu), at.slot(zj, qj), pl.ds(part * half, half)]
-
-    if halves:
-        local = pltpu.make_async_copy(x_ref.at[member], out_ref.at[member, own], ls.at[0])
-        swap = remote(x_ref.at[1 - member], out_ref.at[member, own], ls.at[1], ls.at[2], at.partner, b)
-        swap_in = remote(x_ref.at[1 - member], out_ref.at[1 - member, own], ls.at[1], ls.at[2], at.partner, b)
-        swap.start()
-        passes = [(member, 1), (1 - member, 1)]
-    else:
-        local = pltpu.make_async_copy(x_ref, out_ref.at[:, own], ls.at[0])
-        passes = [(0, 2)]
-    local.start()
 
     def z_copy(k, us, zj, sign):
         way = 0 if sign > 0 else 1
@@ -202,13 +190,17 @@
 
         guarded(present(zi, sign, d, levels), go)
 
-    local.wait()
     waves = [
         [(k, us, sign, d) for sign in ((0,) if d == 0 else (-1, 1))] for k, us in enumerate(passes) for d in range(levels)
     ]
     for i, wave in enumerate(waves):
-        if halves and wave[0][0] == 1 and wave[0][3] == 0:
-            swap_in.wait_recv()
+        k, (u0, nu), _, d = wave[0]
+        if d == 0:
+            if ready is not None:
+                ready(k)
+            local = pltpu.make_async_copy(x_ref.at[pl.ds(u0, nu)], out_ref.at[pl.ds(u0, nu), own], ls.at[k])
+            local.start()
+            local.wait()
         for group in wave:
             arrive(*group)
             yield
@@ -222,8 +214,6 @@
     for wave in waves:
         for group in wave:
             finish(*group)
-    if halves:
-        swap.wait_send()
 
 
 def run(steps):
@@ -231,20 +221,20 @@
         pass
 
 
-def gather(grid, x, levels, halves, cid):
+def gather(grid, x, levels, cid):
     count = levels * grid.plane
 
     def kernel(x_ref, out_ref, *sems):
         at = Place(grid, levels)
-        at.greet_near(halves)
-        run(gather_steps(at, halves, x_ref, out_ref, *sems))
+        at.greet_near(False)
+        run(gather_steps(at, x_ref, out_ref, *sems))
 
     return pl.pallas_call(
         kernel,
         out_shape=jax.ShapeDtypeStruct((2, count) + x.shape[1:], x.dtype),
         in_specs=[INVMEM],
         out_specs=ANY,
-        scratch_shapes=gather_sems(grid, levels, halves),
+        scratch_shapes=gather_sems(grid, levels),
         compiler_params=params(cid, 50),
         name="gather_%d" % count,
     )(x)
@@ -294,11 +284,15 @@
 
     def onward(self, sign, d):
         zj = self.at.zi + sign * d
-        for step in range(1, self.at.steps + 1):
+        for step in range(1, self.at.steps):
             for way in (0, 1):
                 self.r_copy(zj, way, step, True).wait_recv()
-                if step < self.at.steps:
-                    self.r_copy(zj, way, step + 1).start()
+                self.r_copy(zj, way, step + 1).start()
+
+    def landed(self, sign, d):
+        zj = self.at.zi + sign * d
+        for way in (0, 1):
+            self.r_copy(zj, way, self.at.steps, True).wait_recv()
 
     def finish(self):
         at = self.at
@@ -313,28 +307,38 @@
 
         lax.fori_loop(0, at.levels, one, 0)
 
-    def run(self, compute):
+    def run(self, compute, first=None):
         at = self.at
         zi, levels = at.zi, at.levels
 
-        def one(t, carry):
+        def wave(t):
             pl.when((t < levels) & (zi - t >= 0))(lambda: self.arrive(-1, t))
             pl.when((t < levels) & (zi + t < levels))(lambda: self.arrive(1, t))
+
+        def both(d, action):
+            pl.when((d < levels) & (zi - d >= 0))(lambda: action(-1, d))
+            pl.when((d > 0) & (d < levels) & (zi + d < levels))(lambda: action(1, d))
+
+        def one(t, carry):
+            wave(t)
+            both(t - 1, self.onward)
+            if first is not None:
+                pl.when(t == 2)(first)
             e = t - 2
+            both(e, self.landed)
 
             def side(i, carry):
                 zj = zi + (2 * i - 1) * e
-                here = (e >= 0) & (zj >= 0) & (zj < levels) & ((e > 0) | (i == 0))
+                here = (zj >= 0) & (zj < levels) & ((e > 0) | (i == 0))
                 pl.when(here)(lambda: compute(zj, e == 0))
                 return carry
 
             lax.fori_loop(0, 2, side, 0)
-            d = t - 1
-            pl.when((d < levels) & (zi - d >= 0))(lambda: self.onward(-1, d))
-            pl.when((d > 0) & (d < levels) & (zi + d < levels))(lambda: self.onward(1, d))
             return carry
 
-        lax.fori_loop(1, levels + 2, one, 0)
+        wave(1)
+        both(0, self.onward)
+        lax.fori_loop(2, levels + 2, one, 0)
         self.finish()
 
 
@@ -379,11 +383,13 @@
     def copies(self):
         window = self.codes.shape[1] // 2
         gate, up, down = self.sources
-        return [
-            pltpu.make_async_copy(gate, self.codes.at[:, pl.ds(0, window)], self.sems.at[0]),
-            pltpu.make_async_copy(up, self.codes.at[:, pl.ds(window, window)], self.sems.at[1]),
-            pltpu.make_async_copy(down, self.down_codes, self.sems.at[2]),
-        ]
+        copies = [pltpu.make_async_copy(down, self.down_codes, self.sems.at[2])]
+        if gate is not None:
+            copies += [
+                pltpu.make_async_copy(gate, self.codes.at[:, pl.ds(0, window)], self.sems.at[0]),
+                pltpu.make_async_copy(up, self.codes.at[:, pl.ds(window, window)], self.sems.at[1]),
+            ]
+        return copies
 
     def keeps(self):
         return [
@@ -424,50 +430,97 @@
     return 4 if grid.plane % 4 == 0 else grid.plane
 
 
-def each_chunk(grid, group, zj, fresh, loads, stores, compute, after=None):
+def each_chunk(grid, zj, fresh, loads, stores, compute):
     size = feed_blocks(grid)
-    count = grid.plane // size
-
-    def first(i):
-        return zj * grid.plane + i * size
-
-    for m in range(group):
-        for copy in loads(m, first(0)):
+    m = zj // (grid.planes // 2)
+
+    def one(i, carry):
+        first = zj * grid.plane + i * size
+        reads, writes = loads(first), stores(first)
+        for copy in reads:
             copy.start()
 
-    def one(i, carry):
-        for m in range(group):
-            reads, writes = loads(m, first(i)), stores(m, first(i))
-
-            @pl.when(jnp.logical_not(fresh & (i == 0)))
-            def _():
-                for copy in writes:
-                    copy.wait()
-
-            compute(m, reads)
+        @pl.when(jnp.logical_not(fresh & (i == 0)))
+        def _():
             for copy in writes:
-                copy.start()
-        if after is not None:
-            after([loads(m, first(i)) for m in range(group)])
-
-        @pl.when(i + 1 < count)
-        def _():
-            for m in range(group):
-                for copy in loads(m, first(i + 1)):
-                    copy.start()
-
+                copy.wait()
+
+        compute(m, reads)
+        for copy in writes:
+            copy.start()
         return carry
 
-    lax.fori_loop(0, count, one, 0)
+    lax.fori_loop(0, grid.plane // size, one, 0)
+
+
+def copies_of(blocks, pairs, sems, first):
+    return [
+        pltpu.make_async_copy(a.at[:, blocks] if far_a else a, b if far_a else b.at[:, blocks], sems.at[first + k])
+        for k, (a, b, far_a) in enumerate(pairs)
+    ]
+
+
+def forward_chunks(weights, all_ref, pair_ref, part_ref, xs, gu, part, sems):
+    _, size, rows, _ = xs.shape
+    window = weights.down.shape[1]
+
+    def loads(first):
+        return copies_of(pl.ds(first, size), [(all_ref, xs, True)], sems, 0)
+
+    def stores(first):
+        return copies_of(pl.ds(first, size), [(gu, pair_ref, False), (part, part_ref, False)], sems, 1)
+
+    def compute(m, reads):
+        reads[0].wait()
+        both = dot(xs[...].reshape(2 * size * rows, D), weights.pair[m])
+        gu[...] = both.astype(BF16).reshape(gu.shape)
+        gate, up = both[:, :window], both[:, window:]
+        bend = jnp.tanh(GELU_A * (gate + GELU_B * gate * gate * gate))
+        hidden = (0.5 * gate * (1.0 + bend) * up).astype(BF16)
+        part[...] = dot(hidden, weights.down[m]).astype(BF16).reshape(part.shape)
+
+    return loads, stores, compute
+
+
+def backward_chunks(wp, wd, all_ref, pair_ref, part_ref, dgu_ref, hid_ref, ys, gu, part, dgu, hid, sems):
+    _, size, rows, _ = ys.shape
+    window = wd.shape[1]
+    count = 2 * size * rows
+
+    def loads(first):
+        return copies_of(pl.ds(first, size), [(all_ref, ys, True), (pair_ref, gu, True)], sems, 0)
+
+    def stores(first):
+        pairs = [(part, part_ref, False), (dgu, dgu_ref, False), (hid, hid_ref, False)]
+        return copies_of(pl.ds(first, size), pairs, sems, 2)
+
+    def compute(m, reads):
+        reads[0].wait()
+        grad_hidden = dot_t(ys[...].reshape(count, D), wd[m])
+        reads[1].wait()
+        both = gu[...].reshape(count, 2 * window).astype(F32)
+        gate, up = both[:, :window], both[:, window:]
+        bend = jnp.tanh(GELU_A * (gate + GELU_B * gate * gate * gate))
+        bell = 0.5 * gate * (1.0 + bend)
+        slope = 0.5 * (1.0 + bend) + 0.5 * gate * (1.0 - bend * bend) * GELU_A * (1.0 + 3.0 * GELU_B * gate * gate)
+        dgu[:, :, :, :window] = (grad_hidden * up * slope).astype(BF16).reshape(hid.shape)
+        dgu[:, :, :, window:] = (grad_hidden * bell).astype(BF16).reshape(hid.shape)
+        hid[...] = (bell * up).astype(BF16).reshape(hid.shape)
+        part[...] = dot_t(dgu[...].reshape(count, 2 * window), wp[m]).astype(BF16).reshape(part.shape)
+
+    return loads, stores, compute
+
+
+def chunk_buffers(size, rows, *widths):
+    return [pltpu.VMEM((2, size, rows, width), BF16) for width in widths]
 
 
 def feed_forward(grid, x, gate_codes, up_codes, down_codes, pair_scale, down_scale, cid):
     group, rows, _ = x.shape
     n, levels = grid.n, grid.planes
     units, window, _ = feed_windows(grid)
-    gs, ws = gather_sems(grid, levels, False), FeedWeights.scratch(group, units, window)
+    gs, ws = gather_sems(grid, levels), FeedWeights.scratch(group, units, window)
     size = feed_blocks(grid)
-    count = size * rows
 
     def kernel(
         x_ref, gate_ref, up_ref, down_ref, ps_ref, ds_ref, all_ref, pair_ref, part_ref, wp_ref, wd_ref, *scratch
@@ -477,33 +530,13 @@
         weights = FeedWeights(at, group, units, gate_ref, up_ref, down_ref, (wp_ref, wd_ref), refs.take(len(ws)))
         weights.load()
         moving = LevelGather(at, x_ref, all_ref, *refs.take(len(gs)))
-        xs, gu, part, sems = refs.take(4)
+        loads, stores, compute = forward_chunks(weights, all_ref, pair_ref, part_ref, *refs.take(4))
         at.greet_near(False)
         moving.begin()
         weights.make(ps_ref, ds_ref)
-
-        def loads(m, first):
-            return [pltpu.make_async_copy(all_ref.at[m, pl.ds(first, size)], xs.at[m], sems.at[0, m])]
-
-        def stores(m, first):
-            return [
-                pltpu.make_async_copy(gu.at[m], pair_ref.at[m, pl.ds(first, size)], sems.at[1, m]),
-                pltpu.make_async_copy(part.at[m], part_ref.at[m, pl.ds(first, size)], sems.at[2, m]),
-            ]
-
-        def compute(m, reads):
-            reads[0].wait()
-            both = dot(xs[m].reshape(count, D), weights.pair[m])
-            gu[m] = both.astype(BF16).reshape(size, rows, 2 * window)
-            gate, up = both[:, :window], both[:, window:]
-            bend = jnp.tanh(GELU_A * (gate + GELU_B * gate * gate * gate))
-            hidden = (0.5 * gate * (1.0 + bend) * up).astype(BF16)
-            part[m] = dot(hidden, weights.down[m]).astype(BF16).reshape(size, rows, D)
-
-        moving.run(lambda zj, fresh: each_chunk(grid, group, zj, fresh, loads, stores, compute))
-        for m in range(group):
-            for copy in stores(m, 0):
-                copy.wait()
+        moving.run(lambda zj, fresh: each_chunk(grid, zj, fresh, loads, stores, compute))
+        for copy in stores(0):
+            copy.wait()
         weights.finish()
 
     def blocks(width):
@@ -520,173 +553,78 @@
         ),
         in_specs=[INVMEM, ANY, ANY, ANY, INVMEM, INVMEM],
         out_specs=(ANY,) * 5,
-        scratch_shapes=ws
-        + gs
-        + [
-            pltpu.VMEM((group, size, rows, D), BF16),
-            pltpu.VMEM((group, size, rows, 2 * window), BF16),
-            pltpu.VMEM((group, size, rows, D), BF16),
-            dma(3, group),
-        ],
+        scratch_shapes=ws + gs + chunk_buffers(size, rows, D, 2 * window, D) + [dma(3)],
         compiler_params=params(cid, 60),
         name="feed_forward",
     )(x, gate_codes, up_codes, down_codes, pair_scale, down_scale)
 
 
-def feed_backward(grid, x, fed, pair, pair_matrices, down_matrices, cid):
+def feed_backward(grid, x, pair, pair_matrices, down_matrices, cid):
     group, rows, _ = x.shape
     n, levels = grid.n, grid.planes
-    units, window, _ = feed_windows(grid)
-    gs = gather_sems(grid, levels, False)
+    _, window, _ = feed_windows(grid)
+    gs = gather_sems(grid, levels)
     size = feed_blocks(grid)
-    count = size * rows
-    tile = 256
-
-    def kernel(x_ref, fed_ref, pair_ref, wp_ref, wd_ref, all_ref, part_ref, pg_ref, dg_ref, *scratch):
+
+    def kernel(x_ref, pair_ref, wp_ref, wd_ref, all_ref, part_ref, dgu_ref, hid_ref, *scratch):
         refs = Split(scratch)
         at = Place(grid, levels)
         moving = LevelGather(at, x_ref, all_ref, *refs.take(len(gs)))
-        wp, wd, xs, ys, gu, part, pair_sum, down_sum, dgu, hid, sems = refs.take(11)
+        wp, wd, fetch_sems = refs.take(3)
         fetch = [
-            pltpu.make_async_copy(wp_ref, wp, sems.at[4, 0]),
-            pltpu.make_async_copy(wd_ref, wd, sems.at[4, 1]),
+            pltpu.make_async_copy(wp_ref, wp, fetch_sems.at[0]),
+            pltpu.make_async_copy(wd_ref, wd, fetch_sems.at[1]),
         ]
         for copy in fetch:
             copy.start()
+        loads, stores, compute = backward_chunks(
+            wp, wd, all_ref, pair_ref, part_ref, dgu_ref, hid_ref, *refs.take(6)
+        )
         at.greet_near(False)
         moving.begin()
-
-        def clear(i, carry):
-            pair_sum[pl.ds(pl.multiple_of(i * 8, 8), 8)] = jnp.zeros((8, 2 * window), F32)
-            return carry
-
-        lax.fori_loop(0, D // 8, clear, 0)
-
-        def clear_down(i, carry):
-            down_sum[pl.ds(pl.multiple_of(i * 8, 8), 8)] = jnp.zeros((8, D), F32)
-            return carry
-
-        lax.fori_loop(0, window // 8, clear_down, 0)
         for copy in fetch:
             copy.wait()
-
-        def loads(m, first):
-            blocks = pl.ds(first, size)
-            return [
-                pltpu.make_async_copy(all_ref.at[m, blocks], ys.at[m], sems.at[0, m]),
-                pltpu.make_async_copy(pair_ref.at[m, blocks], gu.at[m], sems.at[1, m]),
-                pltpu.make_async_copy(fed_ref.at[m, blocks], xs.at[m], sems.at[2, m]),
-            ]
-
-        def stores(m, first):
-            return [pltpu.make_async_copy(part.at[m], part_ref.at[m, pl.ds(first, size)], sems.at[3, m])]
-
-        def compute(m, reads):
-            reads[0].wait()
-            grad_hidden = dot_t(ys[m].reshape(count, D), wd[m])
-            reads[1].wait()
-            both = gu[m].reshape(count, 2 * window).astype(F32)
-            gate, up = both[:, :window], both[:, window:]
-            bend = jnp.tanh(GELU_A * (gate + GELU_B * gate * gate * gate))
-            bell = 0.5 * gate * (1.0 + bend)
-            slope = 0.5 * (1.0 + bend) + 0.5 * gate * (1.0 - bend * bend) * GELU_A * (1.0 + 3.0 * GELU_B * gate * gate)
-            mine = pl.ds(m * count, count)
-            dgu[mine, :window] = (grad_hidden * up * slope).astype(BF16)
-            dgu[mine, window:] = (grad_hidden * bell).astype(BF16)
-            hid[mine] = (bell * up).astype(BF16)
-            part[m] = dot_t(dgu[mine], wp[m]).astype(BF16).reshape(size, rows, D)
-
-        def weight_sums(reads):
-            for read in reads:
-                read[2].wait()
-
-            def one(j, carry):
-                cols = pl.ds(pl.multiple_of(j * tile, tile), tile)
-                pair_sum[cols] = pair_sum[cols] + t_dot(xs[:, :, :, cols].reshape(group * count, tile), dgu[...])
-                down_sum[:, cols] = down_sum[:, cols] + t_dot(hid[...], ys[:, :, :, cols].reshape(group * count, tile))
-                return carry
-
-            lax.fori_loop(0, D // tile, one, 0)
-
-        moving.run(lambda zj, fresh: each_chunk(grid, group, zj, fresh, loads, stores, compute, weight_sums))
-
-        def low(i, carry):
-            r = pl.ds(pl.multiple_of(i * 16, 16), 16)
-            wp[0, r] = pair_sum[r].astype(BF16)
-            return carry
-
-        lax.fori_loop(0, D // 16, low, 0)
-        give_pair = pltpu.make_async_copy(wp.at[0], pg_ref, sems.at[4, 0])
-        give_pair.start()
-
-        def low_down(i, carry):
-            r = pl.ds(pl.multiple_of(i * 16, 16), 16)
-            wd[0, r] = down_sum[r].astype(BF16)
-            return carry
-
-        lax.fori_loop(0, window // 16, low_down, 0)
-        give_down = pltpu.make_async_copy(wd.at[0], dg_ref, sems.at[4, 1])
-        give_down.start()
-        for m in range(group):
-            for copy in stores(m, 0):
-                copy.wait()
-        give_pair.wait()
-        give_down.wait()
+        moving.run(lambda zj, fresh: each_chunk(grid, zj, fresh, loads, stores, compute))
+        for copy in stores(0):
+            copy.wait()
 
     def blocks(width):
         return jax.ShapeDtypeStruct((group, n, rows, width), BF16)
 
     return pl.pallas_call(
         kernel,
-        out_shape=(
-            blocks(D),
-            blocks(D),
-            jax.ShapeDtypeStruct((D, 2 * window), BF16),
-            jax.ShapeDtypeStruct((window, D), BF16),
-        ),
-        in_specs=[INVMEM] + [ANY] * 4,
+        out_shape=(blocks(D), blocks(D), blocks(2 * window), blocks(window)),
+        in_specs=[INVMEM] + [ANY] * 3,
         out_specs=(ANY,) * 4,
         scratch_shapes=gs
-        + [
-            pltpu.VMEM((group, D, 2 * window), BF16),
-            pltpu.VMEM((group, window, D), BF16),
-            pltpu.VMEM((group, size, rows, D), BF16),
-            pltpu.VMEM((group, size, rows, D), BF16),
-            pltpu.VMEM((group, size, rows, 2 * window), BF16),
-            pltpu.VMEM((group, size, rows, D), BF16),
-            pltpu.VMEM((D, 2 * window), F32),
-            pltpu.VMEM((window, D), F32),
-            pltpu.VMEM((group * count, 2 * window), BF16),
-            pltpu.VMEM((group * count, window), BF16),
-            dma(5, group),
-        ],
+        + [pltpu.VMEM((group, D, 2 * window), BF16), pltpu.VMEM((group, window, D), BF16), dma(2)]
+        + chunk_buffers(size, rows, D, 2 * window, D, 2 * window, window)
+        + [dma(5)],
         compiler_params=params(cid, 62),
         name="feed_backward",
-    )(x, fed, pair, pair_matrices, down_matrices)
-
-
-def scatter_scratch(grid, levels, halves, rows, width):
-    passes, steps = (2 if halves else 1), grid.plane // 2
+    )(x, pair, pair_matrices, down_matrices)
+
+
+def scatter_scratch(grid, levels, rows, width):
+    steps = grid.plane // 2
     return [
         pltpu.VMEM((2, levels * grid.plane, rows, width), BF16),
         pltpu.VMEM((2, levels, 2, rows // 2, width), BF16),
         pltpu.VMEM((2, max(steps - 1, 1), levels, 2, rows, width), BF16),
         pltpu.VMEM((2, levels, 2, rows, width), BF16),
-        pltpu.VMEM((rows, width), BF16),
-        dma(3),
-        dma(passes, 2, levels),
-        dma(passes, 2, levels),
-        dma(passes, 2, steps, levels),
-        dma(passes, 2, steps, levels),
+        dma(1),
+        dma(1, 2, levels),
+        dma(1, 2, levels),
+        dma(1, 2, steps, levels),
+        dma(1, 2, steps, levels),
     ]
 
 
-def scatter_steps(at, halves, out_ref, acc, ring_half, ring_full, line, swapped, ls, zs, zr, rs, rr):
+def scatter_steps(at, out_ref, acc, ring_half, ring_full, line, ls, zs, zr, rs, rr):
     levels, steps, zi, q, pn, b = at.levels, at.steps, at.zi, at.q, at.pn, at.b
     rows = acc.shape[2]
     half = rows // 2
-    member = at.member
-    passes = [(1 - member, 1), (member, 1)] if halves else [(0, 2)]
+    passes = [(0, 2)]
 
     def block(us, zj, qj, part=None):
         u0, nu = us
@@ -739,20 +677,28 @@
 
         guarded(present(zi, sign, d, levels), go)
 
-    def onward(k, us, sign, d):
+    def middle(k, us, sign, d):
         zj = zi + sign * d
 
         def go():
-            for step in range(1, steps + 1):
+            for step in range(1, steps):
                 for way in (0, 1):
                     r_copy(k, us, zj, way, step).wait_recv()
-                    if step < steps:
-                        s = at.slot(zj, q + (1 if way == 0 else -1) * (steps - step))
-                        if step == 1:
-                            add(us, s, [half_at(way, zj)], way * half, half)
-                        else:
-                            add(us, s, [full_at(way, step, zj)], 0, rows)
-                        r_copy(k, us, zj, way, step + 1).start()
+                    s = at.slot(zj, q + (1 if way == 0 else -1) * (steps - step))
+                    if step == 1:
+                        add(us, s, [half_at(way, zj)], way * half, half)
+                    else:
+                        add(us, s, [full_at(way, step, zj)], 0, rows)
+                    r_copy(k, us, zj, way, step + 1).start()
+
+        guarded(present(zi, sign, d, levels), go)
+
+    def last(k, us, sign, d):
+        zj = zi + sign * d
+
+        def go():
+            for way in (0, 1):
+                r_copy(k, us, zj, way, steps).wait_recv()
             s = at.slot(zj, q)
             if steps > 1:
                 add(us, s, [full_at(0, steps, zj), full_at(1, steps, zj)], 0, rows)
@@ -793,21 +739,21 @@
         for d in range(levels - 1, -1, -1)
     ]
     own = at.slot(zi, q)
-    if halves:
-        swap = remote(acc.at[1 - member, own], swapped, ls.at[1], ls.at[2], at.partner, b)
-    for group in waves[0]:
-        begin(*group)
+    def each(action, i):
+        if i < len(waves):
+            for group in waves[i]:
+                action(*group)
+
+    each(begin, 0)
+    each(begin, 1)
+    each(middle, 0)
     yield
-    for i, wave in enumerate(waves):
-        if i + 1 < len(waves):
-            for group in waves[i + 1]:
-                begin(*group)
-            yield
-        for group in wave:
-            onward(*group)
-            yield
-        if halves and wave[0][0] == 0 and wave[0][3] == 0:
-            swap.start()
+    for i in range(len(waves)):
+        each(begin, i + 2)
+        each(middle, i + 1)
+        yield
+        each(last, i)
+    yield
 
     def give(src, u):
         def one(i, carry):
@@ -816,18 +762,11 @@
 
         lax.fori_loop(0, rows // 16, one, 0)
 
-    if halves:
-        give(acc.at[member, own], member)
-        swap.wait_recv()
-        give(swapped, 1 - member)
-    else:
-        give(acc.at[0, own], 0)
-        give(acc.at[1, own], 1)
+    give(acc.at[0, own], 0)
+    give(acc.at[1, own], 1)
     for wave in waves:
         for group in wave:
             finish(*group)
-    if halves:
-        swap.wait_send()
 
 
 def scatter_parts(grid, levels, rows, width):
@@ -1011,7 +950,7 @@
     lax.fori_loop(0, rows // step, one, 0)
 
 
-def return_task(at, x_ref, out_ref, mine, theirs, ls, ps, pr, ss, sr, fs, fr):
+def return_task(at, x_ref, out_ref, mine, theirs, ls, ps, pr, ss, sr, fs, fr, given=None, fill=None, prepare=None):
     n, c, b = at.n, at.c, at.b
     half = n // 2
     to, frm = pairwise(n, c, b)
@@ -1021,7 +960,8 @@
         return pltpu.make_async_copy(x_ref.at[to(i)], mine.at[i], ls.at[i])
 
     def give(i):
-        return at.sibling(x_ref.at[other_to(i)], theirs.at[i], ps.at[i], pr.at[i])
+        source = x_ref.at[other_to(i)] if given is None else given.at[i]
+        return at.sibling(source, theirs.at[i], ps.at[i], pr.at[i])
 
     def out_copy(i):
         return remote(mine.at[i], out_ref.at[c], ss.at[i], sr.at[i], to(i), b)
@@ -1037,19 +977,26 @@
     order = middle_out(half) + [0]
 
     def issue():
+        if prepare is not None:
+            yield from prepare()
         for i in order:
-            load(i).start()
+            if fill is None:
+                load(i).start()
+            else:
+                fill(i)
             give(i).start()
-        for i in order:
-            load(i).wait()
+        for j, i in enumerate(order):
+            if fill is None:
+                load(i).wait()
             give(i).wait_recv()
-            add_rows(mine.at[i], theirs.at[i], x_ref.shape[1])
+            add_rows(mine.at[i], theirs.at[i], mine.shape[1])
             if i > 0:
                 out_copy(i).start()
             else:
                 pl.when(b == 1)(lambda: out_copy(0).start())
                 pl.when(b == 0)(lambda: local.start())
-            yield
+            if j % 2 == 1:
+                yield
 
     def finish():
         for i in order:
@@ -1156,7 +1103,7 @@
 
         def one(r, carry):
             rows = pl.ds(pl.multiple_of(r * 16, 16), 16)
-            out_ref[rows] = x_ref[rows].astype(F32) + other[rows].astype(F32)
+            out_ref[rows] = (x_ref[rows].astype(F32) + other[rows].astype(F32)).astype(out_ref.dtype)
             return carry
 
         lax.fori_loop(0, x_ref.shape[0] // 16, one, 0)
@@ -1184,52 +1131,142 @@
         finish()
 
 
-def open_kernel(grid, x, qkv_parts, out_codes, small, cid):
+def narrow_task(sources, targets, wide, low, loads, stores):
+    width = wide.shape[2]
+    pieces = [(k, i) for k in range(len(sources)) for i in range(sources[k].shape[1] // width)]
+
+    def load(j):
+        k, i = pieces[j]
+        return pltpu.make_async_copy(sources[k].at[:, pl.ds(i * width, width)], wide.at[j % 2], loads.at[j % 2])
+
+    def store(j):
+        k, i = pieces[j]
+        return pltpu.make_async_copy(low.at[j % 2], targets[k].at[:, pl.ds(i * width, width)], stores.at[j % 2])
+
+    def issue():
+        load(0).start()
+        load(1).start()
+        yield
+        for j in range(len(pieces)):
+            load(j).wait()
+            if j >= 2:
+                store(j - 2).wait()
+            low[j % 2] = wide[j % 2].astype(F32).astype(BF16)
+            store(j).start()
+            if j + 2 < len(pieces):
+                load(j + 2).start()
+            yield
+
+    def finish():
+        for j in range(len(pieces) - 2, len(pieces)):
+            store(j).wait()
+
+    return issue(), finish
+
+
+def swap_copy(at, source, target, send, recv):
+    return remote(source, target.at[at.member], send, recv, at.partner, at.b)
+
+
+def swap_task(at, source, target, sems):
+    there = swap_copy(at, source, target, sems.at[0], sems.at[1])
+    here = remote(source, target.at[1 - at.member], sems.at[0], sems.at[1], at.partner, at.b)
+
+    def issue():
+        there.start()
+        yield
+
+    def finish():
+        here.wait_recv()
+        there.wait_send()
+
+    return issue(), finish
+
+
+def open_kernel(grid, tokens, cotangent, gain, qkv_parts, out_codes, small, gate_codes, up_codes, cid):
+    x = tokens
     n, levels = grid.n, grid.planes // 2
     rows_d, width = qkv_parts.shape[1:]
     flat = rows_d % 16 == 0
     copies = n // HEADS
-    gs, ss, ts, hs = gather_sems(grid, levels, True), share_sems(grid, 1), [dma(n), dma(n)], head_rows_sems(grid)
-
-    def kernel(x_ref, w_ref, o_ref, small_ref, seen_ref, codes_ref, rows_ref, all_ref, *scratch):
+    gs, ss, ts, hs = gather_sems(grid, levels, 2), share_sems(grid, 1), [dma(n), dma(n)], head_rows_sems(grid)
+
+    piece = FF // 2
+    ns = [
+        pltpu.VMEM((2, rows_d, piece), jnp.int32),
+        pltpu.VMEM((2, rows_d, piece), BF16),
+        dma(2),
+        dma(2),
+    ]
+
+    def kernel(
+        x_ref, cot_ref, gain_ref, w_ref, o_ref, small_ref, gate_ref, up_ref,
+        kept_ref, kept_cot_ref, seen_ref, codes_ref, rows_ref, all_ref, gl_ref, ul_ref, *scratch,
+    ):
         at = Place(grid, levels)
         refs = Split(scratch)
+        normed_ref, token_sems, cot_sems = refs.take(3)
+        member = at.member
         at.greet_all()
+        token_issue, token_finish = swap_task(at, x_ref.at[1 - member], kept_ref, token_sems)
+        run(token_issue)
 
         def view(j):
             return codes_ref.at[pl.ds(j * rows_d, rows_d)] if flat else codes_ref.at[j]
 
+        def ready(k):
+            u = member if k == 0 else 1 - member
+            if k == 1:
+                token_finish()
+
+            def one(_, r):
+                if k == 0:
+                    kept_ref[u, r] = x_ref[u, r]
+                    kept_cot_ref[u, r] = cot_ref[u, r]
+                value = kept_ref[u, r].astype(F32)
+                normed_ref[u, r] = (value * inverse_rms(value) * gain_ref[...]).astype(BF16)
+
+            each_rows(1, x_ref.shape[1], one)
+
         together(
-            gather_steps(at, True, x_ref, seen_ref, *refs.take(len(gs))),
+            gather_steps(
+                at, normed_ref, seen_ref, *refs.take(len(gs)), passes=[(member, 1), (1 - member, 1)], ready=ready
+            ),
+            narrow_task([gate_ref, up_ref], [gl_ref, ul_ref], *refs.take(4)),
             tell_task(at, small_ref, all_ref, *refs.take(2)),
             share_task(at, [lambda to: w_ref.at[to % HEADS]], [view], *refs.take(len(ss))),
             head_rows_task(at, o_ref, rows_ref, *refs.take(4)),
+            swap_task(at, cot_ref.at[1 - member], kept_cot_ref, cot_sems),
         )
 
     codes_shape = (n * rows_d, width) if flat else (n, rows_d, width)
     return pl.pallas_call(
         kernel,
         out_shape=(
+            jax.ShapeDtypeStruct(x.shape, BF16),
+            jax.ShapeDtypeStruct(x.shape, BF16),
             jax.ShapeDtypeStruct((2, levels * grid.plane) + x.shape[1:], BF16),
             jax.ShapeDtypeStruct(codes_shape, BF16),
             jax.ShapeDtypeStruct((copies,) + out_codes.shape, BF16),
             jax.ShapeDtypeStruct((n,) + small.shape, small.dtype),
+            jax.ShapeDtypeStruct(gate_codes.shape, BF16),
+            jax.ShapeDtypeStruct(up_codes.shape, BF16),
         ),
-        in_specs=[INVMEM] * 4,
-        out_specs=(ANY,) * 4,
-        scratch_shapes=gs + ts + ss + hs,
+        in_specs=[INVMEM] * 6 + [ANY] * 2,
+        out_specs=(INVMEM, INVMEM) + (ANY,) * 6,
+        scratch_shapes=[pltpu.VMEM(x.shape, BF16), dma(2), dma(2)] + gs + ns + ts + ss + hs,
         compiler_params=params(cid, 50),
         name="open",
-    )(x, qkv_parts, out_codes, small)
-
-
-def scatter_kernel(grid, levels, halves, cid, name, tasks=None):
+    )(tokens, cotangent, gain, qkv_parts, out_codes, small, gate_codes, up_codes)
+
+
+def scatter_kernel(grid, levels, cid, name, tasks=None, end=None):
     made, in_specs, out_shapes, out_specs, extra_scratch = tasks if tasks else (None, [], (), (), [])
 
     def call(p, extra):
         rows, width = p.shape[2:]
         more = () if extra is None else tuple(extra)
-        own = scatter_scratch(grid, levels, halves, rows, width)
+        own = scatter_scratch(grid, levels, rows, width)
 
         def kernel(*refs):
             refs = Split(refs)
@@ -1239,15 +1276,24 @@
             out_refs = refs.take(len(out_shapes) if more else 0)
             mine = refs.take(len(own))
             at = Place(grid, levels)
-            load = pltpu.make_async_copy(p_ref, mine[0], mine[5].at[0])
+            load = pltpu.make_async_copy(p_ref, mine[0], mine[4].at[0])
             load.start()
             if more:
                 at.greet_all()
             else:
-                at.greet_near(halves)
+                at.greet_near(False)
             load.wait()
+            sums = refs.take(1)[0] if end else out_ref
             others = made(at, more_refs, out_refs, refs) if more else []
-            together(scatter_steps(at, halves, out_ref, *mine), *others)
+            if end is None:
+                together(scatter_steps(at, out_ref, *mine), *others)
+                return
+            for _ in scatter_steps(at, sums, *mine):
+                for issue, _finish in others:
+                    next(issue, None)
+            last = end(at, more_refs, sums, out_ref, refs)
+            together((), *others)
+            last()
 
         return pl.pallas_call(
             kernel,
@@ -1288,7 +1334,6 @@
     call = scatter_kernel(
         grid,
         levels,
-        True,
         cid,
         "attention_sums",
         (tasks, [INVMEM, INVMEM], (jax.ShapeDtypeStruct(shape, BF16),) * 2, (ANY, ANY), ss),
@@ -1297,7 +1342,7 @@
 
 
 def feed_sums(grid, p, cid):
-    return in_parts(grid, grid.planes, scatter_kernel(grid, grid.planes, False, cid, "feed_sums"), p, None)[0]
+    return in_parts(grid, grid.planes, scatter_kernel(grid, grid.planes, cid, "feed_sums"), p, None)[0]
 
 
 def feed_back_sums(grid, p, pair_grad, cid):
@@ -1309,7 +1354,6 @@
     call = scatter_kernel(
         grid,
         grid.planes,
-        False,
         cid,
         "feed_back_sums",
         (tasks, [ANY], (jax.ShapeDtypeStruct(pair_grad.shape, BF16),), (ANY,), rs),
@@ -1317,61 +1361,463 @@
     return in_parts(grid, grid.planes, call, p, (pair_grad,))
 
 
-def attention_back_sums(grid, p, qkv_grad, out_grad, down_grad, cid):
+def attention_back_sums(grid, p, qkv_grad, out_grad, down_grad, gains, merged, cid):
     n, levels = grid.n, grid.planes // 2
     rs, hs = return_scratch(grid, qkv_grad.shape[1:]), head_return_scratch(grid, out_grad.shape[1:])
     ps = [pltpu.VMEM(down_grad.shape, BF16), dma(2)]
+    gs = [pltpu.VMEM(gains.shape, F32), pltpu.VMEM(gains.shape, F32), dma(2)] + share_sems(grid, 1)
+    us = assemble_scratch(grid) if merged else []
+    rows, width = p.shape[2:]
+    tail = [pltpu.VMEM((2, rows, width), BF16), dma(2)] if merged else []
+    inputs = [qkv_grad, out_grad, down_grad, gains] + list(merged)
+    in_specs = [ANY, ANY, INVMEM, INVMEM] + ([ANY] + [INVMEM] * 3 if merged else [])
+    shapes = (
+        jax.ShapeDtypeStruct(qkv_grad.shape, BF16),
+        jax.ShapeDtypeStruct(out_grad.shape, BF16),
+        jax.ShapeDtypeStruct(down_grad.shape, BF16),
+        jax.ShapeDtypeStruct((n,) + gains.shape, F32),
+    ) + (jax.ShapeDtypeStruct((D // n, FF), BF16),) * (2 if merged else 0)
+    out_specs = (ANY, ANY, INVMEM, INVMEM) + ((ANY, ANY) if merged else ())
+    sums = [pltpu.VMEM((2, rows, width), BF16)] if merged else []
+    scratch = sums + rs + hs + ps + gs + us + tail
 
     def tasks(at, ins, outs, refs):
-        return [
+        made = [
             return_task(at, ins[0], outs[0], *refs.take(len(rs))),
             head_return_task(at, ins[1], outs[1], *refs.take(len(hs))),
             pair_task(at, ins[2], outs[2], *refs.take(2)),
+            gains_task(at, ins[3], outs[3], *refs.take(len(gs))),
         ]
+        if merged:
+            made.insert(0, assemble_task(grid, ins[4], outs[4:6], *refs.take(len(us))))
+        return made
+
+    def end(at, ins, sums, out_ref, refs):
+        kept, sems = refs.take(2)
+        grad_ref, tokens_ref, gain_ref = ins[5:8]
+
+        def one(u, r):
+            dy, v = sums[u, r].astype(F32), tokens_ref[u, r].astype(F32)
+            kept[u, r] = (grad_ref[u, r] + norm_back(v, inverse_rms(v), dy * gain_ref[...])).astype(BF16)
+
+        each_rows(2, rows, one)
+        issue, finish = swap_task(at, kept.at[1 - at.member], out_ref, sems)
+        run(issue)
+        out_ref[at.member] = kept[at.member]
+        return finish
 
     call = scatter_kernel(
         grid,
         levels,
-        True,
         cid,
         "attention_back_sums",
-        (
-            tasks,
-            [ANY, ANY, INVMEM],
-            (
-                jax.ShapeDtypeStruct(qkv_grad.shape, BF16),
-                jax.ShapeDtypeStruct(out_grad.shape, BF16),
-                jax.ShapeDtypeStruct(down_grad.shape, F32),
-            ),
-            (ANY, ANY, INVMEM),
-            rs + hs + ps,
+        (tasks, in_specs, shapes, out_specs, scratch),
+        end if merged else None,
+    )
+    return in_parts(grid, levels, call, p, inputs)
+
+
+def inverse_rms(v):
+    return lax.rsqrt(jnp.mean(v * v, axis=-1, keepdims=True) + 1e-06)
+
+
+def norm_back(v, r, weighted):
+    return r * weighted - v * (r * r * r * jnp.mean(weighted * v, axis=-1, keepdims=True))
+
+
+def each_rows(group, rows, step):
+    def one(i, carry):
+        step(i // (rows // 16), pl.ds(pl.multiple_of((i % (rows // 16)) * 16, 16), 16))
+        return carry
+
+    lax.fori_loop(0, group * (rows // 16), one, 0)
+
+
+def fits(grid, rows):
+    return (D // grid.n) % 16 == 0 and scatter_parts(grid, grid.planes, rows, D) == 1
+
+
+def forward_kernel(
+    grid, p, tokens, gate_codes, up_codes, down_codes, pair_scale, down_scale, post_gain, feed_gain, cid
+):
+    n, levels = grid.n, grid.planes
+    group, rows, _ = tokens.shape
+    rows_d = gate_codes.shape[0]
+    units, window, start = feed_windows(grid)
+    size = feed_blocks(grid)
+    sc = scatter_scratch(grid, levels // 2, rows, D)
+    ss = share_sems(grid, 2)
+    ws, gs = FeedWeights.scratch(group, units, window), gather_sems(grid, levels)
+
+    def kernel(
+        p_ref, tokens_ref, gate_ref, up_ref, down_ref, ps_ref, ds_ref, pg_ref, fg_ref,
+        raw_ref, mixed_ref, all_ref, pair_ref, part_ref, wp_ref, wd_ref, *scratch,
+    ):
+        refs = Split(scratch)
+        half_at, at = Place(grid, levels // 2), Place(grid, levels)
+        mine = refs.take(len(sc))
+        share_refs = refs.take(len(ss))
+        weights = FeedWeights(at, group, units, None, None, down_ref, (wp_ref, wd_ref), refs.take(len(ws)))
+        gather_refs = refs.take(len(gs))
+        (x,) = refs.take(1)
+        loads, stores, compute = forward_chunks(weights, all_ref, pair_ref, part_ref, *refs.take(4))
+        load = pltpu.make_async_copy(p_ref, mine[0], mine[4].at[0])
+        load.start()
+        weights.sources = (None, None, down_ref)
+        weights.load()
+        at.greet_all()
+        load.wait()
+
+        def source(ref):
+            return lambda to: ref.at[:, pl.ds(pl.multiple_of(start(to), 128), window)]
+
+        def view(k):
+            return lambda j: weights.codes.at[
+                pl.ds(pl.multiple_of(j * rows_d, 16), rows_d), pl.ds(k * window, window)
+            ]
+
+        issue, finish = share_task(at, [source(gate_ref), source(up_ref)], [view(0), view(1)], *share_refs)
+        for _ in scatter_steps(half_at, raw_ref, *mine):
+            next(issue, None)
+
+        def norms(u, r):
+            raw = raw_ref[u, r].astype(F32)
+            mixed = tokens_ref[u, r].astype(F32) + raw * inverse_rms(raw) * pg_ref[...]
+            mixed_ref[u, r] = mixed
+            x[u, r] = (mixed * inverse_rms(mixed) * fg_ref[...]).astype(BF16)
+
+        each_rows(group, rows, norms)
+        moving = LevelGather(at, x, all_ref, *gather_refs)
+        moving.begin()
+        run(issue)
+
+        def first():
+            finish()
+            weights.make(ps_ref, ds_ref)
+
+        moving.run(lambda zj, fresh: each_chunk(grid, zj, fresh, loads, stores, compute), first)
+        for copy in stores(0):
+            copy.wait()
+        weights.finish()
+
+    def blocks(width):
+        return jax.ShapeDtypeStruct((group, n, rows, width), BF16)
+
+    return pl.pallas_call(
+        kernel,
+        out_shape=(
+            jax.ShapeDtypeStruct(tokens.shape, BF16),
+            jax.ShapeDtypeStruct(tokens.shape, F32),
+            blocks(D),
+            blocks(2 * window),
+            blocks(D),
+            jax.ShapeDtypeStruct((group, D, 2 * window), BF16),
+            jax.ShapeDtypeStruct((group, window, D), BF16),
         ),
-    )
-    return in_parts(grid, levels, call, p, (qkv_grad, out_grad, down_grad))
-
-
-def gains_kernel(grid, gains, cid):
+        in_specs=[ANY, INVMEM, ANY, ANY, ANY, INVMEM, INVMEM, INVMEM, INVMEM],
+        out_specs=(INVMEM, INVMEM) + (ANY,) * 5,
+        scratch_shapes=sc
+        + ss
+        + ws
+        + gs
+        + [pltpu.VMEM(tokens.shape, BF16)]
+        + chunk_buffers(size, rows, D, 2 * window, D)
+        + [dma(3)],
+        compiler_params=params(cid, 62),
+        name="forward",
+    )(p, tokens, gate_codes, up_codes, down_codes, pair_scale, down_scale, post_gain, feed_gain)
+
+
+def turn_kernel(grid, p, mixed, cotangent, pair, pair_matrices, down_matrices, post_gain, cid):
+    n, levels = grid.n, grid.planes
+    group, rows, _ = mixed.shape
+    units, window, _ = feed_windows(grid)
+    size = feed_blocks(grid)
+    sc, gs = scatter_scratch(grid, levels, rows, D), gather_sems(grid, levels)
+
+    def kernel(
+        p_ref, mixed_ref, cot_ref, pair_ref, wp_ref, wd_ref, pg_ref,
+        out_ref, gain_ref, all_ref, part_ref, dgu_ref, hid_ref, *scratch,
+    ):
+        refs = Split(scratch)
+        at = Place(grid, levels)
+        mine, gather_refs = refs.take(len(sc)), refs.take(len(gs))
+        raw, x, kept_out, wp, wd, fetch_sems, swap_sems = refs.take(7)
+        load = pltpu.make_async_copy(p_ref, mine[0], mine[4].at[0])
+        load.start()
+        fetch = [
+            pltpu.make_async_copy(wp_ref, wp, fetch_sems.at[0]),
+            pltpu.make_async_copy(wd_ref, wd, fetch_sems.at[1]),
+        ]
+        loads, stores, compute = backward_chunks(
+            wp, wd, all_ref, pair_ref, part_ref, dgu_ref, hid_ref, *refs.take(6)
+        )
+        at.greet_near(True)
+        load.wait()
+        for copy in fetch:
+            copy.start()
+        run(scatter_steps(at, raw, *mine))
+        gain_ref[...] = jnp.zeros_like(gain_ref)
+
+        def norms(u, r):
+            v, dy = raw[u, r].astype(F32), cot_ref[u, r].astype(F32)
+            inverse, gain = inverse_rms(v), pg_ref[...]
+            kept_out[u, r] = (mixed_ref[u, r] + v * inverse * gain).astype(BF16)
+            x[u, r] = norm_back(v, inverse, dy * gain).astype(BF16)
+            gain_ref[...] += jnp.sum(dy * v * inverse, axis=0, keepdims=True)
+
+        each_rows(group, rows, norms)
+        moving = LevelGather(at, x, all_ref, *gather_refs)
+        moving.begin()
+        give_out, take_out = swap_task(at, kept_out.at[1 - at.member], out_ref, swap_sems)
+        run(give_out)
+        out_ref[at.member] = kept_out[at.member]
+        for copy in fetch:
+            copy.wait()
+
+        moving.run(lambda zj, fresh: each_chunk(grid, zj, fresh, loads, stores, compute))
+        take_out()
+        for copy in stores(0):
+            copy.wait()
+
+    def blocks(width):
+        return jax.ShapeDtypeStruct((group, n, rows, width), BF16)
+
+    return pl.pallas_call(
+        kernel,
+        out_shape=(
+            jax.ShapeDtypeStruct(mixed.shape, BF16),
+            jax.ShapeDtypeStruct((1, D), F32),
+            blocks(D),
+            blocks(D),
+            blocks(2 * window),
+            blocks(window),
+        ),
+        in_specs=[ANY, INVMEM, INVMEM, ANY, ANY, ANY, INVMEM],
+        out_specs=(INVMEM, INVMEM) + (ANY,) * 4,
+        scratch_shapes=sc
+        + gs
+        + [
+            pltpu.VMEM(mixed.shape, BF16),
+            pltpu.VMEM(mixed.shape, BF16),
+            pltpu.VMEM(mixed.shape, BF16),
+            pltpu.VMEM((group, D, 2 * window), BF16),
+            pltpu.VMEM((group, window, D), BF16),
+            dma(2),
+            dma(2),
+        ]
+        + chunk_buffers(size, rows, D, 2 * window, D, 2 * window, window)
+        + [dma(5)],
+        compiler_params=params(cid, 62),
+        name="turn",
+    )(p, mixed, cotangent, pair, pair_matrices, down_matrices, post_gain)
+
+
+def back_kernel(grid, p, fed, down_low, pair_low, hidden, mixed, raw, cotangent, feed_gain, post_gain, cid):
+    n, levels = grid.n, grid.planes
+    group, rows, _ = mixed.shape
+    units, window, _ = feed_windows(grid)
+    size = feed_blocks(grid)
+    chunks = n // size
+    count = group * size * rows
+    rows_d = D // n
+    half = n // 2
+    tile = 256
+    sc, gs = scatter_scratch(grid, levels, rows, D), gather_sems(grid, levels // 2)
+    rs = return_scratch(grid, (rows_d, 2 * window))
+
+    def kernel(
+        p_ref, fed_ref, low_ref, dgu_ref, hid_ref, mixed_ref, raw_ref, cot_ref, fg_ref, pg_ref,
+        grad_ref, feed_ref, post_ref, all_ref, got_ref, down_ref, *scratch,
+    ):
+        refs = Split(scratch)
+        half_at, at = Place(grid, levels // 2), Place(grid, levels)
+        mine, gather_refs, return_refs = refs.take(len(sc)), refs.take(len(gs)), refs.take(len(rs))
+        raw2, x, xs, ys, dgu, hid, pair_sum, down_sum, given, down_out, sems = refs.take(11)
+        load = pltpu.make_async_copy(p_ref, mine[0], mine[4].at[0])
+        load.start()
+
+        def loads(i):
+            at_blocks = pl.ds(i * size, size)
+            return [
+                pltpu.make_async_copy(fed_ref.at[:, at_blocks], xs, sems.at[0]),
+                pltpu.make_async_copy(low_ref.at[:, at_blocks], ys, sems.at[1]),
+                pltpu.make_async_copy(dgu_ref.at[:, at_blocks], dgu, sems.at[2]),
+                pltpu.make_async_copy(hid_ref.at[:, at_blocks], hid, sems.at[3]),
+            ]
+
+        for copy in loads(0):
+            copy.start()
+        at.greet_all()
+        load.wait()
+
+        def sums(i):
+            def one(j, carry):
+                cols = pl.ds(pl.multiple_of(j * tile, tile), tile)
+                pair_term = t_dot(xs[:, :, :, cols].reshape(count, tile), dgu[...].reshape(count, 2 * window))
+                down_term = t_dot(hid[...].reshape(count, window), ys[:, :, :, cols].reshape(count, tile))
+                if i == 0:
+                    pair_sum[cols] = pair_term
+                    down_sum[:, cols] = down_term
+                else:
+                    pair_sum[cols] = pair_sum[cols] + pair_term
+                    down_sum[:, cols] = down_sum[:, cols] + down_term
+                return carry
+
+            for copy in loads(i):
+                copy.wait()
+            lax.fori_loop(0, D // tile, one, 0)
+            if i + 1 < chunks:
+                for copy in loads(i + 1):
+                    copy.start()
+
+        to, _ = pairwise(n, at.c, at.b)
+        other_to, _ = pairwise(n, at.c, 1 - at.b)
+        give_down = pltpu.make_async_copy(down_out, down_ref, sems.at[4])
+
+        def lowered(i):
+            def one(r, carry):
+                here = pl.ds(pl.multiple_of(r * 16, 16), 16)
+                mine_at = pl.ds(pl.multiple_of(to(i) * rows_d + r * 16, 16), 16)
+                other_at = pl.ds(pl.multiple_of(other_to(i) * rows_d + r * 16, 16), 16)
+                return_refs[0][i, here] = pair_sum[mine_at].astype(BF16)
+                given[i, here] = pair_sum[other_at].astype(BF16)
+                return carry
+
+            lax.fori_loop(0, rows_d // 16, one, 0)
+
+        def lowered_down():
+            def one(r, carry):
+                here = pl.ds(pl.multiple_of(r * 16, 16), 16)
+                down_out[here] = down_sum[here].astype(BF16)
+                return carry
+
+            lax.fori_loop(0, window // 16, one, 0)
+            give_down.start()
+
+        def prepare():
+            for i in range(chunks):
+                sums(i)
+                if i % 2 == 1:
+                    yield
+            lowered_down()
+
+        issue, finish = return_task(at, None, got_ref, *return_refs, given=given, fill=lowered, prepare=prepare)
+
+        def main():
+            yield from scatter_steps(at, raw2, *mine)
+            feed_ref[...] = jnp.zeros_like(feed_ref)
+            post_ref[...] = jnp.zeros_like(post_ref)
+
+            def norms(u, r):
+                dy, v = raw2[u, r].astype(F32), mixed_ref[u, r]
+                inverse = inverse_rms(v)
+                grad = cot_ref[u, r].astype(F32) + norm_back(v, inverse, dy * fg_ref[...])
+                feed_ref[...] += jnp.sum(dy * v * inverse, axis=0, keepdims=True)
+                grad_ref[u, r] = grad
+                w = raw_ref[u, r].astype(F32)
+                inverse = inverse_rms(w)
+                x[u, r] = norm_back(w, inverse, grad * pg_ref[...]).astype(BF16)
+                post_ref[...] += jnp.sum(grad * w * inverse, axis=0, keepdims=True)
+
+            each_rows(group, rows, norms)
+            yield from gather_steps(half_at, x, all_ref, *gather_refs)
+
+        together(main(), (issue, finish))
+        give_down.wait()
+
+    return pl.pallas_call(
+        kernel,
+        out_shape=(
+            jax.ShapeDtypeStruct(mixed.shape, F32),
+            jax.ShapeDtypeStruct((1, D), F32),
+            jax.ShapeDtypeStruct((1, D), F32),
+            jax.ShapeDtypeStruct((2, half, rows, D), BF16),
+            jax.ShapeDtypeStruct((n, rows_d, 2 * window), BF16),
+            jax.ShapeDtypeStruct((window, D), BF16),
+        ),
+        in_specs=[ANY] * 5 + [INVMEM] * 5,
+        out_specs=(INVMEM,) * 3 + (ANY,) * 3,
+        scratch_shapes=sc
+        + gs
+        + rs
+        + [
+            pltpu.VMEM(mixed.shape, BF16),
+            pltpu.VMEM(mixed.shape, BF16),
+            pltpu.VMEM((group, size, rows, D), BF16),
+            pltpu.VMEM((group, size, rows, D), BF16),
+            pltpu.VMEM((group, size, rows, 2 * window), BF16),
+            pltpu.VMEM((group, size, rows, window), BF16),
+            pltpu.VMEM((D, 2 * window), F32),
+            pltpu.VMEM((window, D), F32),
+            pltpu.VMEM((half, rows_d, 2 * window), BF16),
+            pltpu.VMEM((window, D), BF16),
+            dma(5),
+        ],
+        compiler_params=params(cid, 63),
+        name="back",
+    )(p, fed, down_low, pair_low, hidden, mixed, raw, cotangent, feed_gain, post_gain)
+
+
+def assemble_task(grid, got_ref, targets, wide, high, load_sem, stores):
     n = grid.n
-    ss = share_sems(grid, 1)
-
-    def kernel(x_ref, out_ref, total, other, sems, *scratch):
-        at = Place(grid, grid.planes)
-        at.greet_all()
-        copy = at.sibling(x_ref, other, sems.at[0], sems.at[1])
+    units, window, _ = feed_windows(grid)
+    inner = n // HEADS
+    whole = inner * units
+    starts = [i * units // 128 * 128 for i in range(inner)]
+    load = pltpu.make_async_copy(got_ref, wide, load_sem.at[0])
+
+    def store(k):
+        return pltpu.make_async_copy(high.at[k], targets[k], stores.at[k])
+
+    def put(g, k):
+        for t in range(0, whole, 128):
+            total = 0.0
+            for i in range(inner):
+                if 0 <= t - starts[i] < window:
+                    total = total + wide[g * inner + i, :, pl.ds(k * window + t - starts[i], 128)].astype(F32)
+            high[k, :, pl.ds(pl.multiple_of(g * whole + t, 128), 128)] = total.astype(BF16)
+
+    def issue():
+        load.start()
+        yield
+        yield
+        load.wait()
+        for k in range(2):
+
+            def one(g, carry):
+                put(g, k)
+                return carry
+
+            lax.fori_loop(0, n // inner, one, 0)
+            store(k).start()
+            yield
+
+    def finish():
+        for k in range(2):
+            store(k).wait()
+
+    return issue(), finish
+
+
+def assemble_scratch(grid):
+    _, window, _ = feed_windows(grid)
+    rows_d = D // grid.n
+    return [pltpu.VMEM((grid.n, rows_d, 2 * window), BF16), pltpu.VMEM((2, rows_d, FF), BF16), dma(1), dma(2)]
+
+
+def gains_task(at, x_ref, out_ref, total, other, sems, *share_refs):
+    copy = at.sibling(x_ref, other, sems.at[0], sems.at[1])
+    later, finish = share_task(at, [lambda to: total], [lambda j: out_ref.at[j]], *share_refs)
+
+    def issue():
         copy.start()
+        yield
         copy.wait()
         total[...] = x_ref[...] + other[...]
-        together((), share_task(at, [lambda to: total], [lambda j: out_ref.at[j]], *scratch))
-
-    return pl.pallas_call(
-        kernel,
-        out_shape=jax.ShapeDtypeStruct((n,) + gains.shape, F32),
-        in_specs=[INVMEM],
-        out_specs=INVMEM,
-        scratch_shapes=[pltpu.VMEM(gains.shape, F32), pltpu.VMEM(gains.shape, F32), dma(2)] + ss,
-        compiler_params=params(cid),
-        name="gains",
-    )(gains)
+        yield from later
+
+    return issue(), finish
 
 
 def normed(value, gain):
@@ -1470,15 +1916,22 @@
     rows_d = D // n
     units, window, _ = feed_windows(grid)
 
-    source = tokens.astype(F32)
-    first_normed = normed(source, attention_gain).astype(BF16)
     q_parts = jnp.transpose(query_codes.reshape(rows_d, HEADS, HEAD), (1, 0, 2))
     k_parts = jnp.repeat(jnp.transpose(key_codes.reshape(rows_d, KV_HEADS, HEAD), (1, 0, 2)), pairs, axis=0)
     v_parts = jnp.repeat(jnp.transpose(value_codes.reshape(rows_d, KV_HEADS, HEAD), (1, 0, 2)), pairs, axis=0)
     qkv_parts = jnp.concatenate([q_parts, k_parts, v_parts], axis=-1).astype(BF16)
     small = jnp.zeros((8, 128), jnp.int32).at[:group, :block].set(positions)
-    seen, qkv_codes, out_codes, all_places = open_kernel(
-        grid, first_normed, qkv_parts, output_codes.astype(BF16), small, 1
+    tokens, cotangent, seen, qkv_codes, out_codes, all_places, gate_low, up_low = open_kernel(
+        grid,
+        tokens,
+        cotangent,
+        attention_gain[None],
+        qkv_parts,
+        output_codes.astype(BF16),
+        small,
+        gate_codes,
+        up_codes,
+        1,
     )
     seen = seen.reshape(length, D)
 
@@ -1517,56 +1970,88 @@
     attended = dot(kernel_low, values) / totals
     attended_low = attended.astype(BF16)
 
+    def swapped_back(kept):
+        own, other = (lax.dynamic_index_in_dim(kept, u, 0, False) for u in (member, 1 - member))
+        other = lax.ppermute(other, "seq", [(c, (c + half) % n) for c in range(n)])
+        return jnp.where(member == 0, jnp.stack([own, other]), jnp.stack([other, own]))
+
     def spread(part):
         if parts > 1:
             part = lax.dynamic_update_slice_in_dim(jnp.zeros((length, D), BF16), part, first_asked, 0)
         return part.reshape(2, half, block, D)
 
-    attention_raw, gate_got, up_got = attention_sums(
-        grid,
-        spread(dot(attended_low, out_matrix).astype(BF16)),
-        gate_codes.astype(BF16),
-        up_codes.astype(BF16),
-        2,
-    )
-    attention_raw = attention_raw.astype(F32)
+    out_part = spread(dot(attended_low, out_matrix).astype(BF16))
     first_column = chip * units // 128 * 128
     inset = chip * units - first_column
     pair_scale = jnp.concatenate(
         [lax.dynamic_slice_in_dim(s, first_column, window) for s in (gate_scale, up_scale)]
-    )
-    feed_weights = (
-        gate_got.reshape(D, window),
-        up_got.reshape(D, window),
-        down_codes,
-        pair_scale[None],
-        down_scale[None],
-    )
-
-    mixed = source + normed(attention_raw, attention_post_gain)
-    second_normed = normed(mixed, feed_gain).astype(BF16)
-    fed, gate_up, down_part, pair_matrices, down_matrices = feed_forward(grid, second_normed, *feed_weights, 3)
-    down_raw = feed_sums(grid, down_part, 4).astype(F32)
-    branch, pull_out = jax.vjp(normed, down_raw, feed_post_gain)
-    output = (mixed + branch).astype(BF16)
-    upstream = cotangent.astype(F32)
-    grad_down_raw, grad_post_feed = pull_out(upstream)
-    _, second_part, pair_grad, down_grad = feed_backward(
-        grid, grad_down_raw.astype(BF16), fed, gate_up, pair_matrices, down_matrices, 9
-    )
+    )[None]
+    if fits(grid, block):
+        attention_raw, mixed, fed, gate_up, down_part, pair_matrices, down_matrices = forward_kernel(
+            grid,
+            out_part,
+            tokens,
+            gate_low,
+            up_low,
+            down_codes,
+            pair_scale,
+            down_scale[None],
+            attention_post_gain[None],
+            feed_gain[None],
+            2,
+        )
+        output, grad_post_feed, down_low, second_part, pair_low, hidden = turn_kernel(
+            grid, down_part, mixed, cotangent, gate_up, pair_matrices, down_matrices, feed_post_gain[None], 3
+        )
+        grad_mixed, grad_pre_feed, grad_post_attention, attention_low, pair_got, down_grad = back_kernel(
+            grid,
+            second_part,
+            fed,
+            down_low,
+            pair_low,
+            hidden,
+            mixed,
+            attention_raw,
+            cotangent,
+            feed_gain[None],
+            attention_post_gain[None],
+            4,
+        )
+    else:
+        attention_raw, gate_got, up_got = attention_sums(grid, out_part, gate_low, up_low, 2)
+        attention_raw = attention_raw.astype(F32)
+        feed_weights = (
+            gate_got.reshape(D, window),
+            up_got.reshape(D, window),
+            down_codes,
+            pair_scale,
+            down_scale[None],
+        )
+        mixed = tokens.astype(F32) + normed(attention_raw, attention_post_gain)
+        second_normed = normed(mixed, feed_gain).astype(BF16)
+        fed, gate_up, down_part, pair_matrices, down_matrices = feed_forward(grid, second_normed, *feed_weights, 3)
+        down_raw = feed_sums(grid, down_part, 4).astype(F32)
+        branch, pull_out = jax.vjp(normed, down_raw, feed_post_gain)
+        output = swapped_back((mixed + branch).astype(BF16))
+        upstream = cotangent.astype(F32)
+        grad_down_raw, grad_post_feed = pull_out(upstream)
+        down_low, second_part, pair_low, hidden = feed_backward(
+            grid, grad_down_raw.astype(BF16), gate_up, pair_matrices, down_matrices, 9
+        )
+        count = group * length
+        pair_grad = t_dot(fed.reshape(count, D), pair_low.reshape(count, 2 * window)).astype(BF16)
+        down_grad = t_dot(hidden.reshape(count, window), down_low.reshape(count, D)).astype(BF16)
+        grad_second, pair_got = feed_back_sums(grid, second_part, pair_grad.reshape(n, rows_d, 2 * window), 5)
+        gate_grad, up_grad = (unwindowed(grid, pair_got[..., i * window : (i + 1) * window]) for i in range(2))
+        _, pull_feed = jax.vjp(normed, mixed, feed_gain)
+        grad_mixed_part, grad_pre_feed = pull_feed(grad_second.astype(F32))
+        grad_mixed = upstream + grad_mixed_part
+        _, pull_post = jax.vjp(normed, attention_raw, attention_post_gain)
+        grad_attention, grad_post_attention = pull_post(grad_mixed)
+        attention_low = gather(grid, grad_attention.astype(BF16), grid.planes // 2, 6)
     down_grad = lax.dynamic_slice(down_grad, (inset, 0), (units, D))
-    grad_second, pair_got = feed_back_sums(
-        grid, second_part, pair_grad.reshape(n, rows_d, 2 * window), 5
-    )
-    grad_second = grad_second.astype(F32)
-    gate_grad, up_grad = (unwindowed(grid, pair_got[..., i * window : (i + 1) * window]) for i in range(2))
-
-    _, pull_feed = jax.vjp(normed, mixed, feed_gain)
-    grad_mixed_part, grad_pre_feed = pull_feed(grad_second)
-    grad_mixed = upstream + grad_mixed_part
-    _, pull_post = jax.vjp(normed, attention_raw, attention_post_gain)
-    grad_attention, grad_post_attention = pull_post(grad_mixed)
-    attention_low = gather(grid, grad_attention.astype(BF16), grid.planes // 2, True, 6).reshape(length, D)
+
+    attention_low = attention_low.reshape(length, D)
     if parts > 1:
         attention_low = lax.dynamic_slice_in_dim(attention_low, first_asked, asked)
     grad_attended = dot_t(attention_low, out_matrix)
@@ -1590,27 +2075,37 @@
             first_part, lax.dynamic_slice_in_dim(first_part, first_asked, asked) + q_back, first_asked, 0
         )
         qkv_grad = jnp.concatenate([t_dot(seen_asked, q_low), t_dot(seen, kv_low)], axis=-1)
+    first_part = first_part.astype(BF16)
+    grad_pre_attention = jnp.sum(first_part.astype(F32) * seen.astype(F32), axis=0) / attention_gain
+    gains = jnp.stack(
+        [g.reshape(D) for g in (grad_pre_attention, grad_post_attention, grad_pre_feed, grad_post_feed)]
+    )
     out_part = t_dot(attended_low, attention_low).astype(BF16).reshape(copies, HEAD // copies, D)
-    grad_first, qkv_got, out_got, down_grad = attention_back_sums(
+    merged = (pair_got, grad_mixed, tokens, attention_gain[None]) if fits(grid, block) else ()
+    grad_in, qkv_got, out_got, down_grad, gains, *assembled = attention_back_sums(
         grid,
-        first_part.astype(BF16).reshape(2, half, block, D),
+        first_part.reshape(2, half, block, D),
         qkv_grad.astype(BF16).reshape(n, rows_d, 3 * HEAD),
         out_part,
         down_grad,
+        gains.reshape(8, D // 2),
+        merged,
         7,
     )
-    grad_first = grad_first.astype(F32)
-    _, pull_in = jax.vjp(normed, source, attention_gain)
-    grad_source_part, grad_pre_attention = pull_in(grad_first)
-    grad_in = (grad_mixed + grad_source_part).astype(BF16)
+    if merged:
+        gate_grad, up_grad = (a.astype(F32) for a in assembled)
+    else:
+        _, pull_in = jax.vjp(lambda value: normed(value, attention_gain), tokens.astype(F32))
+        (grad_source_part,) = pull_in(grad_in.astype(F32))
+        grad_in = swapped_back((grad_mixed + grad_source_part).astype(BF16))
+    down_grad = down_grad.astype(F32)
     qkv_got = jnp.sum(qkv_got.astype(F32).reshape(copies, HEADS, rows_d, 3 * HEAD), axis=0)
     query_grad = jnp.transpose(qkv_got[..., :HEAD], (1, 0, 2)).reshape(rows_d, HEADS * HEAD)
     kv_grad = jnp.sum(qkv_got[..., HEAD:].reshape(KV_HEADS, pairs, rows_d, 2 * HEAD), axis=1)
     key_grad = jnp.transpose(kv_grad[..., :HEAD], (1, 0, 2)).reshape(rows_d, KV_HEADS * HEAD)
     value_grad = jnp.transpose(kv_grad[..., HEAD:], (1, 0, 2)).reshape(rows_d, KV_HEADS * HEAD)
     out_grad = jnp.sum(out_got.astype(F32), axis=0)
-    gains = jnp.stack([grad_pre_attention, grad_post_attention, grad_pre_feed, grad_post_feed])
-    gains = jnp.sum(gains_kernel(grid, gains.reshape(8, D // 2), 8), axis=0).reshape(4, D)
+    gains = jnp.sum(gains, axis=0).reshape(4, D)
     return (
         output,
         grad_in,

time: 969 us -> 885 us (0.913)
  Pallas kernels: 842 us -> 771 us
  other arithmetic: 49.1 us -> 32.6 us
    pallas_call x4 -> x1, Pallas kernels: 437 us -> 102 us  [call(): pl.pallas_call(kernel, out_shape=(jax.ShapeDtypeStruct((2, rows, width),...]
    pallas_call x5 -> x4, Pallas kernels: 405 us -> 669 us  [the longest x1 195 us: forward_kernel(): pl.pallas_call(kernel, out_shape=(jax.ShapeDtypeStruct(tokens.shape, BF16...]
where the time goes in v4:
time: 885 us; the launch traced here: 873 us
  Pallas kernels  771 us (87%)
  matrix products  40.9 us (5%)
  other arithmetic  32.6 us (4%)
  local copies, waits for them, and re-layouts  27.4 us (3%)
    pallas_call x1, Pallas kernels, forward_kernel(): pl.pallas_call(kernel, out_shape=(jax.ShapeDtypeStruct(tokens.shape, BF16...  195 us
    pallas_call x1, Pallas kernels, back_kernel(): pl.pallas_call(kernel, out_shape=(jax.ShapeDtypeStruct(mixed.shape, F32),...  187 us
    pallas_call x1, Pallas kernels, turn_kernel(): pl.pallas_call(kernel, out_shape=(jax.ShapeDtypeStruct(mixed.shape, BF16)...  186 us
    pallas_call x1, Pallas kernels, call(): pl.pallas_call(kernel, out_shape=(jax.ShapeDtypeStruct((2, rows, width),...  102 us
    pallas_call x1, Pallas kernels, open_kernel(): pl.pallas_call(kernel, out_shape=(jax.ShapeDtypeStruct(x.shape, BF16), ja...  101 us

profile of v4, /device:TPU:0, one launch (start us, length us, event | category | flops | bytes accessed | tf_op | source)
XLA Modules:
  0.0 873.5 jit_solution(14309488225663898480)
XLA Ops:
  4.9 0.8 dynamic_slice.26
  5.6 0.8 dynamic_slice.27
  7.0 1.3 broadcast_in_dim.48.pg_ref
  8.3 1.3 broadcast_in_dim.49.fg_ref
  10.4 1.3 broadcast_in_dim.47.ds_ref
  11.7 1.3 broadcast_in_dim.50.pg_ref
  13.0 1.1 convert.61
  14.4 1.1 convert.62
  16.0 1.3 pad_maximum_fusion.w_ref
  17.4 100.5 %open.1 = (bf16[2,64,2304]{2,1,0:T(8,128)(2,1)S(1)}, bf16[2,64,2304]{2,1,0:T(8,128)(2,1)S(1)}, bf16[2,8,64,2304]{3,2,1,0:T(8,128)(2,1)}, bf16[2304,768]{1,0:T(8,...) custom-call(bf16[2,64,2304]{2,1,0:T(8,128)(2,1)S(1)} %copy-done.2, ...), custom_call_target="tpu_custom_call" | custom-call | tf_op jit(solution)/shard_map/open/pallas_call | solution.py:1243
  118.0 0.8 copy-done
  118.8 0.8 copy-done.1
  119.7 7.5 fusion.51
  127.3 2.4 fusion.31
  129.8 1.5 multiply_convert_fusion.2
  131.4 1.8 fusion.2
  133.3 1.7 convolution_divide_fusion
  135.3 3.6 convolution_convert_fusion.1
  138.9 195.1 %forward.1 = (bf16[2,64,2304]{2,1,0:T(8,128)(2,1)}, f32[2,64,2304]{2,1,0:T(8,128)}, bf16[2,16,64,2304]{3,2,1,0:T(8,128)(2,1)}, bf16[2,16,64,1280]{3,2,1,0:T(8,12...) custom-call(bf16[2,8,64,2304]{3,2,1,0:T(8,128)(2,1)} %bitcast.49, ...), custom_call_target="tpu_custom_call" | custom-call | tf_op jit(solution)/shard_map/forward/pallas_call | solution.py:1506
  334.1 185.5 %turn.1 = (bf16[2,64,2304]{2,1,0:T(8,128)(2,1)}, f32[1,2304]{1,0:T(1,128)}, bf16[2,16,64,2304]{3,2,1,0:T(8,128)(2,1)}, bf16[2,16,64,2304]{3,2,1,0:T(8,128)(2,1)}...) custom-call(bf16[2,16,64,2304]{3,2,1,0:T(8,128)(2,1)} %get-tuple-element.66.p_ref, ...), custom_call_target="tpu_custom_call" | custom-call | tf_op jit(solution)/shard_map/turn/pallas_call | solution.py:1586
  519.6 187.5 %back.1 = (f32[2,64,2304]{2,1,0:T(8,128)}, f32[1,2304]{1,0:T(1,128)}, f32[1,2304]{1,0:T(1,128)}, bf16[2,8,64,2304]{3,2,1,0:T(8,128)(2,1)}, bf16[16,144,1280]{2,1,0:T(8,128)(2,1)}, /*index=5*/bf16[640,2304]{1,0:T(8,128)(2,1)}) custom-call(bf16[2,16,64,2304]{3,2,1,0:T(8,128)(2,1)} %get-tuple-element.73.p_ref, ...), custom_call_target="tpu_custom_call" | custom-call | tf_op jit(solution)/shard_map/back/pallas_call | solution.py:1729
  707.1 4.5 multiply_reduce_fusion.1
  711.8 2.4 convolution_convert_fusion.3
  714.2 4.0 multiply_convert_fusion.1
  719.7 2.3 fusion.42
  722.0 2.3 fusion.41
  724.3 2.3 fusion.40
  726.5 2.3 fusion.39
  728.8 1.8 fusion.4
  731.0 6.6 multiply_reduce_fusion
  737.7 5.4 convolution_convert_fusion.2
  743.8 1.7 constant_dynamic-slice_fusion.refs_3_
  745.5 102.0 %attention_back_sums.1 = (bf16[2,64,2304]{2,1,0:T(8,128)(2,1)}, bf16[16,144,768]{2,1,0:T(8,128)(2,1)}, bf16[2,128,2304]{2,1,0:T(8,128)(2,1)}, bf16[576,2304]{1,0...) custom-call(bf16[2,8,64,2304]{3,2,1,0:T(8,128)(2,1)} %bitcast.50, ...), custom_call_target="tpu_custom_call" | custom-call | tf_op jit(solution)/shard_map/attention_back_sums/pallas_call | solution.py:1298
  847.5 3.0 convert_reduce_fusion
  850.4 1.7 reduce_sum.69
  852.2 1.5 fusion.52
  853.7 1.3 squeeze.17
  855.0 1.3 squeeze.16
  856.3 1.3 squeeze.15
  858.5 1.1 copy.64
  859.8 0.9 copy.66
  860.7 0.9 copy.65
  861.5 1.2 convert_reduce_fusion.1
  862.7 2.9 convert_element_type.97
  865.7 2.9 convert_element_type.98
  868.6 2.8 convert_element_type.99
  871.4 0.8 copy.75
  872.2 0.8 copy.76
  (99 shorter events, 10.5 us)
Async XLA Ops:
  0.6 15.2 %copy-start.12 = (s32[144,2048]{1,0:T(8,128)S(1)}, s32[144,2048]{1,0:T(8,128)}, u32[]{:S(2)}) copy-start(s32[144,2048]{1,0:T(8,128)} %param.27) | copy-start | bytes 3538948
  10.3 7.0 copy-start.4
  15.5 1.8 copy-start.13
  15.8 1.6 copy-start.2
  15.8 1.6 copy-start.3
  17.4 102.3 %copy-start.26 = (f32[768]{0:T(1024)S(1)}, f32[768]{0:T(1024)}, u32[]{:S(2)}) copy-start(f32[768]{0:T(1024)} %pad_maximum_fusion.9) | copy-start | bytes 9220
  118.0 0.8 copy-start
  118.8 0.8 copy-start.1
  119.7 7.6 copy-start.22
  119.7 10.0 %copy-start.15 = (bf16[2,128,2304]{2,1,0:T(8,128)(2,1)S(1)}, bf16[2,128,2304]{2,1,0:T(8,128)(2,1)}, u32[]{:S(2)}) copy-start(bf16[2,128,2304]{2,1,0:T(8,128)(2,1)} %get-tuple-element.62) | copy-start | bytes 3538948
  119.7 10.0 %copy-start.21 = (f32[2304]{0:T(1024)S(1)}, f32[2304]{0:T(1024)}, u32[]{:S(2)}) copy-start(f32[2304]{0:T(1024)} %param.37) | copy-start | bytes 27652
  127.3 6.0 copy-start.11
  129.7 3.5 copy-start.18
  133.3 2.0 copy-start.29
  135.3 3.6 copy-start.9
  707.1 4.6 copy-start.10
  707.1 4.7 copy-start.27
  711.8 2.4 copy-start.30
  714.2 4.0 copy-start.19
  724.3 6.4 slice-start
  728.8 1.8 slice-start.1
  728.8 2.2 copy-start.28
  737.6 5.4 copy-start.20
  737.6 5.4 copy-start.23
  737.6 5.4 copy-start.24
  737.6 5.5 copy-start.25
  737.6 6.1 copy-start.8
  858.4 3.1 copy-start.14
  858.5 4.2 copy-start.7
  862.7 2.9 copy-start.6
  865.7 2.9 copy-start.5
  868.6 2.8 copy-start.16
  868.6 3.6 copy-start.17

commit v5 on v4

--- a/solution.py
+++ b/solution.py
@@ -240,47 +240,77 @@
     )(x)
 
 
+def level_sems(grid, levels):
+    steps = grid.plane // 2
+    return gather_sems(grid, levels) + [dma(2, levels), dma(2, levels), dma(2, steps), dma(2, steps)]
+
+
 class LevelGather:
-    def __init__(self, at, x_ref, out_ref, zs, zr, rs, rr, ls):
+    def __init__(self, split, at, x_ref, out_ref, zs, zr, rs, rr, ls, lzs, lzr, lrs, lrr):
         self.at, self.x, self.out = at, x_ref, out_ref
         self.zs, self.zr, self.rs, self.rr, self.ls = zs, zr, rs, rr, ls
-        self.half = x_ref.shape[1] // 2
-
-    def block(self, zj, qj, part=None):
-        if part is None:
-            return self.out.at[:, self.at.slot(zj, qj)]
-        return self.out.at[:, self.at.slot(zj, qj), pl.ds(part * self.half, self.half)]
+        self.lzs, self.lzr, self.lrs, self.lrr = lzs, lzr, lrs, lrr
+        rows = x_ref.shape[1]
+        cut = rows * 3 // 4 // 16 * 16 if split else rows
+        self.split, self.first, self.last = split, pl.ds(0, cut), pl.ds(cut, rows - cut)
+
+    def block(self, zj, qj, part, rows):
+        which = pl.ds(0, 2) if part is None else pl.ds(part, 1)
+        return self.out.at[which, self.at.slot(zj, qj), rows]
 
     def z_copy(self, zj, way):
-        at, ref = self.at, self.block(zj, self.at.q)
+        at, ref = self.at, self.block(zj, self.at.q, None, self.first)
         to = at.c + (at.pn if way == 0 else -at.pn)
         return remote(ref, ref, self.zs.at[0, way, zj], self.zr.at[0, way, zj], to, at.b)
 
-    def r_copy(self, zj, way, step, landing=False):
+    def ring_copy(self, zj, way, step, landing, rows, send, recv):
         at = self.at
         away = step if landing else step - 1
-        ref = self.block(zj, at.q - away if way == 0 else at.q + away, way if step == at.steps else None)
-        to = at.right if way == 0 else at.left
-        return remote(ref, ref, self.rs.at[0, way, step - 1, zj], self.rr.at[0, way, step - 1, zj], to, at.b)
+        ref = self.block(zj, at.q - away if way == 0 else at.q + away, way if step == at.steps else None, rows)
+        return remote(ref, ref, send, recv, at.right if way == 0 else at.left, at.b)
+
+    def r_copy(self, zj, way, step, landing=False):
+        sems = self.rs.at[0, way, step - 1, zj], self.rr.at[0, way, step - 1, zj]
+        return self.ring_copy(zj, way, step, landing, self.first, *sems)
+
+    def low_copy(self, way, step, landing=False):
+        sems = self.lrs.at[way, step - 1], self.lrr.at[way, step - 1]
+        return self.ring_copy(self.at.zi, way, step, landing, self.last, *sems)
+
+    def low_z_copy(self, zj, way):
+        at = self.at
+        ref = self.out.at[:, pl.ds(zj * at.pn, at.pn), self.last]
+        to = at.c + (at.pn if way == 0 else -at.pn)
+        return remote(ref, ref, self.lzs.at[way, zj], self.lzr.at[way, zj], to, at.b)
 
     def begin(self):
-        local = pltpu.make_async_copy(self.x, self.block(self.at.zi, self.at.q), self.ls.at[0])
+        at = self.at
+        local = pltpu.make_async_copy(self.x, self.out.at[:, at.slot(at.zi, at.q)], self.ls.at[0])
         local.start()
         local.wait()
         self.send(0)
-
-    def send(self, offset):
+        if self.split:
+            for way in (0, 1):
+                self.low_copy(way, 1).start()
+
+    def along(self, offset, copy):
         at = self.at
         zj = at.zi + offset
-        pl.when((offset <= 0) & (at.zi < at.levels - 1))(lambda: self.z_copy(zj, 0).start())
-        pl.when((offset >= 0) & (at.zi > 0))(lambda: self.z_copy(zj, 1).start())
+        pl.when((offset <= 0) & (at.zi < at.levels - 1))(lambda: copy(zj, 0).start())
+        pl.when((offset >= 0) & (at.zi > 0))(lambda: copy(zj, 1).start())
+
+    def send(self, offset):
+        self.along(offset, self.z_copy)
         for way in (0, 1):
-            self.r_copy(zj, way, 1).start()
+            self.r_copy(self.at.zi + offset, way, 1).start()
 
     def arrive(self, sign, d):
-        zj = self.at.zi + sign * d
-        self.z_copy(zj, 0 if sign < 0 else 1).wait_recv()
+        self.z_copy(self.at.zi + sign * d, 0 if sign < 0 else 1).wait_recv()
         self.send(sign * d)
+
+    def low_arrive(self, sign, d):
+        self.low_z_copy(self.at.zi + sign * d, 0 if sign < 0 else 1).wait_recv()
+        self.along(sign * d, self.low_z_copy)
 
     def onward(self, sign, d):
         zj = self.at.zi + sign * d
@@ -289,6 +319,17 @@
                 self.r_copy(zj, way, step, True).wait_recv()
                 self.r_copy(zj, way, step + 1).start()
 
+    def low_onward(self):
+        for step in range(1, self.at.steps):
+            for way in (0, 1):
+                self.low_copy(way, step, True).wait_recv()
+                self.low_copy(way, step + 1).start()
+
+    def low_landed(self):
+        for way in (0, 1):
+            self.low_copy(way, self.at.steps, True).wait_recv()
+        self.along(0, self.low_z_copy)
+
     def landed(self, sign, d):
         zj = self.at.zi + sign * d
         for way in (0, 1):
@@ -298,14 +339,18 @@
         at = self.at
 
         def one(zj, carry):
-            pl.when((zj <= at.zi) & (at.zi < at.levels - 1))(lambda: self.z_copy(zj, 0).wait_send())
-            pl.when((zj >= at.zi) & (at.zi > 0))(lambda: self.z_copy(zj, 1).wait_send())
+            for copy in (self.z_copy, self.low_z_copy)[: 2 if self.split else 1]:
+                pl.when((zj <= at.zi) & (at.zi < at.levels - 1))(lambda: copy(zj, 0).wait_send())
+                pl.when((zj >= at.zi) & (at.zi > 0))(lambda: copy(zj, 1).wait_send())
             for way in (0, 1):
                 for step in range(1, at.steps + 1):
                     self.r_copy(zj, way, step).wait_send()
             return carry
 
         lax.fori_loop(0, at.levels, one, 0)
+        for way in (0, 1) if self.split else ():
+            for step in range(1, at.steps + 1):
+                self.low_copy(way, step).wait_send()
 
     def run(self, compute, first=None):
         at = self.at
@@ -315,16 +360,20 @@
             pl.when((t < levels) & (zi - t >= 0))(lambda: self.arrive(-1, t))
             pl.when((t < levels) & (zi + t < levels))(lambda: self.arrive(1, t))
 
-        def both(d, action):
-            pl.when((d < levels) & (zi - d >= 0))(lambda: action(-1, d))
+        def both(d, action, least=0):
+            pl.when((d >= least) & (d < levels) & (zi - d >= 0))(lambda: action(-1, d))
             pl.when((d > 0) & (d < levels) & (zi + d < levels))(lambda: action(1, d))
 
         def one(t, carry):
             wave(t)
+            if self.split:
+                pl.when(t == 2)(self.low_landed)
             both(t - 1, self.onward)
             if first is not None:
                 pl.when(t == 2)(first)
             e = t - 2
+            if self.split:
+                both(e, self.low_arrive, 1)
             both(e, self.landed)
 
             def side(i, carry):
@@ -338,6 +387,8 @@
 
         wave(1)
         both(0, self.onward)
+        if self.split:
+            self.low_onward()
         lax.fori_loop(2, levels + 2, one, 0)
         self.finish()
 
@@ -362,6 +413,9 @@
 
 GELU_A = 0.7978845608028654
 GELU_B = 0.044715
+
+
+EARLY = 4
 
 
 class FeedWeights:
@@ -461,7 +515,7 @@
 
 
 def forward_chunks(weights, all_ref, pair_ref, part_ref, xs, gu, part, sems):
-    _, size, rows, _ = xs.shape
+    _, size, rows, _ = gu.shape
     window = weights.down.shape[1]
 
     def loads(first):
@@ -519,7 +573,7 @@
     group, rows, _ = x.shape
     n, levels = grid.n, grid.planes
     units, window, _ = feed_windows(grid)
-    gs, ws = gather_sems(grid, levels), FeedWeights.scratch(group, units, window)
+    gs, ws = level_sems(grid, levels), FeedWeights.scratch(group, units, window)
     size = feed_blocks(grid)
 
     def kernel(
@@ -529,7 +583,7 @@
         at = Place(grid, levels)
         weights = FeedWeights(at, group, units, gate_ref, up_ref, down_ref, (wp_ref, wd_ref), refs.take(len(ws)))
         weights.load()
-        moving = LevelGather(at, x_ref, all_ref, *refs.take(len(gs)))
+        moving = LevelGather(True, at, x_ref, all_ref, *refs.take(len(gs)))
         loads, stores, compute = forward_chunks(weights, all_ref, pair_ref, part_ref, *refs.take(4))
         at.greet_near(False)
         moving.begin()
@@ -563,13 +617,13 @@
     group, rows, _ = x.shape
     n, levels = grid.n, grid.planes
     _, window, _ = feed_windows(grid)
-    gs = gather_sems(grid, levels)
+    gs = level_sems(grid, levels)
     size = feed_blocks(grid)
 
     def kernel(x_ref, pair_ref, wp_ref, wd_ref, all_ref, part_ref, dgu_ref, hid_ref, *scratch):
         refs = Split(scratch)
         at = Place(grid, levels)
-        moving = LevelGather(at, x_ref, all_ref, *refs.take(len(gs)))
+        moving = LevelGather(True, at, x_ref, all_ref, *refs.take(len(gs)))
         wp, wd, fetch_sems = refs.take(3)
         fetch = [
             pltpu.make_async_copy(wp_ref, wp, fetch_sems.at[0]),
@@ -1183,7 +1237,7 @@
     return issue(), finish
 
 
-def open_kernel(grid, tokens, cotangent, gain, qkv_parts, out_codes, small, gate_codes, up_codes, cid):
+def open_kernel(grid, tokens, gain, qkv_parts, out_codes, small, gate_codes, up_codes, cid):
     x = tokens
     n, levels = grid.n, grid.planes // 2
     rows_d, width = qkv_parts.shape[1:]
@@ -1200,12 +1254,12 @@
     ]
 
     def kernel(
-        x_ref, cot_ref, gain_ref, w_ref, o_ref, small_ref, gate_ref, up_ref,
-        kept_ref, kept_cot_ref, seen_ref, codes_ref, rows_ref, all_ref, gl_ref, ul_ref, *scratch,
+        x_ref, gain_ref, w_ref, o_ref, small_ref, gate_ref, up_ref,
+        kept_ref, seen_ref, codes_ref, rows_ref, all_ref, gl_ref, ul_ref, *scratch,
     ):
         at = Place(grid, levels)
         refs = Split(scratch)
-        normed_ref, token_sems, cot_sems = refs.take(3)
+        normed_ref, token_sems = refs.take(2)
         member = at.member
         at.greet_all()
         token_issue, token_finish = swap_task(at, x_ref.at[1 - member], kept_ref, token_sems)
@@ -1222,9 +1276,8 @@
             def one(_, r):
                 if k == 0:
                     kept_ref[u, r] = x_ref[u, r]
-                    kept_cot_ref[u, r] = cot_ref[u, r]
                 value = kept_ref[u, r].astype(F32)
-                normed_ref[u, r] = (value * inverse_rms(value) * gain_ref[...]).astype(BF16)
+                normed_ref[u, r] = (value * inverse_rms(value) * gain_ref[0:1]).astype(BF16)
 
             each_rows(1, x_ref.shape[1], one)
 
@@ -1236,14 +1289,12 @@
             tell_task(at, small_ref, all_ref, *refs.take(2)),
             share_task(at, [lambda to: w_ref.at[to % HEADS]], [view], *refs.take(len(ss))),
             head_rows_task(at, o_ref, rows_ref, *refs.take(4)),
-            swap_task(at, cot_ref.at[1 - member], kept_cot_ref, cot_sems),
         )
 
     codes_shape = (n * rows_d, width) if flat else (n, rows_d, width)
     return pl.pallas_call(
         kernel,
         out_shape=(
-            jax.ShapeDtypeStruct(x.shape, BF16),
             jax.ShapeDtypeStruct(x.shape, BF16),
             jax.ShapeDtypeStruct((2, levels * grid.plane) + x.shape[1:], BF16),
             jax.ShapeDtypeStruct(codes_shape, BF16),
@@ -1252,12 +1303,12 @@
             jax.ShapeDtypeStruct(gate_codes.shape, BF16),
             jax.ShapeDtypeStruct(up_codes.shape, BF16),
         ),
-        in_specs=[INVMEM] * 6 + [ANY] * 2,
-        out_specs=(INVMEM, INVMEM) + (ANY,) * 6,
-        scratch_shapes=[pltpu.VMEM(x.shape, BF16), dma(2), dma(2)] + gs + ns + ts + ss + hs,
+        in_specs=[INVMEM] * 5 + [ANY] * 2,
+        out_specs=(INVMEM,) + (ANY,) * 6,
+        scratch_shapes=[pltpu.VMEM(x.shape, BF16), dma(2)] + gs + ns + ts + ss + hs,
         compiler_params=params(cid, 50),
         name="open",
-    )(tokens, cotangent, gain, qkv_parts, out_codes, small, gate_codes, up_codes)
+    )(tokens, gain, qkv_parts, out_codes, small, gate_codes, up_codes)
 
 
 def scatter_kernel(grid, levels, cid, name, tasks=None, end=None):
@@ -1365,7 +1416,8 @@
     n, levels = grid.n, grid.planes // 2
     rs, hs = return_scratch(grid, qkv_grad.shape[1:]), head_return_scratch(grid, out_grad.shape[1:])
     ps = [pltpu.VMEM(down_grad.shape, BF16), dma(2)]
-    gs = [pltpu.VMEM(gains.shape, F32), pltpu.VMEM(gains.shape, F32), dma(2)] + share_sems(grid, 1)
+    every = pltpu.VMEM((n,) + gains.shape, F32)
+    gs = [pltpu.VMEM(gains.shape, F32), pltpu.VMEM(gains.shape, F32), every, dma(2)] + share_sems(grid, 1)
     us = assemble_scratch(grid) if merged else []
     rows, width = p.shape[2:]
     tail = [pltpu.VMEM((2, rows, width), BF16), dma(2)] if merged else []
@@ -1375,7 +1427,7 @@
         jax.ShapeDtypeStruct(qkv_grad.shape, BF16),
         jax.ShapeDtypeStruct(out_grad.shape, BF16),
         jax.ShapeDtypeStruct(down_grad.shape, BF16),
-        jax.ShapeDtypeStruct((n,) + gains.shape, F32),
+        jax.ShapeDtypeStruct(gains.shape, F32),
     ) + (jax.ShapeDtypeStruct((D // n, FF), BF16),) * (2 if merged else 0)
     out_specs = (ANY, ANY, INVMEM, INVMEM) + ((ANY, ANY) if merged else ())
     sums = [pltpu.VMEM((2, rows, width), BF16)] if merged else []
@@ -1398,7 +1450,7 @@
 
         def one(u, r):
             dy, v = sums[u, r].astype(F32), tokens_ref[u, r].astype(F32)
-            kept[u, r] = (grad_ref[u, r] + norm_back(v, inverse_rms(v), dy * gain_ref[...])).astype(BF16)
+            kept[u, r] = (grad_ref[u, r] + norm_back(v, inverse_rms(v), dy * gain_ref[0:1])).astype(BF16)
 
         each_rows(2, rows, one)
         issue, finish = swap_task(at, kept.at[1 - at.member], out_ref, sems)
@@ -1417,6 +1469,128 @@
     return in_parts(grid, levels, call, p, inputs)
 
 
+SCALE = HEAD ** (-0.5)
+
+
+def rotated(u, cosine, sine):
+    half = u.shape[1] // 2
+    first, second = u[:, :half], u[:, half:]
+    return jnp.concatenate([first * cosine - second * sine, second * cosine + first * sine], axis=1)
+
+
+def scores(q, k, start, first):
+    bent = jnp.tanh(dot_t(q, k) * (SCALE / cap_limit))
+    key = lax.broadcasted_iota(jnp.int32, bent.shape, 1)
+    query = first + lax.broadcasted_iota(jnp.int32, bent.shape, 0)
+    return jnp.where((key <= query) & (key >= start), jnp.exp(cap_limit * bent), 0.0), bent
+
+
+def scale_rows(core, member, codes, column_scale, into, rows):
+    step = member_step(core, 2, member)
+    offset = jnp.where(step > 1.0, 0.5 * step, 0.0)
+
+    def one(i, carry):
+        r = pl.ds(pl.multiple_of(i * 16, 16), 16)
+        level = jnp.floor(codes[r].astype(F32) * (1.0 / step)) * step + offset
+        into[r] = (level * column_scale).astype(BF16)
+        return carry
+
+    lax.fori_loop(0, rows // 16, one, 0)
+
+
+def attention_body(w, o, x_rows, put, cos_ref, sin_ref, start_ref, q_ref, k_ref, v_ref, a_ref, t_ref, block=256):
+    length = q_ref.shape[0]
+    for i in range(length // block):
+        r = pl.ds(i * block, block)
+        lin = dot(x_rows(i), w[...])
+        q_ref[r] = rotated(lin[:, :HEAD], cos_ref[r], sin_ref[r]).astype(BF16)
+        k_ref[r] = rotated(lin[:, HEAD : 2 * HEAD], cos_ref[r], sin_ref[r]).astype(BF16)
+        v_ref[r] = lin[:, 2 * HEAD :].astype(BF16)
+    for i in range(length // block):
+        r, keys = pl.ds(i * block, block), pl.ds(0, (i + 1) * block)
+        e, _ = scores(q_ref[r], k_ref[keys], start_ref[r], i * block)
+        total = jnp.sum(e, axis=1, keepdims=True)
+        attended = (dot(e.astype(BF16), v_ref[keys]) / total).astype(BF16)
+        a_ref[r] = attended
+        t_ref[r] = total
+        put(i, dot(attended, o[...]).astype(BF16))
+
+
+def attention_backward(seen, grad, w, o, q, k, v, attended, totals, vectors, cosine, sine, start):
+    length = seen.shape[0]
+    block, tile = 256, 256
+
+    def kernel(
+        x_ref, g_ref, w_ref, o_ref, q_ref, k_ref, v_ref, a_ref, t_ref, vec_ref, cos_ref, sin_ref, start_ref,
+        part_ref, wg_ref, og_ref, gain_ref, xs, gs, dk, dv, low, sems,
+    ):
+        load_g = pltpu.make_async_copy(g_ref, gs, sems.at[0])
+        load_x = pltpu.make_async_copy(x_ref, xs, sems.at[1])
+        load_g.start()
+        load_x.start()
+        dk[...] = jnp.zeros_like(dk)
+        dv[...] = jnp.zeros_like(dv)
+        load_g.wait()
+        for i in range(length // block):
+            r, keys = pl.ds(i * block, block), pl.ds(0, (i + 1) * block)
+            grad_attended = dot_t(gs[r], o_ref[...])
+            total = t_ref[r]
+            grad_sums = (grad_attended / total).astype(BF16)
+            offset = jnp.sum(grad_attended * a_ref[r].astype(F32), axis=1, keepdims=True) / total
+            e, bent = scores(q_ref[r], k_ref[keys], start_ref[r], i * block)
+            grad_e = dot_t(grad_sums, v_ref[keys]) - offset
+            grad_s = (e * grad_e * (1.0 - bent * bent)).astype(BF16)
+            dv[keys] += t_dot(e.astype(BF16), grad_sums)
+            dk[keys] += t_dot(grad_s, q_ref[r])
+            low[r, :HEAD] = rotated(dot(grad_s, k_ref[keys]) * SCALE, cos_ref[r], -sin_ref[r]).astype(BF16)
+        for i in range(length // block):
+            r = pl.ds(i * block, block)
+            low[r, HEAD : 2 * HEAD] = rotated(dk[r] * SCALE, cos_ref[r], -sin_ref[r]).astype(BF16)
+            low[r, 2 * HEAD :] = dv[r].astype(BF16)
+        load_x.wait()
+        gain_ref[...] = jnp.zeros_like(gain_ref)
+
+        def parts(i, carry):
+            r = pl.ds(pl.multiple_of(i * block, block), block)
+            term = dot_t(low[r], w_ref[...])
+            part_ref[r] = term.astype(BF16)
+            gain_ref[...] += jnp.sum(term * xs[r].astype(F32), axis=0, keepdims=True)
+            return carry
+
+        lax.fori_loop(0, length // block, parts, 0)
+        gain_ref[...] = gain_ref[...] / vec_ref[0:1]
+
+        def grads(j, carry):
+            cols = pl.ds(pl.multiple_of(j * tile, tile), tile)
+            wg_ref[cols] = t_dot(xs[:, cols], low[...]).astype(BF16)
+            og_ref[:, cols] = t_dot(a_ref[...], gs[:, cols]).astype(BF16)
+            return carry
+
+        lax.fori_loop(0, D // tile, grads, 0)
+
+    return pl.pallas_call(
+        kernel,
+        out_shape=(
+            jax.ShapeDtypeStruct((length, D), BF16),
+            jax.ShapeDtypeStruct((D, 3 * HEAD), BF16),
+            jax.ShapeDtypeStruct((HEAD, D), BF16),
+            jax.ShapeDtypeStruct((1, D), F32),
+        ),
+        in_specs=[ANY, ANY] + [INVMEM] * 11,
+        out_specs=(INVMEM,) * 4,
+        scratch_shapes=[
+            pltpu.VMEM(seen.shape, BF16),
+            pltpu.VMEM(seen.shape, BF16),
+            pltpu.VMEM((length, HEAD), F32),
+            pltpu.VMEM((length, HEAD), F32),
+            pltpu.VMEM((length, 3 * HEAD), BF16),
+            dma(2),
+        ],
+        compiler_params=pltpu.CompilerParams(vmem_limit_bytes=60 * 2**20),
+        name="attention_backward",
+    )(seen, grad, w, o, q, k, v, attended, totals, vectors, cosine, sine, start)
+
+
 def inverse_rms(v):
     return lax.rsqrt(jnp.mean(v * v, axis=-1, keepdims=True) + 1e-06)
 
@@ -1438,7 +1612,8 @@
 
 
 def forward_kernel(
-    grid, p, tokens, gate_codes, up_codes, down_codes, pair_scale, down_scale, post_gain, feed_gain, cid
+    grid, seen, qkv_codes, out_codes, qkv_scale, cosine, sine, begins, tokens, cotangent, gate_codes, up_codes, down_codes,
+    pair_scale, vectors, cid,
 ):
     n, levels = grid.n, grid.planes
     group, rows, _ = tokens.shape
@@ -1447,11 +1622,17 @@
     size = feed_blocks(grid)
     sc = scatter_scratch(grid, levels // 2, rows, D)
     ss = share_sems(grid, 2)
-    ws, gs = FeedWeights.scratch(group, units, window), gather_sems(grid, levels)
+    ws, gs = FeedWeights.scratch(group, units, window), level_sems(grid, levels)
+
+    length = seen.shape[0]
+    block = 256
+    here = block // rows
 
     def kernel(
-        p_ref, tokens_ref, gate_ref, up_ref, down_ref, ps_ref, ds_ref, pg_ref, fg_ref,
-        raw_ref, mixed_ref, all_ref, pair_ref, part_ref, wp_ref, wd_ref, *scratch,
+        x_ref, codes_ref, rows_ref, scale_ref, cos_ref, sin_ref, start_ref, tokens_ref, cot_ref, gate_ref, up_ref, down_ref,
+        ps_ref, vec_ref,
+        w_ref, o_ref, q_ref, k_ref, v_ref, a_ref, t_ref,
+        kept_cot_ref, raw_ref, mixed_ref, all_ref, pair_ref, part_ref, wp_ref, wd_ref, *scratch,
     ):
         refs = Split(scratch)
         half_at, at = Place(grid, levels // 2), Place(grid, levels)
@@ -1459,14 +1640,19 @@
         share_refs = refs.take(len(ss))
         weights = FeedWeights(at, group, units, None, None, down_ref, (wp_ref, wd_ref), refs.take(len(ws)))
         gather_refs = refs.take(len(gs))
-        (x,) = refs.take(1)
+        x, xs, head_sems, cot_sems = refs.take(4)
         loads, stores, compute = forward_chunks(weights, all_ref, pair_ref, part_ref, *refs.take(4))
-        load = pltpu.make_async_copy(p_ref, mine[0], mine[4].at[0])
-        load.start()
+        w = weights.pair.at[0, :, pl.ds(0, 3 * HEAD)]
+        w_codes = weights.pair.at[1, :, pl.ds(0, 3 * HEAD)]
+        o = weights.down.at[0, pl.ds(0, HEAD)]
+        acc = mine[0]
+        load_w = pltpu.make_async_copy(codes_ref, w_codes, head_sems.at[0])
+        load_x = pltpu.make_async_copy(x_ref, xs, head_sems.at[1])
+        load_w.start()
+        load_x.start()
         weights.sources = (None, None, down_ref)
         weights.load()
         at.greet_all()
-        load.wait()
 
         def source(ref):
             return lambda to: ref.at[:, pl.ds(pl.multiple_of(start(to), 128), window)]
@@ -1477,35 +1663,80 @@
             ]
 
         issue, finish = share_task(at, [source(gate_ref), source(up_ref)], [view(0), view(1)], *share_refs)
+        for _ in range(EARLY):
+            next(issue, None)
+        scale_rows(at.b, at.member, rows_ref, vec_ref[4:5], o, HEAD)
+        load_w.wait()
+        scale_rows(at.b, at.member, w_codes, scale_ref[...], w, D)
+        keep_w = pltpu.make_async_copy(w, w_ref, head_sems.at[2])
+        keep_o = pltpu.make_async_copy(o, o_ref, head_sems.at[3])
+        keep_w.start()
+        keep_o.start()
+        load_x.wait()
+
+        def put(i, value):
+            first = i * here
+            half = grid.n // 2
+            acc[first // half, pl.ds(first % half, here)] = value.reshape(here, rows, D)
+
+        attention_body(
+            w,
+            o,
+            lambda i: xs[pl.ds(i * block, block)],
+            put,
+            cos_ref,
+            sin_ref,
+            start_ref,
+            q_ref,
+            k_ref,
+            v_ref,
+            a_ref,
+            t_ref,
+        )
         for _ in scatter_steps(half_at, raw_ref, *mine):
             next(issue, None)
 
         def norms(u, r):
             raw = raw_ref[u, r].astype(F32)
-            mixed = tokens_ref[u, r].astype(F32) + raw * inverse_rms(raw) * pg_ref[...]
+            mixed = tokens_ref[u, r].astype(F32) + raw * inverse_rms(raw) * vec_ref[1:2]
             mixed_ref[u, r] = mixed
-            x[u, r] = (mixed * inverse_rms(mixed) * fg_ref[...]).astype(BF16)
+            x[u, r] = (mixed * inverse_rms(mixed) * vec_ref[2:3]).astype(BF16)
 
         each_rows(group, rows, norms)
-        moving = LevelGather(at, x, all_ref, *gather_refs)
+        moving = LevelGather(False, at, x, all_ref, *gather_refs)
         moving.begin()
         run(issue)
+        give_cot, take_cot = swap_task(at, cot_ref.at[1 - at.member], kept_cot_ref, cot_sems)
+        run(give_cot)
+        kept_cot_ref[at.member] = cot_ref[at.member]
 
         def first():
             finish()
-            weights.make(ps_ref, ds_ref)
+            keep_w.wait()
+            keep_o.wait()
+            weights.make(ps_ref, vec_ref.at[5:6])
 
         moving.run(lambda zj, fresh: each_chunk(grid, zj, fresh, loads, stores, compute), first)
         for copy in stores(0):
             copy.wait()
         weights.finish()
+        take_cot()
 
     def blocks(width):
         return jax.ShapeDtypeStruct((group, n, rows, width), BF16)
 
+    head = jax.ShapeDtypeStruct((length, HEAD), BF16)
     return pl.pallas_call(
         kernel,
         out_shape=(
+            jax.ShapeDtypeStruct((D, 3 * HEAD), BF16),
+            jax.ShapeDtypeStruct((HEAD, D), BF16),
+            head,
+            head,
+            head,
+            head,
+            jax.ShapeDtypeStruct((length, 1), F32),
+            jax.ShapeDtypeStruct(tokens.shape, BF16),
             jax.ShapeDtypeStruct(tokens.shape, BF16),
             jax.ShapeDtypeStruct(tokens.shape, F32),
             blocks(D),
@@ -1514,29 +1745,32 @@
             jax.ShapeDtypeStruct((group, D, 2 * window), BF16),
             jax.ShapeDtypeStruct((group, window, D), BF16),
         ),
-        in_specs=[ANY, INVMEM, ANY, ANY, ANY, INVMEM, INVMEM, INVMEM, INVMEM],
-        out_specs=(INVMEM, INVMEM) + (ANY,) * 5,
+        in_specs=[ANY, ANY] + [INVMEM] * 7 + [ANY] * 3 + [INVMEM] * 2,
+        out_specs=(ANY, ANY) + (INVMEM,) * 8 + (ANY,) * 5,
         scratch_shapes=sc
         + ss
         + ws
         + gs
-        + [pltpu.VMEM(tokens.shape, BF16)]
+        + [pltpu.VMEM(tokens.shape, BF16), pltpu.VMEM(seen.shape, BF16), dma(4), dma(2)]
         + chunk_buffers(size, rows, D, 2 * window, D)
         + [dma(3)],
         compiler_params=params(cid, 62),
         name="forward",
-    )(p, tokens, gate_codes, up_codes, down_codes, pair_scale, down_scale, post_gain, feed_gain)
-
-
-def turn_kernel(grid, p, mixed, cotangent, pair, pair_matrices, down_matrices, post_gain, cid):
+    )(
+        seen, qkv_codes, out_codes, qkv_scale, cosine, sine, begins, tokens, cotangent, gate_codes, up_codes, down_codes,
+        pair_scale, vectors,
+    )
+
+
+def turn_kernel(grid, p, mixed, cotangent, pair, pair_matrices, down_matrices, vectors, cid):
     n, levels = grid.n, grid.planes
     group, rows, _ = mixed.shape
     units, window, _ = feed_windows(grid)
     size = feed_blocks(grid)
-    sc, gs = scatter_scratch(grid, levels, rows, D), gather_sems(grid, levels)
+    sc, gs = scatter_scratch(grid, levels, rows, D), level_sems(grid, levels)
 
     def kernel(
-        p_ref, mixed_ref, cot_ref, pair_ref, wp_ref, wd_ref, pg_ref,
+        p_ref, mixed_ref, cot_ref, pair_ref, wp_ref, wd_ref, vec_ref,
         out_ref, gain_ref, all_ref, part_ref, dgu_ref, hid_ref, *scratch,
     ):
         refs = Split(scratch)
@@ -1561,13 +1795,13 @@
 
         def norms(u, r):
             v, dy = raw[u, r].astype(F32), cot_ref[u, r].astype(F32)
-            inverse, gain = inverse_rms(v), pg_ref[...]
+            inverse, gain = inverse_rms(v), vec_ref[3:4]
             kept_out[u, r] = (mixed_ref[u, r] + v * inverse * gain).astype(BF16)
             x[u, r] = norm_back(v, inverse, dy * gain).astype(BF16)
             gain_ref[...] += jnp.sum(dy * v * inverse, axis=0, keepdims=True)
 
         each_rows(group, rows, norms)
-        moving = LevelGather(at, x, all_ref, *gather_refs)
+        moving = LevelGather(True, at, x, all_ref, *gather_refs)
         moving.begin()
         give_out, take_out = swap_task(at, kept_out.at[1 - at.member], out_ref, swap_sems)
         run(give_out)
@@ -1610,10 +1844,10 @@
         + [dma(5)],
         compiler_params=params(cid, 62),
         name="turn",
-    )(p, mixed, cotangent, pair, pair_matrices, down_matrices, post_gain)
-
-
-def back_kernel(grid, p, fed, down_low, pair_low, hidden, mixed, raw, cotangent, feed_gain, post_gain, cid):
+    )(p, mixed, cotangent, pair, pair_matrices, down_matrices, vectors)
+
+
+def back_kernel(grid, p, fed, down_low, pair_low, hidden, mixed, raw, cotangent, vectors, cid):
     n, levels = grid.n, grid.planes
     group, rows, _ = mixed.shape
     units, window, _ = feed_windows(grid)
@@ -1627,7 +1861,7 @@
     rs = return_scratch(grid, (rows_d, 2 * window))
 
     def kernel(
-        p_ref, fed_ref, low_ref, dgu_ref, hid_ref, mixed_ref, raw_ref, cot_ref, fg_ref, pg_ref,
+        p_ref, fed_ref, low_ref, dgu_ref, hid_ref, mixed_ref, raw_ref, cot_ref, vec_ref,
         grad_ref, feed_ref, post_ref, all_ref, got_ref, down_ref, *scratch,
     ):
         refs = Split(scratch)
@@ -1712,12 +1946,12 @@
             def norms(u, r):
                 dy, v = raw2[u, r].astype(F32), mixed_ref[u, r]
                 inverse = inverse_rms(v)
-                grad = cot_ref[u, r].astype(F32) + norm_back(v, inverse, dy * fg_ref[...])
+                grad = cot_ref[u, r].astype(F32) + norm_back(v, inverse, dy * vec_ref[2:3])
                 feed_ref[...] += jnp.sum(dy * v * inverse, axis=0, keepdims=True)
                 grad_ref[u, r] = grad
                 w = raw_ref[u, r].astype(F32)
                 inverse = inverse_rms(w)
-                x[u, r] = norm_back(w, inverse, grad * pg_ref[...]).astype(BF16)
+                x[u, r] = norm_back(w, inverse, grad * vec_ref[1:2]).astype(BF16)
                 post_ref[...] += jnp.sum(grad * w * inverse, axis=0, keepdims=True)
 
             each_rows(group, rows, norms)
@@ -1736,7 +1970,7 @@
             jax.ShapeDtypeStruct((n, rows_d, 2 * window), BF16),
             jax.ShapeDtypeStruct((window, D), BF16),
         ),
-        in_specs=[ANY] * 5 + [INVMEM] * 5,
+        in_specs=[ANY] * 5 + [INVMEM] * 4,
         out_specs=(INVMEM,) * 3 + (ANY,) * 3,
         scratch_shapes=sc
         + gs
@@ -1756,7 +1990,7 @@
         ],
         compiler_params=params(cid, 63),
         name="back",
-    )(p, fed, down_low, pair_low, hidden, mixed, raw, cotangent, feed_gain, post_gain)
+    )(p, fed, down_low, pair_low, hidden, mixed, raw, cotangent, vectors)
 
 
 def assemble_task(grid, got_ref, targets, wide, high, load_sem, stores):
@@ -1806,9 +2040,9 @@
     return [pltpu.VMEM((grid.n, rows_d, 2 * window), BF16), pltpu.VMEM((2, rows_d, FF), BF16), dma(1), dma(2)]
 
 
-def gains_task(at, x_ref, out_ref, total, other, sems, *share_refs):
+def gains_task(at, x_ref, out_ref, total, other, every, sems, *share_refs):
     copy = at.sibling(x_ref, other, sems.at[0], sems.at[1])
-    later, finish = share_task(at, [lambda to: total], [lambda j: out_ref.at[j]], *share_refs)
+    later, end = share_task(at, [lambda to: total], [lambda j: every.at[j]], *share_refs)
 
     def issue():
         copy.start()
@@ -1816,6 +2050,10 @@
         copy.wait()
         total[...] = x_ref[...] + other[...]
         yield from later
+
+    def finish():
+        end()
+        out_ref[...] = jnp.sum(every[...], axis=0)
 
     return issue(), finish
 
@@ -1916,16 +2154,19 @@
     rows_d = D // n
     units, window, _ = feed_windows(grid)
 
+    vectors = jnp.stack(
+        [attention_gain, attention_post_gain, feed_gain, feed_post_gain, output_scale, down_scale]
+    )
+
     q_parts = jnp.transpose(query_codes.reshape(rows_d, HEADS, HEAD), (1, 0, 2))
     k_parts = jnp.repeat(jnp.transpose(key_codes.reshape(rows_d, KV_HEADS, HEAD), (1, 0, 2)), pairs, axis=0)
     v_parts = jnp.repeat(jnp.transpose(value_codes.reshape(rows_d, KV_HEADS, HEAD), (1, 0, 2)), pairs, axis=0)
     qkv_parts = jnp.concatenate([q_parts, k_parts, v_parts], axis=-1).astype(BF16)
     small = jnp.zeros((8, 128), jnp.int32).at[:group, :block].set(positions)
-    tokens, cotangent, seen, qkv_codes, out_codes, all_places, gate_low, up_low = open_kernel(
+    tokens, seen, qkv_codes, out_codes, all_places, gate_low, up_low = open_kernel(
         grid,
         tokens,
-        cotangent,
-        attention_gain[None],
+        vectors,
         qkv_parts,
         output_codes.astype(BF16),
         small,
@@ -1942,34 +2183,6 @@
             lax.dynamic_slice_in_dim(value_scale, kv_head * HEAD, HEAD),
         ]
     )
-    qkv_matrix = dequantized(qkv_codes.reshape(D, 3 * HEAD), qkv_scale, step)
-    out_matrix = dequantized(out_codes.reshape(HEAD, D), output_scale, step)
-
-    places_all = lax.dynamic_index_in_dim(all_places[:, :group, :block], member, 1, False).reshape(length)
-    turn = angles(places_all, HEAD)
-    cosine, sine = jnp.cos(turn), jnp.sin(turn)
-    if parts == 1:
-        seen_asked, places_asked, cosine_q, sine_q = seen, places_all, cosine, sine
-        projected = dot(seen, qkv_matrix)
-        q_lin, kv_lin = projected[:, :HEAD], projected[:, HEAD:]
-    else:
-        seen_asked, places_asked, cosine_q, sine_q = [
-            lax.dynamic_slice_in_dim(a, first_asked, asked) for a in (seen, places_all, cosine, sine)
-        ]
-        q_lin, kv_lin = dot(seen_asked, qkv_matrix[:, :HEAD]), dot(seen, qkv_matrix[:, HEAD:])
-    queries = rotate(q_lin, cosine_q, sine_q).astype(BF16)
-    keys = rotate(kv_lin[:, :HEAD], cosine, sine).astype(BF16)
-    values = kv_lin[:, HEAD:].astype(BF16)
-    q_index = first_asked + jnp.arange(asked, dtype=jnp.int32)
-    key_index = jnp.arange(length, dtype=jnp.int32)
-    allowed = (key_index[None, :] <= q_index[:, None]) & (key_index[None, :] >= (q_index - places_asked)[:, None])
-    bent = jnp.tanh(dot_t(queries, keys) * scale / cap_limit)
-    kernel = jnp.where(allowed, jnp.exp(cap_limit * bent), 0.0)
-    totals = jnp.sum(kernel, axis=-1, keepdims=True)
-    kernel_low = kernel.astype(BF16)
-    attended = dot(kernel_low, values) / totals
-    attended_low = attended.astype(BF16)
-
     def swapped_back(kept):
         own, other = (lax.dynamic_index_in_dim(kept, u, 0, False) for u in (member, 1 - member))
         other = lax.ppermute(other, "seq", [(c, (c + half) % n) for c in range(n)])
@@ -1980,28 +2193,66 @@
             part = lax.dynamic_update_slice_in_dim(jnp.zeros((length, D), BF16), part, first_asked, 0)
         return part.reshape(2, half, block, D)
 
-    out_part = spread(dot(attended_low, out_matrix).astype(BF16))
-    first_column = chip * units // 128 * 128
-    inset = chip * units - first_column
+    places_all = lax.dynamic_index_in_dim(all_places[:, :group, :block], member, 1, False).reshape(length)
+    turn = angles(places_all, HEAD)
+    cosine, sine = jnp.cos(turn), jnp.sin(turn)
+    q_index = first_asked + jnp.arange(asked, dtype=jnp.int32)
+    whole = fits(grid, block) and parts == 1
     pair_scale = jnp.concatenate(
-        [lax.dynamic_slice_in_dim(s, first_column, window) for s in (gate_scale, up_scale)]
+        [lax.dynamic_slice_in_dim(s, chip * units // 128 * 128, window) for s in (gate_scale, up_scale)]
     )[None]
-    if fits(grid, block):
-        attention_raw, mixed, fed, gate_up, down_part, pair_matrices, down_matrices = forward_kernel(
+    if whole:
+        start = (q_index - places_all)[:, None]
+        (
+            *kept_heads, cotangent, attention_raw, mixed, fed, gate_up, down_part, pair_matrices, down_matrices,
+        ) = forward_kernel(
             grid,
-            out_part,
+            seen,
+            qkv_codes.reshape(D, 3 * HEAD),
+            out_codes.reshape(HEAD, D),
+            qkv_scale[None],
+            cosine,
+            sine,
+            start,
             tokens,
+            cotangent,
             gate_low,
             up_low,
             down_codes,
             pair_scale,
-            down_scale[None],
-            attention_post_gain[None],
-            feed_gain[None],
+            vectors,
             2,
         )
+    else:
+        qkv_matrix = dequantized(qkv_codes.reshape(D, 3 * HEAD), qkv_scale, step)
+        out_matrix = dequantized(out_codes.reshape(HEAD, D), output_scale, step)
+        if parts == 1:
+            seen_asked, places_asked, cosine_q, sine_q = seen, places_all, cosine, sine
+            projected = dot(seen, qkv_matrix)
+            q_lin, kv_lin = projected[:, :HEAD], projected[:, HEAD:]
+        else:
+            seen_asked, places_asked, cosine_q, sine_q = [
+                lax.dynamic_slice_in_dim(a, first_asked, asked) for a in (seen, places_all, cosine, sine)
+            ]
+            q_lin, kv_lin = dot(seen_asked, qkv_matrix[:, :HEAD]), dot(seen, qkv_matrix[:, HEAD:])
+        queries = rotate(q_lin, cosine_q, sine_q).astype(BF16)
+        keys = rotate(kv_lin[:, :HEAD], cosine, sine).astype(BF16)
+        values = kv_lin[:, HEAD:].astype(BF16)
+        key_index = jnp.arange(length, dtype=jnp.int32)
+        allowed = (key_index[None, :] <= q_index[:, None]) & (key_index[None, :] >= (q_index - places_asked)[:, None])
+        bent = jnp.tanh(dot_t(queries, keys) * scale / cap_limit)
+        kernel = jnp.where(allowed, jnp.exp(cap_limit * bent), 0.0)
+        totals = jnp.sum(kernel, axis=-1, keepdims=True)
+        kernel_low = kernel.astype(BF16)
+        attended = dot(kernel_low, values) / totals
+        attended_low = attended.astype(BF16)
+
+        out_part = spread(dot(attended_low, out_matrix).astype(BF16))
+    first_column = chip * units // 128 * 128
+    inset = chip * units - first_column
+    if whole:
         output, grad_post_feed, down_low, second_part, pair_low, hidden = turn_kernel(
-            grid, down_part, mixed, cotangent, gate_up, pair_matrices, down_matrices, feed_post_gain[None], 3
+            grid, down_part, mixed, cotangent, gate_up, pair_matrices, down_matrices, vectors, 3
         )
         grad_mixed, grad_pre_feed, grad_post_attention, attention_low, pair_got, down_grad = back_kernel(
             grid,
@@ -2013,11 +2264,11 @@
             mixed,
             attention_raw,
             cotangent,
-            feed_gain[None],
-            attention_post_gain[None],
+            vectors,
             4,
         )
     else:
+        cotangent = swapped_back(cotangent)
         attention_raw, gate_got, up_got = attention_sums(grid, out_part, gate_low, up_low, 2)
         attention_raw = attention_raw.astype(F32)
         feed_weights = (
@@ -2052,43 +2303,49 @@
     down_grad = lax.dynamic_slice(down_grad, (inset, 0), (units, D))
 
     attention_low = attention_low.reshape(length, D)
-    if parts > 1:
-        attention_low = lax.dynamic_slice_in_dim(attention_low, first_asked, asked)
-    grad_attended = dot_t(attention_low, out_matrix)
-    grad_sums = (grad_attended / totals).astype(BF16)
-    offsets = jnp.sum(grad_attended * attended, axis=-1, keepdims=True) / totals
-    grad_kernel = dot_t(grad_sums, values) - offsets
-    grad_raw = (kernel * grad_kernel * (1.0 - bent * bent)).astype(BF16)
-    grad_q = dot(grad_raw, keys) * scale
-    grad_k = t_dot(grad_raw, queries) * scale
-    grad_v = t_dot(kernel_low, grad_sums)
-    q_low = rotate(grad_q, cosine_q, -sine_q).astype(BF16)
-    kv_low = jnp.concatenate([rotate(grad_k, cosine, -sine), grad_v], axis=-1).astype(BF16)
-    if parts == 1:
-        qkv_low = jnp.concatenate([q_low, kv_low], axis=-1)
-        first_part = dot_t(qkv_low, qkv_matrix)
-        qkv_grad = t_dot(seen, qkv_low)
+    if whole:
+        first_part, qkv_grad, out_part, grad_pre_attention = attention_backward(
+            seen, attention_low, *kept_heads, vectors, cosine, sine, start
+        )
     else:
-        first_part = dot_t(kv_low, qkv_matrix[:, HEAD:])
-        q_back = dot_t(q_low, qkv_matrix[:, :HEAD])
-        first_part = lax.dynamic_update_slice_in_dim(
-            first_part, lax.dynamic_slice_in_dim(first_part, first_asked, asked) + q_back, first_asked, 0
-        )
-        qkv_grad = jnp.concatenate([t_dot(seen_asked, q_low), t_dot(seen, kv_low)], axis=-1)
-    first_part = first_part.astype(BF16)
-    grad_pre_attention = jnp.sum(first_part.astype(F32) * seen.astype(F32), axis=0) / attention_gain
+        if parts > 1:
+            attention_low = lax.dynamic_slice_in_dim(attention_low, first_asked, asked)
+        grad_attended = dot_t(attention_low, out_matrix)
+        grad_sums = (grad_attended / totals).astype(BF16)
+        offsets = jnp.sum(grad_attended * attended, axis=-1, keepdims=True) / totals
+        grad_kernel = dot_t(grad_sums, values) - offsets
+        grad_raw = (kernel * grad_kernel * (1.0 - bent * bent)).astype(BF16)
+        grad_q = dot(grad_raw, keys) * scale
+        grad_k = t_dot(grad_raw, queries) * scale
+        grad_v = t_dot(kernel_low, grad_sums)
+        q_low = rotate(grad_q, cosine_q, -sine_q).astype(BF16)
+        kv_low = jnp.concatenate([rotate(grad_k, cosine, -sine), grad_v], axis=-1).astype(BF16)
+        if parts == 1:
+            qkv_low = jnp.concatenate([q_low, kv_low], axis=-1)
+            first_part = dot_t(qkv_low, qkv_matrix)
+            qkv_grad = t_dot(seen, qkv_low)
+        else:
+            first_part = dot_t(kv_low, qkv_matrix[:, HEAD:])
+            q_back = dot_t(q_low, qkv_matrix[:, :HEAD])
+            first_part = lax.dynamic_update_slice_in_dim(
+                first_part, lax.dynamic_slice_in_dim(first_part, first_asked, asked) + q_back, first_asked, 0
+            )
+            qkv_grad = jnp.concatenate([t_dot(seen_asked, q_low), t_dot(seen, kv_low)], axis=-1)
+        first_part = first_part.astype(BF16)
+        grad_pre_attention = jnp.sum(first_part.astype(F32) * seen.astype(F32), axis=0) / attention_gain
+        out_part = t_dot(attended_low, attention_low).astype(BF16)
     gains = jnp.stack(
         [g.reshape(D) for g in (grad_pre_attention, grad_post_attention, grad_pre_feed, grad_post_feed)]
     )
-    out_part = t_dot(attended_low, attention_low).astype(BF16).reshape(copies, HEAD // copies, D)
-    merged = (pair_got, grad_mixed, tokens, attention_gain[None]) if fits(grid, block) else ()
+    out_part = out_part.reshape(copies, HEAD // copies, D)
+    merged = (pair_got, grad_mixed, tokens, vectors) if whole else ()
     grad_in, qkv_got, out_got, down_grad, gains, *assembled = attention_back_sums(
         grid,
         first_part.reshape(2, half, block, D),
         qkv_grad.astype(BF16).reshape(n, rows_d, 3 * HEAD),
         out_part,
         down_grad,
-        gains.reshape(8, D // 2),
+        gains,
         merged,
         7,
     )
@@ -2105,7 +2362,6 @@
     key_grad = jnp.transpose(kv_grad[..., :HEAD], (1, 0, 2)).reshape(rows_d, KV_HEADS * HEAD)
     value_grad = jnp.transpose(kv_grad[..., HEAD:], (1, 0, 2)).reshape(rows_d, KV_HEADS * HEAD)
     out_grad = jnp.sum(out_got.astype(F32), axis=0)
-    gains = jnp.sum(gains, axis=0).reshape(4, D)
     return (
         output,
         grad_in,

time: 885 us -> 854 us (0.965)
  matrix products: 40.9 us -> 0 us
  Pallas kernels: 771 us -> 802 us
  other arithmetic: 32.6 us -> 21.1 us
    dot_general x12 -> x0, matrix products: 40.9 us -> none  [the longest x4 17 us: dot_t(): lax.dot_general(left, right, (((1,), (1,)), ((), ())), preferred_element_...]
    pallas_call x1 -> x2, Pallas kernels: 195 us -> 226 us  [the longest x1 201 us: forward_kernel(): pl.pallas_call(kernel, out_shape=(jax.ShapeDtypeStruct((D, 3 * HEAD), BF1...]
    unnamed x5 -> x0, other arithmetic: 9.05 us -> none
where the time goes in v5:
time: 854 us; the launch traced here: 845 us
  Pallas kernels  802 us (94%)
  other arithmetic  21.1 us (2%)
  local copies, waits for them, and re-layouts  20.8 us (2%)
    pallas_call x1, Pallas kernels, forward_kernel(): pl.pallas_call(kernel, out_shape=(jax.ShapeDtypeStruct((D, 3 * HEAD), BF1...  201 us
    pallas_call x1, Pallas kernels, turn_kernel(): pl.pallas_call(kernel, out_shape=(jax.ShapeDtypeStruct(mixed.shape, BF16)...  191 us
    pallas_call x1, Pallas kernels, back_kernel(): pl.pallas_call(kernel, out_shape=(jax.ShapeDtypeStruct(mixed.shape, F32),...  180 us
    pallas_call x1, Pallas kernels, call(): pl.pallas_call(kernel, out_shape=(jax.ShapeDtypeStruct((2, rows, width),...  102 us
    pallas_call x1, Pallas kernels, open_kernel(): pl.pallas_call(kernel, out_shape=(jax.ShapeDtypeStruct(x.shape, BF16), ja...  102 us
    pallas_call x1, Pallas kernels, attention_backward(): pl.pallas_call(kernel, out_shape=(jax.ShapeDtypeStruct((length, D), BF16)...  25.2 us

profile of v5, /device:TPU:0, one launch (start us, length us, event | category | flops | bytes accessed | tf_op | source)
XLA Modules:
  0.0 845.1 jit_solution(937110608544885343)
XLA Ops:
  0.7 0.8 dynamic_slice.22
  1.6 0.8 dynamic_slice.23
  2.3 0.8 dynamic_slice.24
  3.1 0.6 broadcast_in_dim.18.scale_ref
  3.7 0.7 scatter.4.small_ref
  4.4 0.8 dynamic_slice.26
  5.1 0.8 dynamic_slice.27
  5.9 0.6 broadcast_in_dim.19.ps_ref
  6.5 0.7 stack.28
  7.2 0.7 stack.29
  8.0 0.7 stack.24
  8.7 0.7 stack.25
  9.4 0.7 stack.26
  10.1 0.7 stack.27
  10.8 0.1 stack.30.gain_ref.vec_ref.refs_8_
  10.9 1.2 convert.21
  12.1 0.2 reshape.164
  12.5 0.2 reshape.165
  12.8 0.1 convert.16
  13.0 1.3 pad_maximum_fusion.w_ref
  14.4 0.5 copy-done.3
  14.9 102.1 %open.1 = (bf16[2,64,2304]{2,1,0:T(8,128)(2,1)S(1)}, bf16[2,8,64,2304]{3,2,1,0:T(8,128)(2,1)}, bf16[2304,768]{1,0:T(8,128)(2,1)}, bf16[2,128,2304]{2,1,0:T(8,128...) custom-call(bf16[2,64,2304]{2,1,0:T(8,128)(2,1)S(1)} %copy-done.3, ...), custom_call_target="tpu_custom_call" | custom-call | tf_op jit(solution)/shard_map/open/pallas_call | solution.py:1295
  117.0 0.8 copy-done.1
  117.8 1.0 copy-done.2
  119.0 0.5 reshape.166
  119.5 0.9 add_subtract_fusion.start_ref
  120.3 3.0 multiply_sine_fusion
  123.3 200.8 %forward.1 = (bf16[2304,768]{1,0:T(8,128)(2,1)}, bf16[256,2304]{1,0:T(8,128)(2,1)}, bf16[1024,256]{1,0:T(8,128)(2,1)}, bf16[1024,256]{1,0:T(8,128)(2,1)}, bf16[1...) custom-call(bf16[1024,2304]{1,0:T(8,128)(2,1)} %bitcast.34, ...), custom_call_target="tpu_custom_call" | custom-call | tf_op jit(solution)/shard_map/forward/pallas_call | solution.py:1729
  324.1 190.9 %turn.1 = (bf16[2,64,2304]{2,1,0:T(8,128)(2,1)}, f32[1,2304]{1,0:T(1,128)}, bf16[2,16,64,2304]{3,2,1,0:T(8,128)(2,1)}, bf16[2,16,64,2304]{3,2,1,0:T(8,128)(2,1)}...) custom-call(bf16[2,16,64,2304]{3,2,1,0:T(8,128)(2,1)} %get-tuple-element.77.p_ref, ...), custom_call_target="tpu_custom_call" | custom-call | tf_op jit(solution)/shard_map/turn/pallas_call | solution.py:1820
  515.0 180.3 %back.1 = (f32[2,64,2304]{2,1,0:T(8,128)}, f32[1,2304]{1,0:T(1,128)}, f32[1,2304]{1,0:T(1,128)}, bf16[2,8,64,2304]{3,2,1,0:T(8,128)(2,1)}, bf16[16,144,1280]{2,1,0:T(8,128)(2,1)}, /*index=5*/bf16[640,2304]{1,0:T(8,128)(2,1)}) custom-call(bf16[2,16,64,2304]{3,2,1,0:T(8,128)(2,1)} %get-tuple-element.84.p_ref, ...), custom_call_target="tpu_custom_call" | custom-call | tf_op jit(solution)/shard_map/back/pallas_call | solution.py:1963
  695.4 25.2 %attention_backward.1 = (bf16[1024,2304]{1,0:T(8,128)(2,1)}, bf16[2304,768]{1,0:T(8,128)(2,1)}, bf16[256,2304]{1,0:T(8,128)(2,1)}, f32[1,2304]{1,0:T(1,128)}) custom-call(bf16[1024,2304]{1,0:T(8,128)(2,1)} %bitcast.35, bf16[1024,2304]{1,0:T(8,128)(2,1)} %bitcast.37, bf16[2304,768]{1,0:T(8,128)(2,1)} %get-tuple-element.91.w_ref, ...), custom_call_target="tpu_custom_call" | custom-call | tf_op jit(solution)/shard_map/attention_backward/pallas_call | solution.py:1571
  720.6 1.4 pad_maximum_fusion.1.refs_4_
  722.0 1.7 constant_dynamic-slice_fusion.refs_3_
  723.7 102.4 %attention_back_sums.1 = (bf16[2,64,2304]{2,1,0:T(8,128)(2,1)}, bf16[16,144,768]{2,1,0:T(8,128)(2,1)}, bf16[2,128,2304]{2,1,0:T(8,128)(2,1)}, bf16[576,2304]{1,0...) custom-call(bf16[2,8,64,2304]{3,2,1,0:T(8,128)(2,1)} %bitcast.36, ...), custom_call_target="tpu_custom_call" | custom-call | tf_op jit(solution)/shard_map/attention_back_sums/pallas_call | solution.py:1349
  826.1 3.1 convert_reduce_fusion
  829.2 0.7 slice_reduce_fusion
  829.9 0.2 bitcast_reduce_fusion
  830.1 0.1 slice_bitcast_fusion
  830.2 1.1 copy.62
  831.3 0.1 slice_bitcast_fusion.1
  831.4 0.9 copy.64
  832.3 0.9 copy.63
  833.2 1.2 convert_reduce_fusion.1
  834.4 2.9 convert_element_type.31
  837.3 2.9 convert_element_type.32
  840.3 2.8 convert_element_type.33
  843.0 0.8 copy.69
  843.9 0.8 copy.70
  (47 shorter events, 0.5 us)
Async XLA Ops:
  0.6 11.8 %copy-start.11 = (s32[144,1024]{1,0:T(8,128)S(1)}, s32[144,1024]{1,0:T(8,128)}, u32[]{:S(2)}) copy-start(s32[144,1024]{1,0:T(8,128)} %param.29) | copy-start | bytes 1769476
  10.9 3.4 copy-start
  10.9 1.9 copy-start.8
  12.8 1.5 copy-start.9
  12.9 1.9 copy-start.3
  117.0 0.8 copy-start.1
  117.8 1.0 copy-start.2
  695.3 25.3 %copy-start.15 = (f32[1,2304]{1,0:T(1,128)S(1)}, f32[1,2304]{1,0:T(1,128)}, u32[]{:S(2)}) copy-start(f32[1,2304]{1,0:T(1,128)} %get-tuple-element.105) | copy-start | bytes 27652
  695.3 25.3 %copy-start.16 = (f32[1,2304]{1,0:T(1,128)S(1)}, f32[1,2304]{1,0:T(1,128)}, u32[]{:S(2)}) copy-start(f32[1,2304]{1,0:T(1,128)} %get-tuple-element.104) | copy-start | bytes 27652
  695.3 25.3 %copy-start.17 = (f32[1,2304]{1,0:T(1,128)S(1)}, f32[1,2304]{1,0:T(1,128)}, u32[]{:S(2)}) copy-start(f32[1,2304]{1,0:T(1,128)} %get-tuple-element.103) | copy-start | bytes 27652
  695.3 26.6 %copy-start.7 = (bf16[640,2304]{1,0:T(8,128)(2,1)S(1)}, bf16[640,2304]{1,0:T(8,128)(2,1)}, u32[]{:S(2)}) copy-start(bf16[640,2304]{1,0:T(8,128)(2,1)} %get-tuple-element.101) | copy-start | bytes 8847364
  826.1 3.1 copy-start.14
  831.3 1.9 copy-start.10
  831.4 3.0 copy-start.6
  834.4 2.9 copy-start.5
  837.3 2.9 copy-start.4
  840.3 2.8 copy-start.12
  840.3 3.6 copy-start.13

commit v6 on v5

--- a/solution.py
+++ b/solution.py
@@ -416,6 +416,7 @@
 
 
 EARLY = 4
+PER = 4
 
 
 class FeedWeights:
@@ -823,6 +824,236 @@
             finish(*group)
 
 
+def split_scratch(grid, levels, rows, width):
+    steps, pn = grid.plane // 2, grid.plane
+    cut = rows * 3 // 4 // 16 * 16
+    more = max(steps - 1, 1)
+    return [
+        pltpu.VMEM((2, levels * pn, rows, width), BF16),
+        pltpu.VMEM((2, levels, cut, width), BF16),
+        pltpu.VMEM((2, more, levels, 2, cut, width), BF16),
+        pltpu.VMEM((2, levels, 2, cut, width), BF16),
+        pltpu.VMEM((2, rows - cut, width), BF16),
+        pltpu.VMEM((2, more, 2, rows - cut, width), BF16),
+        pltpu.VMEM((2, levels, 2, pn, rows - cut, width), BF16),
+        dma(1),
+        dma(2, levels),
+        dma(2, levels),
+        dma(2, steps, levels),
+        dma(2, steps, levels),
+        dma(2, levels),
+        dma(2, levels),
+        dma(2, steps),
+        dma(2, steps),
+    ]
+
+
+def split_scatter_steps(
+    at, out_ref, acc, half_ref, full_ref, line_ref, low_half, low_full, low_line,
+    ls, zs, zr, rs, rr, lzs, lzr, lrs, lrr,
+):
+    levels, steps, zi, q, pn, b = at.levels, at.steps, at.zi, at.q, at.pn, at.b
+    rows = acc.shape[2]
+    cut = half_ref.shape[2]
+    upper, lower = pl.ds(0, cut), pl.ds(cut, rows - cut)
+
+    def add(target, others, pieces):
+        def one(i, carry):
+            total = target(i)[...].astype(F32)
+            for other in others:
+                total = total + other(i)[...].astype(F32)
+            target(i)[...] = total.astype(BF16)
+            return carry
+
+        lax.fori_loop(0, pieces, one, 0)
+
+    def spans(ref, first, count):
+        per = count // 16
+        return lambda i: ref.at[i // per, pl.ds(pl.multiple_of(first + (i % per) * 16, 16), 16)]
+
+    def along(way):
+        return at.c + (pn if way == 0 else -pn)
+
+    def r_copy(zj, way, step):
+        target = at.slot(zj, q + (1 if way == 0 else -1) * (steps + 1 - step))
+        if step == 1:
+            src, dst = acc.at[way, target, upper], half_ref.at[way, zj]
+        else:
+            src, dst = acc.at[:, target, upper], full_ref.at[way, step - 2, zj]
+        to = at.right if way == 0 else at.left
+        return remote(src, dst, rs.at[way, step - 1, zj], rr.at[way, step - 1, zj], to, b)
+
+    def z_copy(zj, way):
+        return remote(
+            acc.at[:, at.slot(zj, q), upper], line_ref.at[way, zj], zs.at[way, zj], zr.at[way, zj], along(way), b
+        )
+
+    def begin(sign, d):
+        for way in (0, 1):
+            r_copy(zi + sign * d, way, 1).start()
+
+    def middle(sign, d):
+        zj = zi + sign * d
+        for step in range(1, steps):
+            for way in (0, 1):
+                r_copy(zj, way, step).wait_recv()
+                s = at.slot(zj, q + (1 if way == 0 else -1) * (steps - step))
+                if step == 1:
+                    add(
+                        lambda i: acc.at[way, s, pl.ds(pl.multiple_of(i * 16, 16), 16)],
+                        [lambda i: half_ref.at[way, zj, pl.ds(pl.multiple_of(i * 16, 16), 16)]],
+                        cut // 16,
+                    )
+                else:
+                    add(spans(acc.at[:, s], 0, cut), [spans(full_ref.at[way, step - 2, zj], 0, cut)], 2 * cut // 16)
+                r_copy(zj, way, step + 1).start()
+
+    def last(sign, d):
+        zj = zi + sign * d
+        for way in (0, 1):
+            r_copy(zj, way, steps).wait_recv()
+        s = at.slot(zj, q)
+        mine = spans(acc.at[:, s], 0, cut)
+        add(mine, [spans(full_ref.at[way, steps - 2, zj], 0, cut) for way in (0, 1)], 2 * cut // 16)
+
+        def passed(way):
+            z_copy(zj, way).wait_recv()
+            add(mine, [spans(line_ref.at[way, zj], 0, cut)], 2 * cut // 16)
+
+        if sign >= 0:
+            pl.when(zi > 0)(lambda: passed(0))
+        if sign <= 0:
+            pl.when(zi < levels - 1)(lambda: passed(1))
+        if sign != 0:
+            z_copy(zj, 0 if sign > 0 else 1).start()
+
+    def done(sign, d):
+        zj = zi + sign * d
+        for way in (0, 1):
+            for step in range(1, steps + 1):
+                r_copy(zj, way, step).wait_send()
+        if sign != 0:
+            z_copy(zj, 0 if sign > 0 else 1).wait_send()
+
+    def low_z_copy(zj, way):
+        ref = acc.at[:, pl.ds(zj * pn, pn), lower]
+        return remote(ref, low_line.at[way, zj], lzs.at[way, zj], lzr.at[way, zj], along(way), b)
+
+    def low_passed(zj, way):
+        low_z_copy(zj, way).wait_recv()
+        per = (rows - cut) // 16
+
+        def piece(i):
+            return i // (pn * per), (i // per) % pn, (i % per) * 16
+
+        def into(i):
+            u, j, r = piece(i)
+            return acc.at[u, zj * pn + j, pl.ds(pl.multiple_of(cut + r, 16), 16)]
+
+        def come(i):
+            u, j, r = piece(i)
+            return low_line.at[way, zj, u, j, pl.ds(pl.multiple_of(r, 16), 16)]
+
+        add(into, [come], 2 * pn * per)
+
+    def low_start():
+        for zj in range(levels - 1, 0, -1):
+            pl.when(zi == 0)(lambda: low_z_copy(zj, 0).start())
+        for zj in range(levels - 1):
+            pl.when(zi == levels - 1)(lambda: low_z_copy(zj, 1).start())
+
+    def low_stage(a):
+        up, down = zi + levels - 1 - a, a - (levels - 1 - zi)
+
+        def from_below():
+            low_passed(up, 0)
+            pl.when(up > zi)(lambda: low_z_copy(up, 0).start())
+
+        def from_above():
+            low_passed(down, 1)
+            pl.when(down < zi)(lambda: low_z_copy(down, 1).start())
+
+        pl.when((zi > 0) & (up >= zi) & (up < levels))(from_below)
+        pl.when((zi < levels - 1) & (down >= 0) & (down <= zi))(from_above)
+
+    def low_r_copy(way, step):
+        target = at.slot(zi, q + (1 if way == 0 else -1) * (steps + 1 - step))
+        if step == 1:
+            src, dst = acc.at[way, target, lower], low_half.at[way]
+        else:
+            src, dst = acc.at[:, target, lower], low_full.at[way, step - 2]
+        to = at.right if way == 0 else at.left
+        return remote(src, dst, lrs.at[way, step - 1], lrr.at[way, step - 1], to, b)
+
+    def low_middle():
+        for step in range(1, steps):
+            for way in (0, 1):
+                low_r_copy(way, step).wait_recv()
+                s = at.slot(zi, q + (1 if way == 0 else -1) * (steps - step))
+                if step == 1:
+                    add(
+                        lambda i: acc.at[way, s, pl.ds(pl.multiple_of(cut + i * 16, 16), 16)],
+                        [lambda i: low_half.at[way, pl.ds(pl.multiple_of(i * 16, 16), 16)]],
+                        (rows - cut) // 16,
+                    )
+                else:
+                    add(
+                        spans(acc.at[:, s], cut, rows - cut),
+                        [spans(low_full.at[way, step - 2], 0, rows - cut)],
+                        2 * (rows - cut) // 16,
+                    )
+                low_r_copy(way, step + 1).start()
+
+    def low_last():
+        for way in (0, 1):
+            low_r_copy(way, steps).wait_recv()
+        add(
+            spans(acc.at[:, at.slot(zi, q)], cut, rows - cut),
+            [spans(low_full.at[way, steps - 2], 0, rows - cut) for way in (0, 1)],
+            2 * (rows - cut) // 16,
+        )
+
+    def each(action, d):
+        if d >= 0:
+            for sign in (0,) if d == 0 else (-1, 1):
+                guarded(present(zi, sign, d, levels), lambda: action(sign, d))
+
+    far = levels - 1
+    each(begin, far)
+    low_start()
+    each(begin, far - 1)
+    each(middle, far)
+    yield
+    for a in range(1, levels):
+        low_stage(a)
+        d = far - a
+        each(begin, d - 1)
+        each(middle, d)
+        yield
+        each(last, d + 1)
+    for way in (0, 1):
+        low_r_copy(way, 1).start()
+    low_middle()
+    each(last, 0)
+    low_last()
+    yield
+
+    def give(i, carry):
+        r = pl.ds(pl.multiple_of((i % (rows // 16)) * 16, 16), 16)
+        out_ref[i // (rows // 16), r] = acc[i // (rows // 16), at.slot(zi, q), r]
+        return carry
+
+    lax.fori_loop(0, 2 * (rows // 16), give, 0)
+    for d in range(levels):
+        each(done, d)
+    for zj in range(levels):
+        pl.when(zj > zi)(lambda: low_z_copy(zj, 0).wait_send())
+        pl.when(zj < zi)(lambda: low_z_copy(zj, 1).wait_send())
+    for way in (0, 1):
+        for step in range(1, steps + 1):
+            low_r_copy(way, step).wait_send()
+
+
 def scatter_parts(grid, levels, rows, width):
     blocks = 2 * (2 * levels * (grid.plane // 2 + 2) + levels * grid.plane)
     parts = 1
@@ -1004,7 +1235,7 @@
     lax.fori_loop(0, rows // step, one, 0)
 
 
-def return_task(at, x_ref, out_ref, mine, theirs, ls, ps, pr, ss, sr, fs, fr, given=None, fill=None, prepare=None):
+def return_task(at, x_ref, out_ref, mine, theirs, ls, ps, pr, ss, sr, fs, fr, given=None, fill=None, prepare=None, per=2):
     n, c, b = at.n, at.c, at.b
     half = n // 2
     to, frm = pairwise(n, c, b)
@@ -1049,7 +1280,7 @@
             else:
                 pl.when(b == 1)(lambda: out_copy(0).start())
                 pl.when(b == 0)(lambda: local.start())
-            if j % 2 == 1:
+            if j % per == per - 1:
                 yield
 
     def finish():
@@ -1237,7 +1468,7 @@
     return issue(), finish
 
 
-def open_kernel(grid, tokens, gain, qkv_parts, out_codes, small, gate_codes, up_codes, cid):
+def open_kernel(grid, tokens, gain, qkv_parts, out_codes, small, gate_codes, up_codes, rows_too, cid):
     x = tokens
     n, levels = grid.n, grid.planes // 2
     rows_d, width = qkv_parts.shape[1:]
@@ -1288,8 +1519,10 @@
             narrow_task([gate_ref, up_ref], [gl_ref, ul_ref], *refs.take(4)),
             tell_task(at, small_ref, all_ref, *refs.take(2)),
             share_task(at, [lambda to: w_ref.at[to % HEADS]], [view], *refs.take(len(ss))),
-            head_rows_task(at, o_ref, rows_ref, *refs.take(4)),
+            *([head_rows_task(at, o_ref, rows_ref, *refs.take(4))] if rows_too else []),
         )
+        if not rows_too:
+            rows_ref[...] = o_ref[...]
 
     codes_shape = (n * rows_d, width) if flat else (n, rows_d, width)
     return pl.pallas_call(
@@ -1298,13 +1531,13 @@
             jax.ShapeDtypeStruct(x.shape, BF16),
             jax.ShapeDtypeStruct((2, levels * grid.plane) + x.shape[1:], BF16),
             jax.ShapeDtypeStruct(codes_shape, BF16),
-            jax.ShapeDtypeStruct((copies,) + out_codes.shape, BF16),
+            jax.ShapeDtypeStruct((copies,) + out_codes.shape if rows_too else out_codes.shape, BF16),
             jax.ShapeDtypeStruct((n,) + small.shape, small.dtype),
             jax.ShapeDtypeStruct(gate_codes.shape, BF16),
             jax.ShapeDtypeStruct(up_codes.shape, BF16),
         ),
         in_specs=[INVMEM] * 5 + [ANY] * 2,
-        out_specs=(INVMEM,) + (ANY,) * 6,
+        out_specs=(INVMEM, ANY, ANY, ANY if rows_too else INVMEM) + (ANY,) * 3,
         scratch_shapes=[pltpu.VMEM(x.shape, BF16), dma(2)] + gs + ns + ts + ss + hs,
         compiler_params=params(cid, 50),
         name="open",
@@ -1435,7 +1668,7 @@
 
     def tasks(at, ins, outs, refs):
         made = [
-            return_task(at, ins[0], outs[0], *refs.take(len(rs))),
+            return_task(at, ins[0], outs[0], *refs.take(len(rs)), per=PER),
             head_return_task(at, ins[1], outs[1], *refs.take(len(hs))),
             pair_task(at, ins[2], outs[2], *refs.take(2)),
             gains_task(at, ins[3], outs[3], *refs.take(len(gs))),
@@ -1498,7 +1731,7 @@
     lax.fori_loop(0, rows // 16, one, 0)
 
 
-def attention_body(w, o, x_rows, put, cos_ref, sin_ref, start_ref, q_ref, k_ref, v_ref, a_ref, t_ref, block=256):
+def attention_body(w, o, x_rows, put, ready, cos_ref, sin_ref, start_ref, q_ref, k_ref, v_ref, a_ref, t_ref, block=256):
     length = q_ref.shape[0]
     for i in range(length // block):
         r = pl.ds(i * block, block)
@@ -1506,6 +1739,7 @@
         q_ref[r] = rotated(lin[:, :HEAD], cos_ref[r], sin_ref[r]).astype(BF16)
         k_ref[r] = rotated(lin[:, HEAD : 2 * HEAD], cos_ref[r], sin_ref[r]).astype(BF16)
         v_ref[r] = lin[:, 2 * HEAD :].astype(BF16)
+    ready()
     for i in range(length // block):
         r, keys = pl.ds(i * block, block), pl.ds(0, (i + 1) * block)
         e, _ = scores(q_ref[r], k_ref[keys], start_ref[r], i * block)
@@ -1627,6 +1861,7 @@
     length = seen.shape[0]
     block = 256
     here = block // rows
+    hs = head_rows_sems(grid)
 
     def kernel(
         x_ref, codes_ref, rows_ref, scale_ref, cos_ref, sin_ref, start_ref, tokens_ref, cot_ref, gate_ref, up_ref, down_ref,
@@ -1640,7 +1875,8 @@
         share_refs = refs.take(len(ss))
         weights = FeedWeights(at, group, units, None, None, down_ref, (wp_ref, wd_ref), refs.take(len(ws)))
         gather_refs = refs.take(len(gs))
-        x, xs, head_sems, cot_sems = refs.take(4)
+        x, xs, o_codes, head_sems, cot_sems = refs.take(5)
+        head_refs = refs.take(len(hs))
         loads, stores, compute = forward_chunks(weights, all_ref, pair_ref, part_ref, *refs.take(4))
         w = weights.pair.at[0, :, pl.ds(0, 3 * HEAD)]
         w_codes = weights.pair.at[1, :, pl.ds(0, 3 * HEAD)]
@@ -1662,17 +1898,24 @@
                 pl.ds(pl.multiple_of(j * rows_d, 16), rows_d), pl.ds(k * window, window)
             ]
 
+        heads, heads_finish = head_rows_task(at, rows_ref, o_codes, *head_refs)
+        run(heads)
         issue, finish = share_task(at, [source(gate_ref), source(up_ref)], [view(0), view(1)], *share_refs)
-        for _ in range(EARLY):
-            next(issue, None)
-        scale_rows(at.b, at.member, rows_ref, vec_ref[4:5], o, HEAD)
         load_w.wait()
         scale_rows(at.b, at.member, w_codes, scale_ref[...], w, D)
         keep_w = pltpu.make_async_copy(w, w_ref, head_sems.at[2])
         keep_o = pltpu.make_async_copy(o, o_ref, head_sems.at[3])
         keep_w.start()
-        keep_o.start()
         load_x.wait()
+
+        def ready():
+            heads_finish()
+            for _ in range(EARLY):
+                next(issue, None)
+            each = o_codes.shape[1]
+            for j in range(o_codes.shape[0]):
+                scale_rows(at.b, at.member, o_codes.at[j], vec_ref[4:5], o.at[pl.ds(j * each, each)], each)
+            keep_o.start()
 
         def put(i, value):
             first = i * here
@@ -1684,6 +1927,7 @@
             o,
             lambda i: xs[pl.ds(i * block, block)],
             put,
+            ready,
             cos_ref,
             sin_ref,
             start_ref,
@@ -1751,7 +1995,14 @@
         + ss
         + ws
         + gs
-        + [pltpu.VMEM(tokens.shape, BF16), pltpu.VMEM(seen.shape, BF16), dma(4), dma(2)]
+        + [
+            pltpu.VMEM(tokens.shape, BF16),
+            pltpu.VMEM(seen.shape, BF16),
+            pltpu.VMEM((n // HEADS,) + out_codes.shape, BF16),
+            dma(4),
+            dma(2),
+        ]
+        + hs
         + chunk_buffers(size, rows, D, 2 * window, D)
         + [dma(3)],
         compiler_params=params(cid, 62),
@@ -1767,7 +2018,7 @@
     group, rows, _ = mixed.shape
     units, window, _ = feed_windows(grid)
     size = feed_blocks(grid)
-    sc, gs = scatter_scratch(grid, levels, rows, D), level_sems(grid, levels)
+    sc, gs = split_scratch(grid, levels, rows, D), level_sems(grid, levels)
 
     def kernel(
         p_ref, mixed_ref, cot_ref, pair_ref, wp_ref, wd_ref, vec_ref,
@@ -1777,7 +2028,7 @@
         at = Place(grid, levels)
         mine, gather_refs = refs.take(len(sc)), refs.take(len(gs))
         raw, x, kept_out, wp, wd, fetch_sems, swap_sems = refs.take(7)
-        load = pltpu.make_async_copy(p_ref, mine[0], mine[4].at[0])
+        load = pltpu.make_async_copy(p_ref, mine[0], mine[7].at[0])
         load.start()
         fetch = [
             pltpu.make_async_copy(wp_ref, wp, fetch_sems.at[0]),
@@ -1790,7 +2041,7 @@
         load.wait()
         for copy in fetch:
             copy.start()
-        run(scatter_steps(at, raw, *mine))
+        run(split_scatter_steps(at, raw, *mine))
         gain_ref[...] = jnp.zeros_like(gain_ref)
 
         def norms(u, r):
@@ -2154,6 +2405,7 @@
     rows_d = D // n
     units, window, _ = feed_windows(grid)
 
+    whole = fits(grid, block) and parts == 1
     vectors = jnp.stack(
         [attention_gain, attention_post_gain, feed_gain, feed_post_gain, output_scale, down_scale]
     )
@@ -2172,6 +2424,7 @@
         small,
         gate_codes,
         up_codes,
+        not whole,
         1,
     )
     seen = seen.reshape(length, D)
@@ -2197,7 +2450,6 @@
     turn = angles(places_all, HEAD)
     cosine, sine = jnp.cos(turn), jnp.sin(turn)
     q_index = first_asked + jnp.arange(asked, dtype=jnp.int32)
-    whole = fits(grid, block) and parts == 1
     pair_scale = jnp.concatenate(
         [lax.dynamic_slice_in_dim(s, chip * units // 128 * 128, window) for s in (gate_scale, up_scale)]
     )[None]
@@ -2209,7 +2461,7 @@
             grid,
             seen,
             qkv_codes.reshape(D, 3 * HEAD),
-            out_codes.reshape(HEAD, D),
+            out_codes,
             qkv_scale[None],
             cosine,
             sine,

time: 854 us -> 845 us (0.989)
  Pallas kernels: 802 us -> 793 us
    pallas_call x1, Pallas kernels: 102 us -> 86 us  [open_kernel(): pl.pallas_call(kernel, out_shape=(jax.ShapeDtypeStruct(x.shape, BF16), ja...]
    pallas_call x1, Pallas kernels: 201 us -> 216 us  [forward_kernel(): pl.pallas_call(kernel, out_shape=(jax.ShapeDtypeStruct((D, 3 * HEAD), BF1...]
    pallas_call x1, Pallas kernels: 191 us -> 180 us  [turn_kernel(): pl.pallas_call(kernel, out_shape=(jax.ShapeDtypeStruct(mixed.shape, BF16)...]
where the time goes in v6:
time: 845 us; the launch traced here: 836 us
  Pallas kernels  793 us (94%)
  other arithmetic  21 us (2%)
  local copies, waits for them, and re-layouts  20.4 us (2%)
    pallas_call x1, Pallas kernels, forward_kernel(): pl.pallas_call(kernel, out_shape=(jax.ShapeDtypeStruct((D, 3 * HEAD), BF1...  216 us
    pallas_call x1, Pallas kernels, turn_kernel(): pl.pallas_call(kernel, out_shape=(jax.ShapeDtypeStruct(mixed.shape, BF16)...  180 us
    pallas_call x1, Pallas kernels, back_kernel(): pl.pallas_call(kernel, out_shape=(jax.ShapeDtypeStruct(mixed.shape, F32),...  179 us
    pallas_call x1, Pallas kernels, call(): pl.pallas_call(kernel, out_shape=(jax.ShapeDtypeStruct((2, rows, width),...  107 us
    pallas_call x1, Pallas kernels, open_kernel(): pl.pallas_call(kernel, out_shape=(jax.ShapeDtypeStruct(x.shape, BF16), ja...  86 us
    pallas_call x1, Pallas kernels, attention_backward(): pl.pallas_call(kernel, out_shape=(jax.ShapeDtypeStruct((length, D), BF16)...  25.2 us

profile of v6, /device:TPU:0, one launch (start us, length us, event | category | flops | bytes accessed | tf_op | source)
XLA Modules:
  0.0 836.4 jit_solution(8896536220312939283)
XLA Ops:
  0.8 0.9 dynamic_slice.22
  1.6 0.8 dynamic_slice.23
  2.4 0.8 dynamic_slice.24
  3.2 0.6 broadcast_in_dim.18.scale_ref
  3.8 0.7 scatter.4.small_ref
  4.4 0.8 dynamic_slice.26
  5.2 0.8 dynamic_slice.27
  6.0 0.6 broadcast_in_dim.19.ps_ref
  6.6 0.7 stack.28
  7.3 0.7 stack.29
  8.0 0.7 stack.24
  8.7 0.7 stack.25
  9.4 0.7 stack.26
  10.2 0.7 stack.27
  10.9 0.1 stack.30.gain_ref.vec_ref.refs_8_
  11.0 1.1 convert.21
  12.1 0.2 reshape.160
  12.5 0.2 reshape.161
  12.8 0.1 convert.16
  12.9 1.3 pad_maximum_fusion.w_ref
  14.3 0.3 copy-done.2
  14.7 86.0 %open.1 = (bf16[2,64,2304]{2,1,0:T(8,128)(2,1)S(1)}, bf16[2,8,64,2304]{3,2,1,0:T(8,128)(2,1)}, bf16[2304,768]{1,0:T(8,128)(2,1)}, bf16[128,2304]{1,0:T(8,128)(2,...) custom-call(bf16[2,64,2304]{2,1,0:T(8,128)(2,1)S(1)} %copy-done.2, ...), custom_call_target="tpu_custom_call" | custom-call | tf_op jit(solution)/shard_map/open/pallas_call | solution.py:1528
  100.6 0.8 copy-done.1
  101.4 0.8 copy-done.3
  102.4 0.5 reshape.162
  102.9 0.9 add_subtract_fusion.start_ref
  103.7 3.0 multiply_sine_fusion
  106.8 216.3 %forward.1 = (bf16[2304,768]{1,0:T(8,128)(2,1)}, bf16[256,2304]{1,0:T(8,128)(2,1)}, bf16[1024,256]{1,0:T(8,128)(2,1)}, bf16[1024,256]{1,0:T(8,128)(2,1)}, bf16[1...) custom-call(bf16[1024,2304]{1,0:T(8,128)(2,1)} %bitcast.32, ...), custom_call_target="tpu_custom_call" | custom-call | tf_op jit(solution)/shard_map/forward/pallas_call | solution.py:1973
  323.0 179.6 %turn.1 = (bf16[2,64,2304]{2,1,0:T(8,128)(2,1)}, f32[1,2304]{1,0:T(1,128)}, bf16[2,16,64,2304]{3,2,1,0:T(8,128)(2,1)}, bf16[2,16,64,2304]{3,2,1,0:T(8,128)(2,1)}...) custom-call(bf16[2,16,64,2304]{3,2,1,0:T(8,128)(2,1)} %get-tuple-element.77.p_ref, ...), custom_call_target="tpu_custom_call" | custom-call | tf_op jit(solution)/shard_map/turn/pallas_call | solution.py:2071
  502.7 179.2 %back.1 = (f32[2,64,2304]{2,1,0:T(8,128)}, f32[1,2304]{1,0:T(1,128)}, f32[1,2304]{1,0:T(1,128)}, bf16[2,8,64,2304]{3,2,1,0:T(8,128)(2,1)}, bf16[16,144,1280]{2,1,0:T(8,128)(2,1)}, /*index=5*/bf16[640,2304]{1,0:T(8,128)(2,1)}) custom-call(bf16[2,16,64,2304]{3,2,1,0:T(8,128)(2,1)} %get-tuple-element.84.p_ref, ...), custom_call_target="tpu_custom_call" | custom-call | tf_op jit(solution)/shard_map/back/pallas_call | solution.py:2214
  682.0 25.2 %attention_backward.1 = (bf16[1024,2304]{1,0:T(8,128)(2,1)}, bf16[2304,768]{1,0:T(8,128)(2,1)}, bf16[256,2304]{1,0:T(8,128)(2,1)}, f32[1,2304]{1,0:T(1,128)}) custom-call(bf16[1024,2304]{1,0:T(8,128)(2,1)} %bitcast.33, bf16[1024,2304]{1,0:T(8,128)(2,1)} %bitcast.35, bf16[2304,768]{1,0:T(8,128)(2,1)} %get-tuple-element.91.w_ref, ...), custom_call_target="tpu_custom_call" | custom-call | tf_op jit(solution)/shard_map/attention_backward/pallas_call | solution.py:1805
  707.2 1.4 pad_maximum_fusion.1.refs_4_
  708.6 1.7 constant_dynamic-slice_fusion.refs_3_
  710.3 107.1 %attention_back_sums.1 = (bf16[2,64,2304]{2,1,0:T(8,128)(2,1)}, bf16[16,144,768]{2,1,0:T(8,128)(2,1)}, bf16[2,128,2304]{2,1,0:T(8,128)(2,1)}, bf16[576,2304]{1,0...) custom-call(bf16[2,8,64,2304]{3,2,1,0:T(8,128)(2,1)} %bitcast.34, ...), custom_call_target="tpu_custom_call" | custom-call | tf_op jit(solution)/shard_map/attention_back_sums/pallas_call | solution.py:1582
  817.4 3.1 convert_reduce_fusion
  820.4 0.7 slice_reduce_fusion
  821.1 0.2 bitcast_reduce_fusion
  821.3 0.1 slice_bitcast_fusion
  821.4 1.1 copy.62
  822.6 0.1 slice_bitcast_fusion.1
  822.7 0.9 copy.64
  823.6 0.9 copy.63
  824.4 1.2 convert_reduce_fusion.1
  825.6 2.9 convert_element_type.31
  828.6 2.9 convert_element_type.32
  831.5 2.8 convert_element_type.33
  834.3 0.8 copy.69
  835.1 0.8 copy.70
  (47 shorter events, 0.5 us)
Async XLA Ops:
  0.6 11.8 %copy-start.11 = (s32[144,1024]{1,0:T(8,128)S(1)}, s32[144,1024]{1,0:T(8,128)}, u32[]{:S(2)}) copy-start(s32[144,1024]{1,0:T(8,128)} %param.29) | copy-start | bytes 1769476
  0.7 12.1 %copy-start.8 = (s32[144,2048]{1,0:T(8,128)S(1)}, s32[144,2048]{1,0:T(8,128)}, u32[]{:S(2)}) copy-start(s32[144,2048]{1,0:T(8,128)} %param.27) | copy-start | bytes 3538948
  11.0 3.4 copy-start
  12.7 1.5 copy-start.9
  12.9 1.8 copy-start.2
  100.6 0.8 copy-start.1
  101.4 0.8 copy-start.3
  681.9 25.3 %copy-start.15 = (f32[1,2304]{1,0:T(1,128)S(1)}, f32[1,2304]{1,0:T(1,128)}, u32[]{:S(2)}) copy-start(f32[1,2304]{1,0:T(1,128)} %get-tuple-element.105) | copy-start | bytes 27652
  681.9 25.3 %copy-start.16 = (f32[1,2304]{1,0:T(1,128)S(1)}, f32[1,2304]{1,0:T(1,128)}, u32[]{:S(2)}) copy-start(f32[1,2304]{1,0:T(1,128)} %get-tuple-element.104) | copy-start | bytes 27652
  681.9 25.3 %copy-start.17 = (f32[1,2304]{1,0:T(1,128)S(1)}, f32[1,2304]{1,0:T(1,128)}, u32[]{:S(2)}) copy-start(f32[1,2304]{1,0:T(1,128)} %get-tuple-element.103) | copy-start | bytes 27652
  681.9 26.6 %copy-start.7 = (bf16[640,2304]{1,0:T(8,128)(2,1)S(1)}, bf16[640,2304]{1,0:T(8,128)(2,1)}, u32[]{:S(2)}) copy-start(bf16[640,2304]{1,0:T(8,128)(2,1)} %get-tuple-element.101) | copy-start | bytes 8847364
  817.4 3.1 copy-start.14
  821.4 3.0 copy-start.10
  822.6 3.1 copy-start.6
  825.6 2.9 copy-start.5
  828.6 2.9 copy-start.4
  831.5 2.8 copy-start.12
  831.5 3.6 copy-start.13

commit v7 on v6

--- a/solution.py
+++ b/solution.py
@@ -141,7 +141,7 @@
     def z_copy(k, us, zj, sign):
         way = 0 if sign > 0 else 1
         ref = block(us, zj, q)
-        return remote(ref, ref, zs.at[k, way, zj], zr.at[k, way, zj], at.c + sign * pn, b)
+        return remote(ref, ref, zs.at[k, way, zj], zr.at[k, way, zj], (at.c + at.n + sign * pn) % at.n, b)
 
     def r_copy(k, us, zj, way, step, landing=False):
         away = step if landing else step - 1
@@ -260,7 +260,7 @@
 
     def z_copy(self, zj, way):
         at, ref = self.at, self.block(zj, self.at.q, None, self.first)
-        to = at.c + (at.pn if way == 0 else -at.pn)
+        to = (at.c + at.n + (at.pn if way == 0 else -at.pn)) % at.n
         return remote(ref, ref, self.zs.at[0, way, zj], self.zr.at[0, way, zj], to, at.b)
 
     def ring_copy(self, zj, way, step, landing, rows, send, recv):
@@ -280,7 +280,7 @@
     def low_z_copy(self, zj, way):
         at = self.at
         ref = self.out.at[:, pl.ds(zj * at.pn, at.pn), self.last]
-        to = at.c + (at.pn if way == 0 else -at.pn)
+        to = (at.c + at.n + (at.pn if way == 0 else -at.pn)) % at.n
         return remote(ref, ref, self.lzs.at[way, zj], self.lzr.at[way, zj], to, at.b)
 
     def begin(self):
@@ -722,7 +722,7 @@
 
     def z_copy(k, us, zj, way):
         u0, nu = us
-        to = at.c + (pn if way == 0 else -pn)
+        to = (at.c + at.n + (pn if way == 0 else -pn)) % at.n
         return remote(block(us, zj, q), line.at[way, zj, pl.ds(u0, nu)], zs.at[k, way, zj], zr.at[k, way, zj], to, b)
 
     def begin(k, us, sign, d):
@@ -872,7 +872,7 @@
         return lambda i: ref.at[i // per, pl.ds(pl.multiple_of(first + (i % per) * 16, 16), 16)]
 
     def along(way):
-        return at.c + (pn if way == 0 else -pn)
+        return (at.c + at.n + (pn if way == 0 else -pn)) % at.n
 
     def r_copy(zj, way, step):
         target = at.slot(zj, q + (1 if way == 0 else -1) * (steps + 1 - step))
@@ -1376,8 +1376,9 @@
     return [pltpu.VMEM(blocks, BF16), pltpu.VMEM(blocks, BF16)] + [dma(copies) for _ in range(7)]
 
 
-def pair_task(at, x_ref, out_ref, other, sems):
-    copy = at.sibling(x_ref, other, sems.at[0], sems.at[1])
+def pair_task(at, x_ref, first, out_ref, other, sems):
+    count = out_ref.shape[0]
+    copy = at.sibling(x_ref.at[pl.ds(pl.multiple_of(first, 16), count)], other, sems.at[0], sems.at[1])
 
     def issue():
         copy.start()
@@ -1388,10 +1389,11 @@
 
         def one(r, carry):
             rows = pl.ds(pl.multiple_of(r * 16, 16), 16)
-            out_ref[rows] = (x_ref[rows].astype(F32) + other[rows].astype(F32)).astype(out_ref.dtype)
+            mine = x_ref[pl.ds(pl.multiple_of(first + r * 16, 16), 16)]
+            out_ref[rows] = (mine.astype(F32) + other[rows].astype(F32)).astype(out_ref.dtype)
             return carry
 
-        lax.fori_loop(0, x_ref.shape[0] // 16, one, 0)
+        lax.fori_loop(0, count // 16, one, 0)
         copy.wait_send()
 
     return issue(), finish
@@ -1648,7 +1650,8 @@
 def attention_back_sums(grid, p, qkv_grad, out_grad, down_grad, gains, merged, cid):
     n, levels = grid.n, grid.planes // 2
     rs, hs = return_scratch(grid, qkv_grad.shape[1:]), head_return_scratch(grid, out_grad.shape[1:])
-    ps = [pltpu.VMEM(down_grad.shape, BF16), dma(2)]
+    units, _, _ = feed_windows(grid)
+    ps = [pltpu.VMEM((units, D), BF16), dma(2)]
     every = pltpu.VMEM((n,) + gains.shape, F32)
     gs = [pltpu.VMEM(gains.shape, F32), pltpu.VMEM(gains.shape, F32), every, dma(2)] + share_sems(grid, 1)
     us = assemble_scratch(grid) if merged else []
@@ -1659,7 +1662,7 @@
     shapes = (
         jax.ShapeDtypeStruct(qkv_grad.shape, BF16),
         jax.ShapeDtypeStruct(out_grad.shape, BF16),
-        jax.ShapeDtypeStruct(down_grad.shape, BF16),
+        jax.ShapeDtypeStruct((units, D), BF16),
         jax.ShapeDtypeStruct(gains.shape, F32),
     ) + (jax.ShapeDtypeStruct((D // n, FF), BF16),) * (2 if merged else 0)
     out_specs = (ANY, ANY, INVMEM, INVMEM) + ((ANY, ANY) if merged else ())
@@ -1670,7 +1673,7 @@
         made = [
             return_task(at, ins[0], outs[0], *refs.take(len(rs)), per=PER),
             head_return_task(at, ins[1], outs[1], *refs.take(len(hs))),
-            pair_task(at, ins[2], outs[2], *refs.take(2)),
+            pair_task(at, ins[2], (at.c * units) % 128, outs[2], *refs.take(2)),
             gains_task(at, ins[3], outs[3], *refs.take(len(gs))),
         ]
         if merged:
@@ -1756,12 +1759,20 @@
 
     def kernel(
         x_ref, g_ref, w_ref, o_ref, q_ref, k_ref, v_ref, a_ref, t_ref, vec_ref, cos_ref, sin_ref, start_ref,
-        part_ref, wg_ref, og_ref, gain_ref, xs, gs, dk, dv, low, sems,
+        part_ref, wg_ref, og_ref, gain_ref, xs, gs, w, part, wg, dk, dv, low, sems, out_sems,
     ):
+        load_w = pltpu.make_async_copy(w_ref, w, sems.at[2])
+        give_part = pltpu.make_async_copy(part, part_ref, sems.at[3])
+
+        def give_rows(j):
+            rows = pl.ds(pl.multiple_of(j * tile, tile), tile)
+            return pltpu.make_async_copy(wg.at[rows], wg_ref.at[rows], out_sems.at[j])
+
         load_g = pltpu.make_async_copy(g_ref, gs, sems.at[0])
         load_x = pltpu.make_async_copy(x_ref, xs, sems.at[1])
         load_g.start()
         load_x.start()
+        load_w.start()
         dk[...] = jnp.zeros_like(dk)
         dv[...] = jnp.zeros_like(dv)
         load_g.wait()
@@ -1782,25 +1793,31 @@
             low[r, HEAD : 2 * HEAD] = rotated(dk[r] * SCALE, cos_ref[r], -sin_ref[r]).astype(BF16)
             low[r, 2 * HEAD :] = dv[r].astype(BF16)
         load_x.wait()
+        load_w.wait()
         gain_ref[...] = jnp.zeros_like(gain_ref)
 
         def parts(i, carry):
             r = pl.ds(pl.multiple_of(i * block, block), block)
-            term = dot_t(low[r], w_ref[...])
-            part_ref[r] = term.astype(BF16)
+            term = dot_t(low[r], w[...])
+            part[r] = term.astype(BF16)
             gain_ref[...] += jnp.sum(term * xs[r].astype(F32), axis=0, keepdims=True)
             return carry
 
         lax.fori_loop(0, length // block, parts, 0)
+        give_part.start()
         gain_ref[...] = gain_ref[...] / vec_ref[0:1]
 
         def grads(j, carry):
             cols = pl.ds(pl.multiple_of(j * tile, tile), tile)
-            wg_ref[cols] = t_dot(xs[:, cols], low[...]).astype(BF16)
+            wg[cols] = t_dot(xs[:, cols], low[...]).astype(BF16)
+            give_rows(j).start()
             og_ref[:, cols] = t_dot(a_ref[...], gs[:, cols]).astype(BF16)
             return carry
 
         lax.fori_loop(0, D // tile, grads, 0)
+        give_part.wait()
+        for j in range(D // tile):
+            give_rows(j).wait()
 
     return pl.pallas_call(
         kernel,
@@ -1810,15 +1827,19 @@
             jax.ShapeDtypeStruct((HEAD, D), BF16),
             jax.ShapeDtypeStruct((1, D), F32),
         ),
-        in_specs=[ANY, ANY] + [INVMEM] * 11,
-        out_specs=(INVMEM,) * 4,
+        in_specs=[ANY, ANY, ANY] + [INVMEM] * 10,
+        out_specs=(ANY, ANY, INVMEM, INVMEM),
         scratch_shapes=[
             pltpu.VMEM(seen.shape, BF16),
             pltpu.VMEM(seen.shape, BF16),
+            pltpu.VMEM((D, 3 * HEAD), BF16),
+            pltpu.VMEM((length, D), BF16),
+            pltpu.VMEM((D, 3 * HEAD), BF16),
             pltpu.VMEM((length, HEAD), F32),
             pltpu.VMEM((length, HEAD), F32),
             pltpu.VMEM((length, 3 * HEAD), BF16),
-            dma(2),
+            dma(4),
+            dma(D // tile),
         ],
         compiler_params=pltpu.CompilerParams(vmem_limit_bytes=60 * 2**20),
         name="attention_backward",
@@ -2501,7 +2522,6 @@
 
         out_part = spread(dot(attended_low, out_matrix).astype(BF16))
     first_column = chip * units // 128 * 128
-    inset = chip * units - first_column
     if whole:
         output, grad_post_feed, down_low, second_part, pair_low, hidden = turn_kernel(
             grid, down_part, mixed, cotangent, gate_up, pair_matrices, down_matrices, vectors, 3
@@ -2552,7 +2572,6 @@
         _, pull_post = jax.vjp(normed, attention_raw, attention_post_gain)
         grad_attention, grad_post_attention = pull_post(grad_mixed)
         attention_low = gather(grid, grad_attention.astype(BF16), grid.planes // 2, 6)
-    down_grad = lax.dynamic_slice(down_grad, (inset, 0), (units, D))
 
     attention_low = attention_low.reshape(length, D)
     if whole:

time: 845 us -> 841 us (level)
  no operation moved by 1% of the time
where the time goes in v7:
time: 841 us; the launch traced here: 832 us
  Pallas kernels  791 us (94%)
  other arithmetic  21 us (2%)
  local copies, waits for them, and re-layouts  18.8 us (2%)
    pallas_call x1, Pallas kernels, forward_kernel(): pl.pallas_call(kernel, out_shape=(jax.ShapeDtypeStruct((D, 3 * HEAD), BF1...  216 us
    pallas_call x1, Pallas kernels, turn_kernel(): pl.pallas_call(kernel, out_shape=(jax.ShapeDtypeStruct(mixed.shape, BF16)...  180 us
    pallas_call x1, Pallas kernels, back_kernel(): pl.pallas_call(kernel, out_shape=(jax.ShapeDtypeStruct(mixed.shape, F32),...  179 us
    pallas_call x1, Pallas kernels, call(): pl.pallas_call(kernel, out_shape=(jax.ShapeDtypeStruct((2, rows, width),...  107 us
    pallas_call x1, Pallas kernels, open_kernel(): pl.pallas_call(kernel, out_shape=(jax.ShapeDtypeStruct(x.shape, BF16), ja...  86 us
    pallas_call x1, Pallas kernels, attention_backward(): pl.pallas_call(kernel, out_shape=(jax.ShapeDtypeStruct((length, D), BF16)...  23.1 us

profile of v7, /device:TPU:0, one launch (start us, length us, event | category | flops | bytes accessed | tf_op | source)
XLA Modules:
  0.0 832.1 jit_solution(10920143052613714014)
XLA Ops:
  0.8 0.9 dynamic_slice.19
  1.6 0.8 dynamic_slice.20
  2.4 0.8 dynamic_slice.21
  3.2 0.6 broadcast_in_dim.18.scale_ref
  3.8 0.7 scatter.4.small_ref
  4.4 0.8 dynamic_slice.23
  5.2 0.8 dynamic_slice.24
  6.0 0.6 broadcast_in_dim.19.ps_ref
  6.6 0.7 stack.28
  7.3 0.7 stack.29
  8.0 0.7 stack.24
  8.7 0.7 stack.25
  9.4 0.7 stack.26
  10.2 0.7 stack.27
  10.9 0.1 stack.30.gain_ref.vec_ref.refs_8_
  11.0 1.1 convert.21
  12.1 0.2 reshape.160
  12.5 0.2 reshape.161
  12.8 0.1 convert.16
  12.9 1.3 pad_maximum_fusion.w_ref
  14.3 0.3 copy-done.2
  14.6 86.0 %open.1 = (bf16[2,64,2304]{2,1,0:T(8,128)(2,1)S(1)}, bf16[2,8,64,2304]{3,2,1,0:T(8,128)(2,1)}, bf16[2304,768]{1,0:T(8,128)(2,1)}, bf16[128,2304]{1,0:T(8,128)(2,...) custom-call(bf16[2,64,2304]{2,1,0:T(8,128)(2,1)S(1)} %copy-done.2, ...), custom_call_target="tpu_custom_call" | custom-call | tf_op jit(solution)/shard_map/open/pallas_call | solution.py:1530
  100.6 0.8 copy-done.1
  101.4 0.8 copy-done.3
  102.3 0.1 convert_element_type.29
  102.4 0.5 reshape.162
  102.9 0.9 add_subtract_fusion.start_ref
  103.7 3.0 multiply_sine_fusion
  106.8 216.3 %forward.1 = (bf16[2304,768]{1,0:T(8,128)(2,1)}, bf16[256,2304]{1,0:T(8,128)(2,1)}, bf16[1024,256]{1,0:T(8,128)(2,1)}, bf16[1024,256]{1,0:T(8,128)(2,1)}, bf16[1...) custom-call(bf16[1024,2304]{1,0:T(8,128)(2,1)} %bitcast.32, ...), custom_call_target="tpu_custom_call" | custom-call | tf_op jit(solution)/shard_map/forward/pallas_call | solution.py:1994
  323.0 179.6 %turn.1 = (bf16[2,64,2304]{2,1,0:T(8,128)(2,1)}, f32[1,2304]{1,0:T(1,128)}, bf16[2,16,64,2304]{3,2,1,0:T(8,128)(2,1)}, bf16[2,16,64,2304]{3,2,1,0:T(8,128)(2,1)}...) custom-call(bf16[2,16,64,2304]{3,2,1,0:T(8,128)(2,1)} %get-tuple-element.77.p_ref, ...), custom_call_target="tpu_custom_call" | custom-call | tf_op jit(solution)/shard_map/turn/pallas_call | solution.py:2092
  502.7 179.2 %back.1 = (f32[2,64,2304]{2,1,0:T(8,128)}, f32[1,2304]{1,0:T(1,128)}, f32[1,2304]{1,0:T(1,128)}, bf16[2,8,64,2304]{3,2,1,0:T(8,128)(2,1)}, bf16[16,144,1280]{2,1,0:T(8,128)(2,1)}, /*index=5*/bf16[640,2304]{1,0:T(8,128)(2,1)}) custom-call(bf16[2,16,64,2304]{3,2,1,0:T(8,128)(2,1)} %get-tuple-element.84.p_ref, ...), custom_call_target="tpu_custom_call" | custom-call | tf_op jit(solution)/shard_map/back/pallas_call | solution.py:2235
  681.9 23.1 %attention_backward.1 = (bf16[1024,2304]{1,0:T(8,128)(2,1)}, bf16[2304,768]{1,0:T(8,128)(2,1)}, bf16[256,2304]{1,0:T(8,128)(2,1)}, f32[1,2304]{1,0:T(1,128)}) custom-call(bf16[1024,2304]{1,0:T(8,128)(2,1)} %bitcast.33, bf16[1024,2304]{1,0:T(8,128)(2,1)} %bitcast.35, bf16[2304,768]{1,0:T(8,128)(2,1)} %get-tuple-element.91.w_ref, ...), custom_call_target="tpu_custom_call" | custom-call | tf_op jit(solution)/shard_map/attention_backward/pallas_call | solution.py:1822
  705.0 1.4 pad_maximum_fusion.1.refs_4_
  706.4 106.7 %attention_back_sums.1 = (bf16[2,64,2304]{2,1,0:T(8,128)(2,1)}, bf16[16,144,768]{2,1,0:T(8,128)(2,1)}, bf16[2,128,2304]{2,1,0:T(8,128)(2,1)}, bf16[576,2304]{1,0...) custom-call(bf16[2,8,64,2304]{3,2,1,0:T(8,128)(2,1)} %bitcast.34, ...), custom_call_target="tpu_custom_call" | custom-call | tf_op jit(solution)/shard_map/attention_back_sums/pallas_call | solution.py:1584
  813.1 3.1 convert_reduce_fusion
  816.2 0.7 slice_reduce_fusion
  816.8 0.2 bitcast_reduce_fusion
  817.0 0.1 slice_bitcast_fusion
  817.1 1.1 copy.62
  818.3 0.1 slice_bitcast_fusion.1
  818.4 0.9 copy.64
  819.3 0.9 copy.63
  820.2 1.2 convert_reduce_fusion.1
  821.3 2.9 convert_element_type.31
  824.3 2.9 convert_element_type.32
  827.2 2.8 convert_element_type.33
  830.0 0.8 copy.69
  830.8 0.8 copy.70
  (44 shorter events, 0.5 us)
Async XLA Ops:
  0.6 11.8 %copy-start.10 = (s32[144,1024]{1,0:T(8,128)S(1)}, s32[144,1024]{1,0:T(8,128)}, u32[]{:S(2)}) copy-start(s32[144,1024]{1,0:T(8,128)} %param.29) | copy-start | bytes 1769476
  0.7 12.1 %copy-start.7 = (s32[144,2048]{1,0:T(8,128)S(1)}, s32[144,2048]{1,0:T(8,128)}, u32[]{:S(2)}) copy-start(s32[144,2048]{1,0:T(8,128)} %param.27) | copy-start | bytes 3538948
  11.0 3.4 copy-start
  12.7 1.5 copy-start.8
  12.9 1.8 copy-start.2
  100.6 0.8 copy-start.1
  101.4 0.8 copy-start.3
  681.9 23.1 %copy-start.14 = (f32[1,2304]{1,0:T(1,128)S(1)}, f32[1,2304]{1,0:T(1,128)}, u32[]{:S(2)}) copy-start(f32[1,2304]{1,0:T(1,128)} %get-tuple-element.105) | copy-start | bytes 27652
  681.9 23.1 %copy-start.15 = (f32[1,2304]{1,0:T(1,128)S(1)}, f32[1,2304]{1,0:T(1,128)}, u32[]{:S(2)}) copy-start(f32[1,2304]{1,0:T(1,128)} %get-tuple-element.104) | copy-start | bytes 27652
  681.9 23.1 %copy-start.16 = (f32[1,2304]{1,0:T(1,128)S(1)}, f32[1,2304]{1,0:T(1,128)}, u32[]{:S(2)}) copy-start(f32[1,2304]{1,0:T(1,128)} %get-tuple-element.103) | copy-start | bytes 27652
  813.1 3.1 copy-start.13
  817.1 3.0 copy-start.9
  818.3 3.1 copy-start.6
  821.3 2.9 copy-start.5
  824.3 2.9 copy-start.4
  827.2 2.8 copy-start.11
  827.2 3.6 copy-start.12

commit v8 on v7

--- a/solution.py
+++ b/solution.py
@@ -1755,7 +1755,7 @@
 
 def attention_backward(seen, grad, w, o, q, k, v, attended, totals, vectors, cosine, sine, start):
     length = seen.shape[0]
-    block, tile = 256, 256
+    block, tile = 256, 768
 
     def kernel(
         x_ref, g_ref, w_ref, o_ref, q_ref, k_ref, v_ref, a_ref, t_ref, vec_ref, cos_ref, sin_ref, start_ref,

time: 841 us -> 840 us (level)
  no operation moved by 1% of the time
where the time goes in v8:
time: 840 us; the launch traced here: 831 us
  Pallas kernels  790 us (94%)
  other arithmetic  21 us (2%)
  local copies, waits for them, and re-layouts  18.8 us (2%)
    pallas_call x1, Pallas kernels, forward_kernel(): pl.pallas_call(kernel, out_shape=(jax.ShapeDtypeStruct((D, 3 * HEAD), BF1...  216 us
    pallas_call x1, Pallas kernels, turn_kernel(): pl.pallas_call(kernel, out_shape=(jax.ShapeDtypeStruct(mixed.shape, BF16)...  180 us
    pallas_call x1, Pallas kernels, back_kernel(): pl.pallas_call(kernel, out_shape=(jax.ShapeDtypeStruct(mixed.shape, F32),...  179 us
    pallas_call x1, Pallas kernels, call(): pl.pallas_call(kernel, out_shape=(jax.ShapeDtypeStruct((2, rows, width),...  107 us
    pallas_call x1, Pallas kernels, open_kernel(): pl.pallas_call(kernel, out_shape=(jax.ShapeDtypeStruct(x.shape, BF16), ja...  86 us
    pallas_call x1, Pallas kernels, attention_backward(): pl.pallas_call(kernel, out_shape=(jax.ShapeDtypeStruct((length, D), BF16)...  22.1 us

profile of v8, /device:TPU:0, one launch (start us, length us, event | category | flops | bytes accessed | tf_op | source)
XLA Modules:
  0.0 831.1 jit_solution(10180396574601910612)
XLA Ops:
  0.8 0.9 dynamic_slice.19
  1.6 0.8 dynamic_slice.20
  2.4 0.8 dynamic_slice.21
  3.2 0.6 broadcast_in_dim.18.scale_ref
  3.8 0.7 scatter.4.small_ref
  4.4 0.8 dynamic_slice.23
  5.2 0.8 dynamic_slice.24
  6.0 0.6 broadcast_in_dim.19.ps_ref
  6.6 0.7 stack.28
  7.3 0.7 stack.29
  8.0 0.7 stack.24
  8.7 0.7 stack.25
  9.4 0.7 stack.26
  10.2 0.7 stack.27
  10.9 0.1 stack.30.gain_ref.vec_ref.refs_8_
  11.0 1.1 convert.21
  12.1 0.2 reshape.160
  12.5 0.2 reshape.161
  12.8 0.1 convert.16
  12.9 1.3 pad_maximum_fusion.w_ref
  14.3 0.3 copy-done.2
  14.6 86.0 %open.1 = (bf16[2,64,2304]{2,1,0:T(8,128)(2,1)S(1)}, bf16[2,8,64,2304]{3,2,1,0:T(8,128)(2,1)}, bf16[2304,768]{1,0:T(8,128)(2,1)}, bf16[128,2304]{1,0:T(8,128)(2,...) custom-call(bf16[2,64,2304]{2,1,0:T(8,128)(2,1)S(1)} %copy-done.2, ...), custom_call_target="tpu_custom_call" | custom-call | tf_op jit(solution)/shard_map/open/pallas_call | solution.py:1530
  100.6 0.8 copy-done.1
  101.4 0.8 copy-done.3
  102.3 0.1 convert_element_type.29
  102.4 0.5 reshape.162
  102.9 0.9 add_subtract_fusion.start_ref
  103.7 3.0 multiply_sine_fusion
  106.8 216.3 %forward.1 = (bf16[2304,768]{1,0:T(8,128)(2,1)}, bf16[256,2304]{1,0:T(8,128)(2,1)}, bf16[1024,256]{1,0:T(8,128)(2,1)}, bf16[1024,256]{1,0:T(8,128)(2,1)}, bf16[1...) custom-call(bf16[1024,2304]{1,0:T(8,128)(2,1)} %bitcast.32, ...), custom_call_target="tpu_custom_call" | custom-call | tf_op jit(solution)/shard_map/forward/pallas_call | solution.py:1994
  323.0 179.6 %turn.1 = (bf16[2,64,2304]{2,1,0:T(8,128)(2,1)}, f32[1,2304]{1,0:T(1,128)}, bf16[2,16,64,2304]{3,2,1,0:T(8,128)(2,1)}, bf16[2,16,64,2304]{3,2,1,0:T(8,128)(2,1)}...) custom-call(bf16[2,16,64,2304]{3,2,1,0:T(8,128)(2,1)} %get-tuple-element.77.p_ref, ...), custom_call_target="tpu_custom_call" | custom-call | tf_op jit(solution)/shard_map/turn/pallas_call | solution.py:2092
  502.7 179.2 %back.1 = (f32[2,64,2304]{2,1,0:T(8,128)}, f32[1,2304]{1,0:T(1,128)}, f32[1,2304]{1,0:T(1,128)}, bf16[2,8,64,2304]{3,2,1,0:T(8,128)(2,1)}, bf16[16,144,1280]{2,1,0:T(8,128)(2,1)}, /*index=5*/bf16[640,2304]{1,0:T(8,128)(2,1)}) custom-call(bf16[2,16,64,2304]{3,2,1,0:T(8,128)(2,1)} %get-tuple-element.84.p_ref, ...), custom_call_target="tpu_custom_call" | custom-call | tf_op jit(solution)/shard_map/back/pallas_call | solution.py:2235
  681.9 22.1 %attention_backward.1 = (bf16[1024,2304]{1,0:T(8,128)(2,1)}, bf16[2304,768]{1,0:T(8,128)(2,1)}, bf16[256,2304]{1,0:T(8,128)(2,1)}, f32[1,2304]{1,0:T(1,128)}) custom-call(bf16[1024,2304]{1,0:T(8,128)(2,1)} %bitcast.33, bf16[1024,2304]{1,0:T(8,128)(2,1)} %bitcast.35, bf16[2304,768]{1,0:T(8,128)(2,1)} %get-tuple-element.91.w_ref, ...), custom_call_target="tpu_custom_call" | custom-call | tf_op jit(solution)/shard_map/attention_backward/pallas_call | solution.py:1822
  704.0 1.4 pad_maximum_fusion.1.refs_4_
  705.4 106.7 %attention_back_sums.1 = (bf16[2,64,2304]{2,1,0:T(8,128)(2,1)}, bf16[16,144,768]{2,1,0:T(8,128)(2,1)}, bf16[2,128,2304]{2,1,0:T(8,128)(2,1)}, bf16[576,2304]{1,0...) custom-call(bf16[2,8,64,2304]{3,2,1,0:T(8,128)(2,1)} %bitcast.34, ...), custom_call_target="tpu_custom_call" | custom-call | tf_op jit(solution)/shard_map/attention_back_sums/pallas_call | solution.py:1584
  812.1 3.1 convert_reduce_fusion
  815.1 0.7 slice_reduce_fusion
  815.8 0.2 bitcast_reduce_fusion
  816.0 0.1 slice_bitcast_fusion
  816.1 1.1 copy.62
  817.2 0.1 slice_bitcast_fusion.1
  817.4 0.9 copy.64
  818.2 0.9 copy.63
  819.1 1.2 convert_reduce_fusion.1
  820.3 2.9 convert_element_type.31
  823.3 2.9 convert_element_type.32
  826.2 2.8 convert_element_type.33
  829.0 0.8 copy.69
  829.8 0.8 copy.70
  (44 shorter events, 0.5 us)
Async XLA Ops:
  0.6 11.8 %copy-start.10 = (s32[144,1024]{1,0:T(8,128)S(1)}, s32[144,1024]{1,0:T(8,128)}, u32[]{:S(2)}) copy-start(s32[144,1024]{1,0:T(8,128)} %param.29) | copy-start | bytes 1769476
  0.7 12.1 %copy-start.7 = (s32[144,2048]{1,0:T(8,128)S(1)}, s32[144,2048]{1,0:T(8,128)}, u32[]{:S(2)}) copy-start(s32[144,2048]{1,0:T(8,128)} %param.27) | copy-start | bytes 3538948
  11.0 3.4 copy-start
  12.7 1.5 copy-start.8
  12.9 1.8 copy-start.2
  100.6 0.8 copy-start.1
  101.4 0.8 copy-start.3
  681.9 22.1 %copy-start.14 = (f32[1,2304]{1,0:T(1,128)S(1)}, f32[1,2304]{1,0:T(1,128)}, u32[]{:S(2)}) copy-start(f32[1,2304]{1,0:T(1,128)} %get-tuple-element.105) | copy-start | bytes 27652
  681.9 22.1 %copy-start.15 = (f32[1,2304]{1,0:T(1,128)S(1)}, f32[1,2304]{1,0:T(1,128)}, u32[]{:S(2)}) copy-start(f32[1,2304]{1,0:T(1,128)} %get-tuple-element.104) | copy-start | bytes 27652
  681.9 22.1 %copy-start.16 = (f32[1,2304]{1,0:T(1,128)S(1)}, f32[1,2304]{1,0:T(1,128)}, u32[]{:S(2)}) copy-start(f32[1,2304]{1,0:T(1,128)} %get-tuple-element.103) | copy-start | bytes 27652
  812.0 3.1 copy-start.13
  816.1 3.0 copy-start.9
  817.2 3.1 copy-start.6
  820.3 2.9 copy-start.5
  823.3 2.9 copy-start.4
  826.2 2.8 copy-start.11
  826.2 3.6 copy-start.12
